TPU v7x, 32 devices: a whole 2x2x4 slice. The times are simulated.
32 devices in a mesh: dp: 16 (over z, x, core), mp: 2 (over y).
Axes of the slice: x: 2, y: 2, z: 4, core: 2. Of those that a mesh axis runs over, the one named last changes fastest.
Arguments:
- tokens: bfloat16 [48, 512, 768], P('dp', 'mp'), may hold values from -6 to 6
- segment_ids: int32 [48, 512], P('dp'), may hold values from 0 to 3, never falling along the last dimension, each value on 1 to 256 neighbouring positions
- out_grad: bfloat16 [48, 512, 768], P('dp', 'mp'), may hold values from -6 to 6
- t_qkv: bfloat16 [3, 768, 768], P(None, 'dp', 'mp'), may hold values from -0.21875 to 0.21875
- t_qv_bias: bfloat16 [2, 768], P(None, 'mp'), may hold values from -3 to 3
- t_out: bfloat16 [768, 768], P('mp', 'dp'), may hold values from -2 to 2
- t_up: bfloat16 [768, 3072], P('dp', 'mp'), may hold values from -0.21875 to 0.21875
- t_up_bias: bfloat16 [3072], P('mp'), may hold values from -3 to 3
- t_down: bfloat16 [3072, 768], P('mp', 'dp'), may hold values from -0.21875 to 0.21875
- t_gains: bfloat16 [2, 768], P(None, 'dp'), may hold values from 0.5 to 1.5
- t_shifts: bfloat16 [4, 768], P(None, 'dp'), may hold values from -3 to 3
- s_qkv: bfloat16 [3, 768, 384], P(None, 'dp', 'mp'), may hold values from -0.21875 to 0.21875
- s_qv_bias: bfloat16 [2, 384], P(None, 'mp'), may hold values from -3 to 3
- s_out: bfloat16 [384, 768], P('mp', 'dp'), may hold values from -3 to 3
- s_up: bfloat16 [768, 1536], P('dp', 'mp'), may hold values from -0.21875 to 0.21875
- s_up_bias: bfloat16 [1536], P('mp'), may hold values from -3 to 3
- s_down: bfloat16 [1536, 768], P('mp', 'dp'), may hold values from -0.3125 to 0.3125
- s_gains: bfloat16 [2, 768], P(None, 'dp'), may hold values from 0.5 to 1.5
- s_shifts: bfloat16 [4, 768], P(None, 'dp'), may hold values from -3 to 3
Outputs:
- output: float32 [48, 512, 768], P('dp', 'mp')
- input_grad: float32 [48, 512, 768], P('dp', 'mp')
- grad_t_qkv: float32 [3, 768, 768], P(None, 'dp', 'mp')
- grad_t_qv_bias: float32 [2, 768], P(None, 'mp')
- grad_t_out: float32 [768, 768], P('mp', 'dp')
- grad_t_up: float32 [768, 3072], P('dp', 'mp')
- grad_t_up_bias: float32 [3072], P('mp')
- grad_t_down: float32 [3072, 768], P('mp', 'dp')
- grad_t_gains: float32 [2, 768], P(None, 'dp')
- grad_t_shifts: float32 [4, 768], P(None, 'dp')
- grad_s_qkv: float32 [3, 768, 384], P(None, 'dp', 'mp')
- grad_s_qv_bias: float32 [2, 384], P(None, 'mp')
- grad_s_out: float32 [384, 768], P('mp', 'dp')
- grad_s_up: float32 [768, 1536], P('dp', 'mp')
- grad_s_up_bias: float32 [1536], P('mp')
- grad_s_down: float32 [1536, 768], P('mp', 'dp')
- grad_s_gains: float32 [2, 768], P(None, 'dp')
- grad_s_shifts: float32 [4, 768], P(None, 'dp')
Inputs may be any that keep to these rules, and one draw needn't show every extreme that they name: `segment_ids`: segment numbers never fall along a row; a segment holds at most 256 positions of one row.
All inputs are finite; a program needn't handle non-finite values.
Results may differ from a plain program's by a relative error of at most 0.035.
Values may be sent and summed in bfloat16 or wider, within the bound.
No kernel may reach another device: no remote copies, remote signals or barrier semaphores. Data moves between devices by JAX's collectives and lax.ppermute only.
A program may use at most 256 MiB of HBM per device.

v0:
```python
import functools
import math

import jax
import jax.numpy as jnp
from jax import lax
from jax.experimental import pallas as pl
from jax.experimental.pallas import tpu as pltpu
from jax.sharding import PartitionSpec as P

HEAD_DIM = 64
LOW = jnp.bfloat16
F32 = jnp.float32


def ring_of(count):
    return list(range(0, count, 2)) + list(range(1, count, 2))[::-1]


def swap_y(value):
    return lax.ppermute(value, "mp", [(0, 1), (1, 0)])


def swap_x(value):
    n = lax.axis_size("dp")
    return lax.ppermute(value, "dp", [(i, i ^ 2) for i in range(n)])


def swap_core(value):
    n = lax.axis_size("dp")
    return lax.ppermute(value, "dp", [(i, i ^ 1) for i in range(n)])


def ring_shift(value, step):
    count = lax.axis_size("dp") // 4
    ring = ring_of(count)
    pairs = []
    for place in range(count):
        for low in range(4):
            pairs.append((ring[place] * 4 + low, ring[(place + step) % count] * 4 + low))
    return lax.ppermute(value, "dp", pairs)


def feature_order(width):
    n = lax.axis_size("dp")
    count, rows = n // 4, width // n
    me = lax.axis_index("dp")
    z, x, core = me // 4, (me // 2) % 2, me % 2
    place = jnp.where(z % 2 == 0, z // 2, count - 1 - z // 2)
    at = lax.iota(jnp.int32, width)
    row = at % rows
    back = (at // rows) % count
    x_rel = (at // (rows * count)) % 2
    core_rel = at // (rows * count * 2)
    from_place = (place - back + count) % count
    half = (count + 1) // 2
    z_abs = jnp.where(from_place < half, 2 * from_place, 2 * (count - 1 - from_place) + 1)
    block = z_abs * 4 + (x ^ x_rel) * 2 + (core ^ core_rel)
    return block * rows + row


def after(value, *others):
    return lax.optimization_barrier((value, others))[0]


VMEM_BYTES = 48 << 20
TILE = 256


def dot(left, right, left_at, right_at):
    return lax.dot_general(
        left, right, (((left_at,), (right_at,)), ((), ())), preferred_element_type=F32
    )


def call(body, steps, inputs, outputs, scratch, flops, exps=0):
    size = lambda shape, dtype: math.prod(shape) * jnp.dtype(dtype).itemsize
    moved = sum(size(array.shape, array.dtype) for array, _, _ in inputs)
    moved += sum(size(shape, dtype) for shape, dtype, _, _ in outputs)
    return pl.pallas_call(
        body,
        grid=(steps,),
        in_specs=[pl.BlockSpec(block, index) for _, block, index in inputs],
        out_specs=[pl.BlockSpec(block, index) for _, _, block, index in outputs],
        out_shape=[jax.ShapeDtypeStruct(shape, dtype) for shape, dtype, _, _ in outputs],
        scratch_shapes=scratch,
        compiler_params=pltpu.CompilerParams(
            dimension_semantics=("arbitrary",), vmem_limit_bytes=VMEM_BYTES
        ),
        cost_estimate=pl.CostEstimate(
            flops=flops // 2, bytes_accessed=moved // 2, transcendentals=exps // 2
        ),
    )(*[array for array, _, _ in inputs])


def moves(arrays, shapes, copies):
    def body(*refs):
        for source, taken, target, place in copies:
            refs[len(arrays) + target][place] = refs[source][taken]

    moved = 2 * sum(math.prod(shape) for shape in shapes)
    return pl.pallas_call(
        body,
        out_shape=[jax.ShapeDtypeStruct(shape, LOW) for shape in shapes],
        compiler_params=pltpu.CompilerParams(vmem_limit_bytes=VMEM_BYTES),
        cost_estimate=pl.CostEstimate(flops=0, bytes_accessed=moved, transcendentals=0),
    )(*arrays)


def pack(straight, turned, shapes, copies):
    count = len(straight)

    def body(*refs):
        outs = refs[count + len(turned) :]
        rows = turned[0].shape[1]
        at = lambda axis: lax.broadcasted_iota(jnp.int32, (rows, rows), axis)
        same = jnp.where(at(0) == at(1), 1.0, 0.0).astype(LOW)
        for source, taken, target, place in copies:
            if source < count:
                outs[target][place] = refs[source][taken]
            else:
                outs[target][place] = dot(same, refs[source][...], 1, 1).astype(LOW)

    moved = 2 * sum(math.prod(shape) for shape in shapes)
    return pl.pallas_call(
        body,
        out_shape=[jax.ShapeDtypeStruct(shape, LOW) for shape in shapes],
        compiler_params=pltpu.CompilerParams(vmem_limit_bytes=VMEM_BYTES),
        cost_estimate=pl.CostEstimate(flops=0, bytes_accessed=moved, transcendentals=0),
    )(*straight, *turned)


def whole(array):
    rank = array.ndim
    return (array, array.shape, lambda i: (0,) * rank)


def per_group(array, at=lambda i: i):
    return (array, (1,) + array.shape[1:], lambda i: (at(i),) + (0,) * (array.ndim - 1))


def out_whole(shape, dtype):
    return (shape, dtype, shape, lambda i: (0,) * len(shape))


def out_group(shape, dtype, at=lambda i: i):
    return (shape, dtype, (1,) + shape[1:], lambda i: (at(i),) + (0,) * (len(shape) - 1))


class Layer:
    def __init__(self, width, up, down, qkv, out, out_from, norms, bias_qkv, bias_up):
        self.width, self.up, self.down = width, up, down
        self.qkv_blocks, self.out_block, self.out_from = qkv, out, out_from
        self.norms, self.bias_qkv, self.bias_up = norms, bias_qkv, bias_up
        self.used = [block[3] for block in qkv]

    def columns(self, block, at):
        pair, size, place, _ = block
        return [(half, (1, half.shape[1], size), lambda i: (at(i), 0, place)) for half in pair]

    def qkv(self, at=lambda i: i):
        return [one for block in self.qkv_blocks for one in self.columns(block, at)]

    def out(self, at=lambda i: i):
        return self.columns(self.out_block, at)

    def ffn(self, where):
        pair, base = where
        size, per = self.bias_up.shape[2], self.bias_up.shape[0] // 2
        return [(half, (1, half.shape[1], size), lambda i: (i // per, 0, base + i % per)) for half in pair]


def joined(pair, cols=slice(None)):
    return jnp.concatenate([half[0, :, cols] for half in pair], axis=0)


def pairs_of(refs):
    return [refs[at : at + 2] for at in range(0, len(refs), 2)]


def put_projection(rows, weights, used, bias, target):
    start = 0
    for weight, cols in zip(weights, used):
        part = dot(rows, joined(weight, slice(0, cols)), 1, 0) + bias[0, :, start : start + cols]
        target[:, start : start + cols] = part.astype(LOW)
        start += cols


def through_projection(grads, weights, used):
    start = 0
    total = None
    for weight, cols in zip(weights, used):
        part = dot(grads[:, start : start + cols], joined(weight, slice(0, cols)), 1, 1)
        total = part if total is None else total + part
        start += cols
    return total


def head_at(width, part, head):
    return slice(part * width + head * HEAD_DIM, part * width + (head + 1) * HEAD_DIM)


def join(parts, cols):
    picked = [part[:, cols] for part in parts]
    return picked[0] if len(picked) == 1 else jnp.concatenate(picked, axis=0)


def attend(width, kept, mask, logsum):
    scale = jnp.asarray(HEAD_DIM**-0.5, LOW)
    out = []
    for head in range(width // HEAD_DIM):
        query = kept[0][:, head_at(width, 0, head)] * scale
        scores = dot(join(kept, head_at(width, 1, head)), query, 1, 1) + mask[...]
        top = jnp.max(scores, axis=0, keepdims=True)
        expo = jnp.exp(scores - top)
        total = jnp.sum(expo, axis=0, keepdims=True)
        out.append(dot(join(kept, head_at(width, 2, head)), expo.astype(LOW), 0, 0) * (1.0 / total))
        logsum[head : head + 1, :] = top + jnp.log(total)
    return jnp.concatenate(out, axis=0).T.astype(LOW)


def attend_back(width, kept, mask, logsum, d_context, grads, sums):
    scale = jnp.asarray(HEAD_DIM**-0.5, LOW)
    for head in range(width // HEAD_DIM):
        at_q, at_k, at_v = (head_at(width, part, head) for part in range(3))
        query = kept[0][:, at_q] * scale
        keys = join(kept, at_k)
        d_ctx = d_context[:, head * HEAD_DIM : (head + 1) * HEAD_DIM]
        probs = jnp.exp(dot(keys, query, 1, 1) + mask[...] - logsum[head : head + 1, :])
        d_probs = dot(join(kept, at_v), d_ctx, 1, 1)
        both = probs * d_probs
        inner = jnp.sum(both, axis=0, keepdims=True)
        d_scores = (both - probs * inner).astype(LOW)
        d_values = dot(probs.astype(LOW), d_ctx, 1, 0).astype(LOW)
        d_keys = dot(d_scores, query, 1, 0).astype(LOW)
        d_query = dot(keys * scale, d_scores, 0, 0).T.astype(LOW)
        grads[0][:, at_q] = d_query
        start = 0
        for grad in grads:
            rows = grad.shape[0]
            grad[:, at_k] = d_keys[start : start + rows]
            grad[:, at_v] = d_values[start : start + rows]
            start += rows
        for grad in grads[1:]:
            grad[:, at_q] = jnp.zeros((grad.shape[0], HEAD_DIM), LOW)
        sums[0:1, at_q] = jnp.sum(d_query.astype(F32), axis=0, keepdims=True)
        sums[0:1, at_k] = jnp.zeros((1, HEAD_DIM), F32)
        sums[0:1, at_v] = jnp.sum(d_values.astype(F32), axis=0, keepdims=True)


def make_mask(segs_q, segs_k, mask):
    @pl.when(pl.program_id(0) == 0)
    def _():
        mask[...] = jnp.where(segs_k[...] == segs_q[...], 0.0, -1e9)


def normalize(value, gain, shift):
    center = value - jnp.mean(value, axis=-1, keepdims=True)
    recip = lax.rsqrt(jnp.mean(center * center, axis=-1, keepdims=True) + 1e-06)
    normed = center * recip
    return normed * gain + shift, normed, recip


def normalize_back(grad, normed, recip, gain):
    scaled = grad * gain
    mean_one = jnp.mean(scaled, axis=-1, keepdims=True)
    mean_two = jnp.mean(scaled * normed, axis=-1, keepdims=True)
    return recip * (scaled - mean_one - normed * mean_two)


def row_tiles(rows):
    return [slice(start, start + TILE) for start in range(0, rows, TILE)]


def project_call(layer, rows_low, segs, half):
    n, depth = rows_low.shape
    width, wide, own = layer.width, 3 * layer.width, 2 * half
    count = 2 * len(layer.qkv_blocks)

    def body(rows, *refs):
        weights = pairs_of(refs[:count])
        bias, segs_q, segs_k, proj, context, logsum, mask = refs[count:]
        make_mask(segs_q, segs_k, mask)
        put_projection(rows[...], weights, layer.used, bias, proj.at[0])
        context[0] = attend(width, [proj.at[0, :own]], mask, logsum.at[0])

    return call(
        body, 2,
        [whole(rows_low)] + layer.qkv() + [
            per_group(layer.bias_qkv), whole(segs[None, :]), whole(segs[:, None])
        ],
        [
            out_group((2, n, wide), LOW), out_group((2, own, width), LOW), out_group((2, 8, own), F32),
        ],
        [pltpu.VMEM((own, own), F32)],
        flops=4 * n * depth * wide + 8 * own * own * width,
        exps=2 * own * own * width // HEAD_DIM,
    )


def shared_call(layer, rows, proj, away_low, context_own, segs, half):
    n, depth = rows.shape
    width, wide, own = layer.width, 3 * layer.width, 2 * half
    count = 2 * len(layer.qkv_blocks)

    def body(rows, proj, away, *refs):
        weights = pairs_of(refs[:count])
        (
            out_one, out_two, bias, segs_q, segs_k, context_own, norms,
            proj_away, context, logsum, hidden, hidden_low, normed_one, recip_one, mask, total,
        ) = refs[count:]
        i = pl.program_id(0)
        make_mask(segs_q, segs_k, mask)
        put_projection(away[...], weights, layer.used, bias, proj_away.at[0])
        context[0, :own] = context_own[0]
        context[0, own:] = attend(width, [proj.at[0], proj_away.at[0]], mask, logsum.at[0])
        out_cols = joined((out_one, out_two), slice(layer.out_from, layer.out_from + width))

        @pl.when(i == 0)
        def _():
            total[...] = dot(context[0], out_cols, 1, 1)

        @pl.when(i == 1)
        def _():
            for at in row_tiles(n):
                value = rows[at, :].astype(F32) + norms[2:3, :]
                value = value + (total[at, :] + dot(context[0, at], out_cols, 1, 1))
                value, normed, recip = normalize(value, norms[0:1, :], norms[3:4, :])
                hidden[at, :] = value
                hidden_low[at, :] = value.astype(LOW)
                normed_one[at, :] = normed.astype(LOW)
                recip_one[at, :] = recip

    return call(
        body, 2,
        [
            whole(rows), (proj, (1, half, wide), lambda i: (i, 2, 0)), whole(away_low),
        ] + layer.qkv() + layer.out() + [
            per_group(layer.bias_qkv), whole(segs[None, :half]),
            whole(segs[:, None]), per_group(context_own), whole(layer.norms),
        ],
        [
            out_group((2, half, wide), LOW), out_group((2, n, width), LOW), out_group((2, 8, half), F32),
            out_whole((n, depth), F32), out_whole((n, depth), LOW), out_whole((n, depth), LOW),
            out_whole((n, 1), F32),
        ],
        [pltpu.VMEM((own, half), F32), pltpu.VMEM((n, depth), F32)],
        flops=4 * depth * (n * width + half * wide) + 8 * own * half * width,
        exps=2 * own * half * width // HEAD_DIM,
    )


def ffn_call(layer, hidden, hidden_low):
    n, depth = hidden.shape
    steps, _, size = layer.bias_up.shape
    per = steps // 2

    def body(
        hidden, hidden_low, norms, bias_up, up_one, up_two, down_one, down_two,
        act, slope, output, output_low, normed_two, recip_two,
    ):
        i = pl.program_id(0)

        @pl.when(i == 0)
        def _():
            output[...] = hidden[...] + norms[4:5, :]

        up, down = joined((up_one, up_two)), joined((down_one, down_two))
        for at in row_tiles(n):
            pre = dot(hidden_low[at, :], up, 1, 0) + bias_up[0]
            bell = 0.5 + 0.5 * lax.erf(pre * math.sqrt(0.5))
            low = (pre * bell).astype(LOW)
            act[0, at, :] = low
            slope[0, at, :] = (
                bell + pre * (jnp.exp(-0.5 * pre * pre) * (1.0 / math.sqrt(2.0 * math.pi)))
            ).astype(LOW)
            output[at, :] += dot(low, down, 1, 1)

        @pl.when(i == steps - 1)
        def _():
            for at in row_tiles(n):
                value, normed, recip = normalize(output[at, :], norms[1:2, :], norms[5:6, :])
                output[at, :] = value
                output_low[at, :] = value.astype(LOW)
                normed_two[at, :] = normed.astype(LOW)
                recip_two[at, :] = recip

    neurons = per * size
    ffn_out = ((2, n, neurons), LOW, (1, n, size), lambda i: (i // per, 0, i % per))
    return call(
        body, steps,
        [
            whole(hidden), whole(hidden_low), whole(layer.norms), per_group(layer.bias_up),
        ] + layer.ffn(layer.up) + layer.ffn(layer.down),
        [
            ffn_out, ffn_out, out_whole((n, depth), F32), out_whole((n, depth), LOW),
            out_whole((n, depth), LOW), out_whole((n, 1), F32),
        ],
        [],
        flops=8 * n * depth * neurons,
        exps=4 * n * neurons,
    )


def add_rows(sums, row, value, at):
    value = jnp.sum(value, axis=0, keepdims=True)
    if at.start == 0:
        sums[row : row + 1, :] = value
    else:
        sums[row : row + 1, :] += value


def ffn_back_call(layer, grad, extra, kept, half):
    n, depth = grad.shape
    steps, _, size = layer.bias_up.shape
    per = steps // 2
    has_extra = extra is not None

    def body(grad, *refs):
        extra = refs[0] if has_extra else None
        (
            normed_one, recip_one, normed_two, recip_two, norms, slope, up_one, up_two, down_one, down_two,
            d_final_low, d_pre, d_mid, d_mid_low, sums, bias_sums, total,
        ) = refs[1:] if has_extra else refs
        i = pl.program_id(0)
        gain = lambda at: norms[at : at + 1, :]

        @pl.when(i == 0)
        def _():
            sums[...] = jnp.zeros_like(sums)
            for at in row_tiles(n):
                value = grad[at, :].astype(F32)
                if has_extra and at.start >= 2 * half:
                    value = value + extra[at.start - 2 * half : at.stop - 2 * half, :].astype(F32)
                normed = normed_two[at, :].astype(F32)
                back = normalize_back(value, normed, recip_two[at, :], gain(1))
                total[at, :] = back
                d_final_low[at, :] = back.astype(LOW)
                add_rows(sums, 1, value * normed, at)
                add_rows(sums, 5, value, at)
                add_rows(sums, 4, back, at)

        bias = None
        up, down = joined((up_one, up_two)), joined((down_one, down_two))
        for at in row_tiles(n):
            d_act = dot(d_final_low[at, :], down, 1, 0)
            low = (d_act * slope[0, at, :].astype(F32)).astype(LOW)
            d_pre[0, at, :] = low
            one = jnp.sum(low.astype(F32), axis=0, keepdims=True)
            bias = one if bias is None else bias + one
            total[at, :] += dot(low, up, 1, 1)
        bias_sums[0] = bias

        @pl.when(i == steps - 1)
        def _():
            for at in row_tiles(n):
                value = total[at, :]
                normed = normed_one[at, :].astype(F32)
                back = normalize_back(value, normed, recip_one[at, :], gain(0))
                d_mid[at, :] = back
                d_mid_low[at, :] = back.astype(LOW)
                add_rows(sums, 0, value * normed, at)
                add_rows(sums, 3, value, at)
                add_rows(sums, 2, back, at)

    neurons = per * size
    blocks = ((1, n, size), lambda i: (i // per, 0, i % per))
    return call(
        body, steps,
        [whole(grad)] + ([whole(extra)] if has_extra else []) + [
            whole(kept["normed_one"]), whole(kept["recip_one"]), whole(kept["normed_two"]),
            whole(kept["recip_two"]), whole(layer.norms), (kept["slope"],) + blocks,
        ] + layer.ffn(layer.up) + layer.ffn(layer.down),
        [
            out_whole((n, depth), LOW), ((2, n, neurons), LOW) + blocks, out_whole((n, depth), F32),
            out_whole((n, depth), LOW), out_whole((8, depth), F32), out_group((steps, 1, size), F32),
        ],
        [pltpu.VMEM((n, depth), F32)],
        flops=8 * n * depth * neurons,
    )


def ffn_back_first_call(layer, grad, extra, kept, half):
    n, depth = grad.shape
    steps, _, size = layer.bias_up.shape
    per = steps // 2

    def body(
        grad, extra, normed_two, recip_two, norms, slope, down_one, down_two,
        d_final, d_final_low, d_pre, sums, bias_sums,
    ):
        i = pl.program_id(0)

        @pl.when(i == 0)
        def _():
            sums[...] = jnp.zeros_like(sums)
            for at in row_tiles(n):
                value = grad[at, :]
                if at.start >= 2 * half:
                    value = value + extra[at.start - 2 * half : at.stop - 2 * half, :].astype(F32)
                normed = normed_two[at, :].astype(F32)
                back = normalize_back(value, normed, recip_two[at, :], norms[1:2, :])
                d_final[at, :] = back
                d_final_low[at, :] = back.astype(LOW)
                add_rows(sums, 1, value * normed, at)
                add_rows(sums, 5, value, at)
                add_rows(sums, 4, back, at)

        bias = None
        down = joined((down_one, down_two))
        for at in row_tiles(n):
            d_act = dot(d_final_low[at, :], down, 1, 0)
            low = (d_act * slope[0, at, :].astype(F32)).astype(LOW)
            d_pre[0, at, :] = low
            one = jnp.sum(low.astype(F32), axis=0, keepdims=True)
            bias = one if bias is None else bias + one
        bias_sums[0] = bias

    neurons = per * size
    blocks = ((1, n, size), lambda i: (i // per, 0, i % per))
    return call(
        body, steps,
        [
            whole(grad), whole(extra), whole(kept["normed_two"]), whole(kept["recip_two"]),
            whole(layer.norms), (kept["slope"],) + blocks,
        ] + layer.ffn(layer.down),
        [
            out_whole((n, depth), F32), out_whole((n, depth), LOW), ((2, n, neurons), LOW) + blocks,
            out_whole((8, depth), F32), out_group((steps, 1, size), F32),
        ],
        [],
        flops=4 * n * depth * neurons,
    )


def ffn_back_second_call(layer, d_final, d_pre, kept):
    n, depth = d_final.shape
    steps, _, size = layer.bias_up.shape
    per = steps // 2

    def body(d_final, d_pre, normed_one, recip_one, norms, up_one, up_two, d_mid, d_mid_low, sums):
        i = pl.program_id(0)

        @pl.when(i == 0)
        def _():
            d_mid[...] = d_final[...]

        up = joined((up_one, up_two))
        for at in row_tiles(n):
            d_mid[at, :] += dot(d_pre[0, at, :], up, 1, 1)

        @pl.when(i == steps - 1)
        def _():
            sums[...] = jnp.zeros_like(sums)
            for at in row_tiles(n):
                value = d_mid[at, :]
                normed = normed_one[at, :].astype(F32)
                back = normalize_back(value, normed, recip_one[at, :], norms[0:1, :])
                d_mid[at, :] = back
                d_mid_low[at, :] = back.astype(LOW)
                add_rows(sums, 0, value * normed, at)
                add_rows(sums, 3, value, at)
                add_rows(sums, 2, back, at)

    blocks = ((1, n, size), lambda i: (i // per, 0, i % per))
    return call(
        body, steps,
        [
            whole(d_final), (d_pre,) + blocks, whole(kept["normed_one"]), whole(kept["recip_one"]),
            whole(layer.norms),
        ] + layer.ffn(layer.up),
        [out_whole((n, depth), F32), out_whole((n, depth), LOW), out_whole((8, depth), F32)],
        [],
        flops=4 * n * depth * per * size,
    )


def shared_back_call(layer, d_mid_low, kept, segs, half):
    n, depth = d_mid_low.shape
    width, wide, own = layer.width, 3 * layer.width, 2 * half
    count = 2 * len(layer.qkv_blocks)

    def body(d_mid, proj, away, logsum, *refs):
        weights = pairs_of(refs[:count])
        out_one, out_two, segs_q, segs_k, d_proj, d_away, sums, back, mask, total = refs[count:]
        i = pl.program_id(0)
        make_mask(segs_q, segs_k, mask)
        out_cols = joined((out_one, out_two), slice(layer.out_from, layer.out_from + width))
        d_context = dot(d_mid[...], out_cols, 1, 0).astype(LOW)
        attend_back(
            width, [proj.at[0], away.at[0]], mask, logsum.at[0], d_context,
            [d_proj.at[0], d_away.at[0]], sums.at[0],
        )
        part = through_projection(d_away[0], weights, layer.used)

        @pl.when(i == 0)
        def _():
            total[...] = part

        @pl.when(i == 1)
        def _():
            back[...] = (total[...] + part).astype(LOW)

    return call(
        body, 2,
        [
            (d_mid_low, (half, depth), lambda i: (2, 0)), (kept["proj"], (1, half, wide), lambda i: (i, 2, 0)),
            per_group(kept["proj_away"]), per_group(kept["logsum_shared"]),
        ] + layer.qkv() + layer.out() + [whole(segs[None, :half]), whole(segs[:, None])],
        [
            out_group((2, half, wide), LOW), out_group((2, half, wide), LOW), out_group((2, 8, wide), F32),
            out_whole((half, depth), LOW),
        ],
        [pltpu.VMEM((own, half), F32), pltpu.VMEM((half, depth), F32)],
        flops=4 * half * depth * (wide + width) + 20 * own * half * width,
        exps=2 * own * half * width // HEAD_DIM,
    )


def own_back_call(layer, d_mid, d_mid_low, d_shared, kept, segs, half, with_rows):
    n, depth = d_mid_low.shape
    width, wide, own = layer.width, 3 * layer.width, 2 * half
    count = 2 * len(layer.qkv_blocks) if with_rows else 0

    def body(d_mid_low, d_shared, proj, logsum, out_one, out_two, segs_q, segs_k, *refs):
        i = pl.program_id(0)
        if with_rows:
            d_mid, weights = refs[0], pairs_of(refs[1 : count + 1])
            d_proj, sums, d_rows, mask = refs[count + 1 :]
        else:
            d_proj, sums, mask = refs
        make_mask(segs_q, segs_k, mask)
        out_cols = joined((out_one, out_two), slice(layer.out_from, layer.out_from + width))
        d_context = dot(d_mid_low[...], out_cols, 1, 0).astype(LOW)
        attend_back(
            width, [proj.at[0]], mask, logsum.at[0], d_context, [d_proj.at[0, :own]], sums.at[0]
        )
        d_proj[0, own:] = d_shared[0]
        if with_rows:
            part = through_projection(d_proj[0], weights, layer.used)

            @pl.when(i == 0)
            def _():
                d_rows[...] = d_mid[...] + part

            @pl.when(i == 1)
            def _():
                d_rows[...] += part

    return call(
        body, 2,
        [
            (d_mid_low, (own, depth), lambda i: (0, 0)), per_group(d_shared),
            (kept["proj"], (1, own, wide), lambda i: (i, 0, 0)), per_group(kept["logsum_own"]),
        ] + layer.out() + [whole(segs[None, :]), whole(segs[:, None])]
        + ([whole(d_mid)] + layer.qkv() if with_rows else []),
        [out_group((2, n, wide), LOW), out_group((2, 8, wide), F32)]
        + ([out_whole((n, depth), F32)] if with_rows else []),
        [pltpu.VMEM((own, own), F32)],
        flops=4 * depth * (n * wide * with_rows + own * width) + 20 * own * own * width,
        exps=2 * own * own * width // HEAD_DIM,
    )


def rows_back_call(layer, d_mid, d_proj):
    n, depth = d_mid.shape
    wide = 3 * layer.width

    def body(d_mid, d_proj, *refs):
        weights, d_rows = pairs_of(refs[:-1]), refs[-1]

        @pl.when(pl.program_id(0) == 0)
        def _():
            d_rows[...] = d_mid[...]

        d_rows[...] += through_projection(d_proj[0], weights, layer.used)

    return call(
        body, 2, [whole(d_mid), per_group(d_proj)] + layer.qkv(), [out_whole((n, depth), F32)], [],
        flops=4 * depth * n * wide,
    )[0]


class Grads:
    def __init__(self, entries, columns, cut):
        self.entries, self.columns, self.cut = entries, columns, cut
        sizes = [end - start for _, start, end in columns]
        self.size_a, self.size_b = sum(sizes[:cut]), sum(sizes[cut:])

    def inputs(self, at):
        out = []
        for pairs in self.entries:
            for left, right in pairs:
                out += [whole(left), per_group(right, at)]
        return out

    def scratch(self, rows):
        return [pltpu.VMEM((rows, left.shape[0]), LOW) for pairs in self.entries for left, _ in pairs]

    def flops(self, rows):
        depth = self.entries[0][0][0].shape[1]
        return sum(
            2 * rows * left.shape[0] * (2 * right.shape[2] + depth)
            for pairs in self.entries for left, right in pairs
        )

    def turn(self, pick, refs, turned):
        @pl.when(pl.program_id(0) == 0)
        def _():
            for at in range(len(turned)):
                turned[at][...] = dot(pick[...], refs[2 * at][...], 1, 1).astype(LOW)

    def product(self, refs, turned, entry, start, end):
        first = sum(len(pairs) for pairs in self.entries[:entry])
        total = None
        for at in range(first, first + len(self.entries[entry])):
            one = dot(turned[at][...], refs[2 * at + 1][0, :, start:end], 1, 0)
            total = one if total is None else total + one
        return total

    def send(self, pick):
        rows = pick.shape[0]
        size = self.size_a + self.size_b

        def body(pick, *refs):
            count = 2 * sum(len(pairs) for pairs in self.entries)
            out, turned = refs[count], refs[count + 1 :]
            self.turn(pick, refs, turned)
            col = 0
            for entry, start, end in self.columns:
                part = self.product(refs, turned, entry, start, end)
                out[0, :, col : col + end - start] = part.astype(LOW)
                col += end - start

        return call(
            body, 2, [whole(pick)] + self.inputs(lambda i: i), [out_group((2, rows, size), LOW)],
            self.scratch(rows), self.flops(rows),
        )[0]

    def keep(self, pick, got):
        rows = pick.shape[0]
        half = rows // 2
        size = self.size_a + self.size_b

        def body(pick, got, *refs):
            count = 2 * sum(len(pairs) for pairs in self.entries)
            send_a, keep_a, send_b, keep_b = refs[count : count + 4]
            turned = refs[count + 4 :]
            i = pl.program_id(0)
            self.turn(pick, refs, turned)
            col = 0
            for at, (entry, start, end) in enumerate(self.columns):
                part = self.product(refs, turned, entry, start, end)
                part = part + got[0, :, col : col + end - start].astype(F32)
                if at < self.cut:
                    place = slice(col, col + end - start)

                    @pl.when(i == 0)
                    def _():
                        send_a[:, place] = part.astype(LOW)

                    @pl.when(i == 1)
                    def _():
                        keep_a[:, place] = part
                else:
                    place = slice(col - self.size_a, col - self.size_a + end - start)
                    keep_b[0, :, place] = part[:half]
                    send_b[0, :, place] = part[half:].astype(LOW)
                col += end - start

        return call(
            body, 2,
            [whole(pick), per_group(got, lambda i: 1 - i)] + self.inputs(lambda i: 1 - i),
            [
                out_whole((rows, self.size_a), LOW), out_whole((rows, self.size_a), F32),
                out_group((2, half, self.size_b), LOW), out_group((2, half, self.size_b), F32),
            ],
            self.scratch(rows), self.flops(rows),
        )


class Reduce:
    def __init__(self, grads, pick_send, pick_keep):
        self.grads, self.pick_keep = grads, pick_keep
        self.sends = (grads.send(pick_send),)
        self.got = (swap_core(self.sends[0]),)
        self.work = self._run()

    def _run(self):
        count = lax.axis_size("dp") // 4
        send_a, keep_a, send_b, keep_b = self.grads.keep(self.pick_keep, self.got[0])
        fourth = keep_a.shape[0] // 2
        self.sends = (send_a, send_b)
        self.got = (swap_y(send_a), swap_x(send_b))
        yield
        a = keep_a + self.got[0].astype(F32)
        b = keep_b + self.got[1].astype(F32)
        self.sends = (a[fourth:].astype(LOW), b[0].astype(LOW))
        self.got = (swap_x(self.sends[0]), swap_y(self.sends[1]))
        a, b = a[:fourth], b[1]
        yield
        both = jnp.concatenate([a + self.got[0].astype(F32), b + self.got[1].astype(F32)], axis=1)
        both = both.reshape((count, -1) + both.shape[1:])
        self.sends = tuple(both[back].astype(LOW) for back in range(1, count))
        self.got = tuple(ring_shift(send, -back) for back, send in enumerate(self.sends, 1))
        yield
        total = both[0] + sum(got.astype(F32) for got in self.got)
        self.total = total
        self.got = self.sends = ()

    def step(self):
        next(self.work, None)


class Total:
    def __init__(self, value):
        self.total = value
        self.work = self._run()
        self.step()

    def _run(self):
        n = lax.axis_size("dp")
        self.sends = (self.total,)
        self.got = (swap_y(self.total),)
        yield
        self.total = self.total + self.got[0]
        step = 1
        while step < n:
            self.sends = (self.total,)
            self.got = (lax.ppermute(self.total, "dp", [(i, i ^ step) for i in range(n)]),)
            yield
            self.total = self.total + self.got[0]
            step *= 2
        self.got = self.sends = ()

    def step(self):
        next(self.work, None)


def round_of(*works):
    ended = lax.optimization_barrier(tuple(work.got for work in works))
    for work, got in zip(works, ended):
        work.got = got
    for work in works:
        work.step()


def before(value, *works):
    value, ended = lax.optimization_barrier((value, tuple(work.got for work in works)))
    for work, got in zip(works, ended):
        work.got = got
    return value


def forward_attn(layer, rows, proj, context_own, logsum_own, rows_low, away_low, segs, half):
    proj_away, context, logsum_shared, hidden, hidden_low, normed_one, recip_one = shared_call(
        layer, rows, proj, away_low, context_own, segs[1], half
    )
    kept = dict(
        rows_low=rows_low, away_low=away_low, proj=proj, proj_away=proj_away, context=context,
        logsum_own=logsum_own, logsum_shared=logsum_shared, hidden_low=hidden_low,
        normed_one=normed_one, recip_one=recip_one,
    )
    return hidden, kept


def forward_ffn(layer, hidden, kept):
    act, slope, output, output_low, normed_two, recip_two = ffn_call(layer, hidden, kept["hidden_low"])
    kept.update(act=act, slope=slope, normed_two=normed_two, recip_two=recip_two)
    return output, output_low


def backward_ffn(layer, grad, extra, kept, half):
    d_final_low, d_pre, d_mid, d_mid_low, sums, bias_sums = ffn_back_call(layer, grad, extra, kept, half)
    entries = [[(kept["hidden_low"], d_pre)], [(d_final_low, kept["act"])]]
    return d_mid, d_mid_low, sums[:6], bias_sums, entries


def attn_entries(kept, d_proj, d_away, d_mid_low):
    return [[(kept["rows_low"], d_proj), (kept["away_low"], d_away)], [(d_mid_low, kept["context"])]]


def on_device(
    tokens, segment_ids, out_grad,
    t_qkv, t_qv_bias, t_out, t_up, t_up_bias, t_down, t_gains, t_shifts,
    s_qkv, s_qv_bias, s_out, s_up, s_up_bias, s_down, s_gains, s_shifts,
):
    rows, half, width = tokens.shape
    first = lax.axis_index("mp") == 0
    own_row = lambda value: jnp.where(first, value[0], value[2])
    far_row = lambda value: jnp.where(first, value[2], value[0])

    norm_rows = jnp.concatenate([t_gains, t_shifts, s_gains, s_shifts], axis=0)
    norm_rows = jnp.pad(norm_rows, ((0, 128 - norm_rows.shape[0]), (0, 0)))
    t_width, s_width = t_qkv.shape[2], s_qkv.shape[2]
    size = s_up.shape[1]
    per = t_up.shape[1] // size
    count, block = lax.axis_size("dp") // 4, t_up.shape[0]
    together = lambda *values: lax.optimization_barrier(values)
    every = slice(None)

    def columns(start, width):
        return slice(start, start + width)

    t_cut, t_all = 2 * t_width, 4 * t_width + 128
    f_cut = per * size
    s_cut = size + 2 * s_width
    packed_t, packed_f, student_a, student_b = pack(
        [t_qkv, t_up, s_up, s_qkv], [t_out, norm_rows, t_down, s_out, s_down],
        [(block, t_all), (block, 2 * f_cut), (block, s_cut), (block, s_cut)],
        [(0, (i,), 0, (every, columns(i * t_width, t_width))) for i in range(3)]
        + [
            (4, (), 0, (every, columns(3 * t_width, t_width))), (5, (), 0, (every, columns(4 * t_width, 128))),
            (1, (every,), 1, (every, columns(0, f_cut))), (6, (), 1, (every, columns(f_cut, f_cut))),
            (2, (every,), 2, (every, columns(0, size))), (3, (0,), 2, (every, columns(size, s_width))),
            (7, (), 2, (every, columns(size + s_width, s_width))), (8, (), 3, (every, columns(0, size))),
            (3, (1,), 3, (every, columns(size, s_width))), (3, (2,), 3, (every, columns(size + s_width, s_width))),
        ],
    )

    def along_z(value):
        return [value] + [ring_shift(value, at) for at in range(1, count)]

    def of_line(pieces, cut):
        rest = pieces[0].shape[1] - cut
        return moves(
            pieces, [(count, block, cut), (count, block, rest)],
            [(i, (every, columns(start, wide)), at, (i,)) for i in range(count)
             for at, (start, wide) in enumerate(((0, cut), (cut, rest)))],
        )

    def first_plane(a, got_a, b, got_b):
        return moves(
            [a, got_a, b, got_b], [(2,) + a.shape, (2,) + b.shape],
            [(0, (every,), 0, (0,)), (1, (every,), 0, (1,)), (2, (every,), 1, (0,)), (3, (every,), 1, (1,))],
        )

    def both_planes(a, got_a, b, got_b, order):
        copies, col = [], 0
        for of_b, start, wide in order:
            taken, place = (every, every, every, columns(start, wide)), (every, every, columns(col, wide))
            if of_b:
                copies += [(2, taken, 0, (every, 0) + place), (3, taken, 0, (every, 1) + place)]
            else:
                copies += [(0, taken, 0, (0, every) + place), (1, taken, 0, (1, every) + place)]
            col += wide
        out = moves([a, got_a, b, got_b], [(2, 2, count, block, col)], copies)[0]
        return out.reshape(2, width // 2, col)

    def with_core(own):
        return own, swap_core(own)

    bias_parts = [t_qv_bias[0], t_qv_bias[1], t_up_bias, s_qv_bias[0], s_qv_bias[1], s_up_bias]
    line_t, got_own = along_z(packed_t), swap_y(far_row(tokens))
    line_f = along_z(packed_f)
    *line_t, line_f[1], got_own = together(*line_t, line_f[1], got_own)
    attn_a, attn_b = of_line(line_t, t_cut)
    got_a, got_b, student_x, student_y = swap_x(attn_a), swap_y(attn_b), swap_x(student_a), swap_y(student_b)
    got_a, got_b, student_x, student_y, *line_f[2:-1] = together(
        got_a, got_b, student_x, student_y, *line_f[2:-1]
    )
    attn_a, attn_b = first_plane(attn_a, got_a, attn_b, got_b)
    got_a, got_b = swap_y(attn_a), swap_x(attn_b)
    line_s = along_z(moves(
        [student_a, student_x, student_b, student_y], [(2, block, 2 * s_cut)],
        [(i, (every,), 0, (i % 2, every, columns(i // 2 * s_cut, s_cut))) for i in range(4)],
    )[0])
    got_a, got_b, line_f[-1] = together(got_a, got_b, line_f[-1])
    attn = both_planes(
        attn_a, got_a, attn_b, got_b, [(False, 0, t_cut), (True, 0, t_all - t_cut)]
    )
    attn = with_core(attn)
    ffn_a, ffn_b = of_line(line_f, f_cut)
    got_a, got_b = swap_x(ffn_a), swap_y(ffn_b)
    bias_own = jnp.concatenate(bias_parts)
    bias_far = swap_y(bias_own)
    attn, got_a, got_b, bias_far, line_s[1] = together(attn, got_a, got_b, bias_far, line_s[1])
    ffn_a, ffn_b = first_plane(ffn_a, got_a, ffn_b, got_b)
    got_a, got_b = swap_y(ffn_a), swap_x(ffn_b)
    got_shared = swap_y(tokens[1])
    norms = jnp.concatenate([half[0, :, -128:-116] for half in attn], axis=0).T.astype(F32)
    norms_of = lambda at: jnp.pad(norms[at : at + 6], ((0, 2), (0, 0)))
    bias_all = jnp.stack([bias_own, bias_far]).astype(F32)
    cuts = [0]
    for part in bias_parts:
        cuts.append(cuts[-1] + part.shape[0])
    pick = [bias_all[:, cuts[i] : cuts[i + 1]] for i in range(6)]
    bias_qkv = lambda q, v: jnp.concatenate([q, jnp.zeros_like(q), v], axis=1)[:, None, :]
    teacher = Layer(
        t_width, None, None, [(attn, t_width, i, t_width) for i in range(3)], (attn, t_width, 3, t_width), 0,
        norms_of(0), bias_qkv(pick[0], pick[1]), pick[2].reshape(2 * per, 1, size),
    )

    to_own = feature_order(width)
    into = (lax.iota(jnp.int32, width)[:, None] == to_own[None, :]).astype(LOW)
    reorder = lambda value: jnp.dot(value, into, preferred_element_type=F32).astype(LOW)
    pick_all = jnp.eye(width, dtype=LOW)
    pick_keep, pick_send = pick_all[: width // 2], pick_all[width // 2 :]

    inputs = reorder(jnp.concatenate([own_row(tokens), got_own, tokens[1]], axis=0))
    spin = lambda segs: jnp.where(first, segs, jnp.roll(segs, half))
    segs = (spin(own_row(segment_ids)), spin(segment_ids[1]))
    grad_in = jnp.concatenate([own_row(out_grad), swap_y(far_row(out_grad)), out_grad[1]], axis=0)

    inputs, ffn_a, ffn_b = together(inputs, ffn_a, ffn_b)
    proj, context_own, logsum_own = project_call(teacher, inputs, segs[0], half)
    proj, got_shared, *line_s[2:-1] = together(proj, got_shared, *line_s[2:-1])
    away_low = reorder(got_shared)
    hidden, t_kept = forward_attn(
        teacher, inputs, proj, context_own, logsum_own, inputs, away_low, segs, half
    )
    hidden, got_a, got_b, line_s[-1] = together(hidden, got_a, got_b, line_s[-1])
    ffn = both_planes(ffn_a, got_a, ffn_b, got_b, [(False, 0, f_cut), (True, 0, f_cut)])
    ffn = with_core(ffn)
    student_a, student_b = moves(
        line_s, [(2, count, block, s_cut)] * 2,
        [(i, (every, every, columns(at * s_cut, s_cut)), at, (every, i)) for i in range(count) for at in range(2)],
    )
    got_a, got_b = swap_y(student_a), swap_x(student_b)
    hidden, ffn = together(hidden, ffn)
    teacher.up, teacher.down = (ffn, 0), (ffn, per)
    middle, middle_low = forward_ffn(teacher, hidden, t_kept)
    away_low = swap_y(middle_low[2 * half :])
    middle_low, got_a, got_b, grad_in = together(middle_low, got_a, got_b, grad_in)
    grad_in = reorder(grad_in)
    student_w = with_core(both_planes(
        student_a, got_a, student_b, got_b,
        [(False, 0, size), (True, 0, size), (False, size, 2 * s_width), (True, size, 2 * s_width)],
    ))
    narrow = 2 * s_width
    place = 2 * size // narrow
    student = Layer(
        s_width, (student_w, 0), (student_w, 1),
        [(student_w, narrow, place, s_width), (student_w, narrow, place + 1, narrow)],
        (student_w, narrow, place, s_width), s_width, norms_of(6), bias_qkv(pick[3], pick[4]),
        pick[5].reshape(2, 1, size),
    )
    proj, context_own, logsum_own = project_call(student, middle_low, segs[0], half)
    proj, away_low = together(proj, away_low)
    hidden, s_kept = forward_attn(
        student, middle, proj, context_own, logsum_own, middle_low, away_low, segs, half
    )
    last, _ = forward_ffn(student, hidden, s_kept)

    def far_half(value):
        return swap_y(value[half : 2 * half].astype(LOW))

    def to_rows(value, far):
        near = jnp.concatenate([value[:half], value[2 * half :]], axis=0)
        high = near.astype(LOW)
        low = (near - high.astype(F32)).astype(LOW)
        back = lambda part: jnp.einsum("nr,dr->nd", part, into, preferred_element_type=F32)
        near, far = back(high) + back(low), back(far)
        return jnp.stack([jnp.where(first, near[:half], far), near[half:], jnp.where(first, far, near[:half])])

    far_last = far_half(last)

    d_mid, d_mid_low, s_norm_grads, s_up_grad, s_entries = backward_ffn(student, grad_in, None, s_kept, half)
    d_shared, d_away, s_sums_b, back = shared_back_call(student, d_mid_low, s_kept, segs[1], half)
    extra = swap_y(back)
    d_shared, far_last = together(d_shared, far_last)
    d_proj, s_sums_a, d_rows = own_back_call(
        student, d_mid, d_mid_low, d_shared, s_kept, segs[0], half, True
    )
    d_proj, extra = lax.optimization_barrier((d_proj, extra))
    s_entries += attn_entries(s_kept, d_proj, d_away, d_mid_low)
    s_columns = [(0, 0, size), (2, 0, s_width), (3, 0, s_width), (1, 0, size), (2, s_width, 3 * s_width)]
    reduce_s = Reduce(Grads(s_entries, s_columns, 3), pick_send, pick_keep)

    d_rows = after(d_rows, reduce_s.sends)
    d_final, d_final_low, d_pre, t_sums_two, t_up_grad = ffn_back_first_call(
        teacher, d_rows, extra, t_kept, half
    )
    d_pre = before(d_pre, reduce_s)
    reduce_s.step()
    d_pre = after(d_pre, reduce_s.sends)
    f_entries = [[(t_kept["hidden_low"], d_pre)], [(d_final_low, t_kept["act"])]]
    reduce_f = Reduce(
        Grads(f_entries, [(0, 0, per * size), (1, 0, per * size)], 1), pick_send, pick_keep
    )
    d_pre = after(d_pre, reduce_f.sends)
    d_mid, d_mid_low, t_sums_one = ffn_back_second_call(teacher, d_final, d_pre, t_kept)
    t_norm_grads = (t_sums_one + t_sums_two)[:6]
    d_mid_low = before(d_mid_low, reduce_f)
    reduce_f.step()
    reduce_s.got = after(reduce_s.got, reduce_f.sends)
    d_mid_low = before(d_mid_low, reduce_s)
    reduce_s.step()
    d_mid_low = after(d_mid_low, reduce_s.sends)
    d_shared, d_away, t_sums_b, back = shared_back_call(teacher, d_mid_low, t_kept, segs[1], half)
    extra = swap_y(back)
    d_shared = before(d_shared, reduce_s)
    reduce_s.step()
    d_shared = after(d_shared, reduce_s.sends)
    d_proj, t_sums_a = own_back_call(teacher, None, d_mid_low, d_shared, t_kept, segs[0], half, False)
    t_entries = attn_entries(t_kept, d_proj, d_away, d_mid_low)
    reduce_t = Reduce(
        Grads(t_entries, [(0, 0, 2 * t_width), (0, 2 * t_width, 3 * t_width), (1, 0, t_width)], 1),
        pick_send, pick_keep,
    )

    def qv_grad(one, two, wide):
        sums = one[:, 0] + two[:, 0]
        sums = jnp.concatenate([sums[:, :wide], sums[:, 2 * wide :]], axis=1)
        return jnp.pad(sums, ((0, 0), (0, width - 2 * wide)))

    norm_grads = jnp.concatenate([t_norm_grads, s_norm_grads], axis=0)
    norm_grads = jnp.einsum("nr,dr->nd", norm_grads, into.astype(F32), precision=lax.Precision.HIGHEST)
    qv_t, qv_s = qv_grad(t_sums_a, t_sums_b, t_width), qv_grad(s_sums_a, s_sums_b, s_width)
    mine = jnp.concatenate([t_up_grad[:per, 0], s_up_grad[:1, 0], qv_t[:1], qv_s[:1]], axis=0)
    other = jnp.concatenate([t_up_grad[per:, 0], s_up_grad[1:, 0], qv_t[1:], qv_s[1:]], axis=0)
    small = Total(jnp.concatenate(
        [norm_grads, jnp.where(first, mine, other), jnp.where(first, other, mine)], axis=0
    ))
    reduce_f.got = after(reduce_f.got, reduce_t.sends)
    round_of(reduce_f, small)
    reduce_t.got = after(reduce_t.got, reduce_f.sends)
    reduce_t.step()
    reduce_f.got = after(reduce_f.got, reduce_t.sends)
    round_of(reduce_f, reduce_s)
    d_rows = rows_back_call(teacher, *after((d_mid, d_proj), reduce_t.sends))
    reduce_t.got = after(reduce_t.got, d_rows)
    far_rows = far_half(d_rows)
    round_of(reduce_t, small)
    d_rows, last = after((d_rows, last), reduce_t.sends)
    d_rows = jnp.concatenate([d_rows[: 2 * half], d_rows[2 * half :] + extra.astype(F32)], axis=0)
    input_grad, output = to_rows(d_rows, far_rows), to_rows(last, far_last)
    round_of(reduce_t, reduce_f, small)
    round_of(reduce_t, small)
    for work in (reduce_t, reduce_f, reduce_s, small):
        while work.got:
            work.step()
    s_sum, f_sum, t_sum, small = reduce_s.total, reduce_f.total, reduce_t.total, small.total

    piece = width // lax.axis_size("dp")
    norm_sum = lax.dynamic_slice_in_dim(small[:12], lax.axis_index("dp") * piece, piece, 1)
    bias_sum = small[12:].reshape(2, -1, width)
    bias_sum = jnp.where(first, bias_sum[0], bias_sum[1])
    t_qv_sum, s_qv_sum = bias_sum[per + 1], bias_sum[per + 2, : 2 * s_width]

    def cut(value, *sizes):
        out = []
        for one in sizes:
            out.append(value[:, :one])
            value = value[:, one:]
        return out

    tq, tk, tv, to = cut(t_sum, t_width, t_width, t_width, t_width)
    t_up_sum, t_down_sum = cut(f_sum, per * size, per * size)
    s_up_sum, sq, so, s_down_sum, sk, sv = cut(s_sum, size, s_width, s_width, size, s_width, s_width)
    return (
        output, input_grad,
        jnp.stack([tq, tk, tv]), t_qv_sum.reshape(2, -1), to.T, t_up_sum, bias_sum[:per].reshape(-1),
        t_down_sum.T,
        norm_sum[0:2], norm_sum[2:6],
        jnp.stack([sq, sk, sv]), s_qv_sum.reshape(2, -1), so.T, s_up_sum, bias_sum[per], s_down_sum.T,
        norm_sum[6:8], norm_sum[8:12],
    )


def solution(mesh):
    layer = (
        P(None, "dp", "mp"), P(None, "mp"), P("mp", "dp"), P("dp", "mp"), P("mp"), P("mp", "dp"),
        P(None, "dp"), P(None, "dp"),
    )
    rows = P("dp", "mp", None)
    return jax.shard_map(
        on_device,
        mesh=mesh,
        in_specs=(rows, P("dp", None), rows) + layer + layer,
        out_specs=(rows, rows) + layer + layer,
        check_vma=False,
    )
```

profile of v0, /device:TPU:0, one launch (start us, length us, event | category | flops | bytes accessed | tf_op | source)
XLA Modules:
  0.0 453.0 jit_solution(6201982089316339438)
XLA Ops:
  0.8 2.4 select_bitcast_fusion.7
  3.2 3.0 collective-permute-start.4
  7.3 2.6 collective-permute-start.3
  10.0 1.6 collective-permute-start
  12.5 8.4 %collective-permute-done.refs_1_ = bf16[48,1664]{1,0:T(8,128)(2,1)S(1)} collective-permute-done((bf16[48,1664]{1,0:T(8,128)(2,1)S(1)}, bf16[48,1664]{1,0:T(8,128)(2,1)S(1)}, u32[]{:S(2)}, u32[]{:S(2)}) %collective-permute-start) | collective-permute-done | bytes 159776 | tf_op jit(solution)/shard_map/ppermute | solution.py:41
  20.9 5.2 %collective-permute-done.1.refs_2_ = bf16[48,1664]{1,0:T(8,128)(2,1)S(1)} collective-permute-done((bf16[48,1664]{1,0:T(8,128)(2,1)S(1)}, bf16[48,1664]{1,0:T(8,128)(2,1)S(1)}, u32[]{:S(2)}, u32[]{:S(2)}) %collective-permute-start.1) | collective-permute-done | bytes 159776 | tf_op jit(solution)/shard_map/ppermute | solution.py:41
  26.1 5.3 %collective-permute-done.2.refs_3_ = bf16[48,1664]{1,0:T(8,128)(2,1)S(1)} collective-permute-done((bf16[48,1664]{1,0:T(8,128)(2,1)S(1)}, bf16[48,1664]{1,0:T(8,128)(2,1)S(1)}, u32[]{:S(2)}, u32[]{:S(2)}) %collective-permute-start.2) | collective-permute-done | bytes 159776 | tf_op jit(solution)/shard_map/ppermute | solution.py:41
  32.8 2.5 collective-permute-start.9
  39.5 6.5 %collective-permute-done.7.refs_1_ = bf16[48,1152]{1,0:T(8,128)(2,1)S(1)} collective-permute-done((bf16[48,1152]{1,0:T(8,128)(2,1)S(1)}, bf16[48,1152]{1,0:T(8,128)(2,1)S(1)}, u32[]{:S(2)}, u32[]{:S(2)}) %collective-permute-start.7) | collective-permute-done | bytes 110624 | tf_op jit(solution)/shard_map/ppermute | solution.py:26
  48.3 1.6 collective-permute-start.10
  51.3 6.4 %collective-permute-done.12.refs_3_ = bf16[48,3072]{1,0:T(8,128)(2,1)S(1)} collective-permute-done((bf16[48,3072]{1,0:T(8,128)(2,1)S(1)}, bf16[48,3072]{1,0:T(8,128)(2,1)S(1)}, u32[]{:S(2)}, u32[]{:S(2)}) %collective-permute-start.12) | collective-permute-done | bytes 294944 | tf_op jit(solution)/shard_map/ppermute | solution.py:41
  57.7 4.2 collective-permute-done.10.refs_1_
  80.9 3.5 fusion.13.rows.refs_0_
  84.4 2.0 collective-permute-start.18
  86.4 2.5 collective-permute-start.19
  88.9 5.8 %collective-permute-done.14.refs_1_ = bf16[4,48,1536]{2,1,0:T(8,128)(2,1)} collective-permute-done((bf16[4,48,1536]{2,1,0:T(8,128)(2,1)}, bf16[4,48,1536]{2,1,0:T(8,128)(2,1)}, u32[]{:S(2)}, u32[]{:S(2)}) %collective-permute-start.14) | collective-permute-done | bytes 589856 | tf_op jit(solution)/shard_map/ppermute | solution.py:26
  95.6 1.6 collective-permute-done.15.refs_3_
  98.4 1.8 shard_map.328
  101.1 12.9 %shard_map.329 = (bf16[2,768,1152]{2,1,0:T(8,128)(2,1)}, bf16[2,512,384]{2,1,0:T(8,128)(2,1)S(1)}, f32[2,8,512]{2,1,0:T(8,128)S(1)}) custom-call(bf16[768,768]{1,0:T(8,128)(2,1)S(1)} %copy-done.4, bf16[2,384,1664]{2,1,0:T(8,128)(2,1)S(1)} %bitcast.111, bf16[2,384,1664]{2,1,0:T(8,128)(2,1)} %collective-permute-done.13.refs_1_.refs_3_.refs_5_.refs_7_.out_two, ...), custom_call_target="tpu_custom_call" | custom-call | flops 1761607680 | bytes 10443264 | tf_op jit(solution)/shard_map/pallas_call | solution.py:80
  114.0 1.7 fusion.19.away.refs_2_
  115.7 13.6 %shard_map.330 = (bf16[2,256,1152]{2,1,0:T(8,128)(2,1)S(1)}, bf16[2,768,384]{2,1,0:T(8,128)(2,1)S(1)}, f32[2,8,256]{2,1,0:T(8,128)S(1)}, f32[768,768]{1,0:T(8,12...) custom-call(bf16[768,768]{1,0:T(8,128)(2,1)} %fusion.13.rows.refs_0_, ...), custom_call_target="tpu_custom_call" | custom-call | flops 1107296256 | bytes 16739840 | tf_op jit(solution)/shard_map/pallas_call | solution.py:80
  131.4 2.5 shard_map.331
  134.0 2.0 collective-permute-start.26
  136.0 2.4 shard_map.333
  140.0 6.1 %collective-permute-done.26 = bf16[256,768]{1,0:T(8,128)(2,1)S(1)} collective-permute-done((bf16[256,768]{1,0:T(8,128)(2,1)S(1)}, bf16[256,768]{1,0:T(8,128)(2,1)S(1)}, u32[]{:S(2)}, u32[]{:S(2)}) %collective-permute-start.26) | collective-permute-done | bytes 393248 | tf_op jit(solution)/shard_map/ppermute | solution.py:21
  147.2 16.3 %shard_map.332 = (bf16[2,768,1536]{2,1,0:T(8,128)(2,1)}, bf16[2,768,1536]{2,1,0:T(8,128)(2,1)}, f32[768,768]{1,0:T(8,128)}, bf16[768,768]{1,0:T(8,128)(2,1)S(1)}...) custom-call(f32[768,768]{1,0:T(8,128)} %get-tuple-element.236.hidden, ...), custom_call_target="tpu_custom_call" | custom-call | flops 3623878656 | bytes 18304512 | tf_op jit(solution)/shard_map/pallas_call | solution.py:80
  164.8 3.9 shard_map.334
  170.1 2.0 collective-permute-start.28
  172.1 2.2 fusion.14.grad
  175.3 7.3 %shard_map.335 = (bf16[2,768,576]{2,1,0:T(8,128)(2,1)S(1)}, bf16[2,512,192]{2,1,0:T(8,128)(2,1)S(1)}, f32[2,8,512]{2,1,0:T(8,128)S(1)}) custom-call(bf16[768,768]{1,0:T(8,128)(2,1)S(1)} %get-tuple-element.248.rows.refs_4_, bf16[2,384,2304]{2,1,0:T(8,128)(2,1)} %bitcast.132, ...), custom_call_target="tpu_custom_call" | custom-call | flops 880803840 | bytes 8769792 | tf_op jit(solution)/shard_map/pallas_call | solution.py:80
  183.9 9.9 %shard_map.336 = (bf16[2,256,576]{2,1,0:T(8,128)(2,1)S(1)}, bf16[2,768,192]{2,1,0:T(8,128)(2,1)S(1)}, f32[2,8,256]{2,1,0:T(8,128)S(1)}, f32[768,768]{1,0:T(8,128...) custom-call(f32[768,768]{1,0:T(8,128)} %get-tuple-element.247.rows, ...), custom_call_target="tpu_custom_call" | custom-call | flops 553648128 | bytes 16049408 | tf_op jit(solution)/shard_map/pallas_call | solution.py:80
  194.6 12.1 %shard_map.337 = (bf16[2,768,768]{2,1,0:T(8,128)(2,1)}, bf16[2,768,768]{2,1,0:T(8,128)(2,1)}, f32[768,768]{1,0:T(8,128)}, bf16[768,768]{1,0:T(8,128)(2,1)}, bf16...) custom-call(f32[768,768]{1,0:T(8,128)} %get-tuple-element.257.hidden, ...), custom_call_target="tpu_custom_call" | custom-call | flops 1811939328 | bytes 13582848 | tf_op jit(solution)/shard_map/pallas_call | solution.py:80
  209.0 2.0 collective-permute-start.29
  212.2 11.8 %shard_map.338 = (bf16[768,768]{1,0:T(8,128)(2,1)S(1)}, bf16[2,768,768]{2,1,0:T(8,128)(2,1)}, f32[768,768]{1,0:T(8,128)}, bf16[768,768]{1,0:T(8,128)(2,1)S(1)}, ...) custom-call(bf16[768,768]{1,0:T(8,128)(2,1)S(1)} %copy-done.32, bf16[768,768]{1,0:T(8,128)(2,1)S(1)} %copy-done.34, ...), custom_call_target="tpu_custom_call" | custom-call | flops 1811939328 | bytes 13596672 | tf_op jit(solution)/shard_map/pallas_call | solution.py:80
  224.1 7.8 %shard_map.339 = (bf16[2,256,576]{2,1,0:T(8,128)(2,1)S(1)}, bf16[2,256,576]{2,1,0:T(8,128)(2,1)S(1)}, f32[2,8,576]{2,1,0:T(8,128)S(1)}, bf16[256,768]{1,0:T(8,128)(2,1)S(1)}) custom-call(bf16[768,768]{1,0:T(8,128)(2,1)S(1)} %get-tuple-element.262.d_mid.d_mid_low.refs_8_, bf16[2,768,576]{2,1,0:T(8,128)(2,1)S(1)} %copy-done.8, ...), custom_call_target="tpu_custom_call" | custom-call | flops 553648128 | bytes 13200896 | tf_op jit(solution)/shard_map/pallas_call | solution.py:80
  233.1 13.4 %shard_map.340 = (bf16[2,768,576]{2,1,0:T(8,128)(2,1)S(1)}, f32[2,8,576]{2,1,0:T(8,128)S(1)}, f32[768,768]{1,0:T(8,128)}) custom-call(bf16[768,768]{1,0:T(8,128)(2,1)S(1)} %get-tuple-element.262.d_mid.d_mid_low.refs_8_, bf16[2,256,576]{2,1,0:T(8,128)(2,1)S(1)} %get-tuple-element.267.d_shared, bf16[2,768,576]{2,1,0:T(8,128)(2,1)S(1)} %copy-done.8, ...), custom_call_target="tpu_custom_call" | custom-call | flops 1333788672 | bytes 15667200 | tf_op jit(solution)/shard_map/pallas_call | solution.py:80
  247.8 9.9 %shard_map.341 = bf16[2,384,2304]{2,1,0:T(8,128)(2,1)} custom-call(bf16[384,768]{1,0:T(8,128)(2,1)S(1)} %get-tuple-element.390.pick, bf16[768,768]{1,0:T(8,128)(2,1)S(1)} %get-tuple-element.258.hidden_low.refs_0_, bf16[2,768,768]{2,1,0:T(8,128)(2,1)} %get-tuple-element.271.refs_1_, bf16[768,768]{1,0:T(8,128)(2,1)S(1)} %get-tuple-element.272.refs_2_, ...), custom_call_target="tpu_custom_call" | custom-call | flops 2453667840 | bytes 8454144 | tf_op jit(solution)/shard_map/pallas_call | solution.py:80
  257.8 11.1 %shard_map.342 = (f32[768,768]{1,0:T(8,128)S(1)}, bf16[768,768]{1,0:T(8,128)(2,1)S(1)}, bf16[2,768,1536]{2,1,0:T(8,128)(2,1)}, f32[8,768]{1,0:T(8,128)S(1)}, f32[4,1,768]{2,1,0:T(1,128)S(1)}) custom-call(f32[768,768]{1,0:T(8,128)} %get-tuple-element.279.grad, bf16[256,768]{1,0:T(8,128)(2,1)S(1)} %collective-permute-done.30.extra, ...), custom_call_target="tpu_custom_call" | custom-call | flops 1811939328 | bytes 13204992 | tf_op jit(solution)/shard_map/pallas_call | solution.py:80
  268.9 14.0 %shard_map.343 = (bf16[384,1152]{1,0:T(8,128)(2,1)}, f32[384,1152]{1,0:T(8,128)}, bf16[2,192,1152]{2,1,0:T(8,128)(2,1)S(1)}, f32[2,192,1152]{2,1,0:T(8,128)}) custom-call(bf16[384,768]{1,0:T(8,128)(2,1)S(1)} %get-tuple-element.389.pick, bf16[2,384,2304]{2,1,0:T(8,128)(2,1)} %collective-permute-done.31.got, ...), custom_call_target="tpu_custom_call" | custom-call | flops 2453667840 | bytes 11108352 | tf_op jit(solution)/shard_map/pallas_call | solution.py:80
  282.9 9.0 %shard_map.344 = bf16[2,384,3072]{2,1,0:T(8,128)(2,1)} custom-call(bf16[384,768]{1,0:T(8,128)(2,1)S(1)} %get-tuple-element.390.pick, bf16[768,768]{1,0:T(8,128)(2,1)S(1)} %get-tuple-element.237.hidden_low.refs_0_, bf16[2,768,1536]{2,1,0:T(8,128)(2,1)} %get-tuple-element.293.refs_1_.d_pre, bf16[768,768]{1,0:T(8,128)(2,1)S(1)} %get-tuple-element.291.refs_2_, ...), custom_call_target="tpu_custom_call" | custom-call | flops 2264924160 | bytes 8552448 | tf_op jit(solution)/shard_map/pallas_call | solution.py:80
  292.5 1.9 collective-permute-start.33
  296.0 9.6 %shard_map.345 = (f32[768,768]{1,0:T(8,128)S(1)}, bf16[768,768]{1,0:T(8,128)(2,1)S(1)}, f32[8,768]{1,0:T(8,128)S(1)}) custom-call(f32[768,768]{1,0:T(8,128)} %copy-done.26, bf16[2,768,1536]{2,1,0:T(8,128)(2,1)} %get-tuple-element.293.refs_1_.d_pre, bf16[768,768]{1,0:T(8,128)(2,1)S(1)} %copy-done.29, f32[768,1]{1,0:T(8,128)S(1)} %copy-done.37, ...), custom_call_target="tpu_custom_call" | custom-call | flops 1811939328 | bytes 10642944 | tf_op jit(solution)/shard_map/pallas_call | solution.py:80
  307.1 10.8 %shard_map.346 = (bf16[384,1536]{1,0:T(8,128)(2,1)}, f32[384,1536]{1,0:T(8,128)}, bf16[2,192,1536]{2,1,0:T(8,128)(2,1)}, f32[2,192,1536]{2,1,0:T(8,128)}) custom-call(bf16[384,768]{1,0:T(8,128)(2,1)S(1)} %get-tuple-element.389.pick, bf16[2,384,3072]{2,1,0:T(8,128)(2,1)} %collective-permute-done.32.got, ...), custom_call_target="tpu_custom_call" | custom-call | flops 2264924160 | bytes 12091392 | tf_op jit(solution)/shard_map/pallas_call | solution.py:80
  324.0 1.9 collective-permute-start.38
  327.3 10.4 %shard_map.347 = (bf16[2,256,1152]{2,1,0:T(8,128)(2,1)S(1)}, bf16[2,256,1152]{2,1,0:T(8,128)(2,1)S(1)}, f32[2,8,1152]{2,1,0:T(8,128)S(1)}, bf16[256,768]{1,0:T(8,128)(2,1)S(1)}) custom-call(bf16[768,768]{1,0:T(8,128)(2,1)S(1)} %get-tuple-element.309.d_mid.d_mid_low.refs_4_, bf16[2,768,1152]{2,1,0:T(8,128)(2,1)} %get-tuple-element.227.proj, ...), custom_call_target="tpu_custom_call" | custom-call | flops 1107296256 | bytes 14595584 | tf_op jit(solution)/shard_map/pallas_call | solution.py:80
  340.9 13.2 %shard_map.348 = (bf16[2,768,1152]{2,1,0:T(8,128)(2,1)}, f32[2,8,1152]{2,1,0:T(8,128)S(1)}) custom-call(bf16[768,768]{1,0:T(8,128)(2,1)S(1)} %get-tuple-element.309.d_mid.d_mid_low.refs_4_, bf16[2,256,1152]{2,1,0:T(8,128)(2,1)S(1)} %get-tuple-element.316.d_shared, bf16[2,768,1152]{2,1,0:T(8,128)(2,1)} %get-tuple-element.227.proj, ...), custom_call_target="tpu_custom_call" | custom-call | flops 1308622848 | bytes 7329792 | tf_op jit(solution)/shard_map/pallas_call | solution.py:80
  354.2 7.4 %shard_map.349 = bf16[2,384,1536]{2,1,0:T(8,128)(2,1)} custom-call(bf16[384,768]{1,0:T(8,128)(2,1)S(1)} %get-tuple-element.390.pick, bf16[768,768]{1,0:T(8,128)(2,1)S(1)} %copy-done.5, bf16[2,768,1152]{2,1,0:T(8,128)(2,1)} %get-tuple-element.340.refs_1_.d_proj, bf16[256,768]{1,0:T(8,128)(2,1)S(1)} %copy-done.18, ...), custom_call_target="tpu_custom_call" | custom-call | flops 1660944384 | bytes 5799936 | tf_op jit(solution)/shard_map/pallas_call | solution.py:80
  362.5 4.7 %collective-permute-done.40 = f32[22,768]{1,0:T(8,128)S(1)} collective-permute-done((f32[22,768]{1,0:T(8,128)}, f32[22,768]{1,0:T(8,128)S(1)}, u32[]{:S(2)}, u32[]{:S(2)}) %collective-permute-start.40) | collective-permute-done | bytes 67616 | tf_op jit(solution)/shard_map/ppermute | solution.py:21
  367.2 1.7 convert_add_fusion.1
  369.2 1.6 convert_add_fusion
  372.5 2.0 collective-permute-start.50
  377.7 8.7 %shard_map.350 = (bf16[384,768]{1,0:T(8,128)(2,1)S(1)}, f32[384,768]{1,0:T(8,128)S(1)}, bf16[2,192,768]{2,1,0:T(8,128)(2,1)S(1)}, f32[2,192,768]{2,1,0:T(8,128)S(1)}) custom-call(bf16[384,768]{1,0:T(8,128)(2,1)S(1)} %get-tuple-element.389.pick, bf16[2,384,1536]{2,1,0:T(8,128)(2,1)} %collective-permute-done.37.got, bf16[768,768]{1,0:T(8,128)(2,1)S(1)} %copy-done.6, ...), custom_call_target="tpu_custom_call" | custom-call | flops 1660944384 | bytes 7569408 | tf_op jit(solution)/shard_map/pallas_call | solution.py:80
  386.4 1.8 collective-permute-start.44
  388.2 3.0 collective-permute-done.50
  391.3 1.7 collective-permute-start.41
  395.8 1.8 collective-permute-start.53
  398.2 6.2 %shard_map.351 = f32[768,768]{1,0:T(8,128)S(1)} custom-call(f32[768,768]{1,0:T(8,128)S(1)} %copy-done.25, bf16[2,768,1152]{2,1,0:T(8,128)(2,1)} %get-tuple-element.340.refs_1_.d_proj, bf16[2,384,1664]{2,1,0:T(8,128)(2,1)} %bitcast.122, bf16[2,384,1664]{2,1,0:T(8,128)(2,1)} %collective-permute-done.13.refs_1_.refs_3_.refs_5_.refs_7_.out_two, ...), custom_call_target="tpu_custom_call" | custom-call | flops 1358954496 | bytes 11796480 | tf_op jit(solution)/shard_map/pallas_call | solution.py:80
  406.5 2.0 collective-permute-done.41
  408.6 2.4 collective-permute-start.54
  418.9 4.2 collective-permute-done.45
  429.8 1.8 collective-permute-done.56
  435.5 1.7 collective-permute-start.59
  438.9 2.3 collective-permute-done.58
  442.4 4.2 collective-permute-start.61
  (431 shorter events, 102.5 us)
Async XLA Ops:
  3.2 29.0 %collective-permute-start.4 = (bf16[256,768]{1,0:T(8,128)(2,1)S(1)}, bf16[256,768]{1,0:T(8,128)(2,1)S(1)}, u32[]{:S(2)}, u32[]{:S(2)}) collective-permute-start(bf16[256,768]{1,0:T(8,128)(2,1)S(1)} %get-tuple-element.396), channel_id=1, source_target_pairs={{0,1},{1,0},{2,3},{3,2},{4,5},{5,4},{6,7},{7,6},{8,9},{9,8},{10,11... | collective-permute-start | bytes 1179656 | tf_op jit(solution)/shard_map/ppermute | solution.py:21
  7.3 24.1 %collective-permute-start.3 = (bf16[48,3072]{1,0:T(8,128)(2,1)S(1)}, bf16[48,3072]{1,0:T(8,128)(2,1)S(1)}, u32[]{:S(2)}, u32[]{:S(2)}) collective-permute-start(bf16[48,3072]{1,0:T(8,128)(2,1)S(1)} %get-tuple-element.195.refs_0_), channel_id=1, source_target_pairs={{0,16},{2,18},{4,20},{6,22},{16,24},{18,26},{20,28},{22,30},{24,8}... | collective-permute-start | bytes 884744 | tf_op jit(solution)/shard_map/ppermute | solution.py:41
  10.0 10.9 %collective-permute-start = (bf16[48,1664]{1,0:T(8,128)(2,1)S(1)}, bf16[48,1664]{1,0:T(8,128)(2,1)S(1)}, u32[]{:S(2)}, u32[]{:S(2)}) collective-permute-start(bf16[48,1664]{1,0:T(8,128)(2,1)S(1)} %get-tuple-element.198.refs_0_), channel_id=1, source_target_pairs={{0,16},{2,18},{4,20},{6,22},{16,24},{18,26},{20,28},{22,30},{24,8}... | collective-permute-start | bytes 479240 | tf_op jit(solution)/shard_map/ppermute | solution.py:41
  11.6 14.6 %collective-permute-start.1 = (bf16[48,1664]{1,0:T(8,128)(2,1)S(1)}, bf16[48,1664]{1,0:T(8,128)(2,1)S(1)}, u32[]{:S(2)}, u32[]{:S(2)}) collective-permute-start(bf16[48,1664]{1,0:T(8,128)(2,1)S(1)} %get-tuple-element.198.refs_0_), channel_id=1, source_target_pairs={{0,24},{2,26},{4,28},{6,30},{16,8},{18,10},{20,12},{22,14},{24,0},... | collective-permute-start | bytes 479240 | tf_op jit(solution)/shard_map/ppermute | solution.py:41
  11.8 19.7 %collective-permute-start.2 = (bf16[48,1664]{1,0:T(8,128)(2,1)S(1)}, bf16[48,1664]{1,0:T(8,128)(2,1)S(1)}, u32[]{:S(2)}, u32[]{:S(2)}) collective-permute-start(bf16[48,1664]{1,0:T(8,128)(2,1)S(1)} %get-tuple-element.198.refs_0_), channel_id=1, source_target_pairs={{0,8},{2,10},{4,12},{6,14},{16,0},{18,2},{20,4},{22,6},{24,16},{26... | collective-permute-start | bytes 479240 | tf_op jit(solution)/shard_map/ppermute | solution.py:41
  32.2 13.8 %collective-permute-start.6 = (bf16[4,48,896]{2,1,0:T(8,128)(2,1)S(1)}, bf16[4,48,896]{2,1,0:T(8,128)(2,1)S(1)}, u32[]{:S(2)}, u32[]{:S(2)}) collective-permute-start(bf16[4,48,896]{2,1,0:T(8,128)(2,1)S(1)} %get-tuple-element.203.refs_2_), channel_id=1, source_target_pairs={{0,1},{1,0},{2,3},{3,2},{4,5},{5,4},{6,7},{7,6},{8,9},{9,8},{10,11... | collective-permute-start | bytes 1032200 | tf_op jit(solution)/shard_map/ppermute | solution.py:21
  32.8 13.2 %collective-permute-start.9 = (bf16[48,3072]{1,0:T(8,128)(2,1)S(1)}, bf16[48,3072]{1,0:T(8,128)(2,1)S(1)}, u32[]{:S(2)}, u32[]{:S(2)}) collective-permute-start(bf16[48,3072]{1,0:T(8,128)(2,1)S(1)} %get-tuple-element.195.refs_0_), channel_id=1, source_target_pairs={{0,24},{2,26},{4,28},{6,30},{16,8},{18,10},{20,12},{22,14},{24,0},... | collective-permute-start | bytes 884744 | tf_op jit(solution)/shard_map/ppermute | solution.py:41
  35.3 10.8 %collective-permute-start.5 = (bf16[4,48,768]{2,1,0:T(8,128)(2,1)S(1)}, bf16[4,48,768]{2,1,0:T(8,128)(2,1)S(1)}, u32[]{:S(2)}, u32[]{:S(2)}) collective-permute-start(bf16[4,48,768]{2,1,0:T(8,128)(2,1)S(1)} %get-tuple-element.202.refs_0_), channel_id=1, source_target_pairs={{0,4},{2,6},{4,0},{6,2},{8,12},{10,14},{12,8},{14,10},{16,20},{18,... | collective-permute-start | bytes 884744 | tf_op jit(solution)/shard_map/ppermute | solution.py:26
  36.8 9.2 %collective-permute-start.7 = (bf16[48,1152]{1,0:T(8,128)(2,1)S(1)}, bf16[48,1152]{1,0:T(8,128)(2,1)S(1)}, u32[]{:S(2)}, u32[]{:S(2)}) collective-permute-start(bf16[48,1152]{1,0:T(8,128)(2,1)S(1)} %get-tuple-element.204.refs_0_), channel_id=1, source_target_pairs={{0,4},{2,6},{4,0},{6,2},{8,12},{10,14},{12,8},{14,10},{16,20},{18,... | collective-permute-start | bytes 331784 | tf_op jit(solution)/shard_map/ppermute | solution.py:26
  37.3 8.7 %collective-permute-start.8 = (bf16[48,1152]{1,0:T(8,128)(2,1)S(1)}, bf16[48,1152]{1,0:T(8,128)(2,1)S(1)}, u32[]{:S(2)}, u32[]{:S(2)}) collective-permute-start(bf16[48,1152]{1,0:T(8,128)(2,1)S(1)} %get-tuple-element.205.refs_2_), channel_id=1, source_target_pairs={{0,1},{1,0},{2,3},{3,2},{4,5},{5,4},{6,7},{7,6},{8,9},{9,8},{10,11... | collective-permute-start | bytes 331784 | tf_op jit(solution)/shard_map/ppermute | solution.py:21
  46.8 15.9 %collective-permute-start.11 = (bf16[2,4,48,896]{3,2,1,0:T(8,128)(2,1)S(1)}, bf16[2,4,48,896]{3,2,1,0:T(8,128)(2,1)S(1)}, u32[]{:S(2)}, u32[]{:S(2)}) collective-permute-start(bf16[2,4,48,896]{3,2,1,0:T(8,128)(2,1)S(1)} %get-tuple-element.210.refs_2_), channel_id=1, source_target_pairs={{0,4},{2,6},{4,0},{6,2},{8,12},{10,14},{12,8},{14,10},{16,20},{18,... | collective-permute-start | bytes 2064392 | tf_op jit(solution)/shard_map/ppermute | solution.py:26
  48.3 13.6 %collective-permute-start.10 = (bf16[2,4,48,768]{3,2,1,0:T(8,128)(2,1)S(1)}, bf16[2,4,48,768]{3,2,1,0:T(8,128)(2,1)S(1)}, u32[]{:S(2)}, u32[]{:S(2)}) collective-permute-start(bf16[2,4,48,768]{3,2,1,0:T(8,128)(2,1)S(1)} %get-tuple-element.209.refs_0_), channel_id=1, source_target_pairs={{0,1},{1,0},{2,3},{3,2},{4,5},{5,4},{6,7},{7,6},{8,9},{9,8},{10,11... | collective-permute-start | bytes 1769480 | tf_op jit(solution)/shard_map/ppermute | solution.py:21
  49.9 7.8 %collective-permute-start.12 = (bf16[48,3072]{1,0:T(8,128)(2,1)S(1)}, bf16[48,3072]{1,0:T(8,128)(2,1)S(1)}, u32[]{:S(2)}, u32[]{:S(2)}) collective-permute-start(bf16[48,3072]{1,0:T(8,128)(2,1)S(1)} %get-tuple-element.195.refs_0_), channel_id=1, source_target_pairs={{0,8},{2,10},{4,12},{6,14},{16,0},{18,2},{20,4},{22,6},{24,16},{26... | collective-permute-start | bytes 884744 | tf_op jit(solution)/shard_map/ppermute | solution.py:41
  62.9 34.4 %collective-permute-start.13 = (bf16[2,384,1664]{2,1,0:T(8,128)(2,1)S(1)}, bf16[2,384,1664]{2,1,0:T(8,128)(2,1)}, u32[]{:S(2)}, u32[]{:S(2)}) collective-permute-start(bf16[2,384,1664]{2,1,0:T(8,128)(2,1)S(1)} %bitcast.109), channel_id=1, source_target_pairs={{0,2},{2,0},{4,6},{6,4},{8,10},{10,8},{12,14},{14,12},{16,18},{18,... | collective-permute-start | bytes 7667720 | tf_op jit(solution)/shard_map/ppermute | solution.py:31
  63.1 21.2 %collective-permute-start.16 = (bf16[3456]{0:T(1024)(128)(2,1)S(1)}, bf16[3456]{0:T(1024)(128)(2,1)S(1)}, u32[]{:S(2)}, u32[]{:S(2)}) collective-permute-start(bf16[3456]{0:T(1024)(128)(2,1)S(1)} %concatenate.90), channel_id=1, source_target_pairs={{0,1},{1,0},{2,3},{3,2},{4,5},{5,4},{6,7},{7,6},{8,9},{9,8},{10,11... | collective-permute-start | bytes 20744 | tf_op jit(solution)/shard_map/ppermute | solution.py:21
  69.1 106.2 %copy-start.11 = (s32[512,1]{1,0:T(8,128)}, s32[512,1]{1,0:T(8,128)S(1)}, u32[]{:S(2)}) copy-start(s32[512,1]{1,0:T(8,128)S(1)} %broadcast_select_fusion.1.refs_8_.refs_6_.segs_k) | copy-start | bytes 6148
  73.7 12.7 %collective-permute-start.17 = (bf16[2,48,2304]{2,1,0:T(8,128)(2,1)}, bf16[2,48,2304]{2,1,0:T(8,128)(2,1)}, u32[]{:S(2)}, u32[]{:S(2)}) collective-permute-start(bf16[2,48,2304]{2,1,0:T(8,128)(2,1)} %shard_map.327.refs_0_), channel_id=1, source_target_pairs={{0,16},{2,18},{4,20},{6,22},{16,24},{18,26},{20,28},{22,30},{24,8}... | collective-permute-start | bytes 1327112 | tf_op jit(solution)/shard_map/ppermute | solution.py:41
  79.2 15.5 %collective-permute-start.14 = (bf16[4,48,1536]{2,1,0:T(8,128)(2,1)}, bf16[4,48,1536]{2,1,0:T(8,128)(2,1)}, u32[]{:S(2)}, u32[]{:S(2)}) collective-permute-start(bf16[4,48,1536]{2,1,0:T(8,128)(2,1)} %get-tuple-element.212.refs_0_), channel_id=1, source_target_pairs={{0,4},{2,6},{4,0},{6,2},{8,12},{10,14},{12,8},{14,10},{16,20},{18,... | collective-permute-start | bytes 1769480 | tf_op jit(solution)/shard_map/ppermute | solution.py:26
  80.7 16.6 %collective-permute-start.15 = (bf16[4,48,1536]{2,1,0:T(8,128)(2,1)}, bf16[4,48,1536]{2,1,0:T(8,128)(2,1)}, u32[]{:S(2)}, u32[]{:S(2)}) collective-permute-start(bf16[4,48,1536]{2,1,0:T(8,128)(2,1)} %get-tuple-element.215.refs_2_), channel_id=1, source_target_pairs={{0,1},{1,0},{2,3},{3,2},{4,5},{5,4},{6,7},{7,6},{8,9},{9,8},{10,11... | collective-permute-start | bytes 1769480 | tf_op jit(solution)/shard_map/ppermute | solution.py:21
  84.4 29.7 %collective-permute-start.18 = (bf16[256,768]{1,0:T(8,128)(2,1)}, bf16[256,768]{1,0:T(8,128)(2,1)}, u32[]{:S(2)}, u32[]{:S(2)}) collective-permute-start(bf16[256,768]{1,0:T(8,128)(2,1)} %get-tuple-element.395), channel_id=1, source_target_pairs={{0,1},{1,0},{2,3},{3,2},{4,5},{5,4},{6,7},{7,6},{8,9},{9,8},{10,11... | collective-permute-start | bytes 1179656 | tf_op jit(solution)/shard_map/ppermute | solution.py:21
  86.4 27.6 %collective-permute-start.19 = (bf16[2,48,2304]{2,1,0:T(8,128)(2,1)}, bf16[2,48,2304]{2,1,0:T(8,128)(2,1)}, u32[]{:S(2)}, u32[]{:S(2)}) collective-permute-start(bf16[2,48,2304]{2,1,0:T(8,128)(2,1)} %shard_map.327.refs_0_), channel_id=1, source_target_pairs={{0,24},{2,26},{4,28},{6,30},{16,8},{18,10},{20,12},{22,14},{24,0},... | collective-permute-start | bytes 1327112 | tf_op jit(solution)/shard_map/ppermute | solution.py:41
  94.7 36.7 %collective-permute-start.22 = (bf16[2,48,2304]{2,1,0:T(8,128)(2,1)}, bf16[2,48,2304]{2,1,0:T(8,128)(2,1)}, u32[]{:S(2)}, u32[]{:S(2)}) collective-permute-start(bf16[2,48,2304]{2,1,0:T(8,128)(2,1)} %shard_map.327.refs_0_), channel_id=1, source_target_pairs={{0,8},{2,10},{4,12},{6,14},{16,0},{18,2},{20,4},{22,6},{24,16},{26... | collective-permute-start | bytes 1327112 | tf_op jit(solution)/shard_map/ppermute | solution.py:41
  100.3 31.1 %collective-permute-start.20 = (bf16[2,4,48,1536]{3,2,1,0:T(8,128)(2,1)S(1)}, bf16[2,4,48,1536]{3,2,1,0:T(8,128)(2,1)S(1)}, u32[]{:S(2)}, u32[]{:S(2)}) collective-permute-start(bf16[2,4,48,1536]{3,2,1,0:T(8,128)(2,1)S(1)} %get-tuple-element.232.refs_0_), channel_id=1, source_target_pairs={{0,1},{1,0},{2,3},{3,2},{4,5},{5,4},{6,7},{7,6},{8,9},{9,8},{10,11... | collective-permute-start | bytes 3538952 | tf_op jit(solution)/shard_map/ppermute | solution.py:21
  100.3 31.0 %collective-permute-start.21 = (bf16[2,4,48,1536]{3,2,1,0:T(8,128)(2,1)S(1)}, bf16[2,4,48,1536]{3,2,1,0:T(8,128)(2,1)S(1)}, u32[]{:S(2)}, u32[]{:S(2)}) collective-permute-start(bf16[2,4,48,1536]{3,2,1,0:T(8,128)(2,1)S(1)} %get-tuple-element.234.refs_2_), channel_id=1, source_target_pairs={{0,4},{2,6},{4,0},{6,2},{8,12},{10,14},{12,8},{14,10},{16,20},{18,... | collective-permute-start | bytes 3538952 | tf_op jit(solution)/shard_map/ppermute | solution.py:26
  133.9 13.3 %collective-permute-start.23 = (bf16[2,384,3072]{2,1,0:T(8,128)(2,1)}, bf16[2,384,3072]{2,1,0:T(8,128)(2,1)}, u32[]{:S(2)}, u32[]{:S(2)}) collective-permute-start(bf16[2,384,3072]{2,1,0:T(8,128)(2,1)} %bitcast.147), channel_id=1, source_target_pairs={{0,2},{2,0},{4,6},{6,4},{8,10},{10,8},{12,14},{14,12},{16,18},{18,... | collective-permute-start | bytes 14155784 | tf_op jit(solution)/shard_map/ppermute | solution.py:31
  134.0 12.1 %collective-permute-start.26 = (bf16[256,768]{1,0:T(8,128)(2,1)S(1)}, bf16[256,768]{1,0:T(8,128)(2,1)S(1)}, u32[]{:S(2)}, u32[]{:S(2)}) collective-permute-start(bf16[256,768]{1,0:T(8,128)(2,1)S(1)} %get-tuple-element.393), channel_id=1, source_target_pairs={{0,1},{1,0},{2,3},{3,2},{4,5},{5,4},{6,7},{7,6},{8,9},{9,8},{10,11... | collective-permute-start | bytes 1179656 | tf_op jit(solution)/shard_map/ppermute | solution.py:21
  138.4 26.5 %collective-permute-start.24 = (bf16[2,4,48,1152]{3,2,1,0:T(8,128)(2,1)S(1)}, bf16[2,4,48,1152]{3,2,1,0:T(8,128)(2,1)}, u32[]{:S(2)}, u32[]{:S(2)}) collective-permute-start(bf16[2,4,48,1152]{3,2,1,0:T(8,128)(2,1)S(1)} %get-tuple-element.244.refs_0_), channel_id=1, source_target_pairs={{0,1},{1,0},{2,3},{3,2},{4,5},{5,4},{6,7},{7,6},{8,9},{9,8},{10,11... | collective-permute-start | bytes 2654216 | tf_op jit(solution)/shard_map/ppermute | solution.py:21
  138.5 26.4 %collective-permute-start.25 = (bf16[2,4,48,1152]{3,2,1,0:T(8,128)(2,1)}, bf16[2,4,48,1152]{3,2,1,0:T(8,128)(2,1)}, u32[]{:S(2)}, u32[]{:S(2)}) collective-permute-start(bf16[2,4,48,1152]{3,2,1,0:T(8,128)(2,1)} %get-tuple-element.245.refs_2_), channel_id=1, source_target_pairs={{0,4},{2,6},{4,0},{6,2},{8,12},{10,14},{12,8},{14,10},{16,20},{18,... | collective-permute-start | bytes 2654216 | tf_op jit(solution)/shard_map/ppermute | solution.py:26
  164.5 83.3 %copy-start.9 = (bf16[768,768]{1,0:T(8,128)(2,1)}, bf16[768,768]{1,0:T(8,128)(2,1)S(1)}, u32[]{:S(2)}) copy-start(bf16[768,768]{1,0:T(8,128)(2,1)S(1)} %get-tuple-element.248.rows.refs_4_) | copy-start | bytes 3538948
  168.8 6.6 %collective-permute-start.27 = (bf16[2,384,2304]{2,1,0:T(8,128)(2,1)}, bf16[2,384,2304]{2,1,0:T(8,128)(2,1)}, u32[]{:S(2)}, u32[]{:S(2)}) collective-permute-start(bf16[2,384,2304]{2,1,0:T(8,128)(2,1)} %bitcast.131), channel_id=1, source_target_pairs={{0,2},{2,0},{4,6},{6,4},{8,10},{10,8},{12,14},{14,12},{16,18},{18,... | collective-permute-start | bytes 10616840 | tf_op jit(solution)/shard_map/ppermute | solution.py:31
  170.1 13.8 %collective-permute-start.28 = (bf16[256,768]{1,0:T(8,128)(2,1)S(1)}, bf16[256,768]{1,0:T(8,128)(2,1)S(1)}, u32[]{:S(2)}, u32[]{:S(2)}) collective-permute-start(bf16[256,768]{1,0:T(8,128)(2,1)S(1)} %slice.431), channel_id=1, source_target_pairs={{0,1},{1,0},{2,3},{3,2},{4,5},{5,4},{6,7},{7,6},{8,9},{9,8},{10,11... | collective-permute-start | bytes 1179656 | tf_op jit(solution)/shard_map/ppermute | solution.py:21
  209.0 23.2 %collective-permute-start.29 = (bf16[256,768]{1,0:T(8,128)(2,1)S(1)}, bf16[256,768]{1,0:T(8,128)(2,1)S(1)}, u32[]{:S(2)}, u32[]{:S(2)}) collective-permute-start(bf16[256,768]{1,0:T(8,128)(2,1)S(1)} %slice.699), channel_id=1, source_target_pairs={{0,1},{1,0},{2,3},{3,2},{4,5},{5,4},{6,7},{7,6},{8,9},{9,8},{10,11... | collective-permute-start | bytes 1179656 | tf_op jit(solution)/shard_map/ppermute | solution.py:21
  231.9 15.8 %collective-permute-start.30 = (bf16[256,768]{1,0:T(8,128)(2,1)S(1)}, bf16[256,768]{1,0:T(8,128)(2,1)S(1)}, u32[]{:S(2)}, u32[]{:S(2)}) collective-permute-start(bf16[256,768]{1,0:T(8,128)(2,1)S(1)} %get-tuple-element.275), channel_id=1, source_target_pairs={{0,1},{1,0},{2,3},{3,2},{4,5},{5,4},{6,7},{7,6},{8,9},{9,8},{10,11... | collective-permute-start | bytes 1179656 | tf_op jit(solution)/shard_map/ppermute | solution.py:21
  257.8 11.1 %collective-permute-start.31 = (bf16[2,384,2304]{2,1,0:T(8,128)(2,1)}, bf16[2,384,2304]{2,1,0:T(8,128)(2,1)}, u32[]{:S(2)}, u32[]{:S(2)}) collective-permute-start(bf16[2,384,2304]{2,1,0:T(8,128)(2,1)} %shard_map.341), channel_id=1, source_target_pairs={{0,2},{2,0},{4,6},{6,4},{8,10},{10,8},{12,14},{14,12},{16,18},{18,... | collective-permute-start | bytes 10616840 | tf_op jit(solution)/shard_map/ppermute | solution.py:31
  291.9 15.1 %collective-permute-start.32 = (bf16[2,384,3072]{2,1,0:T(8,128)(2,1)}, bf16[2,384,3072]{2,1,0:T(8,128)(2,1)}, u32[]{:S(2)}, u32[]{:S(2)}) collective-permute-start(bf16[2,384,3072]{2,1,0:T(8,128)(2,1)} %shard_map.344), channel_id=1, source_target_pairs={{0,2},{2,0},{4,6},{6,4},{8,10},{10,8},{12,14},{14,12},{16,18},{18,... | collective-permute-start | bytes 14155784 | tf_op jit(solution)/shard_map/ppermute | solution.py:31
  292.5 25.4 %collective-permute-start.33 = (bf16[384,1152]{1,0:T(8,128)(2,1)}, bf16[384,1152]{1,0:T(8,128)(2,1)S(1)}, u32[]{:S(2)}, u32[]{:S(2)}) collective-permute-start(bf16[384,1152]{1,0:T(8,128)(2,1)} %get-tuple-element.288), channel_id=1, source_target_pairs={{0,1},{1,0},{2,3},{3,2},{4,5},{5,4},{6,7},{7,6},{8,9},{9,8},{10,11... | collective-permute-start | bytes 2654216 | tf_op jit(solution)/shard_map/ppermute | solution.py:21
  294.4 23.5 %collective-permute-start.34 = (bf16[2,192,1152]{2,1,0:T(8,128)(2,1)S(1)}, bf16[2,192,1152]{2,1,0:T(8,128)(2,1)S(1)}, u32[]{:S(2)}, u32[]{:S(2)}) collective-permute-start(bf16[2,192,1152]{2,1,0:T(8,128)(2,1)S(1)} %get-tuple-element.289), channel_id=1, source_target_pairs={{0,4},{2,6},{4,0},{6,2},{8,12},{10,14},{12,8},{14,10},{16,20},{18,... | collective-permute-start | bytes 2654216 | tf_op jit(solution)/shard_map/ppermute | solution.py:26
  322.0 15.7 %collective-permute-start.36 = (bf16[192,1152]{1,0:T(8,128)(2,1)S(1)}, bf16[192,1152]{1,0:T(8,128)(2,1)S(1)}, u32[]{:S(2)}, u32[]{:S(2)}) collective-permute-start(bf16[192,1152]{1,0:T(8,128)(2,1)S(1)} %fusion.44), channel_id=1, source_target_pairs={{0,1},{1,0},{2,3},{3,2},{4,5},{5,4},{6,7},{7,6},{8,9},{9,8},{10,11... | collective-permute-start | bytes 1327112 | tf_op jit(solution)/shard_map/ppermute | solution.py:21
  322.3 15.5 %collective-permute-start.35 = (bf16[192,1152]{1,0:T(8,128)(2,1)S(1)}, bf16[192,1152]{1,0:T(8,128)(2,1)S(1)}, u32[]{:S(2)}, u32[]{:S(2)}) collective-permute-start(bf16[192,1152]{1,0:T(8,128)(2,1)S(1)} %slice.697), channel_id=1, source_target_pairs={{0,4},{2,6},{4,0},{6,2},{8,12},{10,14},{12,8},{14,10},{16,20},{18,... | collective-permute-start | bytes 1327112 | tf_op jit(solution)/shard_map/ppermute | solution.py:26
  324.0 38.5 %collective-permute-start.38 = (bf16[384,1536]{1,0:T(8,128)(2,1)}, bf16[384,1536]{1,0:T(8,128)(2,1)}, u32[]{:S(2)}, u32[]{:S(2)}) collective-permute-start(bf16[384,1536]{1,0:T(8,128)(2,1)} %get-tuple-element.300), channel_id=1, source_target_pairs={{0,1},{1,0},{2,3},{3,2},{4,5},{5,4},{6,7},{7,6},{8,9},{9,8},{10,11... | collective-permute-start | bytes 3538952 | tf_op jit(solution)/shard_map/ppermute | solution.py:21
  325.8 36.6 %collective-permute-start.39 = (bf16[2,192,1536]{2,1,0:T(8,128)(2,1)}, bf16[2,192,1536]{2,1,0:T(8,128)(2,1)}, u32[]{:S(2)}, u32[]{:S(2)}) collective-permute-start(bf16[2,192,1536]{2,1,0:T(8,128)(2,1)} %get-tuple-element.301), channel_id=1, source_target_pairs={{0,4},{2,6},{4,0},{6,2},{8,12},{10,14},{12,8},{14,10},{16,20},{18,... | collective-permute-start | bytes 3538952 | tf_op jit(solution)/shard_map/ppermute | solution.py:26
  361.6 14.2 %collective-permute-start.37 = (bf16[2,384,1536]{2,1,0:T(8,128)(2,1)}, bf16[2,384,1536]{2,1,0:T(8,128)(2,1)}, u32[]{:S(2)}, u32[]{:S(2)}) collective-permute-start(bf16[2,384,1536]{2,1,0:T(8,128)(2,1)} %shard_map.349), channel_id=1, source_target_pairs={{0,2},{2,0},{4,6},{6,4},{8,10},{10,8},{12,14},{14,12},{16,18},{18,... | collective-permute-start | bytes 7077896 | tf_op jit(solution)/shard_map/ppermute | solution.py:31
  362.3 4.9 %collective-permute-start.40 = (f32[22,768]{1,0:T(8,128)}, f32[22,768]{1,0:T(8,128)S(1)}, u32[]{:S(2)}, u32[]{:S(2)}) collective-permute-start(f32[22,768]{1,0:T(8,128)} %pad_maximum_fusion.10), channel_id=1, source_target_pairs={{0,1},{1,0},{2,3},{3,2},{4,5},{5,4},{6,7},{7,6},{8,9},{9,8},{10,11... | collective-permute-start | bytes 202760 | tf_op jit(solution)/shard_map/ppermute | solution.py:21
  371.0 15.4 %collective-permute-start.49 = (bf16[192,1536]{1,0:T(8,128)(2,1)S(1)}, bf16[192,1536]{1,0:T(8,128)(2,1)S(1)}, u32[]{:S(2)}, u32[]{:S(2)}) collective-permute-start(bf16[192,1536]{1,0:T(8,128)(2,1)S(1)} %fusion.40), channel_id=1, source_target_pairs={{0,1},{1,0},{2,3},{3,2},{4,5},{5,4},{6,7},{7,6},{8,9},{9,8},{10,11... | collective-permute-start | bytes 1769480 | tf_op jit(solution)/shard_map/ppermute | solution.py:21
  371.3 16.9 %collective-permute-start.48 = (bf16[192,1536]{1,0:T(8,128)(2,1)S(1)}, bf16[192,1536]{1,0:T(8,128)(2,1)S(1)}, u32[]{:S(2)}, u32[]{:S(2)}) collective-permute-start(bf16[192,1536]{1,0:T(8,128)(2,1)S(1)} %slice.696), channel_id=1, source_target_pairs={{0,4},{2,6},{4,0},{6,2},{8,12},{10,14},{12,8},{14,10},{16,20},{18,... | collective-permute-start | bytes 1769480 | tf_op jit(solution)/shard_map/ppermute | solution.py:26
  372.5 18.8 %collective-permute-start.50 = (bf16[48,2304]{1,0:T(8,128)(2,1)S(1)}, bf16[48,2304]{1,0:T(8,128)(2,1)S(1)}, u32[]{:S(2)}, u32[]{:S(2)}) collective-permute-start(bf16[48,2304]{1,0:T(8,128)(2,1)S(1)} %copy-done.82), channel_id=1, source_target_pairs={{0,8},{2,10},{4,12},{6,14},{16,0},{18,2},{20,4},{22,6},{24,16},{26... | collective-permute-start | bytes 663560 | tf_op jit(solution)/shard_map/ppermute | solution.py:41
  374.5 18.6 %collective-permute-start.51 = (bf16[48,2304]{1,0:T(8,128)(2,1)S(1)}, bf16[48,2304]{1,0:T(8,128)(2,1)S(1)}, u32[]{:S(2)}, u32[]{:S(2)}) collective-permute-start(bf16[48,2304]{1,0:T(8,128)(2,1)S(1)} %copy-done.81), channel_id=1, source_target_pairs={{0,24},{2,26},{4,28},{6,30},{16,8},{18,10},{20,12},{22,14},{24,0},... | collective-permute-start | bytes 663560 | tf_op jit(solution)/shard_map/ppermute | solution.py:41
  375.8 18.7 %collective-permute-start.52 = (bf16[48,2304]{1,0:T(8,128)(2,1)S(1)}, bf16[48,2304]{1,0:T(8,128)(2,1)S(1)}, u32[]{:S(2)}, u32[]{:S(2)}) collective-permute-start(bf16[48,2304]{1,0:T(8,128)(2,1)S(1)} %copy-done.80), channel_id=1, source_target_pairs={{0,16},{2,18},{4,20},{6,22},{16,24},{18,26},{20,28},{22,30},{24,8}... | collective-permute-start | bytes 663560 | tf_op jit(solution)/shard_map/ppermute | solution.py:41
  386.4 29.9 %collective-permute-start.44 = (bf16[256,768]{1,0:T(8,128)(2,1)S(1)}, bf16[256,768]{1,0:T(8,128)(2,1)S(1)}, u32[]{:S(2)}, u32[]{:S(2)}) collective-permute-start(bf16[256,768]{1,0:T(8,128)(2,1)S(1)} %copy-done.59), channel_id=1, source_target_pairs={{0,1},{1,0},{2,3},{3,2},{4,5},{5,4},{6,7},{7,6},{8,9},{9,8},{10,11... | collective-permute-start | bytes 1179656 | tf_op jit(solution)/shard_map/ppermute | solution.py:21
  388.2 22.9 %collective-permute-start.43 = (f32[22,768]{1,0:T(8,128)}, f32[22,768]{1,0:T(8,128)S(1)}, u32[]{:S(2)}, u32[]{:S(2)}) collective-permute-start(f32[22,768]{1,0:T(8,128)} %fusion.111), channel_id=1, source_target_pairs={{0,2},{2,0},{4,6},{6,4},{8,10},{10,8},{12,14},{14,12},{16,18},{18,... | collective-permute-start | bytes 202760 | tf_op jit(solution)/shard_map/ppermute | solution.py:830
  391.3 17.3 %collective-permute-start.41 = (bf16[384,768]{1,0:T(8,128)(2,1)S(1)}, bf16[384,768]{1,0:T(8,128)(2,1)S(1)}, u32[]{:S(2)}, u32[]{:S(2)}) collective-permute-start(bf16[384,768]{1,0:T(8,128)(2,1)S(1)} %get-tuple-element.337), channel_id=1, source_target_pairs={{0,1},{1,0},{2,3},{3,2},{4,5},{5,4},{6,7},{7,6},{8,9},{9,8},{10,11... | collective-permute-start | bytes 1769480 | tf_op jit(solution)/shard_map/ppermute | solution.py:21
  393.0 17.9 %collective-permute-start.42 = (bf16[2,192,768]{2,1,0:T(8,128)(2,1)S(1)}, bf16[2,192,768]{2,1,0:T(8,128)(2,1)S(1)}, u32[]{:S(2)}, u32[]{:S(2)}) collective-permute-start(bf16[2,192,768]{2,1,0:T(8,128)(2,1)S(1)} %get-tuple-element.338), channel_id=1, source_target_pairs={{0,4},{2,6},{4,0},{6,2},{8,12},{10,14},{12,8},{14,10},{16,20},{18,... | collective-permute-start | bytes 1769480 | tf_op jit(solution)/shard_map/ppermute | solution.py:26
  395.8 31.5 %collective-permute-start.53 = (bf16[48,3072]{1,0:T(8,128)(2,1)S(1)}, bf16[48,3072]{1,0:T(8,128)(2,1)S(1)}, u32[]{:S(2)}, u32[]{:S(2)}) collective-permute-start(bf16[48,3072]{1,0:T(8,128)(2,1)S(1)} %get-tuple-element.388), channel_id=1, source_target_pairs={{0,8},{2,10},{4,12},{6,14},{16,0},{18,2},{20,4},{22,6},{24,16},{26... | collective-permute-start | bytes 884744 | tf_op jit(solution)/shard_map/ppermute | solution.py:41
  408.6 21.3 %collective-permute-start.54 = (bf16[48,3072]{1,0:T(8,128)(2,1)S(1)}, bf16[48,3072]{1,0:T(8,128)(2,1)S(1)}, u32[]{:S(2)}, u32[]{:S(2)}) collective-permute-start(bf16[48,3072]{1,0:T(8,128)(2,1)S(1)} %get-tuple-element.387), channel_id=1, source_target_pairs={{0,24},{2,26},{4,28},{6,30},{16,8},{18,10},{20,12},{22,14},{24,0},... | collective-permute-start | bytes 884744 | tf_op jit(solution)/shard_map/ppermute | solution.py:41
  411.0 18.9 %collective-permute-start.55 = (bf16[48,3072]{1,0:T(8,128)(2,1)S(1)}, bf16[48,3072]{1,0:T(8,128)(2,1)S(1)}, u32[]{:S(2)}, u32[]{:S(2)}) collective-permute-start(bf16[48,3072]{1,0:T(8,128)(2,1)S(1)} %get-tuple-element.386), channel_id=1, source_target_pairs={{0,16},{2,18},{4,20},{6,22},{16,24},{18,26},{20,28},{22,30},{24,8}... | collective-permute-start | bytes 884744 | tf_op jit(solution)/shard_map/ppermute | solution.py:41
  411.2 11.9 %collective-permute-start.45 = (bf16[256,768]{1,0:T(8,128)(2,1)S(1)}, bf16[256,768]{1,0:T(8,128)(2,1)S(1)}, u32[]{:S(2)}, u32[]{:S(2)}) collective-permute-start(bf16[256,768]{1,0:T(8,128)(2,1)S(1)} %slice.698), channel_id=1, source_target_pairs={{0,1},{1,0},{2,3},{3,2},{4,5},{5,4},{6,7},{7,6},{8,9},{9,8},{10,11... | collective-permute-start | bytes 1179656 | tf_op jit(solution)/shard_map/ppermute | solution.py:21
  416.3 15.4 %collective-permute-start.47 = (bf16[192,768]{1,0:T(8,128)(2,1)S(1)}, bf16[192,768]{1,0:T(8,128)(2,1)S(1)}, u32[]{:S(2)}, u32[]{:S(2)}) collective-permute-start(bf16[192,768]{1,0:T(8,128)(2,1)S(1)} %fusion.47), channel_id=1, source_target_pairs={{0,1},{1,0},{2,3},{3,2},{4,5},{5,4},{6,7},{7,6},{8,9},{9,8},{10,11... | collective-permute-start | bytes 884744 | tf_op jit(solution)/shard_map/ppermute | solution.py:21
  423.0 8.7 %collective-permute-start.46 = (bf16[192,768]{1,0:T(8,128)(2,1)S(1)}, bf16[192,768]{1,0:T(8,128)(2,1)S(1)}, u32[]{:S(2)}, u32[]{:S(2)}) collective-permute-start(bf16[192,768]{1,0:T(8,128)(2,1)S(1)} %slice.700), channel_id=1, source_target_pairs={{0,4},{2,6},{4,0},{6,2},{8,12},{10,14},{12,8},{14,10},{16,20},{18,... | collective-permute-start | bytes 884744 | tf_op jit(solution)/shard_map/ppermute | solution.py:26
  427.3 4.4 collective-permute-start.56
  431.7 6.4 %collective-permute-start.60 = (f32[22,768]{1,0:T(8,128)S(1)}, f32[22,768]{1,0:T(8,128)S(1)}, u32[]{:S(2)}, u32[]{:S(2)}) collective-permute-start(f32[22,768]{1,0:T(8,128)S(1)} %add.243), channel_id=1, source_target_pairs={{0,8},{2,10},{4,12},{6,14},{8,0},{10,2},{12,4},{14,6},{16,24},{18,... | collective-permute-start | bytes 202760 | tf_op jit(solution)/shard_map/ppermute | solution.py:830
  432.8 6.1 %collective-permute-start.57 = (bf16[48,1536]{1,0:T(8,128)(2,1)S(1)}, bf16[48,1536]{1,0:T(8,128)(2,1)S(1)}, u32[]{:S(2)}, u32[]{:S(2)}) collective-permute-start(bf16[48,1536]{1,0:T(8,128)(2,1)S(1)} %get-tuple-element.404), channel_id=1, source_target_pairs={{0,8},{2,10},{4,12},{6,14},{16,0},{18,2},{20,4},{22,6},{24,16},{26... | collective-permute-start | bytes 442376 | tf_op jit(solution)/shard_map/ppermute | solution.py:41
  434.1 7.2 %collective-permute-start.58 = (bf16[48,1536]{1,0:T(8,128)(2,1)S(1)}, bf16[48,1536]{1,0:T(8,128)(2,1)S(1)}, u32[]{:S(2)}, u32[]{:S(2)}) collective-permute-start(bf16[48,1536]{1,0:T(8,128)(2,1)S(1)} %get-tuple-element.403), channel_id=1, source_target_pairs={{0,24},{2,26},{4,28},{6,30},{16,8},{18,10},{20,12},{22,14},{24,0},... | collective-permute-start | bytes 442376 | tf_op jit(solution)/shard_map/ppermute | solution.py:41
  435.5 6.9 %collective-permute-start.59 = (bf16[48,1536]{1,0:T(8,128)(2,1)S(1)}, bf16[48,1536]{1,0:T(8,128)(2,1)S(1)}, u32[]{:S(2)}, u32[]{:S(2)}) collective-permute-start(bf16[48,1536]{1,0:T(8,128)(2,1)S(1)} %get-tuple-element.402), channel_id=1, source_target_pairs={{0,16},{2,18},{4,20},{6,22},{16,24},{18,26},{20,28},{22,30},{24,8}... | collective-permute-start | bytes 442376 | tf_op jit(solution)/shard_map/ppermute | solution.py:41
  442.4 6.6 %collective-permute-start.61 = (f32[22,768]{1,0:T(8,128)S(1)}, f32[22,768]{1,0:T(8,128)S(1)}, u32[]{:S(2)}, u32[]{:S(2)}) collective-permute-start(f32[22,768]{1,0:T(8,128)S(1)} %add.247), channel_id=1, source_target_pairs={{0,16},{2,18},{4,20},{6,22},{8,24},{10,26},{12,28},{14,30},{16,0},... | collective-permute-start | bytes 202760 | tf_op jit(solution)/shard_map/ppermute | solution.py:830
  (101 other events, 781.8 us)
where the time goes:
time: 458 us; the launch traced here: 453 us
  Pallas kernels  229 us (50%)
  starting transfers between devices  74.3 us (16%)
  waiting for transfers between devices  72.9 us (16%)
  local copies, waits for them, and re-layouts  39.6 us (9%)
  other arithmetic  21.6 us (5%)
  matrix products  13.3 us (3%)
    pallas_call x20, Pallas kernels, call(): pl.pallas_call(body, grid=(steps,), in_specs=[pl.BlockSpec(block, index)...  215 us
    ppermute x18, waiting for transfers between devices, ring_shift(): return lax.ppermute(value, 'dp', pairs)  32.8 us
    ppermute x18, starting transfers between devices, ring_shift(): return lax.ppermute(value, 'dp', pairs)  27.2 us
    ppermute x22, starting transfers between devices, swap_y(): return lax.ppermute(value, 'mp', [(0, 1), (1, 0)])  26.7 us
    unnamed x212, local copies, waits for them, and re-layouts  25.4 us
    ppermute x22, waiting for transfers between devices, swap_y(): return lax.ppermute(value, 'mp', [(0, 1), (1, 0)])  23.2 us
    ppermute x12, starting transfers between devices, swap_x(): return lax.ppermute(value, 'dp', [(i, i ^ 2) for i in range(n)])  13.7 us
    ppermute x12, waiting for transfers between devices, swap_x(): return lax.ppermute(value, 'dp', [(i, i ^ 2) for i in range(n)])  13.2 us
  transfers between devices with their start and end apart: 62, of which 21 were waited for; matrix products, arithmetic and copies ran while one was open for 9% of the time, Pallas kernels for 37%

commit v1 on v0

--- a/solution.py
+++ b/solution.py
@@ -687,70 +687,52 @@
         sizes = [end - start for _, start, end in columns]
         self.size_a, self.size_b = sum(sizes[:cut]), sum(sizes[cut:])
 
-    def inputs(self, at):
+    def inputs(self, at, side):
         out = []
         for pairs in self.entries:
             for left, right in pairs:
-                out += [whole(left), per_group(right, at)]
+                half = (left.shape[0], left.shape[1] // 2)
+                out += [(left, half, lambda i: (0, side)), per_group(right, at)]
         return out
 
-    def scratch(self, rows):
-        return [pltpu.VMEM((rows, left.shape[0]), LOW) for pairs in self.entries for left, _ in pairs]
-
     def flops(self, rows):
-        depth = self.entries[0][0][0].shape[1]
         return sum(
-            2 * rows * left.shape[0] * (2 * right.shape[2] + depth)
-            for pairs in self.entries for left, right in pairs
+            4 * rows * left.shape[0] * right.shape[2] for pairs in self.entries for left, right in pairs
         )
 
-    def turn(self, pick, refs, turned):
-        @pl.when(pl.program_id(0) == 0)
-        def _():
-            for at in range(len(turned)):
-                turned[at][...] = dot(pick[...], refs[2 * at][...], 1, 1).astype(LOW)
-
-    def product(self, refs, turned, entry, start, end):
+    def product(self, refs, entry, start, end):
         first = sum(len(pairs) for pairs in self.entries[:entry])
         total = None
         for at in range(first, first + len(self.entries[entry])):
-            one = dot(turned[at][...], refs[2 * at + 1][0, :, start:end], 1, 0)
+            one = dot(refs[2 * at][...], refs[2 * at + 1][0, :, start:end], 0, 0)
             total = one if total is None else total + one
         return total
 
-    def send(self, pick):
-        rows = pick.shape[0]
+    def send(self):
+        rows = self.entries[0][0][0].shape[1] // 2
         size = self.size_a + self.size_b
 
-        def body(pick, *refs):
-            count = 2 * sum(len(pairs) for pairs in self.entries)
-            out, turned = refs[count], refs[count + 1 :]
-            self.turn(pick, refs, turned)
+        def body(*refs):
             col = 0
             for entry, start, end in self.columns:
-                part = self.product(refs, turned, entry, start, end)
-                out[0, :, col : col + end - start] = part.astype(LOW)
+                part = self.product(refs, entry, start, end)
+                refs[-1][0, :, col : col + end - start] = part.astype(LOW)
                 col += end - start
 
         return call(
-            body, 2, [whole(pick)] + self.inputs(lambda i: i), [out_group((2, rows, size), LOW)],
-            self.scratch(rows), self.flops(rows),
+            body, 2, self.inputs(lambda i: i, 1), [out_group((2, rows, size), LOW)], [], self.flops(rows)
         )[0]
 
-    def keep(self, pick, got):
-        rows = pick.shape[0]
+    def keep(self, got):
+        rows = self.entries[0][0][0].shape[1] // 2
         half = rows // 2
-        size = self.size_a + self.size_b
-
-        def body(pick, got, *refs):
-            count = 2 * sum(len(pairs) for pairs in self.entries)
-            send_a, keep_a, send_b, keep_b = refs[count : count + 4]
-            turned = refs[count + 4 :]
+
+        def body(got, *refs):
+            send_a, keep_a, send_b, keep_b = refs[-4:]
             i = pl.program_id(0)
-            self.turn(pick, refs, turned)
             col = 0
             for at, (entry, start, end) in enumerate(self.columns):
-                part = self.product(refs, turned, entry, start, end)
+                part = self.product(refs, entry, start, end)
                 part = part + got[0, :, col : col + end - start].astype(F32)
                 if at < self.cut:
                     place = slice(col, col + end - start)
@@ -770,25 +752,25 @@
 
         return call(
             body, 2,
-            [whole(pick), per_group(got, lambda i: 1 - i)] + self.inputs(lambda i: 1 - i),
+            [per_group(got, lambda i: 1 - i)] + self.inputs(lambda i: 1 - i, 0),
             [
                 out_whole((rows, self.size_a), LOW), out_whole((rows, self.size_a), F32),
                 out_group((2, half, self.size_b), LOW), out_group((2, half, self.size_b), F32),
             ],
-            self.scratch(rows), self.flops(rows),
+            [], self.flops(rows),
         )
 
 
 class Reduce:
-    def __init__(self, grads, pick_send, pick_keep):
-        self.grads, self.pick_keep = grads, pick_keep
-        self.sends = (grads.send(pick_send),)
+    def __init__(self, grads):
+        self.grads = grads
+        self.sends = (grads.send(),)
         self.got = (swap_core(self.sends[0]),)
         self.work = self._run()
 
     def _run(self):
         count = lax.axis_size("dp") // 4
-        send_a, keep_a, send_b, keep_b = self.grads.keep(self.pick_keep, self.got[0])
+        send_a, keep_a, send_b, keep_b = self.grads.keep(self.got[0])
         fourth = keep_a.shape[0] // 2
         self.sends = (send_a, send_b)
         self.got = (swap_y(send_a), swap_x(send_b))
@@ -951,30 +933,41 @@
         return own, swap_core(own)
 
     bias_parts = [t_qv_bias[0], t_qv_bias[1], t_up_bias, s_qv_bias[0], s_qv_bias[1], s_up_bias]
+    to_own = feature_order(width)
+    into = (lax.iota(jnp.int32, width)[:, None] == to_own[None, :]).astype(LOW)
+    def reorder(value):
+        return jnp.dot(value, into, preferred_element_type=F32).astype(LOW)
+
+
+    spin = lambda segs: jnp.where(first, segs, jnp.roll(segs, half))
+    segs = (spin(own_row(segment_ids)), spin(segment_ids[1]))
+
     line_t, got_own = along_z(packed_t), swap_y(far_row(tokens))
+    *line_t, got_own, into, segs, packed_f, student_a, student_b = together(
+        *line_t, got_own, into, segs, packed_f, student_a, student_b
+    )
+    attn_a, attn_b = of_line(line_t, t_cut)
+    got_a, got_b = swap_x(attn_a), swap_y(attn_b)
     line_f = along_z(packed_f)
-    *line_t, line_f[1], got_own = together(*line_t, line_f[1], got_own)
-    attn_a, attn_b = of_line(line_t, t_cut)
-    got_a, got_b, student_x, student_y = swap_x(attn_a), swap_y(attn_b), swap_x(student_a), swap_y(student_b)
-    got_a, got_b, student_x, student_y, *line_f[2:-1] = together(
-        got_a, got_b, student_x, student_y, *line_f[2:-1]
-    )
+    student_x, student_y = swap_x(student_a), swap_y(student_b)
+    got_a, got_b, student_x, student_y, line_f[1] = together(got_a, got_b, student_x, student_y, line_f[1])
+    inputs = reorder(jnp.concatenate([own_row(tokens), got_own, tokens[1]], axis=0))
     attn_a, attn_b = first_plane(attn_a, got_a, attn_b, got_b)
     got_a, got_b = swap_y(attn_a), swap_x(attn_b)
     line_s = along_z(moves(
         [student_a, student_x, student_b, student_y], [(2, block, 2 * s_cut)],
         [(i, (every,), 0, (i % 2, every, columns(i // 2 * s_cut, s_cut))) for i in range(4)],
     )[0])
-    got_a, got_b, line_f[-1] = together(got_a, got_b, line_f[-1])
+    got_a, got_b, inputs, *line_f[2:] = together(got_a, got_b, inputs, *line_f[2:])
     attn = both_planes(
         attn_a, got_a, attn_b, got_b, [(False, 0, t_cut), (True, 0, t_all - t_cut)]
     )
     attn = with_core(attn)
-    ffn_a, ffn_b = of_line(line_f, f_cut)
+    ffn_a, ffn_b = of_line(list(after(line_f, attn[0])), f_cut)
     got_a, got_b = swap_x(ffn_a), swap_y(ffn_b)
     bias_own = jnp.concatenate(bias_parts)
     bias_far = swap_y(bias_own)
-    attn, got_a, got_b, bias_far, line_s[1] = together(attn, got_a, got_b, bias_far, line_s[1])
+    attn, got_a, got_b, bias_far = together(attn, got_a, got_b, bias_far)
     ffn_a, ffn_b = first_plane(ffn_a, got_a, ffn_b, got_b)
     got_a, got_b = swap_y(ffn_a), swap_x(ffn_b)
     got_shared = swap_y(tokens[1])
@@ -991,20 +984,11 @@
         norms_of(0), bias_qkv(pick[0], pick[1]), pick[2].reshape(2 * per, 1, size),
     )
 
-    to_own = feature_order(width)
-    into = (lax.iota(jnp.int32, width)[:, None] == to_own[None, :]).astype(LOW)
-    reorder = lambda value: jnp.dot(value, into, preferred_element_type=F32).astype(LOW)
-    pick_all = jnp.eye(width, dtype=LOW)
-    pick_keep, pick_send = pick_all[: width // 2], pick_all[width // 2 :]
-
-    inputs = reorder(jnp.concatenate([own_row(tokens), got_own, tokens[1]], axis=0))
-    spin = lambda segs: jnp.where(first, segs, jnp.roll(segs, half))
-    segs = (spin(own_row(segment_ids)), spin(segment_ids[1]))
     grad_in = jnp.concatenate([own_row(out_grad), swap_y(far_row(out_grad)), out_grad[1]], axis=0)
 
     inputs, ffn_a, ffn_b = together(inputs, ffn_a, ffn_b)
     proj, context_own, logsum_own = project_call(teacher, inputs, segs[0], half)
-    proj, got_shared, *line_s[2:-1] = together(proj, got_shared, *line_s[2:-1])
+    proj, got_shared, *line_s[1:-1] = together(proj, got_shared, *line_s[1:-1])
     away_low = reorder(got_shared)
     hidden, t_kept = forward_attn(
         teacher, inputs, proj, context_own, logsum_own, inputs, away_low, segs, half
@@ -1065,7 +1049,7 @@
     d_proj, extra = lax.optimization_barrier((d_proj, extra))
     s_entries += attn_entries(s_kept, d_proj, d_away, d_mid_low)
     s_columns = [(0, 0, size), (2, 0, s_width), (3, 0, s_width), (1, 0, size), (2, s_width, 3 * s_width)]
-    reduce_s = Reduce(Grads(s_entries, s_columns, 3), pick_send, pick_keep)
+    reduce_s = Reduce(Grads(s_entries, s_columns, 3))
 
     d_rows = after(d_rows, reduce_s.sends)
     d_final, d_final_low, d_pre, t_sums_two, t_up_grad = ffn_back_first_call(
@@ -1075,9 +1059,7 @@
     reduce_s.step()
     d_pre = after(d_pre, reduce_s.sends)
     f_entries = [[(t_kept["hidden_low"], d_pre)], [(d_final_low, t_kept["act"])]]
-    reduce_f = Reduce(
-        Grads(f_entries, [(0, 0, per * size), (1, 0, per * size)], 1), pick_send, pick_keep
-    )
+    reduce_f = Reduce(Grads(f_entries, [(0, 0, per * size), (1, 0, per * size)], 1))
     d_pre = after(d_pre, reduce_f.sends)
     d_mid, d_mid_low, t_sums_one = ffn_back_second_call(teacher, d_final, d_pre, t_kept)
     t_norm_grads = (t_sums_one + t_sums_two)[:6]
@@ -1095,8 +1077,7 @@
     d_proj, t_sums_a = own_back_call(teacher, None, d_mid_low, d_shared, t_kept, segs[0], half, False)
     t_entries = attn_entries(t_kept, d_proj, d_away, d_mid_low)
     reduce_t = Reduce(
-        Grads(t_entries, [(0, 0, 2 * t_width), (0, 2 * t_width, 3 * t_width), (1, 0, t_width)], 1),
-        pick_send, pick_keep,
+        Grads(t_entries, [(0, 0, 2 * t_width), (0, 2 * t_width, 3 * t_width), (1, 0, t_width)], 1)
     )
 
     def qv_grad(one, two, wide):

time: 458 us -> 449 us (0.980)
  Pallas kernels: 229 us -> 222 us
    pallas_call x20, Pallas kernels: 215 us -> 204 us  [call(): pl.pallas_call(body, grid=(steps,), in_specs=[pl.BlockSpec(block, index)...]
    ppermute x12, waiting for transfers between devices: 13.2 us -> 8.38 us  [swap_x(): return lax.ppermute(value, 'dp', [(i, i ^ 2) for i in range(n)])]
    unnamed x212 -> x184, local copies, waits for them, and re-layouts: 25.4 us -> 27.4 us
  transfers between devices with their start and end apart: 62 -> 62, of which waited for: 21 -> 14; matrix products, arithmetic and copies ran while one was open for 9% -> 9% of each run, Pallas kernels for 37% -> 37%
where the time goes in v1:
time: 449 us; the launch traced here: 444 us
  Pallas kernels  222 us (49%)
  starting transfers between devices  73.5 us (16%)
  waiting for transfers between devices  69.4 us (15%)
  local copies, waits for them, and re-layouts  42.7 us (10%)
  other arithmetic  21.6 us (5%)
  matrix products  12.3 us (3%)
    pallas_call x20, Pallas kernels, call(): pl.pallas_call(body, grid=(steps,), in_specs=[pl.BlockSpec(block, index)...  204 us
    ppermute x18, waiting for transfers between devices, ring_shift(): return lax.ppermute(value, 'dp', pairs)  33.5 us
    ppermute x18, starting transfers between devices, ring_shift(): return lax.ppermute(value, 'dp', pairs)  29.4 us
    unnamed x184, local copies, waits for them, and re-layouts  27.4 us
    ppermute x22, starting transfers between devices, swap_y(): return lax.ppermute(value, 'mp', [(0, 1), (1, 0)])  27.1 us
    ppermute x22, waiting for transfers between devices, swap_y(): return lax.ppermute(value, 'mp', [(0, 1), (1, 0)])  20.8 us
    pallas_call x9, Pallas kernels, moves(): pl.pallas_call(body, out_shape=[jax.ShapeDtypeStruct(shape, LOW) for shap...  17 us
    ppermute x12, starting transfers between devices, swap_x(): return lax.ppermute(value, 'dp', [(i, i ^ 2) for i in range(n)])  11.3 us
  transfers between devices with their start and end apart: 62, of which 14 were waited for; matrix products, arithmetic and copies ran while one was open for 9% of the time, Pallas kernels for 37%

profile of v1, /device:TPU:0, one launch (start us, length us, event | category | flops | bytes accessed | tf_op | source)
XLA Modules:
  0.0 443.7 jit_solution(9782235953906838002)
XLA Ops:
  9.3 4.1 collective-permute-start
  16.5 1.5 collective-permute-start.3
  19.3 3.9 collective-permute-done.1.refs_2_
  23.2 5.7 %collective-permute-done.2.refs_3_ = bf16[48,1664]{1,0:T(8,128)(2,1)S(1)} collective-permute-done((bf16[48,1664]{1,0:T(8,128)(2,1)S(1)}, bf16[48,1664]{1,0:T(8,128)(2,1)S(1)}, u32[]{:S(2)}, u32[]{:S(2)}) %collective-permute-start.2) | collective-permute-done | bytes 159776 | tf_op jit(solution)/shard_map/ppermute | solution.py:41
  28.9 1.6 collective-permute-start.5
  30.5 1.5 collective-permute-start.4
  33.2 8.3 %collective-permute-done.6.refs_1_ = bf16[48,1152]{1,0:T(8,128)(2,1)S(1)} collective-permute-done((bf16[48,1152]{1,0:T(8,128)(2,1)S(1)}, bf16[48,1152]{1,0:T(8,128)(2,1)S(1)}, u32[]{:S(2)}, u32[]{:S(2)}) %collective-permute-start.6) | collective-permute-done | bytes 110624 | tf_op jit(solution)/shard_map/ppermute | solution.py:26
  41.7 1.6 collective-permute-start.10
  44.5 2.5 collective-permute-start.11
  47.0 3.1 convolution_convert_fusion.1.rows.refs_0_
  50.2 6.1 %collective-permute-done.11.refs_2_ = bf16[48,3072]{1,0:T(8,128)(2,1)S(1)} collective-permute-done((bf16[48,3072]{1,0:T(8,128)(2,1)S(1)}, bf16[48,3072]{1,0:T(8,128)(2,1)S(1)}, u32[]{:S(2)}, u32[]{:S(2)}) %collective-permute-start.11) | collective-permute-done | bytes 294944 | tf_op jit(solution)/shard_map/ppermute | solution.py:41
  56.3 6.9 %collective-permute-done.12.refs_3_ = bf16[48,3072]{1,0:T(8,128)(2,1)S(1)} collective-permute-done((bf16[48,3072]{1,0:T(8,128)(2,1)S(1)}, bf16[48,3072]{1,0:T(8,128)(2,1)S(1)}, u32[]{:S(2)}, u32[]{:S(2)}) %collective-permute-start.12) | collective-permute-done | bytes 294944 | tf_op jit(solution)/shard_map/ppermute | solution.py:41
  72.6 9.3 %collective-permute-done.16 = bf16[3456]{0:T(1024)(128)(2,1)} collective-permute-done((bf16[3456]{0:T(1024)(128)(2,1)}, bf16[3456]{0:T(1024)(128)(2,1)}, u32[]{:S(2)}, u32[]{:S(2)}) %collective-permute-start.16) | collective-permute-done | bytes 6944 | tf_op jit(solution)/shard_map/ppermute | solution.py:21
  83.9 3.1 shard_map.327
  93.2 13.0 %shard_map.328 = (bf16[2,768,1152]{2,1,0:T(8,128)(2,1)}, bf16[2,512,384]{2,1,0:T(8,128)(2,1)S(1)}, f32[2,8,512]{2,1,0:T(8,128)S(1)}) custom-call(bf16[768,768]{1,0:T(8,128)(2,1)S(1)} %copy-done.4, bf16[2,384,1664]{2,1,0:T(8,128)(2,1)S(1)} %bitcast.116, bf16[2,384,1664]{2,1,0:T(8,128)(2,1)} %collective-permute-done.13.refs_1_.refs_3_.refs_5_.refs_7_.out_two, ...), custom_call_target="tpu_custom_call" | custom-call | flops 1761607680 | bytes 10443264 | tf_op jit(solution)/shard_map/pallas_call | solution.py:80
  106.8 1.5 convolution_convert_fusion.2.away.refs_2_
  108.2 13.5 %shard_map.330 = (bf16[2,256,1152]{2,1,0:T(8,128)(2,1)S(1)}, bf16[2,768,384]{2,1,0:T(8,128)(2,1)S(1)}, f32[2,8,256]{2,1,0:T(8,128)S(1)}, f32[768,768]{1,0:T(8,12...) custom-call(bf16[768,768]{1,0:T(8,128)(2,1)} %convolution_convert_fusion.1.rows.refs_0_, ...), custom_call_target="tpu_custom_call" | custom-call | flops 1107296256 | bytes 16739840 | tf_op jit(solution)/shard_map/pallas_call | solution.py:80
  124.6 4.9 %shard_map.331 = bf16[2,2,4,48,3072]{4,3,2,1,0:T(8,128)(2,1)} custom-call(bf16[2,4,48,1536]{3,2,1,0:T(8,128)(2,1)} %get-tuple-element.254.refs_0_, bf16[2,4,48,1536]{3,2,1,0:T(8,128)(2,1)} %collective-permute-done.20.refs_1_, bf16[2,4,48,1536]{3,2,1,0:T(8,128)(2,1)} %get-tuple-element.256.refs_2_, bf16[2,4,48,1536]{3,2,1,0:T(8,128)(2,1)} %collective-permute-done.21.refs_3_), custom_call_target="tpu_custom_call" | custom-call | bytes 4718592 | tf_op jit(solution)/shard_map/pallas_call | solution.py:102
  130.9 2.3 shard_map.333
  135.1 6.4 %collective-permute-done.26 = bf16[256,768]{1,0:T(8,128)(2,1)S(1)} collective-permute-done((bf16[256,768]{1,0:T(8,128)(2,1)S(1)}, bf16[256,768]{1,0:T(8,128)(2,1)S(1)}, u32[]{:S(2)}, u32[]{:S(2)}) %collective-permute-start.26) | collective-permute-done | bytes 393248 | tf_op jit(solution)/shard_map/ppermute | solution.py:21
  142.8 16.5 %shard_map.332 = (bf16[2,768,1536]{2,1,0:T(8,128)(2,1)}, bf16[2,768,1536]{2,1,0:T(8,128)(2,1)}, f32[768,768]{1,0:T(8,128)}, bf16[768,768]{1,0:T(8,128)(2,1)S(1)}...) custom-call(f32[768,768]{1,0:T(8,128)} %get-tuple-element.258.hidden, ...), custom_call_target="tpu_custom_call" | custom-call | flops 3623878656 | bytes 18304512 | tf_op jit(solution)/shard_map/pallas_call | solution.py:80
  160.5 4.3 shard_map.334
  166.4 2.1 convolution_convert_fusion.grad
  168.5 2.8 collective-permute-done.27.refs_1_.refs_3_.refs_5_.up_two.down_two.refs_7_.refs_9_.out_two.refs_2_.refs_4_
  171.3 7.2 %shard_map.335 = (bf16[2,768,576]{2,1,0:T(8,128)(2,1)S(1)}, bf16[2,512,192]{2,1,0:T(8,128)(2,1)S(1)}, f32[2,8,512]{2,1,0:T(8,128)S(1)}) custom-call(bf16[768,768]{1,0:T(8,128)(2,1)S(1)} %get-tuple-element.270.rows.refs_4_, bf16[2,384,2304]{2,1,0:T(8,128)(2,1)} %bitcast.142, ...), custom_call_target="tpu_custom_call" | custom-call | flops 880803840 | bytes 8769792 | tf_op jit(solution)/shard_map/pallas_call | solution.py:80
  179.9 9.9 %shard_map.336 = (bf16[2,256,576]{2,1,0:T(8,128)(2,1)S(1)}, bf16[2,768,192]{2,1,0:T(8,128)(2,1)S(1)}, f32[2,8,256]{2,1,0:T(8,128)S(1)}, f32[768,768]{1,0:T(8,128...) custom-call(f32[768,768]{1,0:T(8,128)} %get-tuple-element.269.rows, ...), custom_call_target="tpu_custom_call" | custom-call | flops 553648128 | bytes 16049408 | tf_op jit(solution)/shard_map/pallas_call | solution.py:80
  189.9 12.4 %shard_map.337 = (bf16[2,768,768]{2,1,0:T(8,128)(2,1)}, bf16[2,768,768]{2,1,0:T(8,128)(2,1)}, f32[768,768]{1,0:T(8,128)}, bf16[768,768]{1,0:T(8,128)(2,1)}, bf16...) custom-call(f32[768,768]{1,0:T(8,128)} %get-tuple-element.279.hidden, ...), custom_call_target="tpu_custom_call" | custom-call | flops 1811939328 | bytes 13582848 | tf_op jit(solution)/shard_map/pallas_call | solution.py:80
  207.1 11.9 %shard_map.338 = (bf16[768,768]{1,0:T(8,128)(2,1)S(1)}, bf16[2,768,768]{2,1,0:T(8,128)(2,1)}, f32[768,768]{1,0:T(8,128)}, bf16[768,768]{1,0:T(8,128)(2,1)S(1)}, ...) custom-call(bf16[768,768]{1,0:T(8,128)(2,1)S(1)} %copy-done.28, bf16[768,768]{1,0:T(8,128)(2,1)S(1)} %copy-done.30, ...), custom_call_target="tpu_custom_call" | custom-call | flops 1811939328 | bytes 13596672 | tf_op jit(solution)/shard_map/pallas_call | solution.py:80
  219.0 7.3 %shard_map.339 = (bf16[2,256,576]{2,1,0:T(8,128)(2,1)S(1)}, bf16[2,256,576]{2,1,0:T(8,128)(2,1)S(1)}, f32[2,8,576]{2,1,0:T(8,128)S(1)}, bf16[256,768]{1,0:T(8,128)(2,1)S(1)}) custom-call(bf16[768,768]{1,0:T(8,128)(2,1)S(1)} %get-tuple-element.284.d_mid.d_mid_low.refs_8_, bf16[2,768,576]{2,1,0:T(8,128)(2,1)S(1)} %copy-done.8, ...), custom_call_target="tpu_custom_call" | custom-call | flops 553648128 | bytes 13200896 | tf_op jit(solution)/shard_map/pallas_call | solution.py:80
  227.9 13.2 %shard_map.340 = (bf16[2,768,576]{2,1,0:T(8,128)(2,1)S(1)}, f32[2,8,576]{2,1,0:T(8,128)S(1)}, f32[768,768]{1,0:T(8,128)}) custom-call(bf16[768,768]{1,0:T(8,128)(2,1)S(1)} %get-tuple-element.284.d_mid.d_mid_low.refs_8_, bf16[2,256,576]{2,1,0:T(8,128)(2,1)S(1)} %get-tuple-element.289.d_shared, bf16[2,768,576]{2,1,0:T(8,128)(2,1)S(1)} %copy-done.8, ...), custom_call_target="tpu_custom_call" | custom-call | flops 1333788672 | bytes 15667200 | tf_op jit(solution)/shard_map/pallas_call | solution.py:80
  242.6 7.3 %shard_map.341 = bf16[2,384,2304]{2,1,0:T(8,128)(2,1)} custom-call(bf16[768,768]{1,0:T(8,128)(2,1)S(1)} %get-tuple-element.280.hidden_low.refs_0_, bf16[2,768,768]{2,1,0:T(8,128)(2,1)} %get-tuple-element.293.refs_1_, bf16[768,768]{1,0:T(8,128)(2,1)S(1)} %get-tuple-element.294.refs_2_, bf16[2,768,768]{2,1,0:T(8,128)(2,1)} %get-tuple-element.295.refs_3_, ...), custom_call_target="tpu_custom_call" | custom-call | flops 1472200704 | bytes 8159232 | tf_op jit(solution)/shard_map/pallas_call | solution.py:80
  249.9 11.1 %shard_map.342 = (f32[768,768]{1,0:T(8,128)S(1)}, bf16[768,768]{1,0:T(8,128)(2,1)S(1)}, bf16[2,768,1536]{2,1,0:T(8,128)(2,1)}, f32[8,768]{1,0:T(8,128)S(1)}, f32[4,1,768]{2,1,0:T(1,128)S(1)}) custom-call(f32[768,768]{1,0:T(8,128)} %get-tuple-element.301.grad, bf16[256,768]{1,0:T(8,128)(2,1)S(1)} %collective-permute-done.30.extra, ...), custom_call_target="tpu_custom_call" | custom-call | flops 1811939328 | bytes 13204992 | tf_op jit(solution)/shard_map/pallas_call | solution.py:80
  261.0 11.5 %shard_map.343 = (bf16[384,1152]{1,0:T(8,128)(2,1)}, f32[384,1152]{1,0:T(8,128)}, bf16[2,192,1152]{2,1,0:T(8,128)(2,1)}, f32[2,192,1152]{2,1,0:T(8,128)}) custom-call(bf16[2,384,2304]{2,1,0:T(8,128)(2,1)} %collective-permute-done.31.got, bf16[768,768]{1,0:T(8,128)(2,1)S(1)} %get-tuple-element.280.hidden_low.refs_0_, ...), custom_call_target="tpu_custom_call" | custom-call | flops 1472200704 | bytes 10813440 | tf_op jit(solution)/shard_map/pallas_call | solution.py:80
  272.5 8.0 %shard_map.344 = bf16[2,384,3072]{2,1,0:T(8,128)(2,1)} custom-call(bf16[768,768]{1,0:T(8,128)(2,1)S(1)} %get-tuple-element.259.hidden_low.refs_0_, bf16[2,768,1536]{2,1,0:T(8,128)(2,1)} %get-tuple-element.315.refs_1_.d_pre, bf16[768,768]{1,0:T(8,128)(2,1)S(1)} %get-tuple-element.313.refs_2_, bf16[2,768,1536]{2,1,0:T(8,128)(2,1)} %get-tuple-element.314.refs_3_), custom_call_target="tpu_custom_call" | custom-call | flops 1811939328 | bytes 8257536 | tf_op jit(solution)/shard_map/pallas_call | solution.py:80
  283.1 9.6 %shard_map.345 = (f32[768,768]{1,0:T(8,128)S(1)}, bf16[768,768]{1,0:T(8,128)(2,1)S(1)}, f32[8,768]{1,0:T(8,128)S(1)}) custom-call(f32[768,768]{1,0:T(8,128)} %copy-done.22, bf16[2,768,1536]{2,1,0:T(8,128)(2,1)} %get-tuple-element.315.refs_1_.d_pre, bf16[768,768]{1,0:T(8,128)(2,1)S(1)} %copy-done.25, f32[768,1]{1,0:T(8,128)S(1)} %copy-done.33, ...), custom_call_target="tpu_custom_call" | custom-call | flops 1811939328 | bytes 10642944 | tf_op jit(solution)/shard_map/pallas_call | solution.py:80
  294.1 2.1 copy-done.53
  296.3 9.2 %shard_map.346 = (bf16[384,1536]{1,0:T(8,128)(2,1)}, f32[384,1536]{1,0:T(8,128)}, bf16[2,192,1536]{2,1,0:T(8,128)(2,1)}, f32[2,192,1536]{2,1,0:T(8,128)}) custom-call(bf16[2,384,3072]{2,1,0:T(8,128)(2,1)} %copy-done.53, bf16[768,768]{1,0:T(8,128)(2,1)S(1)} %get-tuple-element.259.hidden_low.refs_0_, bf16[2,768,1536]{2,1,0:T(8,128)(2,1)} %get-tuple-element.315.refs_1_.d_pre, ...), custom_call_target="tpu_custom_call" | custom-call | flops 1811939328 | bytes 11796480 | tf_op jit(solution)/shard_map/pallas_call | solution.py:80
  305.5 1.5 convert_add_fusion.2
  307.3 1.4 convert_add_fusion.3
  308.8 1.4 collective-permute-start.36
  314.0 10.6 %shard_map.347 = (bf16[2,256,1152]{2,1,0:T(8,128)(2,1)S(1)}, bf16[2,256,1152]{2,1,0:T(8,128)(2,1)S(1)}, f32[2,8,1152]{2,1,0:T(8,128)S(1)}, bf16[256,768]{1,0:T(8,128)(2,1)S(1)}) custom-call(bf16[768,768]{1,0:T(8,128)(2,1)S(1)} %get-tuple-element.331.d_mid.d_mid_low.refs_4_, bf16[2,768,1152]{2,1,0:T(8,128)(2,1)} %get-tuple-element.248.proj, ...), custom_call_target="tpu_custom_call" | custom-call | flops 1107296256 | bytes 14595584 | tf_op jit(solution)/shard_map/pallas_call | solution.py:80
  327.8 13.2 %shard_map.348 = (bf16[2,768,1152]{2,1,0:T(8,128)(2,1)}, f32[2,8,1152]{2,1,0:T(8,128)S(1)}) custom-call(bf16[768,768]{1,0:T(8,128)(2,1)S(1)} %get-tuple-element.331.d_mid.d_mid_low.refs_4_, bf16[2,256,1152]{2,1,0:T(8,128)(2,1)S(1)} %get-tuple-element.338.d_shared, bf16[2,768,1152]{2,1,0:T(8,128)(2,1)} %get-tuple-element.248.proj, ...), custom_call_target="tpu_custom_call" | custom-call | flops 1308622848 | bytes 7329792 | tf_op jit(solution)/shard_map/pallas_call | solution.py:80
  341.0 5.7 %shard_map.349 = bf16[2,384,1536]{2,1,0:T(8,128)(2,1)} custom-call(bf16[768,768]{1,0:T(8,128)(2,1)S(1)} %copy-done.5, bf16[2,768,1152]{2,1,0:T(8,128)(2,1)} %get-tuple-element.362.refs_1_.d_proj, bf16[256,768]{1,0:T(8,128)(2,1)S(1)} %convolution_convert_fusion.2.away.refs_2_, bf16[2,256,1152]{2,1,0:T(8,128)(2,1)S(1)} %get-tuple-element.341.refs_3_, ...), custom_call_target="tpu_custom_call" | custom-call | flops 1132462080 | bytes 5505024 | tf_op jit(solution)/shard_map/pallas_call | solution.py:80
  346.9 1.4 collective-permute-start.40
  348.3 3.3 collective-permute-done.40
  351.6 1.7 convert_add_fusion.1
  353.7 1.6 convert_add_fusion
  358.3 5.2 %collective-permute-start.50 = (bf16[48,2304]{1,0:T(8,128)(2,1)S(1)}, bf16[48,2304]{1,0:T(8,128)(2,1)}, u32[]{:S(2)}, u32[]{:S(2)}) collective-permute-start(bf16[48,2304]{1,0:T(8,128)(2,1)S(1)} %copy-done.76), channel_id=1, source_target_pairs={{0,8},{2,10},{4,12},{6,14},{16,0},{18,2},{20,4},{22,6},{24,16},{26... | collective-permute-start | bytes 663560 | tf_op jit(solution)/shard_map/ppermute | solution.py:41
  363.5 2.5 collective-permute-start.51
  366.1 6.8 %shard_map.350 = (bf16[384,768]{1,0:T(8,128)(2,1)S(1)}, f32[384,768]{1,0:T(8,128)S(1)}, bf16[2,192,768]{2,1,0:T(8,128)(2,1)S(1)}, f32[2,192,768]{2,1,0:T(8,128)S(1)}) custom-call(bf16[2,384,1536]{2,1,0:T(8,128)(2,1)} %collective-permute-done.37.got, bf16[768,768]{1,0:T(8,128)(2,1)S(1)} %copy-done.6, bf16[2,768,1152]{2,1,0:T(8,128)(2,1)} %get-tuple-element.362.refs_1_.d_proj, ...), custom_call_target="tpu_custom_call" | custom-call | flops 1132462080 | bytes 7274496 | tf_op jit(solution)/shard_map/pallas_call | solution.py:80
  374.3 6.1 %collective-permute-done.50 = bf16[48,2304]{1,0:T(8,128)(2,1)} collective-permute-done((bf16[48,2304]{1,0:T(8,128)(2,1)S(1)}, bf16[48,2304]{1,0:T(8,128)(2,1)}, u32[]{:S(2)}, u32[]{:S(2)}) %collective-permute-start.50) | collective-permute-done | bytes 221216 | tf_op jit(solution)/shard_map/ppermute | solution.py:41
  384.6 3.0 collective-permute-start.53
  388.7 6.4 %shard_map.351 = f32[768,768]{1,0:T(8,128)S(1)} custom-call(f32[768,768]{1,0:T(8,128)S(1)} %copy-done.21, bf16[2,768,1152]{2,1,0:T(8,128)(2,1)} %get-tuple-element.362.refs_1_.d_proj, bf16[2,384,1664]{2,1,0:T(8,128)(2,1)} %bitcast.127, bf16[2,384,1664]{2,1,0:T(8,128)(2,1)} %collective-permute-done.13.refs_1_.refs_3_.refs_5_.refs_7_.out_two, ...), custom_call_target="tpu_custom_call" | custom-call | flops 1358954496 | bytes 11796480 | tf_op jit(solution)/shard_map/pallas_call | solution.py:80
  402.7 1.5 copy-done.58
  409.5 1.6 collective-permute-done.45
  411.2 1.6 collective-permute-start.46
  414.3 1.6 pad_maximum_fusion.2
  416.3 1.6 pad_maximum_fusion.1
  417.9 2.3 collective-permute-done.56
  421.0 1.6 collective-permute-start.57
  422.6 2.5 collective-permute-start.58
  427.5 4.7 %collective-permute-done.57 = bf16[48,1536]{1,0:T(8,128)(2,1)S(1)} collective-permute-done((bf16[48,1536]{1,0:T(8,128)(2,1)S(1)}, bf16[48,1536]{1,0:T(8,128)(2,1)S(1)}, u32[]{:S(2)}, u32[]{:S(2)}) %collective-permute-start.57) | collective-permute-done | bytes 147488 | tf_op jit(solution)/shard_map/ppermute | solution.py:41
  432.3 4.3 collective-permute-start.61
  438.0 1.7 collective-permute-done.61
  (396 shorter events, 96.8 us)
Async XLA Ops:
  9.3 9.9 %collective-permute-start = (bf16[48,1664]{1,0:T(8,128)(2,1)S(1)}, bf16[48,1664]{1,0:T(8,128)(2,1)S(1)}, u32[]{:S(2)}, u32[]{:S(2)}) collective-permute-start(bf16[48,1664]{1,0:T(8,128)(2,1)S(1)} %get-tuple-element.209.refs_0_), channel_id=1, source_target_pairs={{0,16},{2,18},{4,20},{6,22},{16,24},{18,26},{20,28},{22,30},{24,8}... | collective-permute-start | bytes 479240 | tf_op jit(solution)/shard_map/ppermute | solution.py:41
  13.4 9.8 %collective-permute-start.1 = (bf16[48,1664]{1,0:T(8,128)(2,1)S(1)}, bf16[48,1664]{1,0:T(8,128)(2,1)S(1)}, u32[]{:S(2)}, u32[]{:S(2)}) collective-permute-start(bf16[48,1664]{1,0:T(8,128)(2,1)S(1)} %get-tuple-element.209.refs_0_), channel_id=1, source_target_pairs={{0,24},{2,26},{4,28},{6,30},{16,8},{18,10},{20,12},{22,14},{24,0},... | collective-permute-start | bytes 479240 | tf_op jit(solution)/shard_map/ppermute | solution.py:41
  14.8 14.1 %collective-permute-start.2 = (bf16[48,1664]{1,0:T(8,128)(2,1)S(1)}, bf16[48,1664]{1,0:T(8,128)(2,1)S(1)}, u32[]{:S(2)}, u32[]{:S(2)}) collective-permute-start(bf16[48,1664]{1,0:T(8,128)(2,1)S(1)} %get-tuple-element.209.refs_0_), channel_id=1, source_target_pairs={{0,8},{2,10},{4,12},{6,14},{16,0},{18,2},{20,4},{22,6},{24,16},{26... | collective-permute-start | bytes 479240 | tf_op jit(solution)/shard_map/ppermute | solution.py:41
  16.5 12.3 %collective-permute-start.3 = (bf16[256,768]{1,0:T(8,128)(2,1)}, bf16[256,768]{1,0:T(8,128)(2,1)}, u32[]{:S(2)}, u32[]{:S(2)}) collective-permute-start(bf16[256,768]{1,0:T(8,128)(2,1)} %get-tuple-element.416), channel_id=1, source_target_pairs={{0,1},{1,0},{2,3},{3,2},{4,5},{5,4},{6,7},{7,6},{8,9},{9,8},{10,11... | collective-permute-start | bytes 1179656 | tf_op jit(solution)/shard_map/ppermute | solution.py:21
  28.9 12.6 %collective-permute-start.5 = (bf16[4,48,896]{2,1,0:T(8,128)(2,1)S(1)}, bf16[4,48,896]{2,1,0:T(8,128)(2,1)S(1)}, u32[]{:S(2)}, u32[]{:S(2)}) collective-permute-start(bf16[4,48,896]{2,1,0:T(8,128)(2,1)S(1)} %get-tuple-element.214.refs_2_), channel_id=1, source_target_pairs={{0,1},{1,0},{2,3},{3,2},{4,5},{5,4},{6,7},{7,6},{8,9},{9,8},{10,11... | collective-permute-start | bytes 1032200 | tf_op jit(solution)/shard_map/ppermute | solution.py:21
  30.5 11.0 %collective-permute-start.4 = (bf16[4,48,768]{2,1,0:T(8,128)(2,1)S(1)}, bf16[4,48,768]{2,1,0:T(8,128)(2,1)S(1)}, u32[]{:S(2)}, u32[]{:S(2)}) collective-permute-start(bf16[4,48,768]{2,1,0:T(8,128)(2,1)S(1)} %get-tuple-element.213.refs_0_), channel_id=1, source_target_pairs={{0,4},{2,6},{4,0},{6,2},{8,12},{10,14},{12,8},{14,10},{16,20},{18,... | collective-permute-start | bytes 884744 | tf_op jit(solution)/shard_map/ppermute | solution.py:26
  32.0 9.5 %collective-permute-start.8 = (bf16[48,3072]{1,0:T(8,128)(2,1)S(1)}, bf16[48,3072]{1,0:T(8,128)(2,1)S(1)}, u32[]{:S(2)}, u32[]{:S(2)}) collective-permute-start(bf16[48,3072]{1,0:T(8,128)(2,1)S(1)} %get-tuple-element.230.refs_0_), channel_id=1, source_target_pairs={{0,16},{2,18},{4,20},{6,22},{16,24},{18,26},{20,28},{22,30},{24,8}... | collective-permute-start | bytes 884744 | tf_op jit(solution)/shard_map/ppermute | solution.py:41
  32.1 9.4 %collective-permute-start.6 = (bf16[48,1152]{1,0:T(8,128)(2,1)S(1)}, bf16[48,1152]{1,0:T(8,128)(2,1)S(1)}, u32[]{:S(2)}, u32[]{:S(2)}) collective-permute-start(bf16[48,1152]{1,0:T(8,128)(2,1)S(1)} %get-tuple-element.215.refs_0_), channel_id=1, source_target_pairs={{0,4},{2,6},{4,0},{6,2},{8,12},{10,14},{12,8},{14,10},{16,20},{18,... | collective-permute-start | bytes 331784 | tf_op jit(solution)/shard_map/ppermute | solution.py:26
  32.7 8.9 %collective-permute-start.7 = (bf16[48,1152]{1,0:T(8,128)(2,1)S(1)}, bf16[48,1152]{1,0:T(8,128)(2,1)S(1)}, u32[]{:S(2)}, u32[]{:S(2)}) collective-permute-start(bf16[48,1152]{1,0:T(8,128)(2,1)S(1)} %get-tuple-element.216.refs_2_), channel_id=1, source_target_pairs={{0,1},{1,0},{2,3},{3,2},{4,5},{5,4},{6,7},{7,6},{8,9},{9,8},{10,11... | collective-permute-start | bytes 331784 | tf_op jit(solution)/shard_map/ppermute | solution.py:21
  41.7 21.5 %collective-permute-start.10 = (bf16[2,4,48,896]{3,2,1,0:T(8,128)(2,1)S(1)}, bf16[2,4,48,896]{3,2,1,0:T(8,128)(2,1)S(1)}, u32[]{:S(2)}, u32[]{:S(2)}) collective-permute-start(bf16[2,4,48,896]{3,2,1,0:T(8,128)(2,1)S(1)} %get-tuple-element.221.refs_2_), channel_id=1, source_target_pairs={{0,4},{2,6},{4,0},{6,2},{8,12},{10,14},{12,8},{14,10},{16,20},{18,... | collective-permute-start | bytes 2064392 | tf_op jit(solution)/shard_map/ppermute | solution.py:26
  43.2 19.9 %collective-permute-start.9 = (bf16[2,4,48,768]{3,2,1,0:T(8,128)(2,1)S(1)}, bf16[2,4,48,768]{3,2,1,0:T(8,128)(2,1)S(1)}, u32[]{:S(2)}, u32[]{:S(2)}) collective-permute-start(bf16[2,4,48,768]{3,2,1,0:T(8,128)(2,1)S(1)} %get-tuple-element.220.refs_0_), channel_id=1, source_target_pairs={{0,1},{1,0},{2,3},{3,2},{4,5},{5,4},{6,7},{7,6},{8,9},{9,8},{10,11... | collective-permute-start | bytes 1769480 | tf_op jit(solution)/shard_map/ppermute | solution.py:21
  44.5 11.7 %collective-permute-start.11 = (bf16[48,3072]{1,0:T(8,128)(2,1)S(1)}, bf16[48,3072]{1,0:T(8,128)(2,1)S(1)}, u32[]{:S(2)}, u32[]{:S(2)}) collective-permute-start(bf16[48,3072]{1,0:T(8,128)(2,1)S(1)} %get-tuple-element.230.refs_0_), channel_id=1, source_target_pairs={{0,24},{2,26},{4,28},{6,30},{16,8},{18,10},{20,12},{22,14},{24,0},... | collective-permute-start | bytes 884744 | tf_op jit(solution)/shard_map/ppermute | solution.py:41
  47.0 16.1 %collective-permute-start.12 = (bf16[48,3072]{1,0:T(8,128)(2,1)S(1)}, bf16[48,3072]{1,0:T(8,128)(2,1)S(1)}, u32[]{:S(2)}, u32[]{:S(2)}) collective-permute-start(bf16[48,3072]{1,0:T(8,128)(2,1)S(1)} %get-tuple-element.230.refs_0_), channel_id=1, source_target_pairs={{0,8},{2,10},{4,12},{6,14},{16,0},{18,2},{20,4},{22,6},{24,16},{26... | collective-permute-start | bytes 884744 | tf_op jit(solution)/shard_map/ppermute | solution.py:41
  63.4 19.9 %collective-permute-start.13 = (bf16[2,384,1664]{2,1,0:T(8,128)(2,1)S(1)}, bf16[2,384,1664]{2,1,0:T(8,128)(2,1)}, u32[]{:S(2)}, u32[]{:S(2)}) collective-permute-start(bf16[2,384,1664]{2,1,0:T(8,128)(2,1)S(1)} %bitcast.114), channel_id=1, source_target_pairs={{0,2},{2,0},{4,6},{6,4},{8,10},{10,8},{12,14},{14,12},{16,18},{18,... | collective-permute-start | bytes 7667720 | tf_op jit(solution)/shard_map/ppermute | solution.py:31
  64.7 17.2 %collective-permute-start.14 = (bf16[4,48,1536]{2,1,0:T(8,128)(2,1)}, bf16[4,48,1536]{2,1,0:T(8,128)(2,1)}, u32[]{:S(2)}, u32[]{:S(2)}) collective-permute-start(bf16[4,48,1536]{2,1,0:T(8,128)(2,1)} %get-tuple-element.234.refs_0_), channel_id=1, source_target_pairs={{0,4},{2,6},{4,0},{6,2},{8,12},{10,14},{12,8},{14,10},{16,20},{18,... | collective-permute-start | bytes 1769480 | tf_op jit(solution)/shard_map/ppermute | solution.py:26
  65.2 18.0 %collective-permute-start.15 = (bf16[4,48,1536]{2,1,0:T(8,128)(2,1)}, bf16[4,48,1536]{2,1,0:T(8,128)(2,1)}, u32[]{:S(2)}, u32[]{:S(2)}) collective-permute-start(bf16[4,48,1536]{2,1,0:T(8,128)(2,1)} %get-tuple-element.235.refs_2_), channel_id=1, source_target_pairs={{0,1},{1,0},{2,3},{3,2},{4,5},{5,4},{6,7},{7,6},{8,9},{9,8},{10,11... | collective-permute-start | bytes 1769480 | tf_op jit(solution)/shard_map/ppermute | solution.py:21
  67.3 14.6 %collective-permute-start.16 = (bf16[3456]{0:T(1024)(128)(2,1)}, bf16[3456]{0:T(1024)(128)(2,1)}, u32[]{:S(2)}, u32[]{:S(2)}) collective-permute-start(bf16[3456]{0:T(1024)(128)(2,1)} %concatenate.65), channel_id=1, source_target_pairs={{0,1},{1,0},{2,3},{3,2},{4,5},{5,4},{6,7},{7,6},{8,9},{9,8},{10,11... | collective-permute-start | bytes 20744 | tf_op jit(solution)/shard_map/ppermute | solution.py:21
  68.0 22.6 %collective-permute-start.17 = (bf16[256,768]{1,0:T(8,128)(2,1)}, bf16[256,768]{1,0:T(8,128)(2,1)}, u32[]{:S(2)}, u32[]{:S(2)}) collective-permute-start(bf16[256,768]{1,0:T(8,128)(2,1)} %copy-done.64), channel_id=1, source_target_pairs={{0,1},{1,0},{2,3},{3,2},{4,5},{5,4},{6,7},{7,6},{8,9},{9,8},{10,11... | collective-permute-start | bytes 1179656 | tf_op jit(solution)/shard_map/ppermute | solution.py:21
  81.9 24.9 %collective-permute-start.18 = (bf16[2,48,2304]{2,1,0:T(8,128)(2,1)}, bf16[2,48,2304]{2,1,0:T(8,128)(2,1)}, u32[]{:S(2)}, u32[]{:S(2)}) collective-permute-start(bf16[2,48,2304]{2,1,0:T(8,128)(2,1)} %shard_map.329.refs_0_), channel_id=1, source_target_pairs={{0,16},{2,18},{4,20},{6,22},{16,24},{18,26},{20,28},{22,30},{24,8}... | collective-permute-start | bytes 1327112 | tf_op jit(solution)/shard_map/ppermute | solution.py:41
  81.9 24.9 %collective-permute-start.19 = (bf16[2,48,2304]{2,1,0:T(8,128)(2,1)}, bf16[2,48,2304]{2,1,0:T(8,128)(2,1)}, u32[]{:S(2)}, u32[]{:S(2)}) collective-permute-start(bf16[2,48,2304]{2,1,0:T(8,128)(2,1)} %shard_map.329.refs_0_), channel_id=1, source_target_pairs={{0,24},{2,26},{4,28},{6,30},{16,8},{18,10},{20,12},{22,14},{24,0},... | collective-permute-start | bytes 1327112 | tf_op jit(solution)/shard_map/ppermute | solution.py:41
  87.0 37.5 %collective-permute-start.20 = (bf16[2,4,48,1536]{3,2,1,0:T(8,128)(2,1)}, bf16[2,4,48,1536]{3,2,1,0:T(8,128)(2,1)}, u32[]{:S(2)}, u32[]{:S(2)}) collective-permute-start(bf16[2,4,48,1536]{3,2,1,0:T(8,128)(2,1)} %get-tuple-element.254.refs_0_), channel_id=1, source_target_pairs={{0,1},{1,0},{2,3},{3,2},{4,5},{5,4},{6,7},{7,6},{8,9},{9,8},{10,11... | collective-permute-start | bytes 3538952 | tf_op jit(solution)/shard_map/ppermute | solution.py:21
  88.4 36.2 %collective-permute-start.21 = (bf16[2,4,48,1536]{3,2,1,0:T(8,128)(2,1)}, bf16[2,4,48,1536]{3,2,1,0:T(8,128)(2,1)}, u32[]{:S(2)}, u32[]{:S(2)}) collective-permute-start(bf16[2,4,48,1536]{3,2,1,0:T(8,128)(2,1)} %get-tuple-element.256.refs_2_), channel_id=1, source_target_pairs={{0,4},{2,6},{4,0},{6,2},{8,12},{10,14},{12,8},{14,10},{16,20},{18,... | collective-permute-start | bytes 3538952 | tf_op jit(solution)/shard_map/ppermute | solution.py:26
  90.6 34.0 %collective-permute-start.22 = (bf16[2,48,2304]{2,1,0:T(8,128)(2,1)}, bf16[2,48,2304]{2,1,0:T(8,128)(2,1)S(1)}, u32[]{:S(2)}, u32[]{:S(2)}) collective-permute-start(bf16[2,48,2304]{2,1,0:T(8,128)(2,1)} %shard_map.329.refs_0_), channel_id=1, source_target_pairs={{0,8},{2,10},{4,12},{6,14},{16,0},{18,2},{20,4},{22,6},{24,16},{26... | collective-permute-start | bytes 1327112 | tf_op jit(solution)/shard_map/ppermute | solution.py:41
  129.5 13.3 %collective-permute-start.23 = (bf16[2,384,3072]{2,1,0:T(8,128)(2,1)}, bf16[2,384,3072]{2,1,0:T(8,128)(2,1)}, u32[]{:S(2)}, u32[]{:S(2)}) collective-permute-start(bf16[2,384,3072]{2,1,0:T(8,128)(2,1)} %bitcast.157), channel_id=1, source_target_pairs={{0,2},{2,0},{4,6},{6,4},{8,10},{10,8},{12,14},{14,12},{16,18},{18,... | collective-permute-start | bytes 14155784 | tf_op jit(solution)/shard_map/ppermute | solution.py:31
  129.6 12.0 %collective-permute-start.26 = (bf16[256,768]{1,0:T(8,128)(2,1)S(1)}, bf16[256,768]{1,0:T(8,128)(2,1)S(1)}, u32[]{:S(2)}, u32[]{:S(2)}) collective-permute-start(bf16[256,768]{1,0:T(8,128)(2,1)S(1)} %get-tuple-element.413), channel_id=1, source_target_pairs={{0,1},{1,0},{2,3},{3,2},{4,5},{5,4},{6,7},{7,6},{8,9},{9,8},{10,11... | collective-permute-start | bytes 1179656 | tf_op jit(solution)/shard_map/ppermute | solution.py:21
  133.2 27.2 %collective-permute-start.24 = (bf16[2,4,48,1152]{3,2,1,0:T(8,128)(2,1)S(1)}, bf16[2,4,48,1152]{3,2,1,0:T(8,128)(2,1)}, u32[]{:S(2)}, u32[]{:S(2)}) collective-permute-start(bf16[2,4,48,1152]{3,2,1,0:T(8,128)(2,1)S(1)} %get-tuple-element.266.refs_0_), channel_id=1, source_target_pairs={{0,1},{1,0},{2,3},{3,2},{4,5},{5,4},{6,7},{7,6},{8,9},{9,8},{10,11... | collective-permute-start | bytes 2654216 | tf_op jit(solution)/shard_map/ppermute | solution.py:21
  134.0 26.4 %collective-permute-start.25 = (bf16[2,4,48,1152]{3,2,1,0:T(8,128)(2,1)}, bf16[2,4,48,1152]{3,2,1,0:T(8,128)(2,1)}, u32[]{:S(2)}, u32[]{:S(2)}) collective-permute-start(bf16[2,4,48,1152]{3,2,1,0:T(8,128)(2,1)} %get-tuple-element.267.refs_2_), channel_id=1, source_target_pairs={{0,4},{2,6},{4,0},{6,2},{8,12},{10,14},{12,8},{14,10},{16,20},{18,... | collective-permute-start | bytes 2654216 | tf_op jit(solution)/shard_map/ppermute | solution.py:26
  160.4 82.1 %copy-start.9 = (bf16[768,768]{1,0:T(8,128)(2,1)}, bf16[768,768]{1,0:T(8,128)(2,1)S(1)}, u32[]{:S(2)}) copy-start(bf16[768,768]{1,0:T(8,128)(2,1)S(1)} %get-tuple-element.270.rows.refs_4_) | copy-start | bytes 3538948
  164.8 6.6 %collective-permute-start.27 = (bf16[2,384,2304]{2,1,0:T(8,128)(2,1)}, bf16[2,384,2304]{2,1,0:T(8,128)(2,1)}, u32[]{:S(2)}, u32[]{:S(2)}) collective-permute-start(bf16[2,384,2304]{2,1,0:T(8,128)(2,1)} %bitcast.141), channel_id=1, source_target_pairs={{0,2},{2,0},{4,6},{6,4},{8,10},{10,8},{12,14},{14,12},{16,18},{18,... | collective-permute-start | bytes 10616840 | tf_op jit(solution)/shard_map/ppermute | solution.py:31
  165.1 14.9 %collective-permute-start.28 = (bf16[256,768]{1,0:T(8,128)(2,1)S(1)}, bf16[256,768]{1,0:T(8,128)(2,1)S(1)}, u32[]{:S(2)}, u32[]{:S(2)}) collective-permute-start(bf16[256,768]{1,0:T(8,128)(2,1)S(1)} %slice.423), channel_id=1, source_target_pairs={{0,1},{1,0},{2,3},{3,2},{4,5},{5,4},{6,7},{7,6},{8,9},{9,8},{10,11... | collective-permute-start | bytes 1179656 | tf_op jit(solution)/shard_map/ppermute | solution.py:21
  179.9 62.6 %copy-start.14 = (bf16[256,768]{1,0:T(8,128)(2,1)}, bf16[256,768]{1,0:T(8,128)(2,1)S(1)}, u32[]{:S(2)}) copy-start(bf16[256,768]{1,0:T(8,128)(2,1)S(1)} %collective-permute-done.28.away.refs_6_) | copy-start | bytes 1179652
  204.5 22.7 %collective-permute-start.29 = (bf16[256,768]{1,0:T(8,128)(2,1)S(1)}, bf16[256,768]{1,0:T(8,128)(2,1)S(1)}, u32[]{:S(2)}, u32[]{:S(2)}) collective-permute-start(bf16[256,768]{1,0:T(8,128)(2,1)S(1)} %slice.682), channel_id=1, source_target_pairs={{0,1},{1,0},{2,3},{3,2},{4,5},{5,4},{6,7},{7,6},{8,9},{9,8},{10,11... | collective-permute-start | bytes 1179656 | tf_op jit(solution)/shard_map/ppermute | solution.py:21
  226.4 16.1 %collective-permute-start.30 = (bf16[256,768]{1,0:T(8,128)(2,1)S(1)}, bf16[256,768]{1,0:T(8,128)(2,1)S(1)}, u32[]{:S(2)}, u32[]{:S(2)}) collective-permute-start(bf16[256,768]{1,0:T(8,128)(2,1)S(1)} %get-tuple-element.297), channel_id=1, source_target_pairs={{0,1},{1,0},{2,3},{3,2},{4,5},{5,4},{6,7},{7,6},{8,9},{9,8},{10,11... | collective-permute-start | bytes 1179656 | tf_op jit(solution)/shard_map/ppermute | solution.py:21
  249.8 11.2 %collective-permute-start.31 = (bf16[2,384,2304]{2,1,0:T(8,128)(2,1)}, bf16[2,384,2304]{2,1,0:T(8,128)(2,1)}, u32[]{:S(2)}, u32[]{:S(2)}) collective-permute-start(bf16[2,384,2304]{2,1,0:T(8,128)(2,1)} %shard_map.341), channel_id=1, source_target_pairs={{0,2},{2,0},{4,6},{6,4},{8,10},{10,8},{12,14},{14,12},{16,18},{18,... | collective-permute-start | bytes 10616840 | tf_op jit(solution)/shard_map/ppermute | solution.py:31
  280.5 13.7 %collective-permute-start.32 = (bf16[2,384,3072]{2,1,0:T(8,128)(2,1)}, bf16[2,384,3072]{2,1,0:T(8,128)(2,1)S(1)}, u32[]{:S(2)}, u32[]{:S(2)}) collective-permute-start(bf16[2,384,3072]{2,1,0:T(8,128)(2,1)} %shard_map.344), channel_id=1, source_target_pairs={{0,2},{2,0},{4,6},{6,4},{8,10},{10,8},{12,14},{14,12},{16,18},{18,... | collective-permute-start | bytes 14155784 | tf_op jit(solution)/shard_map/ppermute | solution.py:31
  281.1 24.4 %collective-permute-start.33 = (bf16[384,1152]{1,0:T(8,128)(2,1)}, bf16[384,1152]{1,0:T(8,128)(2,1)}, u32[]{:S(2)}, u32[]{:S(2)}) collective-permute-start(bf16[384,1152]{1,0:T(8,128)(2,1)} %get-tuple-element.310), channel_id=1, source_target_pairs={{0,1},{1,0},{2,3},{3,2},{4,5},{5,4},{6,7},{7,6},{8,9},{9,8},{10,11... | collective-permute-start | bytes 2654216 | tf_op jit(solution)/shard_map/ppermute | solution.py:21
  282.4 23.1 %collective-permute-start.34 = (bf16[2,192,1152]{2,1,0:T(8,128)(2,1)}, bf16[2,192,1152]{2,1,0:T(8,128)(2,1)}, u32[]{:S(2)}, u32[]{:S(2)}) collective-permute-start(bf16[2,192,1152]{2,1,0:T(8,128)(2,1)} %get-tuple-element.311), channel_id=1, source_target_pairs={{0,4},{2,6},{4,0},{6,2},{8,12},{10,14},{12,8},{14,10},{16,20},{18,... | collective-permute-start | bytes 2654216 | tf_op jit(solution)/shard_map/ppermute | solution.py:26
  308.8 15.9 %collective-permute-start.36 = (bf16[192,1152]{1,0:T(8,128)(2,1)S(1)}, bf16[192,1152]{1,0:T(8,128)(2,1)S(1)}, u32[]{:S(2)}, u32[]{:S(2)}) collective-permute-start(bf16[192,1152]{1,0:T(8,128)(2,1)S(1)} %fusion.21), channel_id=1, source_target_pairs={{0,1},{1,0},{2,3},{3,2},{4,5},{5,4},{6,7},{7,6},{8,9},{9,8},{10,11... | collective-permute-start | bytes 1327112 | tf_op jit(solution)/shard_map/ppermute | solution.py:21
  310.2 14.4 %collective-permute-start.35 = (bf16[192,1152]{1,0:T(8,128)(2,1)S(1)}, bf16[192,1152]{1,0:T(8,128)(2,1)S(1)}, u32[]{:S(2)}, u32[]{:S(2)}) collective-permute-start(bf16[192,1152]{1,0:T(8,128)(2,1)S(1)} %slice.680), channel_id=1, source_target_pairs={{0,4},{2,6},{4,0},{6,2},{8,12},{10,14},{12,8},{14,10},{16,20},{18,... | collective-permute-start | bytes 1327112 | tf_op jit(solution)/shard_map/ppermute | solution.py:26
  312.1 36.2 %collective-permute-start.38 = (bf16[384,1536]{1,0:T(8,128)(2,1)}, bf16[384,1536]{1,0:T(8,128)(2,1)}, u32[]{:S(2)}, u32[]{:S(2)}) collective-permute-start(bf16[384,1536]{1,0:T(8,128)(2,1)} %get-tuple-element.322), channel_id=1, source_target_pairs={{0,1},{1,0},{2,3},{3,2},{4,5},{5,4},{6,7},{7,6},{8,9},{9,8},{10,11... | collective-permute-start | bytes 3538952 | tf_op jit(solution)/shard_map/ppermute | solution.py:21
  313.5 34.9 %collective-permute-start.39 = (bf16[2,192,1536]{2,1,0:T(8,128)(2,1)}, bf16[2,192,1536]{2,1,0:T(8,128)(2,1)}, u32[]{:S(2)}, u32[]{:S(2)}) collective-permute-start(bf16[2,192,1536]{2,1,0:T(8,128)(2,1)} %get-tuple-element.323), channel_id=1, source_target_pairs={{0,4},{2,6},{4,0},{6,2},{8,12},{10,14},{12,8},{14,10},{16,20},{18,... | collective-permute-start | bytes 3538952 | tf_op jit(solution)/shard_map/ppermute | solution.py:26
  346.8 19.2 %collective-permute-start.37 = (bf16[2,384,1536]{2,1,0:T(8,128)(2,1)}, bf16[2,384,1536]{2,1,0:T(8,128)(2,1)}, u32[]{:S(2)}, u32[]{:S(2)}) collective-permute-start(bf16[2,384,1536]{2,1,0:T(8,128)(2,1)} %shard_map.349), channel_id=1, source_target_pairs={{0,2},{2,0},{4,6},{6,4},{8,10},{10,8},{12,14},{14,12},{16,18},{18,... | collective-permute-start | bytes 7077896 | tf_op jit(solution)/shard_map/ppermute | solution.py:31
  346.9 4.7 %collective-permute-start.40 = (f32[22,768]{1,0:T(8,128)S(1)}, f32[22,768]{1,0:T(8,128)S(1)}, u32[]{:S(2)}, u32[]{:S(2)}) collective-permute-start(f32[22,768]{1,0:T(8,128)S(1)} %pad_maximum_fusion.10), channel_id=1, source_target_pairs={{0,1},{1,0},{2,3},{3,2},{4,5},{5,4},{6,7},{7,6},{8,9},{9,8},{10,11... | collective-permute-start | bytes 202760 | tf_op jit(solution)/shard_map/ppermute | solution.py:21
  355.5 17.4 %collective-permute-start.49 = (bf16[192,1536]{1,0:T(8,128)(2,1)S(1)}, bf16[192,1536]{1,0:T(8,128)(2,1)S(1)}, u32[]{:S(2)}, u32[]{:S(2)}) collective-permute-start(bf16[192,1536]{1,0:T(8,128)(2,1)S(1)} %fusion.17), channel_id=1, source_target_pairs={{0,1},{1,0},{2,3},{3,2},{4,5},{5,4},{6,7},{7,6},{8,9},{9,8},{10,11... | collective-permute-start | bytes 1769480 | tf_op jit(solution)/shard_map/ppermute | solution.py:21
  356.9 17.4 %collective-permute-start.48 = (bf16[192,1536]{1,0:T(8,128)(2,1)S(1)}, bf16[192,1536]{1,0:T(8,128)(2,1)S(1)}, u32[]{:S(2)}, u32[]{:S(2)}) collective-permute-start(bf16[192,1536]{1,0:T(8,128)(2,1)S(1)} %slice.679), channel_id=1, source_target_pairs={{0,4},{2,6},{4,0},{6,2},{8,12},{10,14},{12,8},{14,10},{16,20},{18,... | collective-permute-start | bytes 1769480 | tf_op jit(solution)/shard_map/ppermute | solution.py:26
  358.3 22.1 %collective-permute-start.50 = (bf16[48,2304]{1,0:T(8,128)(2,1)S(1)}, bf16[48,2304]{1,0:T(8,128)(2,1)}, u32[]{:S(2)}, u32[]{:S(2)}) collective-permute-start(bf16[48,2304]{1,0:T(8,128)(2,1)S(1)} %copy-done.76), channel_id=1, source_target_pairs={{0,8},{2,10},{4,12},{6,14},{16,0},{18,2},{20,4},{22,6},{24,16},{26... | collective-permute-start | bytes 663560 | tf_op jit(solution)/shard_map/ppermute | solution.py:41
  363.5 18.3 %collective-permute-start.51 = (bf16[48,2304]{1,0:T(8,128)(2,1)S(1)}, bf16[48,2304]{1,0:T(8,128)(2,1)S(1)}, u32[]{:S(2)}, u32[]{:S(2)}) collective-permute-start(bf16[48,2304]{1,0:T(8,128)(2,1)S(1)} %copy-done.75), channel_id=1, source_target_pairs={{0,24},{2,26},{4,28},{6,30},{16,8},{18,10},{20,12},{22,14},{24,0},... | collective-permute-start | bytes 663560 | tf_op jit(solution)/shard_map/ppermute | solution.py:41
  366.0 16.5 %collective-permute-start.52 = (bf16[48,2304]{1,0:T(8,128)(2,1)S(1)}, bf16[48,2304]{1,0:T(8,128)(2,1)S(1)}, u32[]{:S(2)}, u32[]{:S(2)}) collective-permute-start(bf16[48,2304]{1,0:T(8,128)(2,1)S(1)} %copy-done.74), channel_id=1, source_target_pairs={{0,16},{2,18},{4,20},{6,22},{16,24},{18,26},{20,28},{22,30},{24,8}... | collective-permute-start | bytes 663560 | tf_op jit(solution)/shard_map/ppermute | solution.py:41
  372.9 33.1 %collective-permute-start.44 = (bf16[256,768]{1,0:T(8,128)(2,1)S(1)}, bf16[256,768]{1,0:T(8,128)(2,1)}, u32[]{:S(2)}, u32[]{:S(2)}) collective-permute-start(bf16[256,768]{1,0:T(8,128)(2,1)S(1)} %copy-done.43), channel_id=1, source_target_pairs={{0,1},{1,0},{2,3},{3,2},{4,5},{5,4},{6,7},{7,6},{8,9},{9,8},{10,11... | collective-permute-start | bytes 1179656 | tf_op jit(solution)/shard_map/ppermute | solution.py:21
  374.3 25.7 %collective-permute-start.43 = (f32[22,768]{1,0:T(8,128)S(1)}, f32[22,768]{1,0:T(8,128)}, u32[]{:S(2)}, u32[]{:S(2)}) collective-permute-start(f32[22,768]{1,0:T(8,128)S(1)} %fusion.102), channel_id=1, source_target_pairs={{0,2},{2,0},{4,6},{6,4},{8,10},{10,8},{12,14},{14,12},{16,18},{18,... | collective-permute-start | bytes 202760 | tf_op jit(solution)/shard_map/ppermute | solution.py:812
  380.4 16.9 %collective-permute-start.41 = (bf16[384,768]{1,0:T(8,128)(2,1)S(1)}, bf16[384,768]{1,0:T(8,128)(2,1)S(1)}, u32[]{:S(2)}, u32[]{:S(2)}) collective-permute-start(bf16[384,768]{1,0:T(8,128)(2,1)S(1)} %get-tuple-element.359), channel_id=1, source_target_pairs={{0,1},{1,0},{2,3},{3,2},{4,5},{5,4},{6,7},{7,6},{8,9},{9,8},{10,11... | collective-permute-start | bytes 1769480 | tf_op jit(solution)/shard_map/ppermute | solution.py:21
  381.8 16.9 %collective-permute-start.42 = (bf16[2,192,768]{2,1,0:T(8,128)(2,1)S(1)}, bf16[2,192,768]{2,1,0:T(8,128)(2,1)}, u32[]{:S(2)}, u32[]{:S(2)}) collective-permute-start(bf16[2,192,768]{2,1,0:T(8,128)(2,1)S(1)} %get-tuple-element.360), channel_id=1, source_target_pairs={{0,4},{2,6},{4,0},{6,2},{8,12},{10,14},{12,8},{14,10},{16,20},{18,... | collective-permute-start | bytes 1769480 | tf_op jit(solution)/shard_map/ppermute | solution.py:26
  384.6 31.3 %collective-permute-start.53 = (bf16[48,3072]{1,0:T(8,128)(2,1)}, bf16[48,3072]{1,0:T(8,128)(2,1)}, u32[]{:S(2)}, u32[]{:S(2)}) collective-permute-start(bf16[48,3072]{1,0:T(8,128)(2,1)} %get-tuple-element.410), channel_id=1, source_target_pairs={{0,8},{2,10},{4,12},{6,14},{16,0},{18,2},{20,4},{22,6},{24,16},{26... | collective-permute-start | bytes 884744 | tf_op jit(solution)/shard_map/ppermute | solution.py:41
  397.3 20.6 %collective-permute-start.54 = (bf16[48,3072]{1,0:T(8,128)(2,1)}, bf16[48,3072]{1,0:T(8,128)(2,1)S(1)}, u32[]{:S(2)}, u32[]{:S(2)}) collective-permute-start(bf16[48,3072]{1,0:T(8,128)(2,1)} %get-tuple-element.409), channel_id=1, source_target_pairs={{0,24},{2,26},{4,28},{6,30},{16,8},{18,10},{20,12},{22,14},{24,0},... | collective-permute-start | bytes 884744 | tf_op jit(solution)/shard_map/ppermute | solution.py:41
  398.7 19.2 %collective-permute-start.55 = (bf16[48,3072]{1,0:T(8,128)(2,1)}, bf16[48,3072]{1,0:T(8,128)(2,1)S(1)}, u32[]{:S(2)}, u32[]{:S(2)}) collective-permute-start(bf16[48,3072]{1,0:T(8,128)(2,1)} %get-tuple-element.408), channel_id=1, source_target_pairs={{0,16},{2,18},{4,20},{6,22},{16,24},{18,26},{20,28},{22,30},{24,8}... | collective-permute-start | bytes 884744 | tf_op jit(solution)/shard_map/ppermute | solution.py:41
  400.0 11.2 %collective-permute-start.45 = (bf16[256,768]{1,0:T(8,128)(2,1)S(1)}, bf16[256,768]{1,0:T(8,128)(2,1)S(1)}, u32[]{:S(2)}, u32[]{:S(2)}) collective-permute-start(bf16[256,768]{1,0:T(8,128)(2,1)S(1)} %slice.681), channel_id=1, source_target_pairs={{0,1},{1,0},{2,3},{3,2},{4,5},{5,4},{6,7},{7,6},{8,9},{9,8},{10,11... | collective-permute-start | bytes 1179656 | tf_op jit(solution)/shard_map/ppermute | solution.py:21
  405.9 14.3 %collective-permute-start.47 = (bf16[192,768]{1,0:T(8,128)(2,1)S(1)}, bf16[192,768]{1,0:T(8,128)(2,1)S(1)}, u32[]{:S(2)}, u32[]{:S(2)}) collective-permute-start(bf16[192,768]{1,0:T(8,128)(2,1)S(1)} %fusion.24), channel_id=1, source_target_pairs={{0,1},{1,0},{2,3},{3,2},{4,5},{5,4},{6,7},{7,6},{8,9},{9,8},{10,11... | collective-permute-start | bytes 884744 | tf_op jit(solution)/shard_map/ppermute | solution.py:21
  411.2 9.1 %collective-permute-start.46 = (bf16[192,768]{1,0:T(8,128)(2,1)S(1)}, bf16[192,768]{1,0:T(8,128)(2,1)S(1)}, u32[]{:S(2)}, u32[]{:S(2)}) collective-permute-start(bf16[192,768]{1,0:T(8,128)(2,1)S(1)} %slice.683), channel_id=1, source_target_pairs={{0,4},{2,6},{4,0},{6,2},{8,12},{10,14},{12,8},{14,10},{16,20},{18,... | collective-permute-start | bytes 884744 | tf_op jit(solution)/shard_map/ppermute | solution.py:26
  415.9 4.4 collective-permute-start.56
  420.3 7.2 %collective-permute-start.60 = (f32[22,768]{1,0:T(8,128)S(1)}, f32[22,768]{1,0:T(8,128)S(1)}, u32[]{:S(2)}, u32[]{:S(2)}) collective-permute-start(f32[22,768]{1,0:T(8,128)S(1)} %add.243), channel_id=1, source_target_pairs={{0,8},{2,10},{4,12},{6,14},{8,0},{10,2},{12,4},{14,6},{16,24},{18,... | collective-permute-start | bytes 202760 | tf_op jit(solution)/shard_map/ppermute | solution.py:812
  421.0 11.3 %collective-permute-start.57 = (bf16[48,1536]{1,0:T(8,128)(2,1)S(1)}, bf16[48,1536]{1,0:T(8,128)(2,1)S(1)}, u32[]{:S(2)}, u32[]{:S(2)}) collective-permute-start(bf16[48,1536]{1,0:T(8,128)(2,1)S(1)} %get-tuple-element.424), channel_id=1, source_target_pairs={{0,8},{2,10},{4,12},{6,14},{16,0},{18,2},{20,4},{22,6},{24,16},{26... | collective-permute-start | bytes 442376 | tf_op jit(solution)/shard_map/ppermute | solution.py:41
  422.6 9.6 %collective-permute-start.58 = (bf16[48,1536]{1,0:T(8,128)(2,1)S(1)}, bf16[48,1536]{1,0:T(8,128)(2,1)S(1)}, u32[]{:S(2)}, u32[]{:S(2)}) collective-permute-start(bf16[48,1536]{1,0:T(8,128)(2,1)S(1)} %get-tuple-element.423), channel_id=1, source_target_pairs={{0,24},{2,26},{4,28},{6,30},{16,8},{18,10},{20,12},{22,14},{24,0},... | collective-permute-start | bytes 442376 | tf_op jit(solution)/shard_map/ppermute | solution.py:41
  425.2 7.1 %collective-permute-start.59 = (bf16[48,1536]{1,0:T(8,128)(2,1)S(1)}, bf16[48,1536]{1,0:T(8,128)(2,1)S(1)}, u32[]{:S(2)}, u32[]{:S(2)}) collective-permute-start(bf16[48,1536]{1,0:T(8,128)(2,1)S(1)} %get-tuple-element.422), channel_id=1, source_target_pairs={{0,16},{2,18},{4,20},{6,22},{16,24},{18,26},{20,28},{22,30},{24,8}... | collective-permute-start | bytes 442376 | tf_op jit(solution)/shard_map/ppermute | solution.py:41
  432.3 7.4 %collective-permute-start.61 = (f32[22,768]{1,0:T(8,128)S(1)}, f32[22,768]{1,0:T(8,128)S(1)}, u32[]{:S(2)}, u32[]{:S(2)}) collective-permute-start(f32[22,768]{1,0:T(8,128)S(1)} %add.247), channel_id=1, source_target_pairs={{0,16},{2,18},{4,20},{6,22},{8,24},{10,26},{12,28},{14,30},{16,0},... | collective-permute-start | bytes 202760 | tf_op jit(solution)/shard_map/ppermute | solution.py:812
  (87 other events, 817.8 us)

commit v2 on v1

--- a/solution.py
+++ b/solution.py
@@ -105,29 +105,6 @@
         compiler_params=pltpu.CompilerParams(vmem_limit_bytes=VMEM_BYTES),
         cost_estimate=pl.CostEstimate(flops=0, bytes_accessed=moved, transcendentals=0),
     )(*arrays)
-
-
-def pack(straight, turned, shapes, copies):
-    count = len(straight)
-
-    def body(*refs):
-        outs = refs[count + len(turned) :]
-        rows = turned[0].shape[1]
-        at = lambda axis: lax.broadcasted_iota(jnp.int32, (rows, rows), axis)
-        same = jnp.where(at(0) == at(1), 1.0, 0.0).astype(LOW)
-        for source, taken, target, place in copies:
-            if source < count:
-                outs[target][place] = refs[source][taken]
-            else:
-                outs[target][place] = dot(same, refs[source][...], 1, 1).astype(LOW)
-
-    moved = 2 * sum(math.prod(shape) for shape in shapes)
-    return pl.pallas_call(
-        body,
-        out_shape=[jax.ShapeDtypeStruct(shape, LOW) for shape in shapes],
-        compiler_params=pltpu.CompilerParams(vmem_limit_bytes=VMEM_BYTES),
-        cost_estimate=pl.CostEstimate(flops=0, bytes_accessed=moved, transcendentals=0),
-    )(*straight, *turned)
 
 
 def whole(array):
@@ -307,7 +284,7 @@
         weights = pairs_of(refs[:count])
         (
             out_one, out_two, bias, segs_q, segs_k, context_own, norms,
-            proj_away, context, logsum, hidden, hidden_low, normed_one, recip_one, mask, total,
+            proj_away, context, logsum, hidden_low, normed_one, recip_one, mask, total,
         ) = refs[count:]
         i = pl.program_id(0)
         make_mask(segs_q, segs_k, mask)
@@ -326,7 +303,6 @@
                 value = rows[at, :].astype(F32) + norms[2:3, :]
                 value = value + (total[at, :] + dot(context[0, at], out_cols, 1, 1))
                 value, normed, recip = normalize(value, norms[0:1, :], norms[3:4, :])
-                hidden[at, :] = value
                 hidden_low[at, :] = value.astype(LOW)
                 normed_one[at, :] = normed.astype(LOW)
                 recip_one[at, :] = recip
@@ -341,8 +317,7 @@
         ],
         [
             out_group((2, half, wide), LOW), out_group((2, n, width), LOW), out_group((2, 8, half), F32),
-            out_whole((n, depth), F32), out_whole((n, depth), LOW), out_whole((n, depth), LOW),
-            out_whole((n, 1), F32),
+            out_whole((n, depth), LOW), out_whole((n, depth), LOW), out_whole((n, 1), F32),
         ],
         [pltpu.VMEM((own, half), F32), pltpu.VMEM((n, depth), F32)],
         flops=4 * depth * (n * width + half * wide) + 8 * own * half * width,
@@ -350,20 +325,20 @@
     )
 
 
-def ffn_call(layer, hidden, hidden_low):
-    n, depth = hidden.shape
+def ffn_call(layer, hidden_low, wide):
+    n, depth = hidden_low.shape
     steps, _, size = layer.bias_up.shape
     per = steps // 2
 
     def body(
-        hidden, hidden_low, norms, bias_up, up_one, up_two, down_one, down_two,
-        act, slope, output, output_low, normed_two, recip_two,
+        hidden_low, norms, bias_up, up_one, up_two, down_one, down_two,
+        act, slope, output, normed_two, recip_two, total,
     ):
         i = pl.program_id(0)
 
         @pl.when(i == 0)
         def _():
-            output[...] = hidden[...] + norms[4:5, :]
+            total[...] = hidden_low[...].astype(F32) + norms[4:5, :]
 
         up, down = joined((up_one, up_two)), joined((down_one, down_two))
         for at in row_tiles(n):
@@ -374,14 +349,13 @@
             slope[0, at, :] = (
                 bell + pre * (jnp.exp(-0.5 * pre * pre) * (1.0 / math.sqrt(2.0 * math.pi)))
             ).astype(LOW)
-            output[at, :] += dot(low, down, 1, 1)
+            total[at, :] += dot(low, down, 1, 1)
 
         @pl.when(i == steps - 1)
         def _():
             for at in row_tiles(n):
-                value, normed, recip = normalize(output[at, :], norms[1:2, :], norms[5:6, :])
-                output[at, :] = value
-                output_low[at, :] = value.astype(LOW)
+                value, normed, recip = normalize(total[at, :], norms[1:2, :], norms[5:6, :])
+                output[at, :] = value.astype(output.dtype)
                 normed_two[at, :] = normed.astype(LOW)
                 recip_two[at, :] = recip
 
@@ -390,13 +364,13 @@
     return call(
         body, steps,
         [
-            whole(hidden), whole(hidden_low), whole(layer.norms), per_group(layer.bias_up),
+            whole(hidden_low), whole(layer.norms), per_group(layer.bias_up),
         ] + layer.ffn(layer.up) + layer.ffn(layer.down),
         [
-            ffn_out, ffn_out, out_whole((n, depth), F32), out_whole((n, depth), LOW),
-            out_whole((n, depth), LOW), out_whole((n, 1), F32),
+            ffn_out, ffn_out, out_whole((n, depth), F32 if wide else LOW), out_whole((n, depth), LOW),
+            out_whole((n, 1), F32),
         ],
-        [],
+        [pltpu.VMEM((n, depth), F32)],
         flops=8 * n * depth * neurons,
         exps=4 * n * neurons,
     )
@@ -420,7 +394,7 @@
         extra = refs[0] if has_extra else None
         (
             normed_one, recip_one, normed_two, recip_two, norms, slope, up_one, up_two, down_one, down_two,
-            d_final_low, d_pre, d_mid, d_mid_low, sums, bias_sums, total,
+            d_final_low, d_pre, d_mid_low, sums, bias_sums, total,
         ) = refs[1:] if has_extra else refs
         i = pl.program_id(0)
         gain = lambda at: norms[at : at + 1, :]
@@ -457,7 +431,6 @@
                 value = total[at, :]
                 normed = normed_one[at, :].astype(F32)
                 back = normalize_back(value, normed, recip_one[at, :], gain(0))
-                d_mid[at, :] = back
                 d_mid_low[at, :] = back.astype(LOW)
                 add_rows(sums, 0, value * normed, at)
                 add_rows(sums, 3, value, at)
@@ -472,8 +445,8 @@
             whole(kept["recip_two"]), whole(layer.norms), (kept["slope"],) + blocks,
         ] + layer.ffn(layer.up) + layer.ffn(layer.down),
         [
-            out_whole((n, depth), LOW), ((2, n, neurons), LOW) + blocks, out_whole((n, depth), F32),
-            out_whole((n, depth), LOW), out_whole((8, depth), F32), out_group((steps, 1, size), F32),
+            out_whole((n, depth), LOW), ((2, n, neurons), LOW) + blocks, out_whole((n, depth), LOW),
+            out_whole((8, depth), F32), out_group((steps, 1, size), F32),
         ],
         [pltpu.VMEM((n, depth), F32)],
         flops=8 * n * depth * neurons,
@@ -487,7 +460,7 @@
 
     def body(
         grad, extra, normed_two, recip_two, norms, slope, down_one, down_two,
-        d_final, d_final_low, d_pre, sums, bias_sums,
+        d_final_low, d_pre, sums, bias_sums,
     ):
         i = pl.program_id(0)
 
@@ -495,12 +468,11 @@
         def _():
             sums[...] = jnp.zeros_like(sums)
             for at in row_tiles(n):
-                value = grad[at, :]
+                value = grad[at, :].astype(F32)
                 if at.start >= 2 * half:
                     value = value + extra[at.start - 2 * half : at.stop - 2 * half, :].astype(F32)
                 normed = normed_two[at, :].astype(F32)
                 back = normalize_back(value, normed, recip_two[at, :], norms[1:2, :])
-                d_final[at, :] = back
                 d_final_low[at, :] = back.astype(LOW)
                 add_rows(sums, 1, value * normed, at)
                 add_rows(sums, 5, value, at)
@@ -525,7 +497,7 @@
             whole(layer.norms), (kept["slope"],) + blocks,
         ] + layer.ffn(layer.down),
         [
-            out_whole((n, depth), F32), out_whole((n, depth), LOW), ((2, n, neurons), LOW) + blocks,
+            out_whole((n, depth), LOW), ((2, n, neurons), LOW) + blocks,
             out_whole((8, depth), F32), out_group((steps, 1, size), F32),
         ],
         [],
@@ -533,30 +505,29 @@
     )
 
 
-def ffn_back_second_call(layer, d_final, d_pre, kept):
-    n, depth = d_final.shape
+def ffn_back_second_call(layer, d_final_low, d_pre, kept):
+    n, depth = d_final_low.shape
     steps, _, size = layer.bias_up.shape
     per = steps // 2
 
-    def body(d_final, d_pre, normed_one, recip_one, norms, up_one, up_two, d_mid, d_mid_low, sums):
+    def body(d_final, d_pre, normed_one, recip_one, norms, up_one, up_two, d_mid_low, sums, total):
         i = pl.program_id(0)
 
         @pl.when(i == 0)
         def _():
-            d_mid[...] = d_final[...]
+            total[...] = d_final[...].astype(F32)
 
         up = joined((up_one, up_two))
         for at in row_tiles(n):
-            d_mid[at, :] += dot(d_pre[0, at, :], up, 1, 1)
+            total[at, :] += dot(d_pre[0, at, :], up, 1, 1)
 
         @pl.when(i == steps - 1)
         def _():
             sums[...] = jnp.zeros_like(sums)
             for at in row_tiles(n):
-                value = d_mid[at, :]
+                value = total[at, :]
                 normed = normed_one[at, :].astype(F32)
                 back = normalize_back(value, normed, recip_one[at, :], norms[0:1, :])
-                d_mid[at, :] = back
                 d_mid_low[at, :] = back.astype(LOW)
                 add_rows(sums, 0, value * normed, at)
                 add_rows(sums, 3, value, at)
@@ -566,11 +537,11 @@
     return call(
         body, steps,
         [
-            whole(d_final), (d_pre,) + blocks, whole(kept["normed_one"]), whole(kept["recip_one"]),
+            whole(d_final_low), (d_pre,) + blocks, whole(kept["normed_one"]), whole(kept["recip_one"]),
             whole(layer.norms),
         ] + layer.ffn(layer.up),
-        [out_whole((n, depth), F32), out_whole((n, depth), LOW), out_whole((8, depth), F32)],
-        [],
+        [out_whole((n, depth), LOW), out_whole((8, depth), F32)],
+        [pltpu.VMEM((n, depth), F32)],
         flops=4 * n * depth * per * size,
     )
 
@@ -617,7 +588,7 @@
     )
 
 
-def own_back_call(layer, d_mid, d_mid_low, d_shared, kept, segs, half, with_rows):
+def own_back_call(layer, d_mid_low, d_shared, kept, segs, half, with_rows):
     n, depth = d_mid_low.shape
     width, wide, own = layer.width, 3 * layer.width, 2 * half
     count = 2 * len(layer.qkv_blocks) if with_rows else 0
@@ -626,7 +597,7 @@
         i = pl.program_id(0)
         if with_rows:
             d_mid, weights = refs[0], pairs_of(refs[1 : count + 1])
-            d_proj, sums, d_rows, mask = refs[count + 1 :]
+            d_proj, sums, d_rows, mask, total = refs[count + 1 :]
         else:
             d_proj, sums, mask = refs
         make_mask(segs_q, segs_k, mask)
@@ -641,11 +612,11 @@
 
             @pl.when(i == 0)
             def _():
-                d_rows[...] = d_mid[...] + part
+                total[...] = d_mid[...].astype(F32) + part
 
             @pl.when(i == 1)
             def _():
-                d_rows[...] += part
+                d_rows[...] = (total[...] + part).astype(LOW)
 
     return call(
         body, 2,
@@ -653,17 +624,17 @@
             (d_mid_low, (own, depth), lambda i: (0, 0)), per_group(d_shared),
             (kept["proj"], (1, own, wide), lambda i: (i, 0, 0)), per_group(kept["logsum_own"]),
         ] + layer.out() + [whole(segs[None, :]), whole(segs[:, None])]
-        + ([whole(d_mid)] + layer.qkv() if with_rows else []),
+        + ([whole(d_mid_low)] + layer.qkv() if with_rows else []),
         [out_group((2, n, wide), LOW), out_group((2, 8, wide), F32)]
-        + ([out_whole((n, depth), F32)] if with_rows else []),
-        [pltpu.VMEM((own, own), F32)],
+        + ([out_whole((n, depth), LOW)] if with_rows else []),
+        [pltpu.VMEM((own, own), F32)] + ([pltpu.VMEM((n, depth), F32)] if with_rows else []),
         flops=4 * depth * (n * wide * with_rows + own * width) + 20 * own * own * width,
         exps=2 * own * own * width // HEAD_DIM,
     )
 
 
-def rows_back_call(layer, d_mid, d_proj):
-    n, depth = d_mid.shape
+def rows_back_call(layer, d_mid_low, d_proj):
+    n, depth = d_mid_low.shape
     wide = 3 * layer.width
 
     def body(d_mid, d_proj, *refs):
@@ -671,12 +642,12 @@
 
         @pl.when(pl.program_id(0) == 0)
         def _():
-            d_rows[...] = d_mid[...]
+            d_rows[...] = d_mid[...].astype(F32)
 
         d_rows[...] += through_projection(d_proj[0], weights, layer.used)
 
     return call(
-        body, 2, [whole(d_mid), per_group(d_proj)] + layer.qkv(), [out_whole((n, depth), F32)], [],
+        body, 2, [whole(d_mid_low), per_group(d_proj)] + layer.qkv(), [out_whole((n, depth), F32)], [],
         flops=4 * depth * n * wide,
     )[0]
 
@@ -835,7 +806,7 @@
 
 
 def forward_attn(layer, rows, proj, context_own, logsum_own, rows_low, away_low, segs, half):
-    proj_away, context, logsum_shared, hidden, hidden_low, normed_one, recip_one = shared_call(
+    proj_away, context, logsum_shared, hidden_low, normed_one, recip_one = shared_call(
         layer, rows, proj, away_low, context_own, segs[1], half
     )
     kept = dict(
@@ -843,19 +814,19 @@
         logsum_own=logsum_own, logsum_shared=logsum_shared, hidden_low=hidden_low,
         normed_one=normed_one, recip_one=recip_one,
     )
-    return hidden, kept
-
-
-def forward_ffn(layer, hidden, kept):
-    act, slope, output, output_low, normed_two, recip_two = ffn_call(layer, hidden, kept["hidden_low"])
+    return hidden_low, kept
+
+
+def forward_ffn(layer, hidden_low, kept, wide):
+    act, slope, output, normed_two, recip_two = ffn_call(layer, hidden_low, wide)
     kept.update(act=act, slope=slope, normed_two=normed_two, recip_two=recip_two)
-    return output, output_low
+    return output
 
 
 def backward_ffn(layer, grad, extra, kept, half):
-    d_final_low, d_pre, d_mid, d_mid_low, sums, bias_sums = ffn_back_call(layer, grad, extra, kept, half)
+    d_final_low, d_pre, d_mid_low, sums, bias_sums = ffn_back_call(layer, grad, extra, kept, half)
     entries = [[(kept["hidden_low"], d_pre)], [(d_final_low, kept["act"])]]
-    return d_mid, d_mid_low, sums[:6], bias_sums, entries
+    return d_mid_low, sums[:6], bias_sums, entries
 
 
 def attn_entries(kept, d_proj, d_away, d_mid_low):
@@ -887,16 +858,23 @@
     t_cut, t_all = 2 * t_width, 4 * t_width + 128
     f_cut = per * size
     s_cut = size + 2 * s_width
-    packed_t, packed_f, student_a, student_b = pack(
-        [t_qkv, t_up, s_up, s_qkv], [t_out, norm_rows, t_down, s_out, s_down],
-        [(block, t_all), (block, 2 * f_cut), (block, s_cut), (block, s_cut)],
+    packed_t = moves(
+        [t_qkv, t_out.T, norm_rows.T], [(block, t_all)],
         [(0, (i,), 0, (every, columns(i * t_width, t_width))) for i in range(3)]
         + [
-            (4, (), 0, (every, columns(3 * t_width, t_width))), (5, (), 0, (every, columns(4 * t_width, 128))),
-            (1, (every,), 1, (every, columns(0, f_cut))), (6, (), 1, (every, columns(f_cut, f_cut))),
-            (2, (every,), 2, (every, columns(0, size))), (3, (0,), 2, (every, columns(size, s_width))),
-            (7, (), 2, (every, columns(size + s_width, s_width))), (8, (), 3, (every, columns(0, size))),
-            (3, (1,), 3, (every, columns(size, s_width))), (3, (2,), 3, (every, columns(size + s_width, s_width))),
+            (1, (every,), 0, (every, columns(3 * t_width, t_width))),
+            (2, (every,), 0, (every, columns(4 * t_width, 128))),
+        ],
+    )[0]
+    packed_f, student_a, student_b = moves(
+        [t_up, t_down.T, s_up, s_qkv, s_out.T, s_down.T],
+        [(block, 2 * f_cut), (block, s_cut), (block, s_cut)],
+        [
+            (0, (every,), 0, (every, columns(0, f_cut))), (1, (every,), 0, (every, columns(f_cut, f_cut))),
+            (2, (every,), 1, (every, columns(0, size))), (3, (0,), 1, (every, columns(size, s_width))),
+            (4, (every,), 1, (every, columns(size + s_width, s_width))),
+            (5, (every,), 2, (every, columns(0, size))), (3, (1,), 2, (every, columns(size, s_width))),
+            (3, (2,), 2, (every, columns(size + s_width, s_width))),
         ],
     )
 
@@ -1003,7 +981,7 @@
     got_a, got_b = swap_y(student_a), swap_x(student_b)
     hidden, ffn = together(hidden, ffn)
     teacher.up, teacher.down = (ffn, 0), (ffn, per)
-    middle, middle_low = forward_ffn(teacher, hidden, t_kept)
+    middle_low = forward_ffn(teacher, hidden, t_kept, False)
     away_low = swap_y(middle_low[2 * half :])
     middle_low, got_a, got_b, grad_in = together(middle_low, got_a, got_b, grad_in)
     grad_in = reorder(grad_in)
@@ -1022,9 +1000,9 @@
     proj, context_own, logsum_own = project_call(student, middle_low, segs[0], half)
     proj, away_low = together(proj, away_low)
     hidden, s_kept = forward_attn(
-        student, middle, proj, context_own, logsum_own, middle_low, away_low, segs, half
-    )
-    last, _ = forward_ffn(student, hidden, s_kept)
+        student, middle_low, proj, context_own, logsum_own, middle_low, away_low, segs, half
+    )
+    last = forward_ffn(student, hidden, s_kept, True)
 
     def far_half(value):
         return swap_y(value[half : 2 * half].astype(LOW))
@@ -1039,12 +1017,12 @@
 
     far_last = far_half(last)
 
-    d_mid, d_mid_low, s_norm_grads, s_up_grad, s_entries = backward_ffn(student, grad_in, None, s_kept, half)
+    d_mid_low, s_norm_grads, s_up_grad, s_entries = backward_ffn(student, grad_in, None, s_kept, half)
     d_shared, d_away, s_sums_b, back = shared_back_call(student, d_mid_low, s_kept, segs[1], half)
     extra = swap_y(back)
     d_shared, far_last = together(d_shared, far_last)
     d_proj, s_sums_a, d_rows = own_back_call(
-        student, d_mid, d_mid_low, d_shared, s_kept, segs[0], half, True
+        student, d_mid_low, d_shared, s_kept, segs[0], half, True
     )
     d_proj, extra = lax.optimization_barrier((d_proj, extra))
     s_entries += attn_entries(s_kept, d_proj, d_away, d_mid_low)
@@ -1052,7 +1030,7 @@
     reduce_s = Reduce(Grads(s_entries, s_columns, 3))
 
     d_rows = after(d_rows, reduce_s.sends)
-    d_final, d_final_low, d_pre, t_sums_two, t_up_grad = ffn_back_first_call(
+    d_final_low, d_pre, t_sums_two, t_up_grad = ffn_back_first_call(
         teacher, d_rows, extra, t_kept, half
     )
     d_pre = before(d_pre, reduce_s)
@@ -1061,7 +1039,7 @@
     f_entries = [[(t_kept["hidden_low"], d_pre)], [(d_final_low, t_kept["act"])]]
     reduce_f = Reduce(Grads(f_entries, [(0, 0, per * size), (1, 0, per * size)], 1))
     d_pre = after(d_pre, reduce_f.sends)
-    d_mid, d_mid_low, t_sums_one = ffn_back_second_call(teacher, d_final, d_pre, t_kept)
+    d_mid_low, t_sums_one = ffn_back_second_call(teacher, d_final_low, d_pre, t_kept)
     t_norm_grads = (t_sums_one + t_sums_two)[:6]
     d_mid_low = before(d_mid_low, reduce_f)
     reduce_f.step()
@@ -1074,7 +1052,7 @@
     d_shared = before(d_shared, reduce_s)
     reduce_s.step()
     d_shared = after(d_shared, reduce_s.sends)
-    d_proj, t_sums_a = own_back_call(teacher, None, d_mid_low, d_shared, t_kept, segs[0], half, False)
+    d_proj, t_sums_a = own_back_call(teacher, d_mid_low, d_shared, t_kept, segs[0], half, False)
     t_entries = attn_entries(t_kept, d_proj, d_away, d_mid_low)
     reduce_t = Reduce(
         Grads(t_entries, [(0, 0, 2 * t_width), (0, 2 * t_width, 3 * t_width), (1, 0, t_width)], 1)
@@ -1098,8 +1076,8 @@
     reduce_t.got = after(reduce_t.got, reduce_f.sends)
     reduce_t.step()
     reduce_f.got = after(reduce_f.got, reduce_t.sends)
-    round_of(reduce_f, reduce_s)
-    d_rows = rows_back_call(teacher, *after((d_mid, d_proj), reduce_t.sends))
+    round_of(reduce_f, reduce_s, small)
+    d_rows = rows_back_call(teacher, *after((d_mid_low, d_proj), reduce_t.sends))
     reduce_t.got = after(reduce_t.got, d_rows)
     far_rows = far_half(d_rows)
     round_of(reduce_t, small)
@@ -1108,10 +1086,10 @@
     input_grad, output = to_rows(d_rows, far_rows), to_rows(last, far_last)
     round_of(reduce_t, reduce_f, small)
     round_of(reduce_t, small)
-    for work in (reduce_t, reduce_f, reduce_s, small):
+    for work in (reduce_f, reduce_s, small):
         while work.got:
             work.step()
-    s_sum, f_sum, t_sum, small = reduce_s.total, reduce_f.total, reduce_t.total, small.total
+    s_sum, f_sum, small = reduce_s.total, reduce_f.total, small.total
 
     piece = width // lax.axis_size("dp")
     norm_sum = lax.dynamic_slice_in_dim(small[:12], lax.axis_index("dp") * piece, piece, 1)
@@ -1126,17 +1104,18 @@
             value = value[:, one:]
         return out
 
-    tq, tk, tv, to = cut(t_sum, t_width, t_width, t_width, t_width)
     t_up_sum, t_down_sum = cut(f_sum, per * size, per * size)
     s_up_sum, sq, so, s_down_sum, sk, sv = cut(s_sum, size, s_width, s_width, size, s_width, s_width)
-    return (
-        output, input_grad,
-        jnp.stack([tq, tk, tv]), t_qv_sum.reshape(2, -1), to.T, t_up_sum, bias_sum[:per].reshape(-1),
-        t_down_sum.T,
-        norm_sum[0:2], norm_sum[2:6],
-        jnp.stack([sq, sk, sv]), s_qv_sum.reshape(2, -1), so.T, s_up_sum, bias_sum[per], s_down_sum.T,
-        norm_sum[6:8], norm_sum[8:12],
-    )
+    done = (
+        output, input_grad, t_qv_sum.reshape(2, -1), t_up_sum, bias_sum[:per].reshape(-1), t_down_sum.T,
+        norm_sum[0:2], norm_sum[2:6], jnp.stack([sq, sk, sv]), s_qv_sum.reshape(2, -1), so.T, s_up_sum,
+        bias_sum[per], s_down_sum.T, norm_sum[6:8], norm_sum[8:12],
+    )
+    done, reduce_t.got = together(done, reduce_t.got)
+    while reduce_t.got:
+        reduce_t.step()
+    tq, tk, tv, to = cut(reduce_t.total, t_width, t_width, t_width, t_width)
+    return done[:2] + (jnp.stack([tq, tk, tv]), done[2], to.T) + done[3:]
 
 
 def solution(mesh):

time: 449 us -> 435 us (0.969)
  Pallas kernels: 222 us -> 207 us
  local copies, waits for them, and re-layouts: 42.7 us -> 35.5 us
  waiting for transfers between devices: 69.4 us -> 74.9 us
    pallas_call x20, Pallas kernels: 204 us -> 191 us  [call(): pl.pallas_call(body, grid=(steps,), in_specs=[pl.BlockSpec(block, index)...]
    ppermute x18, waiting for transfers between devices: 33.5 us -> 22.8 us  [ring_shift(): return lax.ppermute(value, 'dp', pairs)]
    ppermute x22, waiting for transfers between devices: 20.8 us -> 29.9 us  [swap_y(): return lax.ppermute(value, 'mp', [(0, 1), (1, 0)])]
    ppermute x18, starting transfers between devices: 29.4 us -> 38 us  [ring_shift(): return lax.ppermute(value, 'dp', pairs)]
    ppermute x4, waiting for transfers between devices: 4.06 us -> 11.3 us  [_run(): lax.ppermute(self.total, 'dp', [(i, i ^ step) for i in range(n)])]
    unnamed x184 -> x176, local copies, waits for them, and re-layouts: 27.4 us -> 20.8 us
    pallas_call x9 -> x11, Pallas kernels: 17 us -> 16.6 us  [moves(): pl.pallas_call(body, out_shape=[jax.ShapeDtypeStruct(shape, LOW) for shap...]
  transfers between devices with their start and end apart: 62 -> 62, of which waited for: 14 -> 19; matrix products, arithmetic and copies ran while one was open for 9% -> 9% of each run, Pallas kernels for 37% -> 36%
where the time goes in v2:
time: 435 us; the launch traced here: 430 us
  Pallas kernels  207 us (48%)
  starting transfers between devices  75.6 us (17%)
  waiting for transfers between devices  74.9 us (17%)
  local copies, waits for them, and re-layouts  35.5 us (8%)
  other arithmetic  21.3 us (5%)
  matrix products  13.2 us (3%)
    pallas_call x20, Pallas kernels, call(): pl.pallas_call(body, grid=(steps,), in_specs=[pl.BlockSpec(block, index)...  191 us
    ppermute x18, starting transfers between devices, ring_shift(): return lax.ppermute(value, 'dp', pairs)  38 us
    ppermute x22, waiting for transfers between devices, swap_y(): return lax.ppermute(value, 'mp', [(0, 1), (1, 0)])  29.9 us
    ppermute x22, starting transfers between devices, swap_y(): return lax.ppermute(value, 'mp', [(0, 1), (1, 0)])  23.5 us
    ppermute x18, waiting for transfers between devices, ring_shift(): return lax.ppermute(value, 'dp', pairs)  22.8 us
    unnamed x176, local copies, waits for them, and re-layouts  20.8 us
    pallas_call x11, Pallas kernels, moves(): pl.pallas_call(body, out_shape=[jax.ShapeDtypeStruct(shape, LOW) for shap...  16.6 us
    ppermute x12, starting transfers between devices, swap_x(): return lax.ppermute(value, 'dp', [(i, i ^ 2) for i in range(n)])  12.6 us
  transfers between devices with their start and end apart: 62, of which 19 were waited for; matrix products, arithmetic and copies ran while one was open for 9% of the time, Pallas kernels for 36%

profile of v2, /device:TPU:0, one launch (start us, length us, event | category | flops | bytes accessed | tf_op | source)
XLA Modules:
  0.0 430.1 jit_solution(3233345072186979461)
XLA Ops:
  3.2 4.1 collective-permute-start
  9.5 2.2 select_bitcast_fusion.6
  11.7 1.5 collective-permute-start.3
  14.0 3.1 collective-permute-done.1.refs_2_
  17.1 5.7 %collective-permute-done.2.refs_3_ = bf16[48,1664]{1,0:T(8,128)(2,1)S(1)} collective-permute-done((bf16[48,1664]{1,0:T(8,128)(2,1)S(1)}, bf16[48,1664]{1,0:T(8,128)(2,1)S(1)}, u32[]{:S(2)}, u32[]{:S(2)}) %collective-permute-start.2) | collective-permute-done | bytes 159776 | tf_op jit(solution)/shard_map/ppermute | solution.py:41
  22.8 1.6 collective-permute-start.5
  24.4 1.5 collective-permute-start.4
  25.9 1.5 collective-permute-start.8
  28.4 7.0 %collective-permute-done.6.refs_1_ = bf16[48,1152]{1,0:T(8,128)(2,1)S(1)} collective-permute-done((bf16[48,1152]{1,0:T(8,128)(2,1)S(1)}, bf16[48,1152]{1,0:T(8,128)(2,1)S(1)}, u32[]{:S(2)}, u32[]{:S(2)}) %collective-permute-start.6) | collective-permute-done | bytes 110624 | tf_op jit(solution)/shard_map/ppermute | solution.py:26
  35.5 1.6 collective-permute-start.10
  38.4 2.5 collective-permute-start.11
  40.9 3.3 convolution_convert_fusion.1.rows.refs_0_
  44.2 6.0 %collective-permute-done.11.refs_2_ = bf16[48,3072]{1,0:T(8,128)(2,1)S(1)} collective-permute-done((bf16[48,3072]{1,0:T(8,128)(2,1)S(1)}, bf16[48,3072]{1,0:T(8,128)(2,1)S(1)}, u32[]{:S(2)}, u32[]{:S(2)}) %collective-permute-start.11) | collective-permute-done | bytes 294944 | tf_op jit(solution)/shard_map/ppermute | solution.py:41
  50.1 6.7 %collective-permute-done.12.refs_3_ = bf16[48,3072]{1,0:T(8,128)(2,1)S(1)} collective-permute-done((bf16[48,3072]{1,0:T(8,128)(2,1)S(1)}, bf16[48,3072]{1,0:T(8,128)(2,1)S(1)}, u32[]{:S(2)}, u32[]{:S(2)}) %collective-permute-start.12) | collective-permute-done | bytes 294944 | tf_op jit(solution)/shard_map/ppermute | solution.py:41
  65.1 10.5 %collective-permute-done.16 = bf16[3456]{0:T(1024)(128)(2,1)} collective-permute-done((bf16[3456]{0:T(1024)(128)(2,1)}, bf16[3456]{0:T(1024)(128)(2,1)}, u32[]{:S(2)}, u32[]{:S(2)}) %collective-permute-start.16) | collective-permute-done | bytes 6944 | tf_op jit(solution)/shard_map/ppermute | solution.py:21
  77.7 3.1 shard_map.328
  87.0 12.9 %shard_map.329 = (bf16[2,768,1152]{2,1,0:T(8,128)(2,1)}, bf16[2,512,384]{2,1,0:T(8,128)(2,1)S(1)}, f32[2,8,512]{2,1,0:T(8,128)S(1)}) custom-call(bf16[768,768]{1,0:T(8,128)(2,1)S(1)} %copy-done.7, bf16[2,384,1664]{2,1,0:T(8,128)(2,1)S(1)} %bitcast.122, bf16[2,384,1664]{2,1,0:T(8,128)(2,1)} %collective-permute-done.13.refs_1_.refs_3_.refs_5_.refs_7_.out_two, ...), custom_call_target="tpu_custom_call" | custom-call | flops 1761607680 | bytes 10443264 | tf_op jit(solution)/shard_map/pallas_call | solution.py:80
  100.5 1.5 convolution_convert_fusion.2.away.refs_2_
  101.9 12.6 %shard_map.331 = (bf16[2,256,1152]{2,1,0:T(8,128)(2,1)S(1)}, bf16[2,768,384]{2,1,0:T(8,128)(2,1)S(1)}, f32[2,8,256]{2,1,0:T(8,128)S(1)}, bf16[768,768]{1,0:T(8,1...) custom-call(bf16[768,768]{1,0:T(8,128)(2,1)} %convolution_convert_fusion.1.rows.refs_0_, ...), custom_call_target="tpu_custom_call" | custom-call | flops 1107296256 | bytes 15560192 | tf_op jit(solution)/shard_map/pallas_call | solution.py:80
  117.4 4.9 %shard_map.332 = bf16[2,2,4,48,3072]{4,3,2,1,0:T(8,128)(2,1)} custom-call(bf16[2,4,48,1536]{3,2,1,0:T(8,128)(2,1)} %get-tuple-element.263.refs_0_, bf16[2,4,48,1536]{3,2,1,0:T(8,128)(2,1)} %collective-permute-done.20.refs_1_, bf16[2,4,48,1536]{3,2,1,0:T(8,128)(2,1)} %get-tuple-element.265.refs_2_, bf16[2,4,48,1536]{3,2,1,0:T(8,128)(2,1)} %collective-permute-done.21.refs_3_), custom_call_target="tpu_custom_call" | custom-call | bytes 4718592 | tf_op jit(solution)/shard_map/pallas_call | solution.py:102
  123.6 2.3 shard_map.334
  127.6 6.8 %collective-permute-done.26 = bf16[256,768]{1,0:T(8,128)(2,1)S(1)} collective-permute-done((bf16[256,768]{1,0:T(8,128)(2,1)S(1)}, bf16[256,768]{1,0:T(8,128)(2,1)S(1)}, u32[]{:S(2)}, u32[]{:S(2)}) %collective-permute-start.26) | collective-permute-done | bytes 393248 | tf_op jit(solution)/shard_map/ppermute | solution.py:21
  135.6 14.3 %shard_map.333 = (bf16[2,768,1536]{2,1,0:T(8,128)(2,1)}, bf16[2,768,1536]{2,1,0:T(8,128)(2,1)}, bf16[768,768]{1,0:T(8,128)(2,1)S(1)}, bf16[768,768]{1,0:T(8,128)(2,1)S(1)}, f32[768,1]{1,0:T(8,128)S(1)}) custom-call(bf16[768,768]{1,0:T(8,128)(2,1)S(1)} %get-tuple-element.267.hidden_low.refs_0_, f32[8,768]{1,0:T(8,128)S(1)} %slice_select_fusion.1.refs_12_.norms, ...), custom_call_target="tpu_custom_call" | custom-call | flops 3623878656 | bytes 15945216 | tf_op jit(solution)/shard_map/pallas_call | solution.py:80
  150.9 2.1 collective-permute-done.24.refs_1_
  153.1 3.9 shard_map.335
  158.5 2.1 convolution_convert_fusion.grad
  160.6 3.0 collective-permute-done.27.refs_1_.refs_3_.refs_5_.up_two.down_two.refs_7_.refs_9_.out_two.refs_2_.refs_4_
  163.5 7.2 %shard_map.336 = (bf16[2,768,576]{2,1,0:T(8,128)(2,1)S(1)}, bf16[2,512,192]{2,1,0:T(8,128)(2,1)S(1)}, f32[2,8,512]{2,1,0:T(8,128)S(1)}) custom-call(bf16[768,768]{1,0:T(8,128)(2,1)S(1)} %get-tuple-element.277.rows.refs_4_, bf16[2,384,2304]{2,1,0:T(8,128)(2,1)} %bitcast.152, ...), custom_call_target="tpu_custom_call" | custom-call | flops 880803840 | bytes 8769792 | tf_op jit(solution)/shard_map/pallas_call | solution.py:80
  172.1 8.0 %shard_map.337 = (bf16[2,256,576]{2,1,0:T(8,128)(2,1)S(1)}, bf16[2,768,192]{2,1,0:T(8,128)(2,1)S(1)}, f32[2,8,256]{2,1,0:T(8,128)S(1)}, bf16[768,768]{1,0:T(8,12...) custom-call(bf16[768,768]{1,0:T(8,128)(2,1)} %copy-done.5, bf16[2,768,576]{2,1,0:T(8,128)(2,1)} %copy-done.10, ...), custom_call_target="tpu_custom_call" | custom-call | flops 553648128 | bytes 14279936 | tf_op jit(solution)/shard_map/pallas_call | solution.py:80
  181.0 10.1 %shard_map.338 = (bf16[2,768,768]{2,1,0:T(8,128)(2,1)S(1)}, bf16[2,768,768]{2,1,0:T(8,128)(2,1)}, f32[768,768]{1,0:T(8,128)}, bf16[768,768]{1,0:T(8,128)(2,1)S(1)}, f32[768,1]{1,0:T(8,128)S(1)}) custom-call(bf16[768,768]{1,0:T(8,128)(2,1)S(1)} %get-tuple-element.286.hidden_low.refs_0_, f32[8,768]{1,0:T(8,128)S(1)} %pad.17.refs_10_.norms.refs_4_, ...), custom_call_target="tpu_custom_call" | custom-call | flops 1811939328 | bytes 11813376 | tf_op jit(solution)/shard_map/pallas_call | solution.py:80
  197.2 11.1 %shard_map.339 = (bf16[768,768]{1,0:T(8,128)(2,1)S(1)}, bf16[2,768,768]{2,1,0:T(8,128)(2,1)}, bf16[768,768]{1,0:T(8,128)(2,1)S(1)}, f32[8,768]{1,0:T(8,128)S(1)}, f32[2,1,768]{2,1,0:T(1,128)S(1)}) custom-call(bf16[768,768]{1,0:T(8,128)(2,1)S(1)} %copy-done.24, bf16[768,768]{1,0:T(8,128)(2,1)S(1)} %copy-done.26, f32[768,1]{1,0:T(8,128)S(1)} %get-tuple-element.285.refs_1_, ...), custom_call_target="tpu_custom_call" | custom-call | flops 1811939328 | bytes 12417024 | tf_op jit(solution)/shard_map/pallas_call | solution.py:80
  208.3 7.3 %shard_map.340 = (bf16[2,256,576]{2,1,0:T(8,128)(2,1)S(1)}, bf16[2,256,576]{2,1,0:T(8,128)(2,1)S(1)}, f32[2,8,576]{2,1,0:T(8,128)S(1)}, bf16[256,768]{1,0:T(8,128)(2,1)S(1)}) custom-call(bf16[768,768]{1,0:T(8,128)(2,1)S(1)} %get-tuple-element.290.d_mid.d_mid_low.refs_0_.refs_8_, bf16[2,768,576]{2,1,0:T(8,128)(2,1)S(1)} %copy-done.11, ...), custom_call_target="tpu_custom_call" | custom-call | flops 553648128 | bytes 13200896 | tf_op jit(solution)/shard_map/pallas_call | solution.py:80
  217.3 10.8 %shard_map.341 = (bf16[2,768,576]{2,1,0:T(8,128)(2,1)S(1)}, f32[2,8,576]{2,1,0:T(8,128)S(1)}, bf16[768,768]{1,0:T(8,128)(2,1)S(1)}) custom-call(bf16[768,768]{1,0:T(8,128)(2,1)S(1)} %get-tuple-element.290.d_mid.d_mid_low.refs_0_.refs_8_, bf16[2,256,576]{2,1,0:T(8,128)(2,1)S(1)} %get-tuple-element.295.d_shared, bf16[2,768,576]{2,1,0:T(8,128)(2,1)} %copy-done.10, ...), custom_call_target="tpu_custom_call" | custom-call | flops 1333788672 | bytes 14487552 | tf_op jit(solution)/shard_map/pallas_call | solution.py:80
  229.4 7.2 %shard_map.342 = bf16[2,384,2304]{2,1,0:T(8,128)(2,1)} custom-call(bf16[768,768]{1,0:T(8,128)(2,1)S(1)} %get-tuple-element.286.hidden_low.refs_0_, bf16[2,768,768]{2,1,0:T(8,128)(2,1)} %get-tuple-element.298.refs_1_, bf16[768,768]{1,0:T(8,128)(2,1)S(1)} %get-tuple-element.299.refs_2_, bf16[2,768,768]{2,1,0:T(8,128)(2,1)} %copy-done.12, ...), custom_call_target="tpu_custom_call" | custom-call | flops 1472200704 | bytes 8159232 | tf_op jit(solution)/shard_map/pallas_call | solution.py:80
  236.7 10.1 %shard_map.343 = (bf16[768,768]{1,0:T(8,128)(2,1)S(1)}, bf16[2,768,1536]{2,1,0:T(8,128)(2,1)}, f32[8,768]{1,0:T(8,128)S(1)}, f32[4,1,768]{2,1,0:T(1,128)S(1)}) custom-call(bf16[768,768]{1,0:T(8,128)(2,1)S(1)} %get-tuple-element.306.grad, bf16[256,768]{1,0:T(8,128)(2,1)S(1)} %collective-permute-done.30.extra, bf16[768,768]{1,0:T(8,128)(2,1)S(1)} %copy-done.23, ...), custom_call_target="tpu_custom_call" | custom-call | flops 1811939328 | bytes 11435520 | tf_op jit(solution)/shard_map/pallas_call | solution.py:80
  246.8 10.3 %shard_map.344 = (bf16[384,1152]{1,0:T(8,128)(2,1)S(1)}, f32[384,1152]{1,0:T(8,128)}, bf16[2,192,1152]{2,1,0:T(8,128)(2,1)S(1)}, f32[2,192,1152]{2,1,0:T(8,128)}) custom-call(bf16[2,384,2304]{2,1,0:T(8,128)(2,1)} %collective-permute-done.31.got, bf16[768,768]{1,0:T(8,128)(2,1)S(1)} %get-tuple-element.286.hidden_low.refs_0_, ...), custom_call_target="tpu_custom_call" | custom-call | flops 1472200704 | bytes 10813440 | tf_op jit(solution)/shard_map/pallas_call | solution.py:80
  257.1 8.3 %shard_map.345 = bf16[2,384,3072]{2,1,0:T(8,128)(2,1)} custom-call(bf16[768,768]{1,0:T(8,128)(2,1)S(1)} %get-tuple-element.267.hidden_low.refs_0_, bf16[2,768,1536]{2,1,0:T(8,128)(2,1)} %get-tuple-element.319.refs_1_.d_pre, bf16[768,768]{1,0:T(8,128)(2,1)S(1)} %get-tuple-element.311.refs_2_.d_final, bf16[2,768,1536]{2,1,0:T(8,128)(2,1)} %get-tuple-element.318.refs_3_), custom_call_target="tpu_custom_call" | custom-call | flops 1811939328 | bytes 8257536 | tf_op jit(solution)/shard_map/pallas_call | solution.py:80
  267.9 8.4 %shard_map.346 = (bf16[768,768]{1,0:T(8,128)(2,1)S(1)}, f32[8,768]{1,0:T(8,128)S(1)}) custom-call(bf16[768,768]{1,0:T(8,128)(2,1)S(1)} %get-tuple-element.311.refs_2_.d_final, bf16[2,768,1536]{2,1,0:T(8,128)(2,1)} %get-tuple-element.319.refs_1_.d_pre, bf16[768,768]{1,0:T(8,128)(2,1)S(1)} %copy-done.21, f32[768,1]{1,0:T(8,128)S(1)} %copy-done.31, ...), custom_call_target="tpu_custom_call" | custom-call | flops 1811939328 | bytes 8873472 | tf_op jit(solution)/shard_map/pallas_call | solution.py:80
  276.3 9.5 %shard_map.347 = (bf16[384,1536]{1,0:T(8,128)(2,1)}, f32[384,1536]{1,0:T(8,128)}, bf16[2,192,1536]{2,1,0:T(8,128)(2,1)}, f32[2,192,1536]{2,1,0:T(8,128)}) custom-call(bf16[2,384,3072]{2,1,0:T(8,128)(2,1)} %collective-permute-done.32.got, bf16[768,768]{1,0:T(8,128)(2,1)S(1)} %get-tuple-element.267.hidden_low.refs_0_, ...), custom_call_target="tpu_custom_call" | custom-call | flops 1811939328 | bytes 11796480 | tf_op jit(solution)/shard_map/pallas_call | solution.py:80
  285.8 1.9 collective-permute-done.33
  289.4 1.5 convert_add_fusion.2
  295.1 1.5 collective-permute-start.39
  296.6 10.9 %shard_map.348 = (bf16[2,256,1152]{2,1,0:T(8,128)(2,1)S(1)}, bf16[2,256,1152]{2,1,0:T(8,128)(2,1)S(1)}, f32[2,8,1152]{2,1,0:T(8,128)S(1)}, bf16[256,768]{1,0:T(8,128)(2,1)S(1)}) custom-call(bf16[768,768]{1,0:T(8,128)(2,1)S(1)} %get-tuple-element.364.d_mid.d_mid_low.refs_4_, bf16[2,768,1152]{2,1,0:T(8,128)(2,1)} %get-tuple-element.257.proj, ...), custom_call_target="tpu_custom_call" | custom-call | flops 1107296256 | bytes 14595584 | tf_op jit(solution)/shard_map/pallas_call | solution.py:80
  310.6 13.2 %shard_map.349 = (bf16[2,768,1152]{2,1,0:T(8,128)(2,1)}, f32[2,8,1152]{2,1,0:T(8,128)S(1)}) custom-call(bf16[768,768]{1,0:T(8,128)(2,1)S(1)} %get-tuple-element.364.d_mid.d_mid_low.refs_4_, bf16[2,256,1152]{2,1,0:T(8,128)(2,1)S(1)} %get-tuple-element.341.d_shared, bf16[2,768,1152]{2,1,0:T(8,128)(2,1)} %get-tuple-element.257.proj, ...), custom_call_target="tpu_custom_call" | custom-call | flops 1308622848 | bytes 7329792 | tf_op jit(solution)/shard_map/pallas_call | solution.py:80
  323.8 5.6 %shard_map.350 = bf16[2,384,1536]{2,1,0:T(8,128)(2,1)} custom-call(bf16[768,768]{1,0:T(8,128)(2,1)S(1)} %copy-done.8, bf16[2,768,1152]{2,1,0:T(8,128)(2,1)} %get-tuple-element.365.refs_1_.d_proj, bf16[256,768]{1,0:T(8,128)(2,1)S(1)} %convolution_convert_fusion.2.away.refs_2_, bf16[2,256,1152]{2,1,0:T(8,128)(2,1)S(1)} %get-tuple-element.344.refs_3_, ...), custom_call_target="tpu_custom_call" | custom-call | flops 1132462080 | bytes 5505024 | tf_op jit(solution)/shard_map/pallas_call | solution.py:80
  330.5 3.8 collective-permute-done.40
  334.3 2.5 convert_add_fusion
  337.7 1.6 convert_add_fusion.1
  342.9 5.1 %collective-permute-start.45 = (bf16[48,2304]{1,0:T(8,128)(2,1)S(1)}, bf16[48,2304]{1,0:T(8,128)(2,1)S(1)}, u32[]{:S(2)}, u32[]{:S(2)}) collective-permute-start(bf16[48,2304]{1,0:T(8,128)(2,1)S(1)} %copy-done.77), channel_id=1, source_target_pairs={{0,8},{2,10},{4,12},{6,14},{16,0},{18,2},{20,4},{22,6},{24,16},{26... | collective-permute-start | bytes 663560 | tf_op jit(solution)/shard_map/ppermute | solution.py:41
  348.0 2.5 collective-permute-start.46
  351.8 6.7 %shard_map.351 = (bf16[384,768]{1,0:T(8,128)(2,1)S(1)}, f32[384,768]{1,0:T(8,128)S(1)}, bf16[2,192,768]{2,1,0:T(8,128)(2,1)S(1)}, f32[2,192,768]{2,1,0:T(8,128)S(1)}) custom-call(bf16[2,384,1536]{2,1,0:T(8,128)(2,1)} %collective-permute-done.37.got, bf16[768,768]{1,0:T(8,128)(2,1)S(1)} %copy-done.9, bf16[2,768,1152]{2,1,0:T(8,128)(2,1)} %get-tuple-element.365.refs_1_.d_proj, ...), custom_call_target="tpu_custom_call" | custom-call | flops 1132462080 | bytes 7274496 | tf_op jit(solution)/shard_map/pallas_call | solution.py:80
  361.6 1.5 collective-permute-start.42
  364.2 1.6 fusion.6
  366.9 6.8 %collective-permute-start.54 = (bf16[48,3072]{1,0:T(8,128)(2,1)}, bf16[48,3072]{1,0:T(8,128)(2,1)}, u32[]{:S(2)}, u32[]{:S(2)}) collective-permute-start(bf16[48,3072]{1,0:T(8,128)(2,1)} %get-tuple-element.430), channel_id=1, source_target_pairs={{0,8},{2,10},{4,12},{6,14},{16,0},{18,2},{20,4},{22,6},{24,16},{26... | collective-permute-start | bytes 884744 | tf_op jit(solution)/shard_map/ppermute | solution.py:41
  374.4 6.1 %shard_map.352 = f32[768,768]{1,0:T(8,128)S(1)} custom-call(bf16[768,768]{1,0:T(8,128)(2,1)S(1)} %copy-done.3, bf16[2,768,1152]{2,1,0:T(8,128)(2,1)} %get-tuple-element.365.refs_1_.d_proj, bf16[2,384,1664]{2,1,0:T(8,128)(2,1)S(1)} %bitcast.134, bf16[2,384,1664]{2,1,0:T(8,128)(2,1)} %collective-permute-done.13.refs_1_.refs_3_.refs_5_.refs_7_.out_two, ...), custom_call_target="tpu_custom_call" | custom-call | flops 1358954496 | bytes 11206656 | tf_op jit(solution)/shard_map/pallas_call | solution.py:80
  382.9 2.5 collective-permute-start.55
  385.4 4.0 collective-permute-start.56
  398.2 3.3 collective-permute-done.51
  403.4 1.6 pad_maximum_fusion.2
  405.0 1.6 pad_maximum_fusion.1
  406.6 4.3 %collective-permute-done.57 = f32[22,768]{1,0:T(8,128)S(1)} collective-permute-done((f32[22,768]{1,0:T(8,128)S(1)}, f32[22,768]{1,0:T(8,128)S(1)}, u32[]{:S(2)}, u32[]{:S(2)}) %collective-permute-start.57) | collective-permute-done | bytes 67616 | tf_op jit(solution)/shard_map/ppermute | solution.py:783
  411.2 2.3 collective-permute-start.59
  413.5 1.9 collective-permute-start.60
  417.6 7.0 %collective-permute-done.61 = f32[22,768]{1,0:T(8,128)S(1)} collective-permute-done((f32[22,768]{1,0:T(8,128)S(1)}, f32[22,768]{1,0:T(8,128)S(1)}, u32[]{:S(2)}, u32[]{:S(2)}) %collective-permute-start.61) | collective-permute-done | bytes 67616 | tf_op jit(solution)/shard_map/ppermute | solution.py:783
  (391 shorter events, 90.2 us)
Async XLA Ops:
  3.2 10.8 %collective-permute-start = (bf16[48,1664]{1,0:T(8,128)(2,1)S(1)}, bf16[48,1664]{1,0:T(8,128)(2,1)S(1)}, u32[]{:S(2)}, u32[]{:S(2)}) collective-permute-start(bf16[48,1664]{1,0:T(8,128)(2,1)S(1)} %shard_map.322.refs_0_), channel_id=1, source_target_pairs={{0,16},{2,18},{4,20},{6,22},{16,24},{18,26},{20,28},{22,30},{24,8}... | collective-permute-start | bytes 479240 | tf_op jit(solution)/shard_map/ppermute | solution.py:41
  7.3 9.8 %collective-permute-start.1 = (bf16[48,1664]{1,0:T(8,128)(2,1)S(1)}, bf16[48,1664]{1,0:T(8,128)(2,1)S(1)}, u32[]{:S(2)}, u32[]{:S(2)}) collective-permute-start(bf16[48,1664]{1,0:T(8,128)(2,1)S(1)} %shard_map.322.refs_0_), channel_id=1, source_target_pairs={{0,24},{2,26},{4,28},{6,30},{16,8},{18,10},{20,12},{22,14},{24,0},... | collective-permute-start | bytes 479240 | tf_op jit(solution)/shard_map/ppermute | solution.py:41
  8.6 14.1 %collective-permute-start.2 = (bf16[48,1664]{1,0:T(8,128)(2,1)S(1)}, bf16[48,1664]{1,0:T(8,128)(2,1)S(1)}, u32[]{:S(2)}, u32[]{:S(2)}) collective-permute-start(bf16[48,1664]{1,0:T(8,128)(2,1)S(1)} %shard_map.322.refs_0_), channel_id=1, source_target_pairs={{0,8},{2,10},{4,12},{6,14},{16,0},{18,2},{20,4},{22,6},{24,16},{26... | collective-permute-start | bytes 479240 | tf_op jit(solution)/shard_map/ppermute | solution.py:41
  11.7 11.0 %collective-permute-start.3 = (bf16[256,768]{1,0:T(8,128)(2,1)}, bf16[256,768]{1,0:T(8,128)(2,1)}, u32[]{:S(2)}, u32[]{:S(2)}) collective-permute-start(bf16[256,768]{1,0:T(8,128)(2,1)} %get-tuple-element.436), channel_id=1, source_target_pairs={{0,1},{1,0},{2,3},{3,2},{4,5},{5,4},{6,7},{7,6},{8,9},{9,8},{10,11... | collective-permute-start | bytes 1179656 | tf_op jit(solution)/shard_map/ppermute | solution.py:21
  14.0 49.5 %copy-start.80 = (s32[512]{0:T(512)}, s32[512]{0:T(512)S(1)}, u32[]{:S(2)}) copy-start(s32[512]{0:T(512)S(1)} %add_select_fusion.7) | copy-start | bytes 6148
  22.8 12.6 %collective-permute-start.5 = (bf16[4,48,896]{2,1,0:T(8,128)(2,1)S(1)}, bf16[4,48,896]{2,1,0:T(8,128)(2,1)S(1)}, u32[]{:S(2)}, u32[]{:S(2)}) collective-permute-start(bf16[4,48,896]{2,1,0:T(8,128)(2,1)S(1)} %get-tuple-element.223.refs_2_), channel_id=1, source_target_pairs={{0,1},{1,0},{2,3},{3,2},{4,5},{5,4},{6,7},{7,6},{8,9},{9,8},{10,11... | collective-permute-start | bytes 1032200 | tf_op jit(solution)/shard_map/ppermute | solution.py:21
  24.4 11.0 %collective-permute-start.4 = (bf16[4,48,768]{2,1,0:T(8,128)(2,1)S(1)}, bf16[4,48,768]{2,1,0:T(8,128)(2,1)S(1)}, u32[]{:S(2)}, u32[]{:S(2)}) collective-permute-start(bf16[4,48,768]{2,1,0:T(8,128)(2,1)S(1)} %get-tuple-element.222.refs_0_), channel_id=1, source_target_pairs={{0,4},{2,6},{4,0},{6,2},{8,12},{10,14},{12,8},{14,10},{16,20},{18,... | collective-permute-start | bytes 884744 | tf_op jit(solution)/shard_map/ppermute | solution.py:26
  25.9 9.5 %collective-permute-start.8 = (bf16[48,3072]{1,0:T(8,128)(2,1)S(1)}, bf16[48,3072]{1,0:T(8,128)(2,1)S(1)}, u32[]{:S(2)}, u32[]{:S(2)}) collective-permute-start(bf16[48,3072]{1,0:T(8,128)(2,1)S(1)} %get-tuple-element.239.refs_0_), channel_id=1, source_target_pairs={{0,16},{2,18},{4,20},{6,22},{16,24},{18,26},{20,28},{22,30},{24,8}... | collective-permute-start | bytes 884744 | tf_op jit(solution)/shard_map/ppermute | solution.py:41
  27.3 8.1 %collective-permute-start.6 = (bf16[48,1152]{1,0:T(8,128)(2,1)S(1)}, bf16[48,1152]{1,0:T(8,128)(2,1)S(1)}, u32[]{:S(2)}, u32[]{:S(2)}) collective-permute-start(bf16[48,1152]{1,0:T(8,128)(2,1)S(1)} %get-tuple-element.224.refs_0_), channel_id=1, source_target_pairs={{0,4},{2,6},{4,0},{6,2},{8,12},{10,14},{12,8},{14,10},{16,20},{18,... | collective-permute-start | bytes 331784 | tf_op jit(solution)/shard_map/ppermute | solution.py:26
  27.9 7.5 %collective-permute-start.7 = (bf16[48,1152]{1,0:T(8,128)(2,1)S(1)}, bf16[48,1152]{1,0:T(8,128)(2,1)S(1)}, u32[]{:S(2)}, u32[]{:S(2)}) collective-permute-start(bf16[48,1152]{1,0:T(8,128)(2,1)S(1)} %get-tuple-element.225.refs_2_), channel_id=1, source_target_pairs={{0,1},{1,0},{2,3},{3,2},{4,5},{5,4},{6,7},{7,6},{8,9},{9,8},{10,11... | collective-permute-start | bytes 331784 | tf_op jit(solution)/shard_map/ppermute | solution.py:21
  35.5 21.3 %collective-permute-start.10 = (bf16[2,4,48,896]{3,2,1,0:T(8,128)(2,1)S(1)}, bf16[2,4,48,896]{3,2,1,0:T(8,128)(2,1)S(1)}, u32[]{:S(2)}, u32[]{:S(2)}) collective-permute-start(bf16[2,4,48,896]{3,2,1,0:T(8,128)(2,1)S(1)} %get-tuple-element.230.refs_2_), channel_id=1, source_target_pairs={{0,4},{2,6},{4,0},{6,2},{8,12},{10,14},{12,8},{14,10},{16,20},{18,... | collective-permute-start | bytes 2064392 | tf_op jit(solution)/shard_map/ppermute | solution.py:26
  37.1 19.8 %collective-permute-start.9 = (bf16[2,4,48,768]{3,2,1,0:T(8,128)(2,1)S(1)}, bf16[2,4,48,768]{3,2,1,0:T(8,128)(2,1)S(1)}, u32[]{:S(2)}, u32[]{:S(2)}) collective-permute-start(bf16[2,4,48,768]{3,2,1,0:T(8,128)(2,1)S(1)} %get-tuple-element.229.refs_0_), channel_id=1, source_target_pairs={{0,1},{1,0},{2,3},{3,2},{4,5},{5,4},{6,7},{7,6},{8,9},{9,8},{10,11... | collective-permute-start | bytes 1769480 | tf_op jit(solution)/shard_map/ppermute | solution.py:21
  38.4 11.7 %collective-permute-start.11 = (bf16[48,3072]{1,0:T(8,128)(2,1)S(1)}, bf16[48,3072]{1,0:T(8,128)(2,1)S(1)}, u32[]{:S(2)}, u32[]{:S(2)}) collective-permute-start(bf16[48,3072]{1,0:T(8,128)(2,1)S(1)} %get-tuple-element.239.refs_0_), channel_id=1, source_target_pairs={{0,24},{2,26},{4,28},{6,30},{16,8},{18,10},{20,12},{22,14},{24,0},... | collective-permute-start | bytes 884744 | tf_op jit(solution)/shard_map/ppermute | solution.py:41
  40.9 16.0 %collective-permute-start.12 = (bf16[48,3072]{1,0:T(8,128)(2,1)S(1)}, bf16[48,3072]{1,0:T(8,128)(2,1)S(1)}, u32[]{:S(2)}, u32[]{:S(2)}) collective-permute-start(bf16[48,3072]{1,0:T(8,128)(2,1)S(1)} %get-tuple-element.239.refs_0_), channel_id=1, source_target_pairs={{0,8},{2,10},{4,12},{6,14},{16,0},{18,2},{20,4},{22,6},{24,16},{26... | collective-permute-start | bytes 884744 | tf_op jit(solution)/shard_map/ppermute | solution.py:41
  57.1 19.9 %collective-permute-start.13 = (bf16[2,384,1664]{2,1,0:T(8,128)(2,1)S(1)}, bf16[2,384,1664]{2,1,0:T(8,128)(2,1)}, u32[]{:S(2)}, u32[]{:S(2)}) collective-permute-start(bf16[2,384,1664]{2,1,0:T(8,128)(2,1)S(1)} %bitcast.120), channel_id=1, source_target_pairs={{0,2},{2,0},{4,6},{6,4},{8,10},{10,8},{12,14},{14,12},{16,18},{18,... | collective-permute-start | bytes 7667720 | tf_op jit(solution)/shard_map/ppermute | solution.py:31
  58.4 17.2 %collective-permute-start.14 = (bf16[4,48,1536]{2,1,0:T(8,128)(2,1)}, bf16[4,48,1536]{2,1,0:T(8,128)(2,1)}, u32[]{:S(2)}, u32[]{:S(2)}) collective-permute-start(bf16[4,48,1536]{2,1,0:T(8,128)(2,1)} %get-tuple-element.243.refs_0_), channel_id=1, source_target_pairs={{0,4},{2,6},{4,0},{6,2},{8,12},{10,14},{12,8},{14,10},{16,20},{18,... | collective-permute-start | bytes 1769480 | tf_op jit(solution)/shard_map/ppermute | solution.py:26
  58.9 18.0 %collective-permute-start.15 = (bf16[4,48,1536]{2,1,0:T(8,128)(2,1)}, bf16[4,48,1536]{2,1,0:T(8,128)(2,1)}, u32[]{:S(2)}, u32[]{:S(2)}) collective-permute-start(bf16[4,48,1536]{2,1,0:T(8,128)(2,1)} %get-tuple-element.244.refs_2_), channel_id=1, source_target_pairs={{0,1},{1,0},{2,3},{3,2},{4,5},{5,4},{6,7},{7,6},{8,9},{9,8},{10,11... | collective-permute-start | bytes 1769480 | tf_op jit(solution)/shard_map/ppermute | solution.py:21
  60.5 15.1 %collective-permute-start.16 = (bf16[3456]{0:T(1024)(128)(2,1)}, bf16[3456]{0:T(1024)(128)(2,1)}, u32[]{:S(2)}, u32[]{:S(2)}) collective-permute-start(bf16[3456]{0:T(1024)(128)(2,1)} %concatenate.65), channel_id=1, source_target_pairs={{0,1},{1,0},{2,3},{3,2},{4,5},{5,4},{6,7},{7,6},{8,9},{9,8},{10,11... | collective-permute-start | bytes 20744 | tf_op jit(solution)/shard_map/ppermute | solution.py:21
  61.7 22.7 %collective-permute-start.17 = (bf16[256,768]{1,0:T(8,128)(2,1)}, bf16[256,768]{1,0:T(8,128)(2,1)}, u32[]{:S(2)}, u32[]{:S(2)}) collective-permute-start(bf16[256,768]{1,0:T(8,128)(2,1)} %get-tuple-element.435), channel_id=1, source_target_pairs={{0,1},{1,0},{2,3},{3,2},{4,5},{5,4},{6,7},{7,6},{8,9},{9,8},{10,11... | collective-permute-start | bytes 1179656 | tf_op jit(solution)/shard_map/ppermute | solution.py:21
  75.6 24.9 %collective-permute-start.18 = (bf16[2,48,2304]{2,1,0:T(8,128)(2,1)}, bf16[2,48,2304]{2,1,0:T(8,128)(2,1)}, u32[]{:S(2)}, u32[]{:S(2)}) collective-permute-start(bf16[2,48,2304]{2,1,0:T(8,128)(2,1)} %shard_map.330.refs_0_), channel_id=1, source_target_pairs={{0,16},{2,18},{4,20},{6,22},{16,24},{18,26},{20,28},{22,30},{24,8}... | collective-permute-start | bytes 1327112 | tf_op jit(solution)/shard_map/ppermute | solution.py:41
  75.6 24.9 %collective-permute-start.19 = (bf16[2,48,2304]{2,1,0:T(8,128)(2,1)}, bf16[2,48,2304]{2,1,0:T(8,128)(2,1)}, u32[]{:S(2)}, u32[]{:S(2)}) collective-permute-start(bf16[2,48,2304]{2,1,0:T(8,128)(2,1)} %shard_map.330.refs_0_), channel_id=1, source_target_pairs={{0,24},{2,26},{4,28},{6,30},{16,8},{18,10},{20,12},{22,14},{24,0},... | collective-permute-start | bytes 1327112 | tf_op jit(solution)/shard_map/ppermute | solution.py:41
  77.6 57.8 %copy-start.66 = (bf16[1,3456]{1,0:T(2,128)(2,1)}, bf16[1,3456]{1,0:T(2,128)(2,1)S(1)}, u32[]{:S(2)}) copy-start(bf16[1,3456]{1,0:T(2,128)(2,1)S(1)} %stack.58) | copy-start | bytes 20740
  80.7 36.6 %collective-permute-start.20 = (bf16[2,4,48,1536]{3,2,1,0:T(8,128)(2,1)}, bf16[2,4,48,1536]{3,2,1,0:T(8,128)(2,1)}, u32[]{:S(2)}, u32[]{:S(2)}) collective-permute-start(bf16[2,4,48,1536]{3,2,1,0:T(8,128)(2,1)} %get-tuple-element.263.refs_0_), channel_id=1, source_target_pairs={{0,1},{1,0},{2,3},{3,2},{4,5},{5,4},{6,7},{7,6},{8,9},{9,8},{10,11... | collective-permute-start | bytes 3538952 | tf_op jit(solution)/shard_map/ppermute | solution.py:21
  81.9 35.5 %collective-permute-start.21 = (bf16[2,4,48,1536]{3,2,1,0:T(8,128)(2,1)}, bf16[2,4,48,1536]{3,2,1,0:T(8,128)(2,1)}, u32[]{:S(2)}, u32[]{:S(2)}) collective-permute-start(bf16[2,4,48,1536]{3,2,1,0:T(8,128)(2,1)} %get-tuple-element.265.refs_2_), channel_id=1, source_target_pairs={{0,4},{2,6},{4,0},{6,2},{8,12},{10,14},{12,8},{14,10},{16,20},{18,... | collective-permute-start | bytes 3538952 | tf_op jit(solution)/shard_map/ppermute | solution.py:26
  84.4 33.0 %collective-permute-start.22 = (bf16[2,48,2304]{2,1,0:T(8,128)(2,1)}, bf16[2,48,2304]{2,1,0:T(8,128)(2,1)S(1)}, u32[]{:S(2)}, u32[]{:S(2)}) collective-permute-start(bf16[2,48,2304]{2,1,0:T(8,128)(2,1)} %shard_map.330.refs_0_), channel_id=1, source_target_pairs={{0,8},{2,10},{4,12},{6,14},{16,0},{18,2},{20,4},{22,6},{24,16},{26... | collective-permute-start | bytes 1327112 | tf_op jit(solution)/shard_map/ppermute | solution.py:41
  122.3 13.2 %collective-permute-start.23 = (bf16[2,384,3072]{2,1,0:T(8,128)(2,1)}, bf16[2,384,3072]{2,1,0:T(8,128)(2,1)}, u32[]{:S(2)}, u32[]{:S(2)}) collective-permute-start(bf16[2,384,3072]{2,1,0:T(8,128)(2,1)} %bitcast.167), channel_id=1, source_target_pairs={{0,2},{2,0},{4,6},{6,4},{8,10},{10,8},{12,14},{14,12},{16,18},{18,... | collective-permute-start | bytes 14155784 | tf_op jit(solution)/shard_map/ppermute | solution.py:31
  122.4 12.0 %collective-permute-start.26 = (bf16[256,768]{1,0:T(8,128)(2,1)S(1)}, bf16[256,768]{1,0:T(8,128)(2,1)S(1)}, u32[]{:S(2)}, u32[]{:S(2)}) collective-permute-start(bf16[256,768]{1,0:T(8,128)(2,1)S(1)} %get-tuple-element.433), channel_id=1, source_target_pairs={{0,1},{1,0},{2,3},{3,2},{4,5},{5,4},{6,7},{7,6},{8,9},{9,8},{10,11... | collective-permute-start | bytes 1179656 | tf_op jit(solution)/shard_map/ppermute | solution.py:21
  125.9 27.2 %collective-permute-start.24 = (bf16[2,4,48,1152]{3,2,1,0:T(8,128)(2,1)S(1)}, bf16[2,4,48,1152]{3,2,1,0:T(8,128)(2,1)}, u32[]{:S(2)}, u32[]{:S(2)}) collective-permute-start(bf16[2,4,48,1152]{3,2,1,0:T(8,128)(2,1)S(1)} %get-tuple-element.274.refs_0_), channel_id=1, source_target_pairs={{0,1},{1,0},{2,3},{3,2},{4,5},{5,4},{6,7},{7,6},{8,9},{9,8},{10,11... | collective-permute-start | bytes 2654216 | tf_op jit(solution)/shard_map/ppermute | solution.py:21
  126.7 26.3 %collective-permute-start.25 = (bf16[2,4,48,1152]{3,2,1,0:T(8,128)(2,1)}, bf16[2,4,48,1152]{3,2,1,0:T(8,128)(2,1)}, u32[]{:S(2)}, u32[]{:S(2)}) collective-permute-start(bf16[2,4,48,1152]{3,2,1,0:T(8,128)(2,1)} %get-tuple-element.275.refs_2_), channel_id=1, source_target_pairs={{0,4},{2,6},{4,0},{6,2},{8,12},{10,14},{12,8},{14,10},{16,20},{18,... | collective-permute-start | bytes 2654216 | tf_op jit(solution)/shard_map/ppermute | solution.py:26
  157.0 6.6 %collective-permute-start.27 = (bf16[2,384,2304]{2,1,0:T(8,128)(2,1)}, bf16[2,384,2304]{2,1,0:T(8,128)(2,1)}, u32[]{:S(2)}, u32[]{:S(2)}) collective-permute-start(bf16[2,384,2304]{2,1,0:T(8,128)(2,1)} %bitcast.151), channel_id=1, source_target_pairs={{0,2},{2,0},{4,6},{6,4},{8,10},{10,8},{12,14},{14,12},{16,18},{18,... | collective-permute-start | bytes 10616840 | tf_op jit(solution)/shard_map/ppermute | solution.py:31
  157.3 14.8 %collective-permute-start.28 = (bf16[256,768]{1,0:T(8,128)(2,1)S(1)}, bf16[256,768]{1,0:T(8,128)(2,1)S(1)}, u32[]{:S(2)}, u32[]{:S(2)}) collective-permute-start(bf16[256,768]{1,0:T(8,128)(2,1)S(1)} %slice.423), channel_id=1, source_target_pairs={{0,1},{1,0},{2,3},{3,2},{4,5},{5,4},{6,7},{7,6},{8,9},{9,8},{10,11... | collective-permute-start | bytes 1179656 | tf_op jit(solution)/shard_map/ppermute | solution.py:21
  194.7 21.9 %collective-permute-start.29 = (bf16[256,768]{1,0:T(8,128)(2,1)S(1)}, bf16[256,768]{1,0:T(8,128)(2,1)S(1)}, u32[]{:S(2)}, u32[]{:S(2)}) collective-permute-start(bf16[256,768]{1,0:T(8,128)(2,1)S(1)} %slice.682), channel_id=1, source_target_pairs={{0,1},{1,0},{2,3},{3,2},{4,5},{5,4},{6,7},{7,6},{8,9},{9,8},{10,11... | collective-permute-start | bytes 1179656 | tf_op jit(solution)/shard_map/ppermute | solution.py:21
  215.6 13.8 %collective-permute-start.30 = (bf16[256,768]{1,0:T(8,128)(2,1)S(1)}, bf16[256,768]{1,0:T(8,128)(2,1)S(1)}, u32[]{:S(2)}, u32[]{:S(2)}) collective-permute-start(bf16[256,768]{1,0:T(8,128)(2,1)S(1)} %get-tuple-element.302), channel_id=1, source_target_pairs={{0,1},{1,0},{2,3},{3,2},{4,5},{5,4},{6,7},{7,6},{8,9},{9,8},{10,11... | collective-permute-start | bytes 1179656 | tf_op jit(solution)/shard_map/ppermute | solution.py:21
  236.7 10.2 %collective-permute-start.31 = (bf16[2,384,2304]{2,1,0:T(8,128)(2,1)}, bf16[2,384,2304]{2,1,0:T(8,128)(2,1)}, u32[]{:S(2)}, u32[]{:S(2)}) collective-permute-start(bf16[2,384,2304]{2,1,0:T(8,128)(2,1)} %shard_map.342), channel_id=1, source_target_pairs={{0,2},{2,0},{4,6},{6,4},{8,10},{10,8},{12,14},{14,12},{16,18},{18,... | collective-permute-start | bytes 10616840 | tf_op jit(solution)/shard_map/ppermute | solution.py:31
  265.4 10.9 %collective-permute-start.32 = (bf16[2,384,3072]{2,1,0:T(8,128)(2,1)}, bf16[2,384,3072]{2,1,0:T(8,128)(2,1)}, u32[]{:S(2)}, u32[]{:S(2)}) collective-permute-start(bf16[2,384,3072]{2,1,0:T(8,128)(2,1)} %shard_map.345), channel_id=1, source_target_pairs={{0,2},{2,0},{4,6},{6,4},{8,10},{10,8},{12,14},{14,12},{16,18},{18,... | collective-permute-start | bytes 14155784 | tf_op jit(solution)/shard_map/ppermute | solution.py:31
  266.0 21.6 %collective-permute-start.33 = (bf16[384,1152]{1,0:T(8,128)(2,1)S(1)}, bf16[384,1152]{1,0:T(8,128)(2,1)S(1)}, u32[]{:S(2)}, u32[]{:S(2)}) collective-permute-start(bf16[384,1152]{1,0:T(8,128)(2,1)S(1)} %get-tuple-element.315), channel_id=1, source_target_pairs={{0,1},{1,0},{2,3},{3,2},{4,5},{5,4},{6,7},{7,6},{8,9},{9,8},{10,11... | collective-permute-start | bytes 2654216 | tf_op jit(solution)/shard_map/ppermute | solution.py:21
  267.2 21.3 %collective-permute-start.34 = (bf16[2,192,1152]{2,1,0:T(8,128)(2,1)S(1)}, bf16[2,192,1152]{2,1,0:T(8,128)(2,1)S(1)}, u32[]{:S(2)}, u32[]{:S(2)}) collective-permute-start(bf16[2,192,1152]{2,1,0:T(8,128)(2,1)S(1)} %get-tuple-element.316), channel_id=1, source_target_pairs={{0,4},{2,6},{4,0},{6,2},{8,12},{10,14},{12,8},{14,10},{16,20},{18,... | collective-permute-start | bytes 2654216 | tf_op jit(solution)/shard_map/ppermute | solution.py:26
  291.4 16.1 %collective-permute-start.36 = (bf16[192,1152]{1,0:T(8,128)(2,1)S(1)}, bf16[192,1152]{1,0:T(8,128)(2,1)S(1)}, u32[]{:S(2)}, u32[]{:S(2)}) collective-permute-start(bf16[192,1152]{1,0:T(8,128)(2,1)S(1)} %fusion.21), channel_id=1, source_target_pairs={{0,1},{1,0},{2,3},{3,2},{4,5},{5,4},{6,7},{7,6},{8,9},{9,8},{10,11... | collective-permute-start | bytes 1327112 | tf_op jit(solution)/shard_map/ppermute | solution.py:21
  292.3 15.2 %collective-permute-start.35 = (bf16[192,1152]{1,0:T(8,128)(2,1)S(1)}, bf16[192,1152]{1,0:T(8,128)(2,1)S(1)}, u32[]{:S(2)}, u32[]{:S(2)}) collective-permute-start(bf16[192,1152]{1,0:T(8,128)(2,1)S(1)} %slice.680), channel_id=1, source_target_pairs={{0,4},{2,6},{4,0},{6,2},{8,12},{10,14},{12,8},{14,10},{16,20},{18,... | collective-permute-start | bytes 1327112 | tf_op jit(solution)/shard_map/ppermute | solution.py:26
  294.2 36.2 %collective-permute-start.38 = (bf16[384,1536]{1,0:T(8,128)(2,1)}, bf16[384,1536]{1,0:T(8,128)(2,1)}, u32[]{:S(2)}, u32[]{:S(2)}) collective-permute-start(bf16[384,1536]{1,0:T(8,128)(2,1)} %get-tuple-element.325), channel_id=1, source_target_pairs={{0,1},{1,0},{2,3},{3,2},{4,5},{5,4},{6,7},{7,6},{8,9},{9,8},{10,11... | collective-permute-start | bytes 3538952 | tf_op jit(solution)/shard_map/ppermute | solution.py:21
  295.1 35.4 %collective-permute-start.39 = (bf16[2,192,1536]{2,1,0:T(8,128)(2,1)}, bf16[2,192,1536]{2,1,0:T(8,128)(2,1)}, u32[]{:S(2)}, u32[]{:S(2)}) collective-permute-start(bf16[2,192,1536]{2,1,0:T(8,128)(2,1)} %get-tuple-element.326), channel_id=1, source_target_pairs={{0,4},{2,6},{4,0},{6,2},{8,12},{10,14},{12,8},{14,10},{16,20},{18,... | collective-permute-start | bytes 3538952 | tf_op jit(solution)/shard_map/ppermute | solution.py:26
  329.4 21.0 %collective-permute-start.37 = (bf16[2,384,1536]{2,1,0:T(8,128)(2,1)}, bf16[2,384,1536]{2,1,0:T(8,128)(2,1)}, u32[]{:S(2)}, u32[]{:S(2)}) collective-permute-start(bf16[2,384,1536]{2,1,0:T(8,128)(2,1)} %shard_map.350), channel_id=1, source_target_pairs={{0,2},{2,0},{4,6},{6,4},{8,10},{10,8},{12,14},{14,12},{16,18},{18,... | collective-permute-start | bytes 7077896 | tf_op jit(solution)/shard_map/ppermute | solution.py:31
  329.5 4.7 %collective-permute-start.40 = (f32[22,768]{1,0:T(8,128)S(1)}, f32[22,768]{1,0:T(8,128)S(1)}, u32[]{:S(2)}, u32[]{:S(2)}) collective-permute-start(f32[22,768]{1,0:T(8,128)S(1)} %pad_maximum_fusion.10), channel_id=1, source_target_pairs={{0,1},{1,0},{2,3},{3,2},{4,5},{5,4},{6,7},{7,6},{8,9},{9,8},{10,11... | collective-permute-start | bytes 202760 | tf_op jit(solution)/shard_map/ppermute | solution.py:21
  336.8 15.0 %collective-permute-start.44 = (bf16[192,1536]{1,0:T(8,128)(2,1)S(1)}, bf16[192,1536]{1,0:T(8,128)(2,1)S(1)}, u32[]{:S(2)}, u32[]{:S(2)}) collective-permute-start(bf16[192,1536]{1,0:T(8,128)(2,1)S(1)} %fusion.17), channel_id=1, source_target_pairs={{0,1},{1,0},{2,3},{3,2},{4,5},{5,4},{6,7},{7,6},{8,9},{9,8},{10,11... | collective-permute-start | bytes 1769480 | tf_op jit(solution)/shard_map/ppermute | solution.py:21
  339.5 19.1 %collective-permute-start.43 = (bf16[192,1536]{1,0:T(8,128)(2,1)S(1)}, bf16[192,1536]{1,0:T(8,128)(2,1)S(1)}, u32[]{:S(2)}, u32[]{:S(2)}) collective-permute-start(bf16[192,1536]{1,0:T(8,128)(2,1)S(1)} %slice.679), channel_id=1, source_target_pairs={{0,4},{2,6},{4,0},{6,2},{8,12},{10,14},{12,8},{14,10},{16,20},{18,... | collective-permute-start | bytes 1769480 | tf_op jit(solution)/shard_map/ppermute | solution.py:26
  342.9 16.6 %collective-permute-start.45 = (bf16[48,2304]{1,0:T(8,128)(2,1)S(1)}, bf16[48,2304]{1,0:T(8,128)(2,1)S(1)}, u32[]{:S(2)}, u32[]{:S(2)}) collective-permute-start(bf16[48,2304]{1,0:T(8,128)(2,1)S(1)} %copy-done.77), channel_id=1, source_target_pairs={{0,8},{2,10},{4,12},{6,14},{16,0},{18,2},{20,4},{22,6},{24,16},{26... | collective-permute-start | bytes 663560 | tf_op jit(solution)/shard_map/ppermute | solution.py:41
  348.0 13.7 %collective-permute-start.46 = (bf16[48,2304]{1,0:T(8,128)(2,1)S(1)}, bf16[48,2304]{1,0:T(8,128)(2,1)S(1)}, u32[]{:S(2)}, u32[]{:S(2)}) collective-permute-start(bf16[48,2304]{1,0:T(8,128)(2,1)S(1)} %copy-done.76), channel_id=1, source_target_pairs={{0,24},{2,26},{4,28},{6,30},{16,8},{18,10},{20,12},{22,14},{24,0},... | collective-permute-start | bytes 663560 | tf_op jit(solution)/shard_map/ppermute | solution.py:41
  350.5 13.0 %collective-permute-start.47 = (bf16[48,2304]{1,0:T(8,128)(2,1)S(1)}, bf16[48,2304]{1,0:T(8,128)(2,1)S(1)}, u32[]{:S(2)}, u32[]{:S(2)}) collective-permute-start(bf16[48,2304]{1,0:T(8,128)(2,1)S(1)} %copy-done.75), channel_id=1, source_target_pairs={{0,16},{2,18},{4,20},{6,22},{16,24},{18,26},{20,28},{22,30},{24,8}... | collective-permute-start | bytes 663560 | tf_op jit(solution)/shard_map/ppermute | solution.py:41
  351.8 12.4 %collective-permute-start.48 = (f32[22,768]{1,0:T(8,128)S(1)}, f32[22,768]{1,0:T(8,128)S(1)}, u32[]{:S(2)}, u32[]{:S(2)}) collective-permute-start(f32[22,768]{1,0:T(8,128)S(1)} %fusion.95), channel_id=1, source_target_pairs={{0,2},{2,0},{4,6},{6,4},{8,10},{10,8},{12,14},{14,12},{16,18},{18,... | collective-permute-start | bytes 202760 | tf_op jit(solution)/shard_map/ppermute | solution.py:783
  358.6 36.6 %collective-permute-start.50 = (bf16[256,768]{1,0:T(8,128)(2,1)S(1)}, bf16[256,768]{1,0:T(8,128)(2,1)S(1)}, u32[]{:S(2)}, u32[]{:S(2)}) collective-permute-start(bf16[256,768]{1,0:T(8,128)(2,1)S(1)} %copy-done.43), channel_id=1, source_target_pairs={{0,1},{1,0},{2,3},{3,2},{4,5},{5,4},{6,7},{7,6},{8,9},{9,8},{10,11... | collective-permute-start | bytes 1179656 | tf_op jit(solution)/shard_map/ppermute | solution.py:21
  359.5 23.4 %collective-permute-start.41 = (bf16[384,768]{1,0:T(8,128)(2,1)S(1)}, bf16[384,768]{1,0:T(8,128)(2,1)}, u32[]{:S(2)}, u32[]{:S(2)}) collective-permute-start(bf16[384,768]{1,0:T(8,128)(2,1)S(1)} %get-tuple-element.362), channel_id=1, source_target_pairs={{0,1},{1,0},{2,3},{3,2},{4,5},{5,4},{6,7},{7,6},{8,9},{9,8},{10,11... | collective-permute-start | bytes 1769480 | tf_op jit(solution)/shard_map/ppermute | solution.py:21
  361.6 23.8 %collective-permute-start.42 = (bf16[2,192,768]{2,1,0:T(8,128)(2,1)S(1)}, bf16[2,192,768]{2,1,0:T(8,128)(2,1)}, u32[]{:S(2)}, u32[]{:S(2)}) collective-permute-start(bf16[2,192,768]{2,1,0:T(8,128)(2,1)S(1)} %get-tuple-element.363), channel_id=1, source_target_pairs={{0,4},{2,6},{4,0},{6,2},{8,12},{10,14},{12,8},{14,10},{16,20},{18,... | collective-permute-start | bytes 1769480 | tf_op jit(solution)/shard_map/ppermute | solution.py:26
  366.9 38.0 %collective-permute-start.54 = (bf16[48,3072]{1,0:T(8,128)(2,1)}, bf16[48,3072]{1,0:T(8,128)(2,1)}, u32[]{:S(2)}, u32[]{:S(2)}) collective-permute-start(bf16[48,3072]{1,0:T(8,128)(2,1)} %get-tuple-element.430), channel_id=1, source_target_pairs={{0,8},{2,10},{4,12},{6,14},{16,0},{18,2},{20,4},{22,6},{24,16},{26... | collective-permute-start | bytes 884744 | tf_op jit(solution)/shard_map/ppermute | solution.py:41
  373.7 15.8 %collective-permute-start.49 = (f32[22,768]{1,0:T(8,128)S(1)}, f32[22,768]{1,0:T(8,128)S(1)}, u32[]{:S(2)}, u32[]{:S(2)}) collective-permute-start(f32[22,768]{1,0:T(8,128)S(1)} %add.233), channel_id=1, source_target_pairs={{0,4},{2,6},{4,0},{6,2},{8,12},{10,14},{12,8},{14,10},{16,20},{18,... | collective-permute-start | bytes 202760 | tf_op jit(solution)/shard_map/ppermute | solution.py:783
  382.9 23.6 %collective-permute-start.55 = (bf16[48,3072]{1,0:T(8,128)(2,1)S(1)}, bf16[48,3072]{1,0:T(8,128)(2,1)S(1)}, u32[]{:S(2)}, u32[]{:S(2)}) collective-permute-start(bf16[48,3072]{1,0:T(8,128)(2,1)S(1)} %copy-done.68), channel_id=1, source_target_pairs={{0,24},{2,26},{4,28},{6,30},{16,8},{18,10},{20,12},{22,14},{24,0},... | collective-permute-start | bytes 884744 | tf_op jit(solution)/shard_map/ppermute | solution.py:41
  385.4 21.1 %collective-permute-start.56 = (bf16[48,3072]{1,0:T(8,128)(2,1)S(1)}, bf16[48,3072]{1,0:T(8,128)(2,1)S(1)}, u32[]{:S(2)}, u32[]{:S(2)}) collective-permute-start(bf16[48,3072]{1,0:T(8,128)(2,1)S(1)} %get-tuple-element.428), channel_id=1, source_target_pairs={{0,16},{2,18},{4,20},{6,22},{16,24},{18,26},{20,28},{22,30},{24,8}... | collective-permute-start | bytes 884744 | tf_op jit(solution)/shard_map/ppermute | solution.py:41
  389.5 12.1 %collective-permute-start.51 = (bf16[256,768]{1,0:T(8,128)(2,1)S(1)}, bf16[256,768]{1,0:T(8,128)(2,1)S(1)}, u32[]{:S(2)}, u32[]{:S(2)}) collective-permute-start(bf16[256,768]{1,0:T(8,128)(2,1)S(1)} %slice.681), channel_id=1, source_target_pairs={{0,1},{1,0},{2,3},{3,2},{4,5},{5,4},{6,7},{7,6},{8,9},{9,8},{10,11... | collective-permute-start | bytes 1179656 | tf_op jit(solution)/shard_map/ppermute | solution.py:21
  395.2 15.7 %collective-permute-start.53 = (bf16[192,768]{1,0:T(8,128)(2,1)S(1)}, bf16[192,768]{1,0:T(8,128)(2,1)S(1)}, u32[]{:S(2)}, u32[]{:S(2)}) collective-permute-start(bf16[192,768]{1,0:T(8,128)(2,1)S(1)} %fusion.24), channel_id=1, source_target_pairs={{0,1},{1,0},{2,3},{3,2},{4,5},{5,4},{6,7},{7,6},{8,9},{9,8},{10,11... | collective-permute-start | bytes 884744 | tf_op jit(solution)/shard_map/ppermute | solution.py:21
  401.5 9.4 %collective-permute-start.52 = (bf16[192,768]{1,0:T(8,128)(2,1)S(1)}, bf16[192,768]{1,0:T(8,128)(2,1)S(1)}, u32[]{:S(2)}, u32[]{:S(2)}) collective-permute-start(bf16[192,768]{1,0:T(8,128)(2,1)S(1)} %slice.683), channel_id=1, source_target_pairs={{0,4},{2,6},{4,0},{6,2},{8,12},{10,14},{12,8},{14,10},{16,20},{18,... | collective-permute-start | bytes 884744 | tf_op jit(solution)/shard_map/ppermute | solution.py:26
  404.9 5.9 %collective-permute-start.57 = (f32[22,768]{1,0:T(8,128)S(1)}, f32[22,768]{1,0:T(8,128)S(1)}, u32[]{:S(2)}, u32[]{:S(2)}) collective-permute-start(f32[22,768]{1,0:T(8,128)S(1)} %add.239), channel_id=1, source_target_pairs={{0,8},{2,10},{4,12},{6,14},{8,0},{10,2},{12,4},{14,6},{16,24},{18,... | collective-permute-start | bytes 202760 | tf_op jit(solution)/shard_map/ppermute | solution.py:783
  411.1 13.5 %collective-permute-start.58 = (bf16[48,1536]{1,0:T(8,128)(2,1)S(1)}, bf16[48,1536]{1,0:T(8,128)(2,1)S(1)}, u32[]{:S(2)}, u32[]{:S(2)}) collective-permute-start(bf16[48,1536]{1,0:T(8,128)(2,1)S(1)} %get-tuple-element.444), channel_id=1, source_target_pairs={{0,8},{2,10},{4,12},{6,14},{16,0},{18,2},{20,4},{22,6},{24,16},{26... | collective-permute-start | bytes 442376 | tf_op jit(solution)/shard_map/ppermute | solution.py:41
  411.2 13.5 %collective-permute-start.59 = (bf16[48,1536]{1,0:T(8,128)(2,1)S(1)}, bf16[48,1536]{1,0:T(8,128)(2,1)S(1)}, u32[]{:S(2)}, u32[]{:S(2)}) collective-permute-start(bf16[48,1536]{1,0:T(8,128)(2,1)S(1)} %get-tuple-element.443), channel_id=1, source_target_pairs={{0,24},{2,26},{4,28},{6,30},{16,8},{18,10},{20,12},{22,14},{24,0},... | collective-permute-start | bytes 442376 | tf_op jit(solution)/shard_map/ppermute | solution.py:41
  413.5 11.1 %collective-permute-start.60 = (bf16[48,1536]{1,0:T(8,128)(2,1)S(1)}, bf16[48,1536]{1,0:T(8,128)(2,1)S(1)}, u32[]{:S(2)}, u32[]{:S(2)}) collective-permute-start(bf16[48,1536]{1,0:T(8,128)(2,1)S(1)} %get-tuple-element.442), channel_id=1, source_target_pairs={{0,16},{2,18},{4,20},{6,22},{16,24},{18,26},{20,28},{22,30},{24,8}... | collective-permute-start | bytes 442376 | tf_op jit(solution)/shard_map/ppermute | solution.py:41
  415.5 9.2 %collective-permute-start.61 = (f32[22,768]{1,0:T(8,128)S(1)}, f32[22,768]{1,0:T(8,128)S(1)}, u32[]{:S(2)}, u32[]{:S(2)}) collective-permute-start(f32[22,768]{1,0:T(8,128)S(1)} %add.242), channel_id=1, source_target_pairs={{0,16},{2,18},{4,20},{6,22},{8,24},{10,26},{12,28},{14,30},{16,0},... | collective-permute-start | bytes 202760 | tf_op jit(solution)/shard_map/ppermute | solution.py:783
  (85 other events, 668.2 us)

commit v3 on v2

--- a/solution.py
+++ b/solution.py
@@ -63,7 +63,7 @@
     return lax.optimization_barrier((value, others))[0]
 
 
-VMEM_BYTES = 48 << 20
+VMEM_BYTES = 26 << 20
 TILE = 256
 
 

time: 435 us -> 423 us (0.972)
  Pallas kernels: 207 us -> 172 us
  local copies, waits for them, and re-layouts: 35.5 us -> 50.6 us
  waiting for transfers between devices: 74.9 us -> 86.1 us
    pallas_call x20, Pallas kernels: 191 us -> 156 us  [call(): pl.pallas_call(body, grid=(steps,), in_specs=[pl.BlockSpec(block, index)...]
    unnamed x176 -> x220, local copies, waits for them, and re-layouts: 20.8 us -> 37.8 us
    ppermute x18, waiting for transfers between devices: 22.8 us -> 29.2 us  [ring_shift(): return lax.ppermute(value, 'dp', pairs)]
    ppermute x22, waiting for transfers between devices: 29.9 us -> 34.3 us  [swap_y(): return lax.ppermute(value, 'mp', [(0, 1), (1, 0)])]
  transfers between devices with their start and end apart: 62 -> 62, of which waited for: 19 -> 21; matrix products, arithmetic and copies ran while one was open for 9% -> 8% of each run, Pallas kernels for 36% -> 32%
where the time goes in v3:
time: 423 us; the launch traced here: 418 us
  Pallas kernels  172 us (41%)
  waiting for transfers between devices  86.1 us (20%)
  starting transfers between devices  76.6 us (18%)
  local copies, waits for them, and re-layouts  50.6 us (12%)
  other arithmetic  18.2 us (4%)
  matrix products  11.6 us (3%)
    pallas_call x20, Pallas kernels, call(): pl.pallas_call(body, grid=(steps,), in_specs=[pl.BlockSpec(block, index)...  156 us
    unnamed x220, local copies, waits for them, and re-layouts  37.8 us
    ppermute x18, starting transfers between devices, ring_shift(): return lax.ppermute(value, 'dp', pairs)  35.6 us
    ppermute x22, waiting for transfers between devices, swap_y(): return lax.ppermute(value, 'mp', [(0, 1), (1, 0)])  34.3 us
    ppermute x18, waiting for transfers between devices, ring_shift(): return lax.ppermute(value, 'dp', pairs)  29.2 us
    ppermute x22, starting transfers between devices, swap_y(): return lax.ppermute(value, 'mp', [(0, 1), (1, 0)])  25.1 us
    pallas_call x11, Pallas kernels, moves(): pl.pallas_call(body, out_shape=[jax.ShapeDtypeStruct(shape, LOW) for shap...  15.2 us
    ppermute x12, starting transfers between devices, swap_x(): return lax.ppermute(value, 'dp', [(i, i ^ 2) for i in range(n)])  13.3 us
  transfers between devices with their start and end apart: 62, of which 21 were waited for; matrix products, arithmetic and copies ran while one was open for 8% of the time, Pallas kernels for 32%

profile of v3, /device:TPU:0, one launch (start us, length us, event | category | flops | bytes accessed | tf_op | source)
XLA Modules:
  0.0 417.7 jit_solution(8313828076835086112)
XLA Ops:
  3.2 4.1 collective-permute-start
  9.5 2.2 select_bitcast_fusion.6
  14.0 3.1 collective-permute-done.1.refs_2_
  17.1 5.7 %collective-permute-done.2.refs_3_ = bf16[48,1664]{1,0:T(8,128)(2,1)S(1)} collective-permute-done((bf16[48,1664]{1,0:T(8,128)(2,1)S(1)}, bf16[48,1664]{1,0:T(8,128)(2,1)S(1)}, u32[]{:S(2)}, u32[]{:S(2)}) %collective-permute-start.2) | collective-permute-done | bytes 159776 | tf_op jit(solution)/shard_map/ppermute | solution.py:41
  28.4 7.0 %collective-permute-done.6.refs_1_ = bf16[48,1152]{1,0:T(8,128)(2,1)S(1)} collective-permute-done((bf16[48,1152]{1,0:T(8,128)(2,1)S(1)}, bf16[48,1152]{1,0:T(8,128)(2,1)S(1)}, u32[]{:S(2)}, u32[]{:S(2)}) %collective-permute-start.6) | collective-permute-done | bytes 110624 | tf_op jit(solution)/shard_map/ppermute | solution.py:26
  38.4 2.5 collective-permute-start.11
  40.9 3.2 convolution_convert_fusion.1.rows.refs_0_
  44.1 6.0 %collective-permute-done.11.refs_2_ = bf16[48,3072]{1,0:T(8,128)(2,1)S(1)} collective-permute-done((bf16[48,3072]{1,0:T(8,128)(2,1)S(1)}, bf16[48,3072]{1,0:T(8,128)(2,1)S(1)}, u32[]{:S(2)}, u32[]{:S(2)}) %collective-permute-start.11) | collective-permute-done | bytes 294944 | tf_op jit(solution)/shard_map/ppermute | solution.py:41
  50.1 6.7 %collective-permute-done.12.refs_3_ = bf16[48,3072]{1,0:T(8,128)(2,1)S(1)} collective-permute-done((bf16[48,3072]{1,0:T(8,128)(2,1)S(1)}, bf16[48,3072]{1,0:T(8,128)(2,1)S(1)}, u32[]{:S(2)}, u32[]{:S(2)}) %collective-permute-start.12) | collective-permute-done | bytes 294944 | tf_op jit(solution)/shard_map/ppermute | solution.py:41
  64.9 10.5 %collective-permute-done.16 = bf16[3456]{0:T(1024)(128)(2,1)} collective-permute-done((bf16[3456]{0:T(1024)(128)(2,1)}, bf16[3456]{0:T(1024)(128)(2,1)}, u32[]{:S(2)}, u32[]{:S(2)}) %collective-permute-start.16) | collective-permute-done | bytes 6944 | tf_op jit(solution)/shard_map/ppermute | solution.py:21
  77.5 3.1 shard_map.328
  84.2 1.6 collective-permute-start.22
  87.1 12.0 %shard_map.329 = (bf16[2,768,1152]{2,1,0:T(8,128)(2,1)S(1)}, bf16[2,512,384]{2,1,0:T(8,128)(2,1)S(1)}, f32[2,8,512]{2,1,0:T(8,128)S(1)}) custom-call(bf16[768,768]{1,0:T(8,128)(2,1)S(1)} %copy-done.6, bf16[2,384,1664]{2,1,0:T(8,128)(2,1)S(1)} %bitcast.138, bf16[2,384,1664]{2,1,0:T(8,128)(2,1)} %collective-permute-done.13.refs_1_.refs_3_.refs_5_.refs_7_.out_two, ...), custom_call_target="tpu_custom_call" | custom-call | flops 1761607680 | bytes 10443264 | tf_op jit(solution)/shard_map/pallas_call | solution.py:80
  99.1 1.8 convolution_convert_fusion.2.away.refs_2_
  100.9 10.3 %shard_map.331 = (bf16[2,256,1152]{2,1,0:T(8,128)(2,1)S(1)}, bf16[2,768,384]{2,1,0:T(8,128)(2,1)S(1)}, f32[2,8,256]{2,1,0:T(8,128)S(1)}, bf16[768,768]{1,0:T(8,1...) custom-call(bf16[768,768]{1,0:T(8,128)(2,1)S(1)} %copy-done.6, ...), custom_call_target="tpu_custom_call" | custom-call | flops 1107296256 | bytes 15560192 | tf_op jit(solution)/shard_map/pallas_call | solution.py:80
  111.3 3.1 collective-permute-done.22.refs_3_
  114.4 4.8 %shard_map.332 = bf16[2,2,4,48,3072]{4,3,2,1,0:T(8,128)(2,1)} custom-call(bf16[2,4,48,1536]{3,2,1,0:T(8,128)(2,1)} %get-tuple-element.263.refs_0_, bf16[2,4,48,1536]{3,2,1,0:T(8,128)(2,1)} %collective-permute-done.20.refs_1_, bf16[2,4,48,1536]{3,2,1,0:T(8,128)(2,1)} %get-tuple-element.265.refs_2_, bf16[2,4,48,1536]{3,2,1,0:T(8,128)(2,1)} %collective-permute-done.21.refs_3_), custom_call_target="tpu_custom_call" | custom-call | bytes 4718592 | tf_op jit(solution)/shard_map/pallas_call | solution.py:102
  120.7 2.6 shard_map.334
  125.7 5.8 %collective-permute-done.26 = bf16[256,768]{1,0:T(8,128)(2,1)S(1)} collective-permute-done((bf16[256,768]{1,0:T(8,128)(2,1)S(1)}, bf16[256,768]{1,0:T(8,128)(2,1)S(1)}, u32[]{:S(2)}, u32[]{:S(2)}) %collective-permute-start.26) | collective-permute-done | bytes 393248 | tf_op jit(solution)/shard_map/ppermute | solution.py:21
  133.9 13.6 %shard_map.333 = (bf16[2,768,1536]{2,1,0:T(8,128)(2,1)S(1)}, bf16[2,768,1536]{2,1,0:T(8,128)(2,1)S(1)}, bf16[768,768]{1,0:T(8,128)(2,1)S(1)}, bf16[768,768]{1,0:T(8,128)(2,1)S(1)}, f32[768,1]{1,0:T(8,128)S(1)}) custom-call(bf16[768,768]{1,0:T(8,128)(2,1)S(1)} %copy-done.10, f32[8,768]{1,0:T(8,128)S(1)} %slice_select_fusion.1.refs_12_.norms, ...), custom_call_target="tpu_custom_call" | custom-call | flops 3623878656 | bytes 15945216 | tf_op jit(solution)/shard_map/pallas_call | solution.py:80
  147.6 2.5 collective-permute-done.24.refs_1_
  150.1 2.4 shard_map.335
  155.2 3.6 collective-permute-done.27.refs_1_.refs_3_.refs_5_.up_two.down_two.refs_7_.refs_9_.out_two.refs_2_.refs_4_
  158.8 6.2 %shard_map.336 = (bf16[2,768,576]{2,1,0:T(8,128)(2,1)S(1)}, bf16[2,512,192]{2,1,0:T(8,128)(2,1)S(1)}, f32[2,8,512]{2,1,0:T(8,128)S(1)}) custom-call(bf16[768,768]{1,0:T(8,128)(2,1)S(1)} %get-tuple-element.277.rows.refs_4_, bf16[2,384,2304]{2,1,0:T(8,128)(2,1)S(1)} %bitcast.121, ...), custom_call_target="tpu_custom_call" | custom-call | flops 880803840 | bytes 8769792 | tf_op jit(solution)/shard_map/pallas_call | solution.py:80
  165.1 6.2 %shard_map.337 = (bf16[2,256,576]{2,1,0:T(8,128)(2,1)S(1)}, bf16[2,768,192]{2,1,0:T(8,128)(2,1)S(1)}, f32[2,8,256]{2,1,0:T(8,128)S(1)}, bf16[768,768]{1,0:T(8,12...) custom-call(bf16[768,768]{1,0:T(8,128)(2,1)S(1)} %get-tuple-element.277.rows.refs_4_, ...), custom_call_target="tpu_custom_call" | custom-call | flops 553648128 | bytes 14279936 | tf_op jit(solution)/shard_map/pallas_call | solution.py:80
  171.3 6.6 %shard_map.338 = (bf16[2,768,768]{2,1,0:T(8,128)(2,1)S(1)}, bf16[2,768,768]{2,1,0:T(8,128)(2,1)S(1)}, f32[768,768]{1,0:T(8,128)S(1)}, bf16[768,768]{1,0:T(8,128)(2,1)S(1)}, f32[768,1]{1,0:T(8,128)S(1)}) custom-call(bf16[768,768]{1,0:T(8,128)(2,1)S(1)} %get-tuple-element.286.hidden_low.refs_0_, f32[8,768]{1,0:T(8,128)S(1)} %pad.17.refs_10_.norms.refs_4_, ...), custom_call_target="tpu_custom_call" | custom-call | flops 1811939328 | bytes 11813376 | tf_op jit(solution)/shard_map/pallas_call | solution.py:80
  179.3 7.7 %shard_map.339 = (bf16[768,768]{1,0:T(8,128)(2,1)S(1)}, bf16[2,768,768]{2,1,0:T(8,128)(2,1)S(1)}, bf16[768,768]{1,0:T(8,128)(2,1)S(1)}, f32[8,768]{1,0:T(8,128)S(1)}, f32[2,1,768]{2,1,0:T(1,128)S(1)}) custom-call(bf16[768,768]{1,0:T(8,128)(2,1)S(1)} %convolution_convert_fusion.grad, bf16[768,768]{1,0:T(8,128)(2,1)S(1)} %get-tuple-element.284.refs_0_, ...), custom_call_target="tpu_custom_call" | custom-call | flops 1811939328 | bytes 12417024 | tf_op jit(solution)/shard_map/pallas_call | solution.py:80
  188.4 5.8 %shard_map.340 = (bf16[2,256,576]{2,1,0:T(8,128)(2,1)S(1)}, bf16[2,256,576]{2,1,0:T(8,128)(2,1)S(1)}, f32[2,8,576]{2,1,0:T(8,128)S(1)}, bf16[256,768]{1,0:T(8,128)(2,1)S(1)}) custom-call(bf16[768,768]{1,0:T(8,128)(2,1)S(1)} %get-tuple-element.290.d_mid.d_mid_low.refs_0_.refs_8_, bf16[2,768,576]{2,1,0:T(8,128)(2,1)S(1)} %get-tuple-element.281.proj, ...), custom_call_target="tpu_custom_call" | custom-call | flops 553648128 | bytes 13200896 | tf_op jit(solution)/shard_map/pallas_call | solution.py:80
  195.5 9.8 %shard_map.341 = (bf16[2,768,576]{2,1,0:T(8,128)(2,1)S(1)}, f32[2,8,576]{2,1,0:T(8,128)S(1)}, bf16[768,768]{1,0:T(8,128)(2,1)S(1)}) custom-call(bf16[768,768]{1,0:T(8,128)(2,1)S(1)} %get-tuple-element.290.d_mid.d_mid_low.refs_0_.refs_8_, bf16[2,256,576]{2,1,0:T(8,128)(2,1)S(1)} %get-tuple-element.295.d_shared, ...), custom_call_target="tpu_custom_call" | custom-call | flops 1333788672 | bytes 14487552 | tf_op jit(solution)/shard_map/pallas_call | solution.py:80
  207.7 1.8 copy-done.21
  211.0 5.3 %shard_map.342 = bf16[2,384,2304]{2,1,0:T(8,128)(2,1)} custom-call(bf16[768,768]{1,0:T(8,128)(2,1)S(1)} %get-tuple-element.286.hidden_low.refs_0_, bf16[2,768,768]{2,1,0:T(8,128)(2,1)S(1)} %copy-done.21, bf16[768,768]{1,0:T(8,128)(2,1)S(1)} %get-tuple-element.299.refs_2_, bf16[2,768,768]{2,1,0:T(8,128)(2,1)S(1)} %get-tuple-element.300.refs_3_, ...), custom_call_target="tpu_custom_call" | custom-call | flops 1472200704 | bytes 8159232 | tf_op jit(solution)/shard_map/pallas_call | solution.py:80
  216.4 2.3 copy-done.29
  221.0 8.3 %shard_map.343 = (bf16[768,768]{1,0:T(8,128)(2,1)S(1)}, bf16[2,768,1536]{2,1,0:T(8,128)(2,1)S(1)}, f32[8,768]{1,0:T(8,128)S(1)}, f32[4,1,768]{2,1,0:T(1,128)S(1)}) custom-call(bf16[768,768]{1,0:T(8,128)(2,1)S(1)} %copy-done.57, bf16[256,768]{1,0:T(8,128)(2,1)S(1)} %copy-done.61, bf16[768,768]{1,0:T(8,128)(2,1)S(1)} %copy-done.55, ...), custom_call_target="tpu_custom_call" | custom-call | flops 1811939328 | bytes 11435520 | tf_op jit(solution)/shard_map/pallas_call | solution.py:80
  230.3 1.8 copy-done.35
  233.3 1.7 copy-done.19
  235.0 1.7 copy-done.22
  239.5 2.0 copy-done.36
  243.7 7.6 %shard_map.344 = (bf16[384,1152]{1,0:T(8,128)(2,1)}, f32[384,1152]{1,0:T(8,128)S(1)}, bf16[2,192,1152]{2,1,0:T(8,128)(2,1)}, f32[2,192,1152]{2,1,0:T(8,128)S(1)}) custom-call(bf16[2,384,2304]{2,1,0:T(8,128)(2,1)S(1)} %copy-done.36, bf16[768,768]{1,0:T(8,128)(2,1)S(1)} %copy-done.17, bf16[2,768,768]{2,1,0:T(8,128)(2,1)S(1)} %copy-done.22, ...), custom_call_target="tpu_custom_call" | custom-call | flops 1472200704 | bytes 10813440 | tf_op jit(solution)/shard_map/pallas_call | solution.py:80
  251.3 5.6 %shard_map.345 = bf16[2,384,3072]{2,1,0:T(8,128)(2,1)} custom-call(bf16[768,768]{1,0:T(8,128)(2,1)S(1)} %copy-done.11, bf16[2,768,1536]{2,1,0:T(8,128)(2,1)S(1)} %get-tuple-element.319.refs_1_.d_pre, bf16[768,768]{1,0:T(8,128)(2,1)S(1)} %copy-done.14, bf16[2,768,1536]{2,1,0:T(8,128)(2,1)S(1)} %get-tuple-element.318.refs_3_), custom_call_target="tpu_custom_call" | custom-call | flops 1811939328 | bytes 8257536 | tf_op jit(solution)/shard_map/pallas_call | solution.py:80
  261.4 7.9 %shard_map.346 = (bf16[768,768]{1,0:T(8,128)(2,1)S(1)}, f32[8,768]{1,0:T(8,128)S(1)}) custom-call(bf16[768,768]{1,0:T(8,128)(2,1)S(1)} %copy-done.14, bf16[2,768,1536]{2,1,0:T(8,128)(2,1)S(1)} %get-tuple-element.319.refs_1_.d_pre, bf16[768,768]{1,0:T(8,128)(2,1)S(1)} %copy-done.53, f32[768,1]{1,0:T(8,128)S(1)} %copy-done.59, ...), custom_call_target="tpu_custom_call" | custom-call | flops 1811939328 | bytes 8873472 | tf_op jit(solution)/shard_map/pallas_call | solution.py:80
  269.3 1.7 copy-done.15
  270.9 5.8 %shard_map.347 = (bf16[384,1536]{1,0:T(8,128)(2,1)}, f32[384,1536]{1,0:T(8,128)S(1)}, bf16[2,192,1536]{2,1,0:T(8,128)(2,1)}, f32[2,192,1536]{2,1,0:T(8,128)S(1)}) custom-call(bf16[2,384,3072]{2,1,0:T(8,128)(2,1)S(1)} %collective-permute-done.32.got, bf16[768,768]{1,0:T(8,128)(2,1)S(1)} %copy-done.12, ...), custom_call_target="tpu_custom_call" | custom-call | flops 1811939328 | bytes 11796480 | tf_op jit(solution)/shard_map/pallas_call | solution.py:80
  288.6 10.2 %shard_map.348 = (bf16[2,256,1152]{2,1,0:T(8,128)(2,1)S(1)}, bf16[2,256,1152]{2,1,0:T(8,128)(2,1)S(1)}, f32[2,8,1152]{2,1,0:T(8,128)S(1)}, bf16[256,768]{1,0:T(8,128)(2,1)S(1)}) custom-call(bf16[768,768]{1,0:T(8,128)(2,1)S(1)} %get-tuple-element.364.d_mid.d_mid_low.refs_4_, bf16[2,768,1152]{2,1,0:T(8,128)(2,1)S(1)} %copy-done.1, ...), custom_call_target="tpu_custom_call" | custom-call | flops 1107296256 | bytes 14595584 | tf_op jit(solution)/shard_map/pallas_call | solution.py:80
  301.0 11.8 %shard_map.349 = (bf16[2,768,1152]{2,1,0:T(8,128)(2,1)S(1)}, f32[2,8,1152]{2,1,0:T(8,128)S(1)}) custom-call(bf16[768,768]{1,0:T(8,128)(2,1)S(1)} %get-tuple-element.364.d_mid.d_mid_low.refs_4_, bf16[2,256,1152]{2,1,0:T(8,128)(2,1)S(1)} %get-tuple-element.341.d_shared, bf16[2,768,1152]{2,1,0:T(8,128)(2,1)S(1)} %copy-done.1, f32[2,8,512]{2,1,0:T(8,128)S(1)} %copy-done.72, ...), custom_call_target="tpu_custom_call" | custom-call | flops 1308622848 | bytes 7329792 | tf_op jit(solution)/shard_map/pallas_call | solution.py:80
  312.9 4.5 %shard_map.350 = bf16[2,384,1536]{2,1,0:T(8,128)(2,1)} custom-call(bf16[768,768]{1,0:T(8,128)(2,1)S(1)} %copy-done.7, bf16[2,768,1152]{2,1,0:T(8,128)(2,1)S(1)} %get-tuple-element.365.refs_1_.d_proj, bf16[256,768]{1,0:T(8,128)(2,1)S(1)} %convolution_convert_fusion.2.away.refs_2_, bf16[2,256,1152]{2,1,0:T(8,128)(2,1)S(1)} %get-tuple-element.344.refs_3_, ...), custom_call_target="tpu_custom_call" | custom-call | flops 1132462080 | bytes 5505024 | tf_op jit(solution)/shard_map/pallas_call | solution.py:80
  320.6 1.7 collective-permute-done.40
  322.3 2.5 convert_add_fusion
  326.2 1.7 convert_add_fusion.1
  329.8 4.9 %collective-permute-start.45 = (bf16[48,2304]{1,0:T(8,128)(2,1)S(1)}, bf16[48,2304]{1,0:T(8,128)(2,1)S(1)}, u32[]{:S(2)}, u32[]{:S(2)}) collective-permute-start(bf16[48,2304]{1,0:T(8,128)(2,1)S(1)} %copy-done.99), channel_id=1, source_target_pairs={{0,8},{2,10},{4,12},{6,14},{16,0},{18,2},{20,4},{22,6},{24,16},{26... | collective-permute-start | bytes 663560 | tf_op jit(solution)/shard_map/ppermute | solution.py:41
  334.7 2.4 collective-permute-start.46
  337.1 2.8 collective-permute-done.44
  339.9 5.7 %shard_map.351 = (bf16[384,768]{1,0:T(8,128)(2,1)S(1)}, f32[384,768]{1,0:T(8,128)S(1)}, bf16[2,192,768]{2,1,0:T(8,128)(2,1)S(1)}, f32[2,192,768]{2,1,0:T(8,128)S(1)}) custom-call(bf16[2,384,1536]{2,1,0:T(8,128)(2,1)} %collective-permute-done.37.got, bf16[768,768]{1,0:T(8,128)(2,1)S(1)} %copy-done.8, bf16[2,768,1152]{2,1,0:T(8,128)(2,1)S(1)} %copy-done.3, ...), custom_call_target="tpu_custom_call" | custom-call | flops 1132462080 | bytes 7274496 | tf_op jit(solution)/shard_map/pallas_call | solution.py:80
  346.9 4.5 %collective-permute-done.45 = bf16[48,2304]{1,0:T(8,128)(2,1)S(1)} collective-permute-done((bf16[48,2304]{1,0:T(8,128)(2,1)S(1)}, bf16[48,2304]{1,0:T(8,128)(2,1)S(1)}, u32[]{:S(2)}, u32[]{:S(2)}) %collective-permute-start.45) | collective-permute-done | bytes 221216 | tf_op jit(solution)/shard_map/ppermute | solution.py:41
  353.8 2.6 collective-permute-start.54
  357.9 5.4 %shard_map.352 = f32[768,768]{1,0:T(8,128)S(1)} custom-call(bf16[768,768]{1,0:T(8,128)(2,1)S(1)} %copy-done.5, bf16[2,768,1152]{2,1,0:T(8,128)(2,1)S(1)} %copy-done.3, bf16[2,384,1664]{2,1,0:T(8,128)(2,1)S(1)} %bitcast.150, bf16[2,384,1664]{2,1,0:T(8,128)(2,1)} %collective-permute-done.13.refs_1_.refs_3_.refs_5_.refs_7_.out_two, ...), custom_call_target="tpu_custom_call" | custom-call | flops 1358954496 | bytes 11206656 | tf_op jit(solution)/shard_map/pallas_call | solution.py:80
  365.5 4.3 %collective-permute-done.41 = bf16[384,768]{1,0:T(8,128)(2,1)S(1)} collective-permute-done((bf16[384,768]{1,0:T(8,128)(2,1)S(1)}, bf16[384,768]{1,0:T(8,128)(2,1)S(1)}, u32[]{:S(2)}, u32[]{:S(2)}) %collective-permute-start.41) | collective-permute-done | bytes 589856 | tf_op jit(solution)/shard_map/ppermute | solution.py:21
  369.8 2.5 collective-permute-start.55
  372.3 3.8 collective-permute-start.56
  383.7 4.5 %collective-permute-done.51 = bf16[256,768]{1,0:T(8,128)(2,1)S(1)} collective-permute-done((bf16[256,768]{1,0:T(8,128)(2,1)S(1)}, bf16[256,768]{1,0:T(8,128)(2,1)S(1)}, u32[]{:S(2)}, u32[]{:S(2)}) %collective-permute-start.51) | collective-permute-done | bytes 393248 | tf_op jit(solution)/shard_map/ppermute | solution.py:21
  392.1 1.6 pad_maximum_fusion.1
  393.7 4.1 collective-permute-done.57
  398.2 4.4 %collective-permute-start.59 = (bf16[48,1536]{1,0:T(8,128)(2,1)S(1)}, bf16[48,1536]{1,0:T(8,128)(2,1)S(1)}, u32[]{:S(2)}, u32[]{:S(2)}) collective-permute-start(bf16[48,1536]{1,0:T(8,128)(2,1)S(1)} %get-tuple-element.443), channel_id=1, source_target_pairs={{0,24},{2,26},{4,28},{6,30},{16,8},{18,10},{20,12},{22,14},{24,0},... | collective-permute-start | bytes 442376 | tf_op jit(solution)/shard_map/ppermute | solution.py:41
  402.6 1.9 collective-permute-start.60
  405.6 6.3 %collective-permute-done.61 = f32[22,768]{1,0:T(8,128)S(1)} collective-permute-done((f32[22,768]{1,0:T(8,128)S(1)}, f32[22,768]{1,0:T(8,128)S(1)}, u32[]{:S(2)}, u32[]{:S(2)}) %collective-permute-start.61) | collective-permute-done | bytes 67616 | tf_op jit(solution)/shard_map/ppermute | solution.py:783
  (435 shorter events, 106.6 us)
Async XLA Ops:
  3.2 10.8 %collective-permute-start = (bf16[48,1664]{1,0:T(8,128)(2,1)S(1)}, bf16[48,1664]{1,0:T(8,128)(2,1)S(1)}, u32[]{:S(2)}, u32[]{:S(2)}) collective-permute-start(bf16[48,1664]{1,0:T(8,128)(2,1)S(1)} %shard_map.322.refs_0_), channel_id=1, source_target_pairs={{0,16},{2,18},{4,20},{6,22},{16,24},{18,26},{20,28},{22,30},{24,8}... | collective-permute-start | bytes 479240 | tf_op jit(solution)/shard_map/ppermute | solution.py:41
  7.3 9.8 %collective-permute-start.1 = (bf16[48,1664]{1,0:T(8,128)(2,1)S(1)}, bf16[48,1664]{1,0:T(8,128)(2,1)S(1)}, u32[]{:S(2)}, u32[]{:S(2)}) collective-permute-start(bf16[48,1664]{1,0:T(8,128)(2,1)S(1)} %shard_map.322.refs_0_), channel_id=1, source_target_pairs={{0,24},{2,26},{4,28},{6,30},{16,8},{18,10},{20,12},{22,14},{24,0},... | collective-permute-start | bytes 479240 | tf_op jit(solution)/shard_map/ppermute | solution.py:41
  8.6 14.1 %collective-permute-start.2 = (bf16[48,1664]{1,0:T(8,128)(2,1)S(1)}, bf16[48,1664]{1,0:T(8,128)(2,1)S(1)}, u32[]{:S(2)}, u32[]{:S(2)}) collective-permute-start(bf16[48,1664]{1,0:T(8,128)(2,1)S(1)} %shard_map.322.refs_0_), channel_id=1, source_target_pairs={{0,8},{2,10},{4,12},{6,14},{16,0},{18,2},{20,4},{22,6},{24,16},{26... | collective-permute-start | bytes 479240 | tf_op jit(solution)/shard_map/ppermute | solution.py:41
  11.7 11.0 %collective-permute-start.3 = (bf16[256,768]{1,0:T(8,128)(2,1)}, bf16[256,768]{1,0:T(8,128)(2,1)}, u32[]{:S(2)}, u32[]{:S(2)}) collective-permute-start(bf16[256,768]{1,0:T(8,128)(2,1)} %get-tuple-element.436), channel_id=1, source_target_pairs={{0,1},{1,0},{2,3},{3,2},{4,5},{5,4},{6,7},{7,6},{8,9},{9,8},{10,11... | collective-permute-start | bytes 1179656 | tf_op jit(solution)/shard_map/ppermute | solution.py:21
  14.0 49.3 %copy-start.102 = (s32[512]{0:T(512)}, s32[512]{0:T(512)S(1)}, u32[]{:S(2)}) copy-start(s32[512]{0:T(512)S(1)} %add_select_fusion.7) | copy-start | bytes 6148
  22.8 12.6 %collective-permute-start.5 = (bf16[4,48,896]{2,1,0:T(8,128)(2,1)S(1)}, bf16[4,48,896]{2,1,0:T(8,128)(2,1)S(1)}, u32[]{:S(2)}, u32[]{:S(2)}) collective-permute-start(bf16[4,48,896]{2,1,0:T(8,128)(2,1)S(1)} %get-tuple-element.223.refs_2_), channel_id=1, source_target_pairs={{0,1},{1,0},{2,3},{3,2},{4,5},{5,4},{6,7},{7,6},{8,9},{9,8},{10,11... | collective-permute-start | bytes 1032200 | tf_op jit(solution)/shard_map/ppermute | solution.py:21
  24.4 11.0 %collective-permute-start.4 = (bf16[4,48,768]{2,1,0:T(8,128)(2,1)S(1)}, bf16[4,48,768]{2,1,0:T(8,128)(2,1)S(1)}, u32[]{:S(2)}, u32[]{:S(2)}) collective-permute-start(bf16[4,48,768]{2,1,0:T(8,128)(2,1)S(1)} %get-tuple-element.222.refs_0_), channel_id=1, source_target_pairs={{0,4},{2,6},{4,0},{6,2},{8,12},{10,14},{12,8},{14,10},{16,20},{18,... | collective-permute-start | bytes 884744 | tf_op jit(solution)/shard_map/ppermute | solution.py:26
  25.9 9.5 %collective-permute-start.8 = (bf16[48,3072]{1,0:T(8,128)(2,1)S(1)}, bf16[48,3072]{1,0:T(8,128)(2,1)S(1)}, u32[]{:S(2)}, u32[]{:S(2)}) collective-permute-start(bf16[48,3072]{1,0:T(8,128)(2,1)S(1)} %get-tuple-element.239.refs_0_), channel_id=1, source_target_pairs={{0,16},{2,18},{4,20},{6,22},{16,24},{18,26},{20,28},{22,30},{24,8}... | collective-permute-start | bytes 884744 | tf_op jit(solution)/shard_map/ppermute | solution.py:41
  27.3 8.1 %collective-permute-start.6 = (bf16[48,1152]{1,0:T(8,128)(2,1)S(1)}, bf16[48,1152]{1,0:T(8,128)(2,1)S(1)}, u32[]{:S(2)}, u32[]{:S(2)}) collective-permute-start(bf16[48,1152]{1,0:T(8,128)(2,1)S(1)} %get-tuple-element.224.refs_0_), channel_id=1, source_target_pairs={{0,4},{2,6},{4,0},{6,2},{8,12},{10,14},{12,8},{14,10},{16,20},{18,... | collective-permute-start | bytes 331784 | tf_op jit(solution)/shard_map/ppermute | solution.py:26
  27.9 7.5 %collective-permute-start.7 = (bf16[48,1152]{1,0:T(8,128)(2,1)S(1)}, bf16[48,1152]{1,0:T(8,128)(2,1)S(1)}, u32[]{:S(2)}, u32[]{:S(2)}) collective-permute-start(bf16[48,1152]{1,0:T(8,128)(2,1)S(1)} %get-tuple-element.225.refs_2_), channel_id=1, source_target_pairs={{0,1},{1,0},{2,3},{3,2},{4,5},{5,4},{6,7},{7,6},{8,9},{9,8},{10,11... | collective-permute-start | bytes 331784 | tf_op jit(solution)/shard_map/ppermute | solution.py:21
  35.5 21.3 %collective-permute-start.10 = (bf16[2,4,48,896]{3,2,1,0:T(8,128)(2,1)S(1)}, bf16[2,4,48,896]{3,2,1,0:T(8,128)(2,1)S(1)}, u32[]{:S(2)}, u32[]{:S(2)}) collective-permute-start(bf16[2,4,48,896]{3,2,1,0:T(8,128)(2,1)S(1)} %get-tuple-element.230.refs_2_), channel_id=1, source_target_pairs={{0,4},{2,6},{4,0},{6,2},{8,12},{10,14},{12,8},{14,10},{16,20},{18,... | collective-permute-start | bytes 2064392 | tf_op jit(solution)/shard_map/ppermute | solution.py:26
  37.1 19.8 %collective-permute-start.9 = (bf16[2,4,48,768]{3,2,1,0:T(8,128)(2,1)S(1)}, bf16[2,4,48,768]{3,2,1,0:T(8,128)(2,1)S(1)}, u32[]{:S(2)}, u32[]{:S(2)}) collective-permute-start(bf16[2,4,48,768]{3,2,1,0:T(8,128)(2,1)S(1)} %get-tuple-element.229.refs_0_), channel_id=1, source_target_pairs={{0,1},{1,0},{2,3},{3,2},{4,5},{5,4},{6,7},{7,6},{8,9},{9,8},{10,11... | collective-permute-start | bytes 1769480 | tf_op jit(solution)/shard_map/ppermute | solution.py:21
  38.4 11.7 %collective-permute-start.11 = (bf16[48,3072]{1,0:T(8,128)(2,1)S(1)}, bf16[48,3072]{1,0:T(8,128)(2,1)S(1)}, u32[]{:S(2)}, u32[]{:S(2)}) collective-permute-start(bf16[48,3072]{1,0:T(8,128)(2,1)S(1)} %get-tuple-element.239.refs_0_), channel_id=1, source_target_pairs={{0,24},{2,26},{4,28},{6,30},{16,8},{18,10},{20,12},{22,14},{24,0},... | collective-permute-start | bytes 884744 | tf_op jit(solution)/shard_map/ppermute | solution.py:41
  40.9 16.0 %collective-permute-start.12 = (bf16[48,3072]{1,0:T(8,128)(2,1)S(1)}, bf16[48,3072]{1,0:T(8,128)(2,1)S(1)}, u32[]{:S(2)}, u32[]{:S(2)}) collective-permute-start(bf16[48,3072]{1,0:T(8,128)(2,1)S(1)} %get-tuple-element.239.refs_0_), channel_id=1, source_target_pairs={{0,8},{2,10},{4,12},{6,14},{16,0},{18,2},{20,4},{22,6},{24,16},{26... | collective-permute-start | bytes 884744 | tf_op jit(solution)/shard_map/ppermute | solution.py:41
  57.0 19.7 %collective-permute-start.13 = (bf16[2,384,1664]{2,1,0:T(8,128)(2,1)S(1)}, bf16[2,384,1664]{2,1,0:T(8,128)(2,1)}, u32[]{:S(2)}, u32[]{:S(2)}) collective-permute-start(bf16[2,384,1664]{2,1,0:T(8,128)(2,1)S(1)} %bitcast.136), channel_id=1, source_target_pairs={{0,2},{2,0},{4,6},{6,4},{8,10},{10,8},{12,14},{14,12},{16,18},{18,... | collective-permute-start | bytes 7667720 | tf_op jit(solution)/shard_map/ppermute | solution.py:31
  58.2 17.2 %collective-permute-start.14 = (bf16[4,48,1536]{2,1,0:T(8,128)(2,1)}, bf16[4,48,1536]{2,1,0:T(8,128)(2,1)}, u32[]{:S(2)}, u32[]{:S(2)}) collective-permute-start(bf16[4,48,1536]{2,1,0:T(8,128)(2,1)} %get-tuple-element.243.refs_0_), channel_id=1, source_target_pairs={{0,4},{2,6},{4,0},{6,2},{8,12},{10,14},{12,8},{14,10},{16,20},{18,... | collective-permute-start | bytes 1769480 | tf_op jit(solution)/shard_map/ppermute | solution.py:26
  58.7 18.0 %collective-permute-start.15 = (bf16[4,48,1536]{2,1,0:T(8,128)(2,1)}, bf16[4,48,1536]{2,1,0:T(8,128)(2,1)}, u32[]{:S(2)}, u32[]{:S(2)}) collective-permute-start(bf16[4,48,1536]{2,1,0:T(8,128)(2,1)} %get-tuple-element.244.refs_2_), channel_id=1, source_target_pairs={{0,1},{1,0},{2,3},{3,2},{4,5},{5,4},{6,7},{7,6},{8,9},{9,8},{10,11... | collective-permute-start | bytes 1769480 | tf_op jit(solution)/shard_map/ppermute | solution.py:21
  60.4 15.0 %collective-permute-start.16 = (bf16[3456]{0:T(1024)(128)(2,1)}, bf16[3456]{0:T(1024)(128)(2,1)}, u32[]{:S(2)}, u32[]{:S(2)}) collective-permute-start(bf16[3456]{0:T(1024)(128)(2,1)} %concatenate.65), channel_id=1, source_target_pairs={{0,1},{1,0},{2,3},{3,2},{4,5},{5,4},{6,7},{7,6},{8,9},{9,8},{10,11... | collective-permute-start | bytes 20744 | tf_op jit(solution)/shard_map/ppermute | solution.py:21
  61.5 22.7 %collective-permute-start.17 = (bf16[256,768]{1,0:T(8,128)(2,1)}, bf16[256,768]{1,0:T(8,128)(2,1)}, u32[]{:S(2)}, u32[]{:S(2)}) collective-permute-start(bf16[256,768]{1,0:T(8,128)(2,1)} %get-tuple-element.435), channel_id=1, source_target_pairs={{0,1},{1,0},{2,3},{3,2},{4,5},{5,4},{6,7},{7,6},{8,9},{9,8},{10,11... | collective-permute-start | bytes 1179656 | tf_op jit(solution)/shard_map/ppermute | solution.py:21
  75.4 23.7 %collective-permute-start.18 = (bf16[2,48,2304]{2,1,0:T(8,128)(2,1)}, bf16[2,48,2304]{2,1,0:T(8,128)(2,1)}, u32[]{:S(2)}, u32[]{:S(2)}) collective-permute-start(bf16[2,48,2304]{2,1,0:T(8,128)(2,1)} %shard_map.330.refs_0_), channel_id=1, source_target_pairs={{0,16},{2,18},{4,20},{6,22},{16,24},{18,26},{20,28},{22,30},{24,8}... | collective-permute-start | bytes 1327112 | tf_op jit(solution)/shard_map/ppermute | solution.py:41
  75.4 23.7 %collective-permute-start.19 = (bf16[2,48,2304]{2,1,0:T(8,128)(2,1)}, bf16[2,48,2304]{2,1,0:T(8,128)(2,1)}, u32[]{:S(2)}, u32[]{:S(2)}) collective-permute-start(bf16[2,48,2304]{2,1,0:T(8,128)(2,1)} %shard_map.330.refs_0_), channel_id=1, source_target_pairs={{0,24},{2,26},{4,28},{6,30},{16,8},{18,10},{20,12},{22,14},{24,0},... | collective-permute-start | bytes 1327112 | tf_op jit(solution)/shard_map/ppermute | solution.py:41
  77.5 55.1 %copy-start.95 = (bf16[1,3456]{1,0:T(2,128)(2,1)}, bf16[1,3456]{1,0:T(2,128)(2,1)S(1)}, u32[]{:S(2)}) copy-start(bf16[1,3456]{1,0:T(2,128)(2,1)S(1)} %stack.58) | copy-start | bytes 20740
  80.6 33.8 %collective-permute-start.20 = (bf16[2,4,48,1536]{3,2,1,0:T(8,128)(2,1)}, bf16[2,4,48,1536]{3,2,1,0:T(8,128)(2,1)}, u32[]{:S(2)}, u32[]{:S(2)}) collective-permute-start(bf16[2,4,48,1536]{3,2,1,0:T(8,128)(2,1)} %get-tuple-element.263.refs_0_), channel_id=1, source_target_pairs={{0,1},{1,0},{2,3},{3,2},{4,5},{5,4},{6,7},{7,6},{8,9},{9,8},{10,11... | collective-permute-start | bytes 3538952 | tf_op jit(solution)/shard_map/ppermute | solution.py:21
  81.7 32.7 %collective-permute-start.21 = (bf16[2,4,48,1536]{3,2,1,0:T(8,128)(2,1)}, bf16[2,4,48,1536]{3,2,1,0:T(8,128)(2,1)}, u32[]{:S(2)}, u32[]{:S(2)}) collective-permute-start(bf16[2,4,48,1536]{3,2,1,0:T(8,128)(2,1)} %get-tuple-element.265.refs_2_), channel_id=1, source_target_pairs={{0,4},{2,6},{4,0},{6,2},{8,12},{10,14},{12,8},{14,10},{16,20},{18,... | collective-permute-start | bytes 3538952 | tf_op jit(solution)/shard_map/ppermute | solution.py:26
  84.2 30.2 %collective-permute-start.22 = (bf16[2,48,2304]{2,1,0:T(8,128)(2,1)}, bf16[2,48,2304]{2,1,0:T(8,128)(2,1)S(1)}, u32[]{:S(2)}, u32[]{:S(2)}) collective-permute-start(bf16[2,48,2304]{2,1,0:T(8,128)(2,1)} %shard_map.330.refs_0_), channel_id=1, source_target_pairs={{0,8},{2,10},{4,12},{6,14},{16,0},{18,2},{20,4},{22,6},{24,16},{26... | collective-permute-start | bytes 1327112 | tf_op jit(solution)/shard_map/ppermute | solution.py:41
  119.3 13.3 %collective-permute-start.23 = (bf16[2,384,3072]{2,1,0:T(8,128)(2,1)}, bf16[2,384,3072]{2,1,0:T(8,128)(2,1)}, u32[]{:S(2)}, u32[]{:S(2)}) collective-permute-start(bf16[2,384,3072]{2,1,0:T(8,128)(2,1)} %bitcast.23.up_one.down_one), channel_id=1, source_target_pairs={{0,2},{2,0},{4,6},{6,4},{8,10},{10,8},{12,14},{14,12},{16,18},{18,... | collective-permute-start | bytes 14155784 | tf_op jit(solution)/shard_map/ppermute | solution.py:31
  119.5 12.0 %collective-permute-start.26 = (bf16[256,768]{1,0:T(8,128)(2,1)S(1)}, bf16[256,768]{1,0:T(8,128)(2,1)S(1)}, u32[]{:S(2)}, u32[]{:S(2)}) collective-permute-start(bf16[256,768]{1,0:T(8,128)(2,1)S(1)} %get-tuple-element.433), channel_id=1, source_target_pairs={{0,1},{1,0},{2,3},{3,2},{4,5},{5,4},{6,7},{7,6},{8,9},{9,8},{10,11... | collective-permute-start | bytes 1179656 | tf_op jit(solution)/shard_map/ppermute | solution.py:21
  123.3 26.8 %collective-permute-start.24 = (bf16[2,4,48,1152]{3,2,1,0:T(8,128)(2,1)}, bf16[2,4,48,1152]{3,2,1,0:T(8,128)(2,1)}, u32[]{:S(2)}, u32[]{:S(2)}) collective-permute-start(bf16[2,4,48,1152]{3,2,1,0:T(8,128)(2,1)} %get-tuple-element.274.refs_0_), channel_id=1, source_target_pairs={{0,1},{1,0},{2,3},{3,2},{4,5},{5,4},{6,7},{7,6},{8,9},{9,8},{10,11... | collective-permute-start | bytes 2654216 | tf_op jit(solution)/shard_map/ppermute | solution.py:21
  124.2 25.9 %collective-permute-start.25 = (bf16[2,4,48,1152]{3,2,1,0:T(8,128)(2,1)}, bf16[2,4,48,1152]{3,2,1,0:T(8,128)(2,1)}, u32[]{:S(2)}, u32[]{:S(2)}) collective-permute-start(bf16[2,4,48,1152]{3,2,1,0:T(8,128)(2,1)} %get-tuple-element.275.refs_2_), channel_id=1, source_target_pairs={{0,4},{2,6},{4,0},{6,2},{8,12},{10,14},{12,8},{14,10},{16,20},{18,... | collective-permute-start | bytes 2654216 | tf_op jit(solution)/shard_map/ppermute | solution.py:26
  152.5 6.3 %collective-permute-start.27 = (bf16[2,384,2304]{2,1,0:T(8,128)(2,1)S(1)}, bf16[2,384,2304]{2,1,0:T(8,128)(2,1)S(1)}, u32[]{:S(2)}, u32[]{:S(2)}) collective-permute-start(bf16[2,384,2304]{2,1,0:T(8,128)(2,1)S(1)} %bitcast.120), channel_id=1, source_target_pairs={{0,2},{2,0},{4,6},{6,4},{8,10},{10,8},{12,14},{14,12},{16,18},{18,... | collective-permute-start | bytes 10616840 | tf_op jit(solution)/shard_map/ppermute | solution.py:31
  152.9 12.1 %collective-permute-start.28 = (bf16[256,768]{1,0:T(8,128)(2,1)S(1)}, bf16[256,768]{1,0:T(8,128)(2,1)S(1)}, u32[]{:S(2)}, u32[]{:S(2)}) collective-permute-start(bf16[256,768]{1,0:T(8,128)(2,1)S(1)} %slice.423), channel_id=1, source_target_pairs={{0,1},{1,0},{2,3},{3,2},{4,5},{5,4},{6,7},{7,6},{8,9},{9,8},{10,11... | collective-permute-start | bytes 1179656 | tf_op jit(solution)/shard_map/ppermute | solution.py:21
  177.9 17.6 %collective-permute-start.29 = (bf16[256,768]{1,0:T(8,128)(2,1)S(1)}, bf16[256,768]{1,0:T(8,128)(2,1)S(1)}, u32[]{:S(2)}, u32[]{:S(2)}) collective-permute-start(bf16[256,768]{1,0:T(8,128)(2,1)S(1)} %slice.682), channel_id=1, source_target_pairs={{0,1},{1,0},{2,3},{3,2},{4,5},{5,4},{6,7},{7,6},{8,9},{9,8},{10,11... | collective-permute-start | bytes 1179656 | tf_op jit(solution)/shard_map/ppermute | solution.py:21
  194.3 13.4 %collective-permute-start.30 = (bf16[256,768]{1,0:T(8,128)(2,1)S(1)}, bf16[256,768]{1,0:T(8,128)(2,1)S(1)}, u32[]{:S(2)}, u32[]{:S(2)}) collective-permute-start(bf16[256,768]{1,0:T(8,128)(2,1)S(1)} %get-tuple-element.302), channel_id=1, source_target_pairs={{0,1},{1,0},{2,3},{3,2},{4,5},{5,4},{6,7},{7,6},{8,9},{9,8},{10,11... | collective-permute-start | bytes 1179656 | tf_op jit(solution)/shard_map/ppermute | solution.py:21
  216.4 14.0 %collective-permute-start.31 = (bf16[2,384,2304]{2,1,0:T(8,128)(2,1)}, bf16[2,384,2304]{2,1,0:T(8,128)(2,1)S(1)}, u32[]{:S(2)}, u32[]{:S(2)}) collective-permute-start(bf16[2,384,2304]{2,1,0:T(8,128)(2,1)} %shard_map.342), channel_id=1, source_target_pairs={{0,2},{2,0},{4,6},{6,4},{8,10},{10,8},{12,14},{14,12},{16,18},{18,... | collective-permute-start | bytes 10616840 | tf_op jit(solution)/shard_map/ppermute | solution.py:31
  256.9 12.3 %collective-permute-start.32 = (bf16[2,384,3072]{2,1,0:T(8,128)(2,1)}, bf16[2,384,3072]{2,1,0:T(8,128)(2,1)S(1)}, u32[]{:S(2)}, u32[]{:S(2)}) collective-permute-start(bf16[2,384,3072]{2,1,0:T(8,128)(2,1)} %shard_map.345), channel_id=1, source_target_pairs={{0,2},{2,0},{4,6},{6,4},{8,10},{10,8},{12,14},{14,12},{16,18},{18,... | collective-permute-start | bytes 14155784 | tf_op jit(solution)/shard_map/ppermute | solution.py:31
  257.6 21.9 %collective-permute-start.33 = (bf16[384,1152]{1,0:T(8,128)(2,1)}, bf16[384,1152]{1,0:T(8,128)(2,1)}, u32[]{:S(2)}, u32[]{:S(2)}) collective-permute-start(bf16[384,1152]{1,0:T(8,128)(2,1)} %get-tuple-element.315), channel_id=1, source_target_pairs={{0,1},{1,0},{2,3},{3,2},{4,5},{5,4},{6,7},{7,6},{8,9},{9,8},{10,11... | collective-permute-start | bytes 2654216 | tf_op jit(solution)/shard_map/ppermute | solution.py:21
  258.5 21.6 %collective-permute-start.34 = (bf16[2,192,1152]{2,1,0:T(8,128)(2,1)}, bf16[2,192,1152]{2,1,0:T(8,128)(2,1)}, u32[]{:S(2)}, u32[]{:S(2)}) collective-permute-start(bf16[2,192,1152]{2,1,0:T(8,128)(2,1)} %get-tuple-element.316), channel_id=1, source_target_pairs={{0,4},{2,6},{4,0},{6,2},{8,12},{10,14},{12,8},{14,10},{16,20},{18,... | collective-permute-start | bytes 2654216 | tf_op jit(solution)/shard_map/ppermute | solution.py:26
  283.4 15.4 %collective-permute-start.36 = (bf16[192,1152]{1,0:T(8,128)(2,1)S(1)}, bf16[192,1152]{1,0:T(8,128)(2,1)S(1)}, u32[]{:S(2)}, u32[]{:S(2)}) collective-permute-start(bf16[192,1152]{1,0:T(8,128)(2,1)S(1)} %fusion.21), channel_id=1, source_target_pairs={{0,1},{1,0},{2,3},{3,2},{4,5},{5,4},{6,7},{7,6},{8,9},{9,8},{10,11... | collective-permute-start | bytes 1327112 | tf_op jit(solution)/shard_map/ppermute | solution.py:21
  284.6 14.2 %collective-permute-start.35 = (bf16[192,1152]{1,0:T(8,128)(2,1)S(1)}, bf16[192,1152]{1,0:T(8,128)(2,1)S(1)}, u32[]{:S(2)}, u32[]{:S(2)}) collective-permute-start(bf16[192,1152]{1,0:T(8,128)(2,1)S(1)} %slice.680), channel_id=1, source_target_pairs={{0,4},{2,6},{4,0},{6,2},{8,12},{10,14},{12,8},{14,10},{16,20},{18,... | collective-permute-start | bytes 1327112 | tf_op jit(solution)/shard_map/ppermute | solution.py:26
  286.9 32.9 %collective-permute-start.38 = (bf16[384,1536]{1,0:T(8,128)(2,1)}, bf16[384,1536]{1,0:T(8,128)(2,1)}, u32[]{:S(2)}, u32[]{:S(2)}) collective-permute-start(bf16[384,1536]{1,0:T(8,128)(2,1)} %get-tuple-element.325), channel_id=1, source_target_pairs={{0,1},{1,0},{2,3},{3,2},{4,5},{5,4},{6,7},{7,6},{8,9},{9,8},{10,11... | collective-permute-start | bytes 3538952 | tf_op jit(solution)/shard_map/ppermute | solution.py:21
  288.1 32.6 %collective-permute-start.39 = (bf16[2,192,1536]{2,1,0:T(8,128)(2,1)}, bf16[2,192,1536]{2,1,0:T(8,128)(2,1)}, u32[]{:S(2)}, u32[]{:S(2)}) collective-permute-start(bf16[2,192,1536]{2,1,0:T(8,128)(2,1)} %get-tuple-element.326), channel_id=1, source_target_pairs={{0,4},{2,6},{4,0},{6,2},{8,12},{10,14},{12,8},{14,10},{16,20},{18,... | collective-permute-start | bytes 3538952 | tf_op jit(solution)/shard_map/ppermute | solution.py:26
  317.4 19.6 %collective-permute-start.37 = (bf16[2,384,1536]{2,1,0:T(8,128)(2,1)}, bf16[2,384,1536]{2,1,0:T(8,128)(2,1)}, u32[]{:S(2)}, u32[]{:S(2)}) collective-permute-start(bf16[2,384,1536]{2,1,0:T(8,128)(2,1)} %shard_map.350), channel_id=1, source_target_pairs={{0,2},{2,0},{4,6},{6,4},{8,10},{10,8},{12,14},{14,12},{16,18},{18,... | collective-permute-start | bytes 7077896 | tf_op jit(solution)/shard_map/ppermute | solution.py:31
  317.6 4.7 %collective-permute-start.40 = (f32[22,768]{1,0:T(8,128)S(1)}, f32[22,768]{1,0:T(8,128)S(1)}, u32[]{:S(2)}, u32[]{:S(2)}) collective-permute-start(f32[22,768]{1,0:T(8,128)S(1)} %pad_maximum_fusion.10), channel_id=1, source_target_pairs={{0,1},{1,0},{2,3},{3,2},{4,5},{5,4},{6,7},{7,6},{8,9},{9,8},{10,11... | collective-permute-start | bytes 202760 | tf_op jit(solution)/shard_map/ppermute | solution.py:21
  324.9 15.0 %collective-permute-start.44 = (bf16[192,1536]{1,0:T(8,128)(2,1)S(1)}, bf16[192,1536]{1,0:T(8,128)(2,1)S(1)}, u32[]{:S(2)}, u32[]{:S(2)}) collective-permute-start(bf16[192,1536]{1,0:T(8,128)(2,1)S(1)} %fusion.17), channel_id=1, source_target_pairs={{0,1},{1,0},{2,3},{3,2},{4,5},{5,4},{6,7},{7,6},{8,9},{9,8},{10,11... | collective-permute-start | bytes 1769480 | tf_op jit(solution)/shard_map/ppermute | solution.py:21
  328.0 17.6 %collective-permute-start.43 = (bf16[192,1536]{1,0:T(8,128)(2,1)S(1)}, bf16[192,1536]{1,0:T(8,128)(2,1)S(1)}, u32[]{:S(2)}, u32[]{:S(2)}) collective-permute-start(bf16[192,1536]{1,0:T(8,128)(2,1)S(1)} %slice.679), channel_id=1, source_target_pairs={{0,4},{2,6},{4,0},{6,2},{8,12},{10,14},{12,8},{14,10},{16,20},{18,... | collective-permute-start | bytes 1769480 | tf_op jit(solution)/shard_map/ppermute | solution.py:26
  329.8 21.6 %collective-permute-start.45 = (bf16[48,2304]{1,0:T(8,128)(2,1)S(1)}, bf16[48,2304]{1,0:T(8,128)(2,1)S(1)}, u32[]{:S(2)}, u32[]{:S(2)}) collective-permute-start(bf16[48,2304]{1,0:T(8,128)(2,1)S(1)} %copy-done.99), channel_id=1, source_target_pairs={{0,8},{2,10},{4,12},{6,14},{16,0},{18,2},{20,4},{22,6},{24,16},{26... | collective-permute-start | bytes 663560 | tf_op jit(solution)/shard_map/ppermute | solution.py:41
  334.7 18.0 %collective-permute-start.46 = (bf16[48,2304]{1,0:T(8,128)(2,1)S(1)}, bf16[48,2304]{1,0:T(8,128)(2,1)S(1)}, u32[]{:S(2)}, u32[]{:S(2)}) collective-permute-start(bf16[48,2304]{1,0:T(8,128)(2,1)S(1)} %copy-done.98), channel_id=1, source_target_pairs={{0,24},{2,26},{4,28},{6,30},{16,8},{18,10},{20,12},{22,14},{24,0},... | collective-permute-start | bytes 663560 | tf_op jit(solution)/shard_map/ppermute | solution.py:41
  337.0 16.2 %collective-permute-start.47 = (bf16[48,2304]{1,0:T(8,128)(2,1)S(1)}, bf16[48,2304]{1,0:T(8,128)(2,1)S(1)}, u32[]{:S(2)}, u32[]{:S(2)}) collective-permute-start(bf16[48,2304]{1,0:T(8,128)(2,1)S(1)} %copy-done.97), channel_id=1, source_target_pairs={{0,16},{2,18},{4,20},{6,22},{16,24},{18,26},{20,28},{22,30},{24,8}... | collective-permute-start | bytes 663560 | tf_op jit(solution)/shard_map/ppermute | solution.py:41
  339.9 13.3 %collective-permute-start.48 = (f32[22,768]{1,0:T(8,128)S(1)}, f32[22,768]{1,0:T(8,128)S(1)}, u32[]{:S(2)}, u32[]{:S(2)}) collective-permute-start(f32[22,768]{1,0:T(8,128)S(1)} %fusion.95), channel_id=1, source_target_pairs={{0,2},{2,0},{4,6},{6,4},{8,10},{10,8},{12,14},{14,12},{16,18},{18,... | collective-permute-start | bytes 202760 | tf_op jit(solution)/shard_map/ppermute | solution.py:783
  345.6 35.3 %collective-permute-start.50 = (bf16[256,768]{1,0:T(8,128)(2,1)S(1)}, bf16[256,768]{1,0:T(8,128)(2,1)S(1)}, u32[]{:S(2)}, u32[]{:S(2)}) collective-permute-start(bf16[256,768]{1,0:T(8,128)(2,1)S(1)} %copy-done.79), channel_id=1, source_target_pairs={{0,1},{1,0},{2,3},{3,2},{4,5},{5,4},{6,7},{7,6},{8,9},{9,8},{10,11... | collective-permute-start | bytes 1179656 | tf_op jit(solution)/shard_map/ppermute | solution.py:21
  351.4 18.4 %collective-permute-start.41 = (bf16[384,768]{1,0:T(8,128)(2,1)S(1)}, bf16[384,768]{1,0:T(8,128)(2,1)S(1)}, u32[]{:S(2)}, u32[]{:S(2)}) collective-permute-start(bf16[384,768]{1,0:T(8,128)(2,1)S(1)} %get-tuple-element.362), channel_id=1, source_target_pairs={{0,1},{1,0},{2,3},{3,2},{4,5},{5,4},{6,7},{7,6},{8,9},{9,8},{10,11... | collective-permute-start | bytes 1769480 | tf_op jit(solution)/shard_map/ppermute | solution.py:21
  352.7 19.6 %collective-permute-start.42 = (bf16[2,192,768]{2,1,0:T(8,128)(2,1)S(1)}, bf16[2,192,768]{2,1,0:T(8,128)(2,1)S(1)}, u32[]{:S(2)}, u32[]{:S(2)}) collective-permute-start(bf16[2,192,768]{2,1,0:T(8,128)(2,1)S(1)} %get-tuple-element.363), channel_id=1, source_target_pairs={{0,4},{2,6},{4,0},{6,2},{8,12},{10,14},{12,8},{14,10},{16,20},{18,... | collective-permute-start | bytes 1769480 | tf_op jit(solution)/shard_map/ppermute | solution.py:26
  353.8 38.2 %collective-permute-start.54 = (bf16[48,3072]{1,0:T(8,128)(2,1)S(1)}, bf16[48,3072]{1,0:T(8,128)(2,1)S(1)}, u32[]{:S(2)}, u32[]{:S(2)}) collective-permute-start(bf16[48,3072]{1,0:T(8,128)(2,1)S(1)} %get-tuple-element.430), channel_id=1, source_target_pairs={{0,8},{2,10},{4,12},{6,14},{16,0},{18,2},{20,4},{22,6},{24,16},{26... | collective-permute-start | bytes 884744 | tf_op jit(solution)/shard_map/ppermute | solution.py:41
  356.4 19.8 %collective-permute-start.49 = (f32[22,768]{1,0:T(8,128)S(1)}, f32[22,768]{1,0:T(8,128)S(1)}, u32[]{:S(2)}, u32[]{:S(2)}) collective-permute-start(f32[22,768]{1,0:T(8,128)S(1)} %add.233), channel_id=1, source_target_pairs={{0,4},{2,6},{4,0},{6,2},{8,12},{10,14},{12,8},{14,10},{16,20},{18,... | collective-permute-start | bytes 202760 | tf_op jit(solution)/shard_map/ppermute | solution.py:783
  369.8 23.9 %collective-permute-start.55 = (bf16[48,3072]{1,0:T(8,128)(2,1)S(1)}, bf16[48,3072]{1,0:T(8,128)(2,1)S(1)}, u32[]{:S(2)}, u32[]{:S(2)}) collective-permute-start(bf16[48,3072]{1,0:T(8,128)(2,1)S(1)} %get-tuple-element.429), channel_id=1, source_target_pairs={{0,24},{2,26},{4,28},{6,30},{16,8},{18,10},{20,12},{22,14},{24,0},... | collective-permute-start | bytes 884744 | tf_op jit(solution)/shard_map/ppermute | solution.py:41
  372.3 21.4 %collective-permute-start.56 = (bf16[48,3072]{1,0:T(8,128)(2,1)S(1)}, bf16[48,3072]{1,0:T(8,128)(2,1)S(1)}, u32[]{:S(2)}, u32[]{:S(2)}) collective-permute-start(bf16[48,3072]{1,0:T(8,128)(2,1)S(1)} %get-tuple-element.428), channel_id=1, source_target_pairs={{0,16},{2,18},{4,20},{6,22},{16,24},{18,26},{20,28},{22,30},{24,8}... | collective-permute-start | bytes 884744 | tf_op jit(solution)/shard_map/ppermute | solution.py:41
  376.2 12.1 %collective-permute-start.51 = (bf16[256,768]{1,0:T(8,128)(2,1)S(1)}, bf16[256,768]{1,0:T(8,128)(2,1)S(1)}, u32[]{:S(2)}, u32[]{:S(2)}) collective-permute-start(bf16[256,768]{1,0:T(8,128)(2,1)S(1)} %slice.681), channel_id=1, source_target_pairs={{0,1},{1,0},{2,3},{3,2},{4,5},{5,4},{6,7},{7,6},{8,9},{9,8},{10,11... | collective-permute-start | bytes 1179656 | tf_op jit(solution)/shard_map/ppermute | solution.py:21
  381.0 16.9 %collective-permute-start.53 = (bf16[192,768]{1,0:T(8,128)(2,1)S(1)}, bf16[192,768]{1,0:T(8,128)(2,1)S(1)}, u32[]{:S(2)}, u32[]{:S(2)}) collective-permute-start(bf16[192,768]{1,0:T(8,128)(2,1)S(1)} %fusion.24), channel_id=1, source_target_pairs={{0,1},{1,0},{2,3},{3,2},{4,5},{5,4},{6,7},{7,6},{8,9},{9,8},{10,11... | collective-permute-start | bytes 884744 | tf_op jit(solution)/shard_map/ppermute | solution.py:21
  388.2 9.7 %collective-permute-start.52 = (bf16[192,768]{1,0:T(8,128)(2,1)S(1)}, bf16[192,768]{1,0:T(8,128)(2,1)S(1)}, u32[]{:S(2)}, u32[]{:S(2)}) collective-permute-start(bf16[192,768]{1,0:T(8,128)(2,1)S(1)} %slice.683), channel_id=1, source_target_pairs={{0,4},{2,6},{4,0},{6,2},{8,12},{10,14},{12,8},{14,10},{16,20},{18,... | collective-permute-start | bytes 884744 | tf_op jit(solution)/shard_map/ppermute | solution.py:26
  392.0 5.9 %collective-permute-start.57 = (f32[22,768]{1,0:T(8,128)S(1)}, f32[22,768]{1,0:T(8,128)S(1)}, u32[]{:S(2)}, u32[]{:S(2)}) collective-permute-start(f32[22,768]{1,0:T(8,128)S(1)} %add.239), channel_id=1, source_target_pairs={{0,8},{2,10},{4,12},{6,14},{8,0},{10,2},{12,4},{14,6},{16,24},{18,... | collective-permute-start | bytes 202760 | tf_op jit(solution)/shard_map/ppermute | solution.py:783
  398.1 13.8 %collective-permute-start.58 = (bf16[48,1536]{1,0:T(8,128)(2,1)S(1)}, bf16[48,1536]{1,0:T(8,128)(2,1)S(1)}, u32[]{:S(2)}, u32[]{:S(2)}) collective-permute-start(bf16[48,1536]{1,0:T(8,128)(2,1)S(1)} %get-tuple-element.444), channel_id=1, source_target_pairs={{0,8},{2,10},{4,12},{6,14},{16,0},{18,2},{20,4},{22,6},{24,16},{26... | collective-permute-start | bytes 442376 | tf_op jit(solution)/shard_map/ppermute | solution.py:41
  398.2 13.8 %collective-permute-start.59 = (bf16[48,1536]{1,0:T(8,128)(2,1)S(1)}, bf16[48,1536]{1,0:T(8,128)(2,1)S(1)}, u32[]{:S(2)}, u32[]{:S(2)}) collective-permute-start(bf16[48,1536]{1,0:T(8,128)(2,1)S(1)} %get-tuple-element.443), channel_id=1, source_target_pairs={{0,24},{2,26},{4,28},{6,30},{16,8},{18,10},{20,12},{22,14},{24,0},... | collective-permute-start | bytes 442376 | tf_op jit(solution)/shard_map/ppermute | solution.py:41
  402.6 9.4 %collective-permute-start.60 = (bf16[48,1536]{1,0:T(8,128)(2,1)S(1)}, bf16[48,1536]{1,0:T(8,128)(2,1)S(1)}, u32[]{:S(2)}, u32[]{:S(2)}) collective-permute-start(bf16[48,1536]{1,0:T(8,128)(2,1)S(1)} %get-tuple-element.442), channel_id=1, source_target_pairs={{0,16},{2,18},{4,20},{6,22},{16,24},{18,26},{20,28},{22,30},{24,8}... | collective-permute-start | bytes 442376 | tf_op jit(solution)/shard_map/ppermute | solution.py:41
  404.5 7.4 %collective-permute-start.61 = (f32[22,768]{1,0:T(8,128)S(1)}, f32[22,768]{1,0:T(8,128)S(1)}, u32[]{:S(2)}, u32[]{:S(2)}) collective-permute-start(f32[22,768]{1,0:T(8,128)S(1)} %add.242), channel_id=1, source_target_pairs={{0,16},{2,18},{4,20},{6,22},{8,24},{10,26},{12,28},{14,30},{16,0},... | collective-permute-start | bytes 202760 | tf_op jit(solution)/shard_map/ppermute | solution.py:783
  (107 other events, 835.5 us)

commit v4 on v3

--- a/solution.py
+++ b/solution.py
@@ -714,10 +714,10 @@
 
                     @pl.when(i == 1)
                     def _():
-                        keep_a[:, place] = part
+                        keep_a[:, place] = part.astype(LOW)
                 else:
                     place = slice(col - self.size_a, col - self.size_a + end - start)
-                    keep_b[0, :, place] = part[:half]
+                    keep_b[0, :, place] = part[:half].astype(LOW)
                     send_b[0, :, place] = part[half:].astype(LOW)
                 col += end - start
 
@@ -725,8 +725,8 @@
             body, 2,
             [per_group(got, lambda i: 1 - i)] + self.inputs(lambda i: 1 - i, 0),
             [
-                out_whole((rows, self.size_a), LOW), out_whole((rows, self.size_a), F32),
-                out_group((2, half, self.size_b), LOW), out_group((2, half, self.size_b), F32),
+                out_whole((rows, self.size_a), LOW), out_whole((rows, self.size_a), LOW),
+                out_group((2, half, self.size_b), LOW), out_group((2, half, self.size_b), LOW),
             ],
             [], self.flops(rows),
         )

time: 423 us -> 416 us (0.983)
  local copies, waits for them, and re-layouts: 50.6 us -> 42.4 us
    unnamed x220 -> x210, local copies, waits for them, and re-layouts: 37.8 us -> 31.1 us
where the time goes in v4:
time: 416 us; the launch traced here: 411 us
  Pallas kernels  171 us (41%)
  waiting for transfers between devices  86.4 us (21%)
  starting transfers between devices  80.2 us (19%)
  local copies, waits for them, and re-layouts  42.4 us (10%)
  other arithmetic  16.5 us (4%)
  matrix products  11.5 us (3%)
    pallas_call x20, Pallas kernels, call(): pl.pallas_call(body, grid=(steps,), in_specs=[pl.BlockSpec(block, index)...  155 us
    ppermute x18, starting transfers between devices, ring_shift(): return lax.ppermute(value, 'dp', pairs)  38 us
    ppermute x22, waiting for transfers between devices, swap_y(): return lax.ppermute(value, 'mp', [(0, 1), (1, 0)])  33.2 us
    unnamed x210, local copies, waits for them, and re-layouts  31.1 us
    ppermute x18, waiting for transfers between devices, ring_shift(): return lax.ppermute(value, 'dp', pairs)  30.1 us
    ppermute x22, starting transfers between devices, swap_y(): return lax.ppermute(value, 'mp', [(0, 1), (1, 0)])  25.3 us
    pallas_call x11, Pallas kernels, moves(): pl.pallas_call(body, out_shape=[jax.ShapeDtypeStruct(shape, LOW) for shap...  15.7 us
    ppermute x12, starting transfers between devices, swap_x(): return lax.ppermute(value, 'dp', [(i, i ^ 2) for i in range(n)])  14.2 us
  transfers between devices with their start and end apart: 62, of which 21 were waited for; matrix products, arithmetic and copies ran while one was open for 8% of the time, Pallas kernels for 32%

profile of v4, /device:TPU:0, one launch (start us, length us, event | category | flops | bytes accessed | tf_op | source)
XLA Modules:
  0.0 410.6 jit_solution(17623364747847087605)
XLA Ops:
  3.2 4.1 collective-permute-start
  9.5 2.2 select_bitcast_fusion.6
  13.9 3.2 collective-permute-done.1.refs_2_
  17.1 5.7 %collective-permute-done.2.refs_3_ = bf16[48,1664]{1,0:T(8,128)(2,1)S(1)} collective-permute-done((bf16[48,1664]{1,0:T(8,128)(2,1)S(1)}, bf16[48,1664]{1,0:T(8,128)(2,1)S(1)}, u32[]{:S(2)}, u32[]{:S(2)}) %collective-permute-start.2) | collective-permute-done | bytes 159776 | tf_op jit(solution)/shard_map/ppermute | solution.py:41
  22.8 1.6 collective-permute-start.5
  28.1 7.3 %collective-permute-done.6.refs_1_ = bf16[48,1152]{1,0:T(8,128)(2,1)S(1)} collective-permute-done((bf16[48,1152]{1,0:T(8,128)(2,1)S(1)}, bf16[48,1152]{1,0:T(8,128)(2,1)S(1)}, u32[]{:S(2)}, u32[]{:S(2)}) %collective-permute-start.6) | collective-permute-done | bytes 110624 | tf_op jit(solution)/shard_map/ppermute | solution.py:26
  36.8 1.6 collective-permute-start.10
  39.1 2.5 collective-permute-start.11
  41.5 3.2 convolution_convert_fusion.1.rows.refs_0_
  44.8 6.0 %collective-permute-done.11.refs_2_ = bf16[48,3072]{1,0:T(8,128)(2,1)S(1)} collective-permute-done((bf16[48,3072]{1,0:T(8,128)(2,1)S(1)}, bf16[48,3072]{1,0:T(8,128)(2,1)S(1)}, u32[]{:S(2)}, u32[]{:S(2)}) %collective-permute-start.11) | collective-permute-done | bytes 294944 | tf_op jit(solution)/shard_map/ppermute | solution.py:41
  50.8 6.7 %collective-permute-done.12.refs_3_ = bf16[48,3072]{1,0:T(8,128)(2,1)S(1)} collective-permute-done((bf16[48,3072]{1,0:T(8,128)(2,1)S(1)}, bf16[48,3072]{1,0:T(8,128)(2,1)S(1)}, u32[]{:S(2)}, u32[]{:S(2)}) %collective-permute-start.12) | collective-permute-done | bytes 294944 | tf_op jit(solution)/shard_map/ppermute | solution.py:41
  65.1 10.9 %collective-permute-done.16 = bf16[3456]{0:T(1024)(128)(2,1)S(1)} collective-permute-done((bf16[3456]{0:T(1024)(128)(2,1)S(1)}, bf16[3456]{0:T(1024)(128)(2,1)S(1)}, u32[]{:S(2)}, u32[]{:S(2)}) %collective-permute-start.16) | collective-permute-done | bytes 6944 | tf_op jit(solution)/shard_map/ppermute | solution.py:21
  77.4 3.1 shard_map.328
  84.6 1.6 collective-permute-start.22
  87.5 11.9 %shard_map.329 = (bf16[2,768,1152]{2,1,0:T(8,128)(2,1)S(1)}, bf16[2,512,384]{2,1,0:T(8,128)(2,1)S(1)}, f32[2,8,512]{2,1,0:T(8,128)S(1)}) custom-call(bf16[768,768]{1,0:T(8,128)(2,1)S(1)} %copy-done.6, bf16[2,384,1664]{2,1,0:T(8,128)(2,1)S(1)} %bitcast.138, bf16[2,384,1664]{2,1,0:T(8,128)(2,1)} %collective-permute-done.13.refs_1_.refs_3_.refs_5_.refs_7_.out_two, ...), custom_call_target="tpu_custom_call" | custom-call | flops 1761607680 | bytes 10443264 | tf_op jit(solution)/shard_map/pallas_call | solution.py:80
  99.4 1.8 convolution_convert_fusion.2.away.refs_2_
  101.2 10.2 %shard_map.331 = (bf16[2,256,1152]{2,1,0:T(8,128)(2,1)S(1)}, bf16[2,768,384]{2,1,0:T(8,128)(2,1)S(1)}, f32[2,8,256]{2,1,0:T(8,128)S(1)}, bf16[768,768]{1,0:T(8,1...) custom-call(bf16[768,768]{1,0:T(8,128)(2,1)S(1)} %copy-done.6, ...), custom_call_target="tpu_custom_call" | custom-call | flops 1107296256 | bytes 15560192 | tf_op jit(solution)/shard_map/pallas_call | solution.py:80
  112.8 2.3 collective-permute-done.22.refs_3_
  115.1 4.9 %shard_map.332 = bf16[2,2,4,48,3072]{4,3,2,1,0:T(8,128)(2,1)} custom-call(bf16[2,4,48,1536]{3,2,1,0:T(8,128)(2,1)} %get-tuple-element.263.refs_0_, bf16[2,4,48,1536]{3,2,1,0:T(8,128)(2,1)} %collective-permute-done.20.refs_1_, bf16[2,4,48,1536]{3,2,1,0:T(8,128)(2,1)} %get-tuple-element.265.refs_2_, bf16[2,4,48,1536]{3,2,1,0:T(8,128)(2,1)} %collective-permute-done.21.refs_3_), custom_call_target="tpu_custom_call" | custom-call | bytes 4718592 | tf_op jit(solution)/shard_map/pallas_call | solution.py:102
  121.6 2.6 shard_map.334
  126.4 5.8 %collective-permute-done.26 = bf16[256,768]{1,0:T(8,128)(2,1)S(1)} collective-permute-done((bf16[256,768]{1,0:T(8,128)(2,1)S(1)}, bf16[256,768]{1,0:T(8,128)(2,1)S(1)}, u32[]{:S(2)}, u32[]{:S(2)}) %collective-permute-start.26) | collective-permute-done | bytes 393248 | tf_op jit(solution)/shard_map/ppermute | solution.py:21
  135.9 13.4 %shard_map.333 = (bf16[2,768,1536]{2,1,0:T(8,128)(2,1)S(1)}, bf16[2,768,1536]{2,1,0:T(8,128)(2,1)S(1)}, bf16[768,768]{1,0:T(8,128)(2,1)S(1)}, bf16[768,768]{1,0:T(8,128)(2,1)S(1)}, f32[768,1]{1,0:T(8,128)S(1)}) custom-call(bf16[768,768]{1,0:T(8,128)(2,1)S(1)} %copy-done.10, f32[8,768]{1,0:T(8,128)S(1)} %slice_select_fusion.1.refs_12_.norms, ...), custom_call_target="tpu_custom_call" | custom-call | flops 3623878656 | bytes 15945216 | tf_op jit(solution)/shard_map/pallas_call | solution.py:80
  150.9 2.8 shard_map.335
  156.6 3.4 collective-permute-done.27.refs_1_.refs_3_.refs_5_.up_two.down_two.refs_7_.refs_9_.out_two.refs_2_.refs_4_
  160.0 6.2 %shard_map.336 = (bf16[2,768,576]{2,1,0:T(8,128)(2,1)S(1)}, bf16[2,512,192]{2,1,0:T(8,128)(2,1)S(1)}, f32[2,8,512]{2,1,0:T(8,128)S(1)}) custom-call(bf16[768,768]{1,0:T(8,128)(2,1)S(1)} %get-tuple-element.277.rows.refs_4_, bf16[2,384,2304]{2,1,0:T(8,128)(2,1)S(1)} %bitcast.121, ...), custom_call_target="tpu_custom_call" | custom-call | flops 880803840 | bytes 8769792 | tf_op jit(solution)/shard_map/pallas_call | solution.py:80
  166.2 6.2 %shard_map.337 = (bf16[2,256,576]{2,1,0:T(8,128)(2,1)S(1)}, bf16[2,768,192]{2,1,0:T(8,128)(2,1)S(1)}, f32[2,8,256]{2,1,0:T(8,128)S(1)}, bf16[768,768]{1,0:T(8,12...) custom-call(bf16[768,768]{1,0:T(8,128)(2,1)S(1)} %get-tuple-element.277.rows.refs_4_, ...), custom_call_target="tpu_custom_call" | custom-call | flops 553648128 | bytes 14279936 | tf_op jit(solution)/shard_map/pallas_call | solution.py:80
  172.4 6.5 %shard_map.338 = (bf16[2,768,768]{2,1,0:T(8,128)(2,1)S(1)}, bf16[2,768,768]{2,1,0:T(8,128)(2,1)S(1)}, f32[768,768]{1,0:T(8,128)S(1)}, bf16[768,768]{1,0:T(8,128)(2,1)S(1)}, f32[768,1]{1,0:T(8,128)S(1)}) custom-call(bf16[768,768]{1,0:T(8,128)(2,1)S(1)} %get-tuple-element.286.hidden_low.refs_0_, f32[8,768]{1,0:T(8,128)S(1)} %pad.17.refs_10_.norms.refs_4_, ...), custom_call_target="tpu_custom_call" | custom-call | flops 1811939328 | bytes 11813376 | tf_op jit(solution)/shard_map/pallas_call | solution.py:80
  180.3 7.4 %shard_map.339 = (bf16[768,768]{1,0:T(8,128)(2,1)S(1)}, bf16[2,768,768]{2,1,0:T(8,128)(2,1)S(1)}, bf16[768,768]{1,0:T(8,128)(2,1)S(1)}, f32[8,768]{1,0:T(8,128)S(1)}, f32[2,1,768]{2,1,0:T(1,128)S(1)}) custom-call(bf16[768,768]{1,0:T(8,128)(2,1)S(1)} %convolution_convert_fusion.grad, bf16[768,768]{1,0:T(8,128)(2,1)S(1)} %get-tuple-element.284.refs_0_, ...), custom_call_target="tpu_custom_call" | custom-call | flops 1811939328 | bytes 12417024 | tf_op jit(solution)/shard_map/pallas_call | solution.py:80
  189.2 5.8 %shard_map.340 = (bf16[2,256,576]{2,1,0:T(8,128)(2,1)S(1)}, bf16[2,256,576]{2,1,0:T(8,128)(2,1)S(1)}, f32[2,8,576]{2,1,0:T(8,128)S(1)}, bf16[256,768]{1,0:T(8,128)(2,1)S(1)}) custom-call(bf16[768,768]{1,0:T(8,128)(2,1)S(1)} %get-tuple-element.290.d_mid.d_mid_low.refs_0_.refs_8_, bf16[2,768,576]{2,1,0:T(8,128)(2,1)S(1)} %get-tuple-element.281.proj, ...), custom_call_target="tpu_custom_call" | custom-call | flops 553648128 | bytes 13200896 | tf_op jit(solution)/shard_map/pallas_call | solution.py:80
  196.4 9.7 %shard_map.341 = (bf16[2,768,576]{2,1,0:T(8,128)(2,1)S(1)}, f32[2,8,576]{2,1,0:T(8,128)S(1)}, bf16[768,768]{1,0:T(8,128)(2,1)S(1)}) custom-call(bf16[768,768]{1,0:T(8,128)(2,1)S(1)} %get-tuple-element.290.d_mid.d_mid_low.refs_0_.refs_8_, bf16[2,256,576]{2,1,0:T(8,128)(2,1)S(1)} %get-tuple-element.295.d_shared, ...), custom_call_target="tpu_custom_call" | custom-call | flops 1333788672 | bytes 14487552 | tf_op jit(solution)/shard_map/pallas_call | solution.py:80
  208.4 1.8 copy-done.20
  211.7 5.2 %shard_map.342 = bf16[2,384,2304]{2,1,0:T(8,128)(2,1)} custom-call(bf16[768,768]{1,0:T(8,128)(2,1)S(1)} %get-tuple-element.286.hidden_low.refs_0_, bf16[2,768,768]{2,1,0:T(8,128)(2,1)S(1)} %copy-done.20, bf16[768,768]{1,0:T(8,128)(2,1)S(1)} %get-tuple-element.299.refs_2_, bf16[2,768,768]{2,1,0:T(8,128)(2,1)S(1)} %get-tuple-element.300.refs_3_, ...), custom_call_target="tpu_custom_call" | custom-call | flops 1472200704 | bytes 8159232 | tf_op jit(solution)/shard_map/pallas_call | solution.py:80
  217.0 2.3 copy-done.28
  221.6 8.2 %shard_map.343 = (bf16[768,768]{1,0:T(8,128)(2,1)S(1)}, bf16[2,768,1536]{2,1,0:T(8,128)(2,1)S(1)}, f32[8,768]{1,0:T(8,128)S(1)}, f32[4,1,768]{2,1,0:T(1,128)S(1)}) custom-call(bf16[768,768]{1,0:T(8,128)(2,1)S(1)} %copy-done.45, bf16[256,768]{1,0:T(8,128)(2,1)S(1)} %copy-done.52, bf16[768,768]{1,0:T(8,128)(2,1)S(1)} %copy-done.43, ...), custom_call_target="tpu_custom_call" | custom-call | flops 1811939328 | bytes 11435520 | tf_op jit(solution)/shard_map/pallas_call | solution.py:80
  229.8 2.1 copy-done.18
  231.9 1.7 copy-done.21
  237.5 8.0 %shard_map.344 = (bf16[384,1152]{1,0:T(8,128)(2,1)S(1)}, bf16[384,1152]{1,0:T(8,128)(2,1)S(1)}, bf16[2,192,1152]{2,1,0:T(8,128)(2,1)S(1)}, bf16[2,192,1152]{2,1,0:T(8,128)(2,1)S(1)}) custom-call(bf16[2,384,2304]{2,1,0:T(8,128)(2,1)} %collective-permute-done.31.got, bf16[768,768]{1,0:T(8,128)(2,1)S(1)} %copy-done.16, bf16[2,768,768]{2,1,0:T(8,128)(2,1)S(1)} %copy-done.21, ...), custom_call_target="tpu_custom_call" | custom-call | flops 1472200704 | bytes 9928704 | tf_op jit(solution)/shard_map/pallas_call | solution.py:80
  245.5 5.6 %shard_map.345 = bf16[2,384,3072]{2,1,0:T(8,128)(2,1)} custom-call(bf16[768,768]{1,0:T(8,128)(2,1)S(1)} %copy-done.11, bf16[2,768,1536]{2,1,0:T(8,128)(2,1)S(1)} %get-tuple-element.319.refs_1_.d_pre, bf16[768,768]{1,0:T(8,128)(2,1)S(1)} %get-tuple-element.311.refs_2_.d_final, bf16[2,768,1536]{2,1,0:T(8,128)(2,1)S(1)} %get-tuple-element.318.refs_3_), custom_call_target="tpu_custom_call" | custom-call | flops 1811939328 | bytes 8257536 | tf_op jit(solution)/shard_map/pallas_call | solution.py:80
  255.5 7.8 %shard_map.346 = (bf16[768,768]{1,0:T(8,128)(2,1)S(1)}, f32[8,768]{1,0:T(8,128)S(1)}) custom-call(bf16[768,768]{1,0:T(8,128)(2,1)S(1)} %copy-done.14, bf16[2,768,1536]{2,1,0:T(8,128)(2,1)S(1)} %get-tuple-element.319.refs_1_.d_pre, bf16[768,768]{1,0:T(8,128)(2,1)S(1)} %copy-done.41, f32[768,1]{1,0:T(8,128)S(1)} %copy-done.50, ...), custom_call_target="tpu_custom_call" | custom-call | flops 1811939328 | bytes 8873472 | tf_op jit(solution)/shard_map/pallas_call | solution.py:80
  263.3 5.6 %shard_map.347 = (bf16[384,1536]{1,0:T(8,128)(2,1)}, bf16[384,1536]{1,0:T(8,128)(2,1)S(1)}, bf16[2,192,1536]{2,1,0:T(8,128)(2,1)}, bf16[2,192,1536]{2,1,0:T(8,128)(2,1)S(1)}) custom-call(bf16[2,384,3072]{2,1,0:T(8,128)(2,1)S(1)} %collective-permute-done.32.got, bf16[768,768]{1,0:T(8,128)(2,1)S(1)} %copy-done.12, ...), custom_call_target="tpu_custom_call" | custom-call | flops 1811939328 | bytes 10616832 | tf_op jit(solution)/shard_map/pallas_call | solution.py:80
  269.0 4.4 %collective-permute-done.33 = bf16[384,1152]{1,0:T(8,128)(2,1)S(1)} collective-permute-done((bf16[384,1152]{1,0:T(8,128)(2,1)S(1)}, bf16[384,1152]{1,0:T(8,128)(2,1)S(1)}, u32[]{:S(2)}, u32[]{:S(2)}) %collective-permute-start.33) | collective-permute-done | bytes 884768 | tf_op jit(solution)/shard_map/ppermute | solution.py:21
  281.0 10.1 %shard_map.348 = (bf16[2,256,1152]{2,1,0:T(8,128)(2,1)S(1)}, bf16[2,256,1152]{2,1,0:T(8,128)(2,1)S(1)}, f32[2,8,1152]{2,1,0:T(8,128)S(1)}, bf16[256,768]{1,0:T(8,128)(2,1)S(1)}) custom-call(bf16[768,768]{1,0:T(8,128)(2,1)S(1)} %get-tuple-element.364.d_mid.d_mid_low.refs_4_, bf16[2,768,1152]{2,1,0:T(8,128)(2,1)S(1)} %copy-done.1, ...), custom_call_target="tpu_custom_call" | custom-call | flops 1107296256 | bytes 14595584 | tf_op jit(solution)/shard_map/pallas_call | solution.py:80
  293.1 11.7 %shard_map.349 = (bf16[2,768,1152]{2,1,0:T(8,128)(2,1)S(1)}, f32[2,8,1152]{2,1,0:T(8,128)S(1)}) custom-call(bf16[768,768]{1,0:T(8,128)(2,1)S(1)} %get-tuple-element.364.d_mid.d_mid_low.refs_4_, bf16[2,256,1152]{2,1,0:T(8,128)(2,1)S(1)} %get-tuple-element.341.d_shared, bf16[2,768,1152]{2,1,0:T(8,128)(2,1)S(1)} %copy-done.1, ...), custom_call_target="tpu_custom_call" | custom-call | flops 1308622848 | bytes 7329792 | tf_op jit(solution)/shard_map/pallas_call | solution.py:80
  304.9 4.5 %shard_map.350 = bf16[2,384,1536]{2,1,0:T(8,128)(2,1)} custom-call(bf16[768,768]{1,0:T(8,128)(2,1)S(1)} %copy-done.7, bf16[2,768,1152]{2,1,0:T(8,128)(2,1)S(1)} %get-tuple-element.365.refs_1_.d_proj, bf16[256,768]{1,0:T(8,128)(2,1)S(1)} %convolution_convert_fusion.2.away.refs_2_, bf16[2,256,1152]{2,1,0:T(8,128)(2,1)S(1)} %get-tuple-element.344.refs_3_, ...), custom_call_target="tpu_custom_call" | custom-call | flops 1132462080 | bytes 5505024 | tf_op jit(solution)/shard_map/pallas_call | solution.py:80
  314.3 2.1 convert_add_fusion
  317.8 1.8 convert_add_fusion.1
  319.7 1.6 collective-permute-start.43
  321.8 6.1 %collective-permute-start.45 = (bf16[48,2304]{1,0:T(8,128)(2,1)S(1)}, bf16[48,2304]{1,0:T(8,128)(2,1)S(1)}, u32[]{:S(2)}, u32[]{:S(2)}) collective-permute-start(bf16[48,2304]{1,0:T(8,128)(2,1)S(1)} %copy-done.95), channel_id=1, source_target_pairs={{0,8},{2,10},{4,12},{6,14},{16,0},{18,2},{20,4},{22,6},{24,16},{26... | collective-permute-start | bytes 663560 | tf_op jit(solution)/shard_map/ppermute | solution.py:41
  327.8 2.5 collective-permute-start.46
  331.5 5.6 %shard_map.351 = (bf16[384,768]{1,0:T(8,128)(2,1)S(1)}, bf16[384,768]{1,0:T(8,128)(2,1)S(1)}, bf16[2,192,768]{2,1,0:T(8,128)(2,1)S(1)}, bf16[2,192,768]{2,1,0:T(8,128)(2,1)S(1)}) custom-call(bf16[2,384,1536]{2,1,0:T(8,128)(2,1)} %collective-permute-done.37.got, bf16[768,768]{1,0:T(8,128)(2,1)S(1)} %copy-done.8, bf16[2,768,1152]{2,1,0:T(8,128)(2,1)S(1)} %copy-done.3, ...), custom_call_target="tpu_custom_call" | custom-call | flops 1132462080 | bytes 6684672 | tf_op jit(solution)/shard_map/pallas_call | solution.py:80
  338.5 6.1 %collective-permute-done.45 = bf16[48,2304]{1,0:T(8,128)(2,1)S(1)} collective-permute-done((bf16[48,2304]{1,0:T(8,128)(2,1)S(1)}, bf16[48,2304]{1,0:T(8,128)(2,1)S(1)}, u32[]{:S(2)}, u32[]{:S(2)}) %collective-permute-start.45) | collective-permute-done | bytes 221216 | tf_op jit(solution)/shard_map/ppermute | solution.py:41
  346.9 2.8 collective-permute-start.54
  349.7 1.6 collective-permute-start.49
  351.3 5.4 %shard_map.352 = f32[768,768]{1,0:T(8,128)S(1)} custom-call(bf16[768,768]{1,0:T(8,128)(2,1)S(1)} %copy-done.5, bf16[2,768,1152]{2,1,0:T(8,128)(2,1)S(1)} %copy-done.3, bf16[2,384,1664]{2,1,0:T(8,128)(2,1)S(1)} %bitcast.150, bf16[2,384,1664]{2,1,0:T(8,128)(2,1)} %collective-permute-done.13.refs_1_.refs_3_.refs_5_.refs_7_.out_two, ...), custom_call_target="tpu_custom_call" | custom-call | flops 1358954496 | bytes 11206656 | tf_op jit(solution)/shard_map/pallas_call | solution.py:80
  358.9 2.5 collective-permute-done.41
  361.4 2.5 collective-permute-start.55
  363.9 5.0 %collective-permute-start.56 = (bf16[48,3072]{1,0:T(8,128)(2,1)S(1)}, bf16[48,3072]{1,0:T(8,128)(2,1)S(1)}, u32[]{:S(2)}, u32[]{:S(2)}) collective-permute-start(bf16[48,3072]{1,0:T(8,128)(2,1)S(1)} %get-tuple-element.428), channel_id=1, source_target_pairs={{0,16},{2,18},{4,20},{6,22},{16,24},{18,26},{20,28},{22,30},{24,8}... | collective-permute-start | bytes 884744 | tf_op jit(solution)/shard_map/ppermute | solution.py:41
  376.3 4.6 %collective-permute-done.51 = bf16[256,768]{1,0:T(8,128)(2,1)S(1)} collective-permute-done((bf16[256,768]{1,0:T(8,128)(2,1)S(1)}, bf16[256,768]{1,0:T(8,128)(2,1)S(1)}, u32[]{:S(2)}, u32[]{:S(2)}) %collective-permute-start.51) | collective-permute-done | bytes 393248 | tf_op jit(solution)/shard_map/ppermute | solution.py:21
  383.1 1.6 pad_maximum_fusion.2
  384.8 1.6 pad_maximum_fusion.1
  386.4 4.5 %collective-permute-done.57 = f32[22,768]{1,0:T(8,128)S(1)} collective-permute-done((f32[22,768]{1,0:T(8,128)S(1)}, f32[22,768]{1,0:T(8,128)S(1)}, u32[]{:S(2)}, u32[]{:S(2)}) %collective-permute-start.57) | collective-permute-done | bytes 67616 | tf_op jit(solution)/shard_map/ppermute | solution.py:783
  391.1 4.4 %collective-permute-start.59 = (bf16[48,1536]{1,0:T(8,128)(2,1)S(1)}, bf16[48,1536]{1,0:T(8,128)(2,1)S(1)}, u32[]{:S(2)}, u32[]{:S(2)}) collective-permute-start(bf16[48,1536]{1,0:T(8,128)(2,1)S(1)} %get-tuple-element.443), channel_id=1, source_target_pairs={{0,24},{2,26},{4,28},{6,30},{16,8},{18,10},{20,12},{22,14},{24,0},... | collective-permute-start | bytes 442376 | tf_op jit(solution)/shard_map/ppermute | solution.py:41
  395.5 1.9 collective-permute-start.60
  398.5 6.3 %collective-permute-done.61 = f32[22,768]{1,0:T(8,128)S(1)} collective-permute-done((f32[22,768]{1,0:T(8,128)S(1)}, f32[22,768]{1,0:T(8,128)S(1)}, u32[]{:S(2)}, u32[]{:S(2)}) %collective-permute-start.61) | collective-permute-done | bytes 67616 | tf_op jit(solution)/shard_map/ppermute | solution.py:783
  (425 shorter events, 98.0 us)
Async XLA Ops:
  3.2 10.7 %collective-permute-start = (bf16[48,1664]{1,0:T(8,128)(2,1)S(1)}, bf16[48,1664]{1,0:T(8,128)(2,1)S(1)}, u32[]{:S(2)}, u32[]{:S(2)}) collective-permute-start(bf16[48,1664]{1,0:T(8,128)(2,1)S(1)} %shard_map.322.refs_0_), channel_id=1, source_target_pairs={{0,16},{2,18},{4,20},{6,22},{16,24},{18,26},{20,28},{22,30},{24,8}... | collective-permute-start | bytes 479240 | tf_op jit(solution)/shard_map/ppermute | solution.py:41
  7.3 9.8 %collective-permute-start.1 = (bf16[48,1664]{1,0:T(8,128)(2,1)S(1)}, bf16[48,1664]{1,0:T(8,128)(2,1)S(1)}, u32[]{:S(2)}, u32[]{:S(2)}) collective-permute-start(bf16[48,1664]{1,0:T(8,128)(2,1)S(1)} %shard_map.322.refs_0_), channel_id=1, source_target_pairs={{0,24},{2,26},{4,28},{6,30},{16,8},{18,10},{20,12},{22,14},{24,0},... | collective-permute-start | bytes 479240 | tf_op jit(solution)/shard_map/ppermute | solution.py:41
  8.6 14.1 %collective-permute-start.2 = (bf16[48,1664]{1,0:T(8,128)(2,1)S(1)}, bf16[48,1664]{1,0:T(8,128)(2,1)S(1)}, u32[]{:S(2)}, u32[]{:S(2)}) collective-permute-start(bf16[48,1664]{1,0:T(8,128)(2,1)S(1)} %shard_map.322.refs_0_), channel_id=1, source_target_pairs={{0,8},{2,10},{4,12},{6,14},{16,0},{18,2},{20,4},{22,6},{24,16},{26... | collective-permute-start | bytes 479240 | tf_op jit(solution)/shard_map/ppermute | solution.py:41
  11.6 11.1 %collective-permute-start.3 = (bf16[256,768]{1,0:T(8,128)(2,1)S(1)}, bf16[256,768]{1,0:T(8,128)(2,1)}, u32[]{:S(2)}, u32[]{:S(2)}) collective-permute-start(bf16[256,768]{1,0:T(8,128)(2,1)S(1)} %get-tuple-element.436), channel_id=1, source_target_pairs={{0,1},{1,0},{2,3},{3,2},{4,5},{5,4},{6,7},{7,6},{8,9},{9,8},{10,11... | collective-permute-start | bytes 1179656 | tf_op jit(solution)/shard_map/ppermute | solution.py:21
  13.7 43.9 %copy-start.73 = (bf16[768,768]{1,0:T(8,128)(2,1)}, bf16[768,768]{1,0:T(8,128)(2,1)S(1)}, u32[]{:S(2)}) copy-start(bf16[768,768]{1,0:T(8,128)(2,1)S(1)} %fusion.1) | copy-start | bytes 3538948
  22.8 13.9 %collective-permute-start.5 = (bf16[4,48,896]{2,1,0:T(8,128)(2,1)S(1)}, bf16[4,48,896]{2,1,0:T(8,128)(2,1)S(1)}, u32[]{:S(2)}, u32[]{:S(2)}) collective-permute-start(bf16[4,48,896]{2,1,0:T(8,128)(2,1)S(1)} %get-tuple-element.223.refs_2_), channel_id=1, source_target_pairs={{0,1},{1,0},{2,3},{3,2},{4,5},{5,4},{6,7},{7,6},{8,9},{9,8},{10,11... | collective-permute-start | bytes 1032200 | tf_op jit(solution)/shard_map/ppermute | solution.py:21
  24.4 12.3 %collective-permute-start.4 = (bf16[4,48,768]{2,1,0:T(8,128)(2,1)S(1)}, bf16[4,48,768]{2,1,0:T(8,128)(2,1)S(1)}, u32[]{:S(2)}, u32[]{:S(2)}) collective-permute-start(bf16[4,48,768]{2,1,0:T(8,128)(2,1)S(1)} %get-tuple-element.222.refs_0_), channel_id=1, source_target_pairs={{0,4},{2,6},{4,0},{6,2},{8,12},{10,14},{12,8},{14,10},{16,20},{18,... | collective-permute-start | bytes 884744 | tf_op jit(solution)/shard_map/ppermute | solution.py:26
  25.9 10.8 %collective-permute-start.8 = (bf16[48,3072]{1,0:T(8,128)(2,1)S(1)}, bf16[48,3072]{1,0:T(8,128)(2,1)S(1)}, u32[]{:S(2)}, u32[]{:S(2)}) collective-permute-start(bf16[48,3072]{1,0:T(8,128)(2,1)S(1)} %get-tuple-element.239.refs_0_), channel_id=1, source_target_pairs={{0,16},{2,18},{4,20},{6,22},{16,24},{18,26},{20,28},{22,30},{24,8}... | collective-permute-start | bytes 884744 | tf_op jit(solution)/shard_map/ppermute | solution.py:41
  27.0 8.4 %collective-permute-start.6 = (bf16[48,1152]{1,0:T(8,128)(2,1)S(1)}, bf16[48,1152]{1,0:T(8,128)(2,1)S(1)}, u32[]{:S(2)}, u32[]{:S(2)}) collective-permute-start(bf16[48,1152]{1,0:T(8,128)(2,1)S(1)} %get-tuple-element.224.refs_0_), channel_id=1, source_target_pairs={{0,4},{2,6},{4,0},{6,2},{8,12},{10,14},{12,8},{14,10},{16,20},{18,... | collective-permute-start | bytes 331784 | tf_op jit(solution)/shard_map/ppermute | solution.py:26
  27.6 8.5 %collective-permute-start.7 = (bf16[48,1152]{1,0:T(8,128)(2,1)S(1)}, bf16[48,1152]{1,0:T(8,128)(2,1)S(1)}, u32[]{:S(2)}, u32[]{:S(2)}) collective-permute-start(bf16[48,1152]{1,0:T(8,128)(2,1)S(1)} %get-tuple-element.225.refs_2_), channel_id=1, source_target_pairs={{0,1},{1,0},{2,3},{3,2},{4,5},{5,4},{6,7},{7,6},{8,9},{9,8},{10,11... | collective-permute-start | bytes 331784 | tf_op jit(solution)/shard_map/ppermute | solution.py:21
  36.8 20.7 %collective-permute-start.10 = (bf16[2,4,48,896]{3,2,1,0:T(8,128)(2,1)S(1)}, bf16[2,4,48,896]{3,2,1,0:T(8,128)(2,1)S(1)}, u32[]{:S(2)}, u32[]{:S(2)}) collective-permute-start(bf16[2,4,48,896]{3,2,1,0:T(8,128)(2,1)S(1)} %get-tuple-element.230.refs_2_), channel_id=1, source_target_pairs={{0,4},{2,6},{4,0},{6,2},{8,12},{10,14},{12,8},{14,10},{16,20},{18,... | collective-permute-start | bytes 2064392 | tf_op jit(solution)/shard_map/ppermute | solution.py:26
  38.4 19.1 %collective-permute-start.9 = (bf16[2,4,48,768]{3,2,1,0:T(8,128)(2,1)S(1)}, bf16[2,4,48,768]{3,2,1,0:T(8,128)(2,1)S(1)}, u32[]{:S(2)}, u32[]{:S(2)}) collective-permute-start(bf16[2,4,48,768]{3,2,1,0:T(8,128)(2,1)S(1)} %get-tuple-element.229.refs_0_), channel_id=1, source_target_pairs={{0,1},{1,0},{2,3},{3,2},{4,5},{5,4},{6,7},{7,6},{8,9},{9,8},{10,11... | collective-permute-start | bytes 1769480 | tf_op jit(solution)/shard_map/ppermute | solution.py:21
  39.1 11.7 %collective-permute-start.11 = (bf16[48,3072]{1,0:T(8,128)(2,1)S(1)}, bf16[48,3072]{1,0:T(8,128)(2,1)S(1)}, u32[]{:S(2)}, u32[]{:S(2)}) collective-permute-start(bf16[48,3072]{1,0:T(8,128)(2,1)S(1)} %get-tuple-element.239.refs_0_), channel_id=1, source_target_pairs={{0,24},{2,26},{4,28},{6,30},{16,8},{18,10},{20,12},{22,14},{24,0},... | collective-permute-start | bytes 884744 | tf_op jit(solution)/shard_map/ppermute | solution.py:41
  41.5 16.0 %collective-permute-start.12 = (bf16[48,3072]{1,0:T(8,128)(2,1)S(1)}, bf16[48,3072]{1,0:T(8,128)(2,1)S(1)}, u32[]{:S(2)}, u32[]{:S(2)}) collective-permute-start(bf16[48,3072]{1,0:T(8,128)(2,1)S(1)} %get-tuple-element.239.refs_0_), channel_id=1, source_target_pairs={{0,8},{2,10},{4,12},{6,14},{16,0},{18,2},{20,4},{22,6},{24,16},{26... | collective-permute-start | bytes 884744 | tf_op jit(solution)/shard_map/ppermute | solution.py:41
  57.8 19.6 %collective-permute-start.13 = (bf16[2,384,1664]{2,1,0:T(8,128)(2,1)S(1)}, bf16[2,384,1664]{2,1,0:T(8,128)(2,1)}, u32[]{:S(2)}, u32[]{:S(2)}) collective-permute-start(bf16[2,384,1664]{2,1,0:T(8,128)(2,1)S(1)} %bitcast.136), channel_id=1, source_target_pairs={{0,2},{2,0},{4,6},{6,4},{8,10},{10,8},{12,14},{14,12},{16,18},{18,... | collective-permute-start | bytes 7667720 | tf_op jit(solution)/shard_map/ppermute | solution.py:31
  58.9 17.1 %collective-permute-start.14 = (bf16[4,48,1536]{2,1,0:T(8,128)(2,1)}, bf16[4,48,1536]{2,1,0:T(8,128)(2,1)}, u32[]{:S(2)}, u32[]{:S(2)}) collective-permute-start(bf16[4,48,1536]{2,1,0:T(8,128)(2,1)} %get-tuple-element.243.refs_0_), channel_id=1, source_target_pairs={{0,4},{2,6},{4,0},{6,2},{8,12},{10,14},{12,8},{14,10},{16,20},{18,... | collective-permute-start | bytes 1769480 | tf_op jit(solution)/shard_map/ppermute | solution.py:26
  59.5 17.9 %collective-permute-start.15 = (bf16[4,48,1536]{2,1,0:T(8,128)(2,1)}, bf16[4,48,1536]{2,1,0:T(8,128)(2,1)}, u32[]{:S(2)}, u32[]{:S(2)}) collective-permute-start(bf16[4,48,1536]{2,1,0:T(8,128)(2,1)} %get-tuple-element.244.refs_2_), channel_id=1, source_target_pairs={{0,1},{1,0},{2,3},{3,2},{4,5},{5,4},{6,7},{7,6},{8,9},{9,8},{10,11... | collective-permute-start | bytes 1769480 | tf_op jit(solution)/shard_map/ppermute | solution.py:21
  61.0 15.0 %collective-permute-start.16 = (bf16[3456]{0:T(1024)(128)(2,1)S(1)}, bf16[3456]{0:T(1024)(128)(2,1)S(1)}, u32[]{:S(2)}, u32[]{:S(2)}) collective-permute-start(bf16[3456]{0:T(1024)(128)(2,1)S(1)} %concatenate.65), channel_id=1, source_target_pairs={{0,1},{1,0},{2,3},{3,2},{4,5},{5,4},{6,7},{7,6},{8,9},{9,8},{10,11... | collective-permute-start | bytes 20744 | tf_op jit(solution)/shard_map/ppermute | solution.py:21
  61.7 23.0 %collective-permute-start.17 = (bf16[256,768]{1,0:T(8,128)(2,1)}, bf16[256,768]{1,0:T(8,128)(2,1)}, u32[]{:S(2)}, u32[]{:S(2)}) collective-permute-start(bf16[256,768]{1,0:T(8,128)(2,1)} %get-tuple-element.435), channel_id=1, source_target_pairs={{0,1},{1,0},{2,3},{3,2},{4,5},{5,4},{6,7},{7,6},{8,9},{9,8},{10,11... | collective-permute-start | bytes 1179656 | tf_op jit(solution)/shard_map/ppermute | solution.py:21
  76.0 23.4 %collective-permute-start.18 = (bf16[2,48,2304]{2,1,0:T(8,128)(2,1)}, bf16[2,48,2304]{2,1,0:T(8,128)(2,1)}, u32[]{:S(2)}, u32[]{:S(2)}) collective-permute-start(bf16[2,48,2304]{2,1,0:T(8,128)(2,1)} %shard_map.330.refs_0_), channel_id=1, source_target_pairs={{0,16},{2,18},{4,20},{6,22},{16,24},{18,26},{20,28},{22,30},{24,8}... | collective-permute-start | bytes 1327112 | tf_op jit(solution)/shard_map/ppermute | solution.py:41
  76.0 23.4 %collective-permute-start.19 = (bf16[2,48,2304]{2,1,0:T(8,128)(2,1)}, bf16[2,48,2304]{2,1,0:T(8,128)(2,1)}, u32[]{:S(2)}, u32[]{:S(2)}) collective-permute-start(bf16[2,48,2304]{2,1,0:T(8,128)(2,1)} %shard_map.330.refs_0_), channel_id=1, source_target_pairs={{0,24},{2,26},{4,28},{6,30},{16,8},{18,10},{20,12},{22,14},{24,0},... | collective-permute-start | bytes 1327112 | tf_op jit(solution)/shard_map/ppermute | solution.py:41
  80.5 34.7 %collective-permute-start.20 = (bf16[2,4,48,1536]{3,2,1,0:T(8,128)(2,1)}, bf16[2,4,48,1536]{3,2,1,0:T(8,128)(2,1)}, u32[]{:S(2)}, u32[]{:S(2)}) collective-permute-start(bf16[2,4,48,1536]{3,2,1,0:T(8,128)(2,1)} %get-tuple-element.263.refs_0_), channel_id=1, source_target_pairs={{0,1},{1,0},{2,3},{3,2},{4,5},{5,4},{6,7},{7,6},{8,9},{9,8},{10,11... | collective-permute-start | bytes 3538952 | tf_op jit(solution)/shard_map/ppermute | solution.py:21
  81.8 33.3 %collective-permute-start.21 = (bf16[2,4,48,1536]{3,2,1,0:T(8,128)(2,1)}, bf16[2,4,48,1536]{3,2,1,0:T(8,128)(2,1)}, u32[]{:S(2)}, u32[]{:S(2)}) collective-permute-start(bf16[2,4,48,1536]{3,2,1,0:T(8,128)(2,1)} %get-tuple-element.265.refs_2_), channel_id=1, source_target_pairs={{0,4},{2,6},{4,0},{6,2},{8,12},{10,14},{12,8},{14,10},{16,20},{18,... | collective-permute-start | bytes 3538952 | tf_op jit(solution)/shard_map/ppermute | solution.py:26
  84.6 30.5 %collective-permute-start.22 = (bf16[2,48,2304]{2,1,0:T(8,128)(2,1)}, bf16[2,48,2304]{2,1,0:T(8,128)(2,1)S(1)}, u32[]{:S(2)}, u32[]{:S(2)}) collective-permute-start(bf16[2,48,2304]{2,1,0:T(8,128)(2,1)} %shard_map.330.refs_0_), channel_id=1, source_target_pairs={{0,8},{2,10},{4,12},{6,14},{16,0},{18,2},{20,4},{22,6},{24,16},{26... | collective-permute-start | bytes 1327112 | tf_op jit(solution)/shard_map/ppermute | solution.py:41
  120.0 14.6 %collective-permute-start.23 = (bf16[2,384,3072]{2,1,0:T(8,128)(2,1)}, bf16[2,384,3072]{2,1,0:T(8,128)(2,1)}, u32[]{:S(2)}, u32[]{:S(2)}) collective-permute-start(bf16[2,384,3072]{2,1,0:T(8,128)(2,1)} %bitcast.23.up_one.down_one), channel_id=1, source_target_pairs={{0,2},{2,0},{4,6},{6,4},{8,10},{10,8},{12,14},{14,12},{16,18},{18,... | collective-permute-start | bytes 14155784 | tf_op jit(solution)/shard_map/ppermute | solution.py:31
  120.2 12.0 %collective-permute-start.26 = (bf16[256,768]{1,0:T(8,128)(2,1)S(1)}, bf16[256,768]{1,0:T(8,128)(2,1)S(1)}, u32[]{:S(2)}, u32[]{:S(2)}) collective-permute-start(bf16[256,768]{1,0:T(8,128)(2,1)S(1)} %get-tuple-element.433), channel_id=1, source_target_pairs={{0,1},{1,0},{2,3},{3,2},{4,5},{5,4},{6,7},{7,6},{8,9},{9,8},{10,11... | collective-permute-start | bytes 1179656 | tf_op jit(solution)/shard_map/ppermute | solution.py:21
  124.2 26.6 %collective-permute-start.24 = (bf16[2,4,48,1152]{3,2,1,0:T(8,128)(2,1)}, bf16[2,4,48,1152]{3,2,1,0:T(8,128)(2,1)}, u32[]{:S(2)}, u32[]{:S(2)}) collective-permute-start(bf16[2,4,48,1152]{3,2,1,0:T(8,128)(2,1)} %get-tuple-element.274.refs_0_), channel_id=1, source_target_pairs={{0,1},{1,0},{2,3},{3,2},{4,5},{5,4},{6,7},{7,6},{8,9},{9,8},{10,11... | collective-permute-start | bytes 2654216 | tf_op jit(solution)/shard_map/ppermute | solution.py:21
  124.9 25.9 %collective-permute-start.25 = (bf16[2,4,48,1152]{3,2,1,0:T(8,128)(2,1)}, bf16[2,4,48,1152]{3,2,1,0:T(8,128)(2,1)}, u32[]{:S(2)}, u32[]{:S(2)}) collective-permute-start(bf16[2,4,48,1152]{3,2,1,0:T(8,128)(2,1)} %get-tuple-element.275.refs_2_), channel_id=1, source_target_pairs={{0,4},{2,6},{4,0},{6,2},{8,12},{10,14},{12,8},{14,10},{16,20},{18,... | collective-permute-start | bytes 2654216 | tf_op jit(solution)/shard_map/ppermute | solution.py:26
  153.7 6.3 %collective-permute-start.27 = (bf16[2,384,2304]{2,1,0:T(8,128)(2,1)S(1)}, bf16[2,384,2304]{2,1,0:T(8,128)(2,1)S(1)}, u32[]{:S(2)}, u32[]{:S(2)}) collective-permute-start(bf16[2,384,2304]{2,1,0:T(8,128)(2,1)S(1)} %bitcast.120), channel_id=1, source_target_pairs={{0,2},{2,0},{4,6},{6,4},{8,10},{10,8},{12,14},{14,12},{16,18},{18,... | collective-permute-start | bytes 10616840 | tf_op jit(solution)/shard_map/ppermute | solution.py:31
  154.1 12.1 %collective-permute-start.28 = (bf16[256,768]{1,0:T(8,128)(2,1)S(1)}, bf16[256,768]{1,0:T(8,128)(2,1)S(1)}, u32[]{:S(2)}, u32[]{:S(2)}) collective-permute-start(bf16[256,768]{1,0:T(8,128)(2,1)S(1)} %slice.423), channel_id=1, source_target_pairs={{0,1},{1,0},{2,3},{3,2},{4,5},{5,4},{6,7},{7,6},{8,9},{9,8},{10,11... | collective-permute-start | bytes 1179656 | tf_op jit(solution)/shard_map/ppermute | solution.py:21
  178.9 17.4 %collective-permute-start.29 = (bf16[256,768]{1,0:T(8,128)(2,1)S(1)}, bf16[256,768]{1,0:T(8,128)(2,1)S(1)}, u32[]{:S(2)}, u32[]{:S(2)}) collective-permute-start(bf16[256,768]{1,0:T(8,128)(2,1)S(1)} %slice.682), channel_id=1, source_target_pairs={{0,1},{1,0},{2,3},{3,2},{4,5},{5,4},{6,7},{7,6},{8,9},{9,8},{10,11... | collective-permute-start | bytes 1179656 | tf_op jit(solution)/shard_map/ppermute | solution.py:21
  195.0 13.3 %collective-permute-start.30 = (bf16[256,768]{1,0:T(8,128)(2,1)S(1)}, bf16[256,768]{1,0:T(8,128)(2,1)S(1)}, u32[]{:S(2)}, u32[]{:S(2)}) collective-permute-start(bf16[256,768]{1,0:T(8,128)(2,1)S(1)} %get-tuple-element.302), channel_id=1, source_target_pairs={{0,1},{1,0},{2,3},{3,2},{4,5},{5,4},{6,7},{7,6},{8,9},{9,8},{10,11... | collective-permute-start | bytes 1179656 | tf_op jit(solution)/shard_map/ppermute | solution.py:21
  217.0 12.8 %collective-permute-start.31 = (bf16[2,384,2304]{2,1,0:T(8,128)(2,1)}, bf16[2,384,2304]{2,1,0:T(8,128)(2,1)}, u32[]{:S(2)}, u32[]{:S(2)}) collective-permute-start(bf16[2,384,2304]{2,1,0:T(8,128)(2,1)} %shard_map.342), channel_id=1, source_target_pairs={{0,2},{2,0},{4,6},{6,4},{8,10},{10,8},{12,14},{14,12},{16,18},{18,... | collective-permute-start | bytes 10616840 | tf_op jit(solution)/shard_map/ppermute | solution.py:31
  251.1 12.2 %collective-permute-start.32 = (bf16[2,384,3072]{2,1,0:T(8,128)(2,1)}, bf16[2,384,3072]{2,1,0:T(8,128)(2,1)S(1)}, u32[]{:S(2)}, u32[]{:S(2)}) collective-permute-start(bf16[2,384,3072]{2,1,0:T(8,128)(2,1)} %shard_map.345), channel_id=1, source_target_pairs={{0,2},{2,0},{4,6},{6,4},{8,10},{10,8},{12,14},{14,12},{16,18},{18,... | collective-permute-start | bytes 14155784 | tf_op jit(solution)/shard_map/ppermute | solution.py:31
  251.8 21.6 %collective-permute-start.33 = (bf16[384,1152]{1,0:T(8,128)(2,1)S(1)}, bf16[384,1152]{1,0:T(8,128)(2,1)S(1)}, u32[]{:S(2)}, u32[]{:S(2)}) collective-permute-start(bf16[384,1152]{1,0:T(8,128)(2,1)S(1)} %get-tuple-element.315), channel_id=1, source_target_pairs={{0,1},{1,0},{2,3},{3,2},{4,5},{5,4},{6,7},{7,6},{8,9},{9,8},{10,11... | collective-permute-start | bytes 2654216 | tf_op jit(solution)/shard_map/ppermute | solution.py:21
  252.6 21.4 %collective-permute-start.34 = (bf16[2,192,1152]{2,1,0:T(8,128)(2,1)S(1)}, bf16[2,192,1152]{2,1,0:T(8,128)(2,1)}, u32[]{:S(2)}, u32[]{:S(2)}) collective-permute-start(bf16[2,192,1152]{2,1,0:T(8,128)(2,1)S(1)} %get-tuple-element.316), channel_id=1, source_target_pairs={{0,4},{2,6},{4,0},{6,2},{8,12},{10,14},{12,8},{14,10},{16,20},{18,... | collective-permute-start | bytes 2654216 | tf_op jit(solution)/shard_map/ppermute | solution.py:26
  263.3 41.6 %copy-start.4 = (bf16[768,768]{1,0:T(8,128)(2,1)}, bf16[768,768]{1,0:T(8,128)(2,1)S(1)}, u32[]{:S(2)}) copy-start(bf16[768,768]{1,0:T(8,128)(2,1)S(1)} %get-tuple-element.364.d_mid.d_mid_low.refs_4_) | copy-start | bytes 3538948
  275.8 15.3 %collective-permute-start.36 = (bf16[192,1152]{1,0:T(8,128)(2,1)S(1)}, bf16[192,1152]{1,0:T(8,128)(2,1)S(1)}, u32[]{:S(2)}, u32[]{:S(2)}) collective-permute-start(bf16[192,1152]{1,0:T(8,128)(2,1)S(1)} %fusion.21), channel_id=1, source_target_pairs={{0,1},{1,0},{2,3},{3,2},{4,5},{5,4},{6,7},{7,6},{8,9},{9,8},{10,11... | collective-permute-start | bytes 1327112 | tf_op jit(solution)/shard_map/ppermute | solution.py:21
  277.1 14.0 %collective-permute-start.35 = (bf16[192,1152]{1,0:T(8,128)(2,1)S(1)}, bf16[192,1152]{1,0:T(8,128)(2,1)S(1)}, u32[]{:S(2)}, u32[]{:S(2)}) collective-permute-start(bf16[192,1152]{1,0:T(8,128)(2,1)S(1)} %slice.680), channel_id=1, source_target_pairs={{0,4},{2,6},{4,0},{6,2},{8,12},{10,14},{12,8},{14,10},{16,20},{18,... | collective-permute-start | bytes 1327112 | tf_op jit(solution)/shard_map/ppermute | solution.py:26
  279.7 32.5 %collective-permute-start.38 = (bf16[384,1536]{1,0:T(8,128)(2,1)}, bf16[384,1536]{1,0:T(8,128)(2,1)}, u32[]{:S(2)}, u32[]{:S(2)}) collective-permute-start(bf16[384,1536]{1,0:T(8,128)(2,1)} %get-tuple-element.325), channel_id=1, source_target_pairs={{0,1},{1,0},{2,3},{3,2},{4,5},{5,4},{6,7},{7,6},{8,9},{9,8},{10,11... | collective-permute-start | bytes 3538952 | tf_op jit(solution)/shard_map/ppermute | solution.py:21
  280.4 32.7 %collective-permute-start.39 = (bf16[2,192,1536]{2,1,0:T(8,128)(2,1)}, bf16[2,192,1536]{2,1,0:T(8,128)(2,1)}, u32[]{:S(2)}, u32[]{:S(2)}) collective-permute-start(bf16[2,192,1536]{2,1,0:T(8,128)(2,1)} %get-tuple-element.326), channel_id=1, source_target_pairs={{0,4},{2,6},{4,0},{6,2},{8,12},{10,14},{12,8},{14,10},{16,20},{18,... | collective-permute-start | bytes 3538952 | tf_op jit(solution)/shard_map/ppermute | solution.py:26
  309.4 20.9 %collective-permute-start.37 = (bf16[2,384,1536]{2,1,0:T(8,128)(2,1)}, bf16[2,384,1536]{2,1,0:T(8,128)(2,1)}, u32[]{:S(2)}, u32[]{:S(2)}) collective-permute-start(bf16[2,384,1536]{2,1,0:T(8,128)(2,1)} %shard_map.350), channel_id=1, source_target_pairs={{0,2},{2,0},{4,6},{6,4},{8,10},{10,8},{12,14},{14,12},{16,18},{18,... | collective-permute-start | bytes 7077896 | tf_op jit(solution)/shard_map/ppermute | solution.py:31
  309.6 4.7 %collective-permute-start.40 = (f32[22,768]{1,0:T(8,128)S(1)}, f32[22,768]{1,0:T(8,128)S(1)}, u32[]{:S(2)}, u32[]{:S(2)}) collective-permute-start(f32[22,768]{1,0:T(8,128)S(1)} %pad_maximum_fusion.10), channel_id=1, source_target_pairs={{0,1},{1,0},{2,3},{3,2},{4,5},{5,4},{6,7},{7,6},{8,9},{9,8},{10,11... | collective-permute-start | bytes 202760 | tf_op jit(solution)/shard_map/ppermute | solution.py:21
  316.5 15.0 %collective-permute-start.44 = (bf16[192,1536]{1,0:T(8,128)(2,1)S(1)}, bf16[192,1536]{1,0:T(8,128)(2,1)S(1)}, u32[]{:S(2)}, u32[]{:S(2)}) collective-permute-start(bf16[192,1536]{1,0:T(8,128)(2,1)S(1)} %fusion.17), channel_id=1, source_target_pairs={{0,1},{1,0},{2,3},{3,2},{4,5},{5,4},{6,7},{7,6},{8,9},{9,8},{10,11... | collective-permute-start | bytes 1769480 | tf_op jit(solution)/shard_map/ppermute | solution.py:21
  319.7 17.5 %collective-permute-start.43 = (bf16[192,1536]{1,0:T(8,128)(2,1)S(1)}, bf16[192,1536]{1,0:T(8,128)(2,1)S(1)}, u32[]{:S(2)}, u32[]{:S(2)}) collective-permute-start(bf16[192,1536]{1,0:T(8,128)(2,1)S(1)} %slice.679), channel_id=1, source_target_pairs={{0,4},{2,6},{4,0},{6,2},{8,12},{10,14},{12,8},{14,10},{16,20},{18,... | collective-permute-start | bytes 1769480 | tf_op jit(solution)/shard_map/ppermute | solution.py:26
  321.8 22.9 %collective-permute-start.45 = (bf16[48,2304]{1,0:T(8,128)(2,1)S(1)}, bf16[48,2304]{1,0:T(8,128)(2,1)S(1)}, u32[]{:S(2)}, u32[]{:S(2)}) collective-permute-start(bf16[48,2304]{1,0:T(8,128)(2,1)S(1)} %copy-done.95), channel_id=1, source_target_pairs={{0,8},{2,10},{4,12},{6,14},{16,0},{18,2},{20,4},{22,6},{24,16},{26... | collective-permute-start | bytes 663560 | tf_op jit(solution)/shard_map/ppermute | solution.py:41
  327.8 17.9 %collective-permute-start.46 = (bf16[48,2304]{1,0:T(8,128)(2,1)S(1)}, bf16[48,2304]{1,0:T(8,128)(2,1)S(1)}, u32[]{:S(2)}, u32[]{:S(2)}) collective-permute-start(bf16[48,2304]{1,0:T(8,128)(2,1)S(1)} %copy-done.94), channel_id=1, source_target_pairs={{0,24},{2,26},{4,28},{6,30},{16,8},{18,10},{20,12},{22,14},{24,0},... | collective-permute-start | bytes 663560 | tf_op jit(solution)/shard_map/ppermute | solution.py:41
  330.3 16.0 %collective-permute-start.47 = (bf16[48,2304]{1,0:T(8,128)(2,1)S(1)}, bf16[48,2304]{1,0:T(8,128)(2,1)S(1)}, u32[]{:S(2)}, u32[]{:S(2)}) collective-permute-start(bf16[48,2304]{1,0:T(8,128)(2,1)S(1)} %get-tuple-element.437), channel_id=1, source_target_pairs={{0,16},{2,18},{4,20},{6,22},{16,24},{18,26},{20,28},{22,30},{24,8}... | collective-permute-start | bytes 663560 | tf_op jit(solution)/shard_map/ppermute | solution.py:41
  331.5 14.8 %collective-permute-start.48 = (f32[22,768]{1,0:T(8,128)S(1)}, f32[22,768]{1,0:T(8,128)S(1)}, u32[]{:S(2)}, u32[]{:S(2)}) collective-permute-start(f32[22,768]{1,0:T(8,128)S(1)} %fusion.95), channel_id=1, source_target_pairs={{0,2},{2,0},{4,6},{6,4},{8,10},{10,8},{12,14},{14,12},{16,18},{18,... | collective-permute-start | bytes 202760 | tf_op jit(solution)/shard_map/ppermute | solution.py:783
  337.2 36.5 %collective-permute-start.50 = (bf16[256,768]{1,0:T(8,128)(2,1)S(1)}, bf16[256,768]{1,0:T(8,128)(2,1)S(1)}, u32[]{:S(2)}, u32[]{:S(2)}) collective-permute-start(bf16[256,768]{1,0:T(8,128)(2,1)S(1)} %copy-done.72), channel_id=1, source_target_pairs={{0,1},{1,0},{2,3},{3,2},{4,5},{5,4},{6,7},{7,6},{8,9},{9,8},{10,11... | collective-permute-start | bytes 1179656 | tf_op jit(solution)/shard_map/ppermute | solution.py:21
  344.7 16.8 %collective-permute-start.41 = (bf16[384,768]{1,0:T(8,128)(2,1)S(1)}, bf16[384,768]{1,0:T(8,128)(2,1)S(1)}, u32[]{:S(2)}, u32[]{:S(2)}) collective-permute-start(bf16[384,768]{1,0:T(8,128)(2,1)S(1)} %get-tuple-element.362), channel_id=1, source_target_pairs={{0,1},{1,0},{2,3},{3,2},{4,5},{5,4},{6,7},{7,6},{8,9},{9,8},{10,11... | collective-permute-start | bytes 1769480 | tf_op jit(solution)/shard_map/ppermute | solution.py:21
  345.8 18.1 %collective-permute-start.42 = (bf16[2,192,768]{2,1,0:T(8,128)(2,1)S(1)}, bf16[2,192,768]{2,1,0:T(8,128)(2,1)S(1)}, u32[]{:S(2)}, u32[]{:S(2)}) collective-permute-start(bf16[2,192,768]{2,1,0:T(8,128)(2,1)S(1)} %get-tuple-element.363), channel_id=1, source_target_pairs={{0,4},{2,6},{4,0},{6,2},{8,12},{10,14},{12,8},{14,10},{16,20},{18,... | collective-permute-start | bytes 1769480 | tf_op jit(solution)/shard_map/ppermute | solution.py:26
  346.9 37.8 %collective-permute-start.54 = (bf16[48,3072]{1,0:T(8,128)(2,1)S(1)}, bf16[48,3072]{1,0:T(8,128)(2,1)S(1)}, u32[]{:S(2)}, u32[]{:S(2)}) collective-permute-start(bf16[48,3072]{1,0:T(8,128)(2,1)S(1)} %get-tuple-element.430), channel_id=1, source_target_pairs={{0,8},{2,10},{4,12},{6,14},{16,0},{18,2},{20,4},{22,6},{24,16},{26... | collective-permute-start | bytes 884744 | tf_op jit(solution)/shard_map/ppermute | solution.py:41
  349.7 19.2 %collective-permute-start.49 = (f32[22,768]{1,0:T(8,128)S(1)}, f32[22,768]{1,0:T(8,128)S(1)}, u32[]{:S(2)}, u32[]{:S(2)}) collective-permute-start(f32[22,768]{1,0:T(8,128)S(1)} %add.233), channel_id=1, source_target_pairs={{0,4},{2,6},{4,0},{6,2},{8,12},{10,14},{12,8},{14,10},{16,20},{18,... | collective-permute-start | bytes 202760 | tf_op jit(solution)/shard_map/ppermute | solution.py:783
  361.4 25.0 %collective-permute-start.55 = (bf16[48,3072]{1,0:T(8,128)(2,1)S(1)}, bf16[48,3072]{1,0:T(8,128)(2,1)S(1)}, u32[]{:S(2)}, u32[]{:S(2)}) collective-permute-start(bf16[48,3072]{1,0:T(8,128)(2,1)S(1)} %get-tuple-element.429), channel_id=1, source_target_pairs={{0,24},{2,26},{4,28},{6,30},{16,8},{18,10},{20,12},{22,14},{24,0},... | collective-permute-start | bytes 884744 | tf_op jit(solution)/shard_map/ppermute | solution.py:41
  363.9 22.5 %collective-permute-start.56 = (bf16[48,3072]{1,0:T(8,128)(2,1)S(1)}, bf16[48,3072]{1,0:T(8,128)(2,1)S(1)}, u32[]{:S(2)}, u32[]{:S(2)}) collective-permute-start(bf16[48,3072]{1,0:T(8,128)(2,1)S(1)} %get-tuple-element.428), channel_id=1, source_target_pairs={{0,16},{2,18},{4,20},{6,22},{16,24},{18,26},{20,28},{22,30},{24,8}... | collective-permute-start | bytes 884744 | tf_op jit(solution)/shard_map/ppermute | solution.py:41
  368.9 12.1 %collective-permute-start.51 = (bf16[256,768]{1,0:T(8,128)(2,1)S(1)}, bf16[256,768]{1,0:T(8,128)(2,1)S(1)}, u32[]{:S(2)}, u32[]{:S(2)}) collective-permute-start(bf16[256,768]{1,0:T(8,128)(2,1)S(1)} %slice.681), channel_id=1, source_target_pairs={{0,1},{1,0},{2,3},{3,2},{4,5},{5,4},{6,7},{7,6},{8,9},{9,8},{10,11... | collective-permute-start | bytes 1179656 | tf_op jit(solution)/shard_map/ppermute | solution.py:21
  373.7 17.1 %collective-permute-start.53 = (bf16[192,768]{1,0:T(8,128)(2,1)S(1)}, bf16[192,768]{1,0:T(8,128)(2,1)S(1)}, u32[]{:S(2)}, u32[]{:S(2)}) collective-permute-start(bf16[192,768]{1,0:T(8,128)(2,1)S(1)} %fusion.24), channel_id=1, source_target_pairs={{0,1},{1,0},{2,3},{3,2},{4,5},{5,4},{6,7},{7,6},{8,9},{9,8},{10,11... | collective-permute-start | bytes 884744 | tf_op jit(solution)/shard_map/ppermute | solution.py:21
  380.9 9.9 %collective-permute-start.52 = (bf16[192,768]{1,0:T(8,128)(2,1)S(1)}, bf16[192,768]{1,0:T(8,128)(2,1)S(1)}, u32[]{:S(2)}, u32[]{:S(2)}) collective-permute-start(bf16[192,768]{1,0:T(8,128)(2,1)S(1)} %slice.683), channel_id=1, source_target_pairs={{0,4},{2,6},{4,0},{6,2},{8,12},{10,14},{12,8},{14,10},{16,20},{18,... | collective-permute-start | bytes 884744 | tf_op jit(solution)/shard_map/ppermute | solution.py:26
  384.6 6.2 %collective-permute-start.57 = (f32[22,768]{1,0:T(8,128)S(1)}, f32[22,768]{1,0:T(8,128)S(1)}, u32[]{:S(2)}, u32[]{:S(2)}) collective-permute-start(f32[22,768]{1,0:T(8,128)S(1)} %add.239), channel_id=1, source_target_pairs={{0,8},{2,10},{4,12},{6,14},{8,0},{10,2},{12,4},{14,6},{16,24},{18,... | collective-permute-start | bytes 202760 | tf_op jit(solution)/shard_map/ppermute | solution.py:783
  391.1 13.8 %collective-permute-start.58 = (bf16[48,1536]{1,0:T(8,128)(2,1)S(1)}, bf16[48,1536]{1,0:T(8,128)(2,1)S(1)}, u32[]{:S(2)}, u32[]{:S(2)}) collective-permute-start(bf16[48,1536]{1,0:T(8,128)(2,1)S(1)} %get-tuple-element.444), channel_id=1, source_target_pairs={{0,8},{2,10},{4,12},{6,14},{16,0},{18,2},{20,4},{22,6},{24,16},{26... | collective-permute-start | bytes 442376 | tf_op jit(solution)/shard_map/ppermute | solution.py:41
  391.1 13.7 %collective-permute-start.59 = (bf16[48,1536]{1,0:T(8,128)(2,1)S(1)}, bf16[48,1536]{1,0:T(8,128)(2,1)S(1)}, u32[]{:S(2)}, u32[]{:S(2)}) collective-permute-start(bf16[48,1536]{1,0:T(8,128)(2,1)S(1)} %get-tuple-element.443), channel_id=1, source_target_pairs={{0,24},{2,26},{4,28},{6,30},{16,8},{18,10},{20,12},{22,14},{24,0},... | collective-permute-start | bytes 442376 | tf_op jit(solution)/shard_map/ppermute | solution.py:41
  395.5 9.4 %collective-permute-start.60 = (bf16[48,1536]{1,0:T(8,128)(2,1)S(1)}, bf16[48,1536]{1,0:T(8,128)(2,1)S(1)}, u32[]{:S(2)}, u32[]{:S(2)}) collective-permute-start(bf16[48,1536]{1,0:T(8,128)(2,1)S(1)} %get-tuple-element.442), channel_id=1, source_target_pairs={{0,16},{2,18},{4,20},{6,22},{16,24},{18,26},{20,28},{22,30},{24,8}... | collective-permute-start | bytes 442376 | tf_op jit(solution)/shard_map/ppermute | solution.py:41
  397.5 7.4 %collective-permute-start.61 = (f32[22,768]{1,0:T(8,128)S(1)}, f32[22,768]{1,0:T(8,128)S(1)}, u32[]{:S(2)}, u32[]{:S(2)}) collective-permute-start(f32[22,768]{1,0:T(8,128)S(1)} %add.242), channel_id=1, source_target_pairs={{0,16},{2,18},{4,20},{6,22},{8,24},{10,26},{12,28},{14,30},{16,0},... | collective-permute-start | bytes 202760 | tf_op jit(solution)/shard_map/ppermute | solution.py:783
  (102 other events, 802.3 us)
